TPU v7x, 32 devices: a whole 2x2x4 slice. The times are simulated.
32 devices in a mesh: users: 4 (over y, x), ctx: 8 (over z, core).
Axes of the slice: x: 2, y: 2, z: 4, core: 2. Of those that a mesh axis runs over, the one named last changes fastest.
Arguments:
- cand_feat: bfloat16 [12288, 1024], P(('users', 'ctx')), may hold values from -27 to 27
- cand_user: int32 [12288, 1], P(('users', 'ctx')), may hold values from 0 to 3; in each aligned block of 384 rows (0 to 383, 384 to 767, ...) at most 192 rows name the same one
- hist_kv: bfloat16 [1, 4, 1024, 2048], P(None, 'users', 'ctx'), may hold values from -27 to 27
- hist_mask: int32 [4, 8], P('users'), may hold values from 0 to 1, as said below
- gain_in: float32 [1, 1024], replicated, may hold values from 0.25 to 1.75
- w_uq: bfloat16 [1, 1024, 2048], replicated, may hold values from -0.1875 to 0.1875
- gain_attn: float32 [1, 1024], replicated, may hold values from 0.25 to 1.75
- w_out: bfloat16 [1, 1024, 1024], replicated, may hold values from -0.1875 to 0.1875
Outputs:
- cand_out: bfloat16 [12288, 1024], P(('users', 'ctx'))
Inputs may be any that keep to these rules, and one draw needn't show every extreme that they name: `cand_user`: within the rows of one device no user is named by more than 192 rows, a bound that some block reaches of them. `hist_mask`: every user has exactly 4 ones among its 8 blocks.
All inputs are finite; a program needn't handle non-finite values.
Results may differ from a plain program's by a relative error of at most 0.0039.
Values may be sent and summed in bfloat16 or wider, within the bound.
No kernel may reach another device: no remote copies, remote signals or barrier semaphores. Data moves between devices by JAX's collectives and lax.ppermute only.
A program may use at most 128 MiB of HBM per device.

v0:
```python
import jax
import jax.numpy as jnp
from jax import lax
from jax.sharding import PartitionSpec as P

H = 8
BLK = 128


def centred_norm(inputs):
    middle = jnp.mean(inputs, axis=-1, keepdims=True)
    shifted = inputs - middle
    spread = jnp.mean(shifted * shifted, axis=-1, keepdims=True)
    return shifted * lax.rsqrt(spread + 1e-05)


def score_block(running, query_heads, kv_block):
    head_count = query_heads.shape[1]
    head_size = query_heads.shape[2]
    feat_width = head_count * head_size
    key_count = kv_block.shape[0]
    key_heads = kv_block[:, :feat_width].reshape(key_count, head_count, head_size)
    value_heads = kv_block[:, feat_width:].reshape(key_count, head_count, head_size)
    scores = jnp.einsum(
        "shd,khd->hsk", query_heads, key_heads, preferred_element_type=jnp.float32
    ) * head_size ** (-0.5)
    attn_weights = jax.nn.silu(scores).astype(jnp.bfloat16)
    combined = jnp.einsum(
        "hsk,khd->shd", attn_weights, value_heads, preferred_element_type=jnp.float32
    )
    return running + combined.reshape(running.shape)


def on_device(cand_feat, cand_user, hist_kv, hist_mask, gain_in, w_uq, gain_attn, w_out):
    owner_count = lax.axis_size("users")
    row_count, feat_width = cand_feat.shape
    slot_cap = 2 * row_count // owner_count
    slot_rows = owner_count * slot_cap
    target_user = cand_user[:, 0]
    one_hot = (target_user[:, None] == jnp.arange(owner_count, dtype=jnp.int32)[None, :]).astype(
        jnp.int32
    )
    earlier = jnp.cumsum(one_hot, axis=0) - one_hot
    send_slot = target_user * slot_cap + jnp.sum(earlier * one_hot, axis=1)
    outgoing = jnp.zeros((slot_rows, feat_width), jnp.bfloat16).at[send_slot].set(cand_feat)
    arrived = lax.all_to_all(
        outgoing.reshape(owner_count, slot_cap, feat_width),
        "users",
        split_axis=0,
        concat_axis=0,
        tiled=True,
    )
    hidden = arrived.reshape(slot_rows, feat_width)
    block_mask = hist_mask[0]
    block_count = block_mask.shape[0]
    block_range = jnp.arange(block_count, dtype=jnp.int32)
    residual = hidden.astype(jnp.float32)
    normed = (centred_norm(residual) * gain_in[0]).astype(jnp.bfloat16)
    projected = jnp.dot(normed, w_uq[0], preferred_element_type=jnp.float32)
    gate_vals = jax.nn.silu(projected[:, :feat_width])
    queries = jax.nn.silu(projected[:, feat_width:]).astype(jnp.bfloat16)
    query_heads = queries.reshape(slot_rows, H, feat_width // H)
    local_kv = hist_kv[0, 0]
    zero_sum = jnp.zeros((slot_rows, feat_width), jnp.float32)
    shard_rows = lax.all_gather(local_kv, "ctx", axis=0, tiled=True)
    piece_blocks = shard_rows.shape[0] // BLK
    key_blocks = shard_rows.reshape(piece_blocks, BLK, shard_rows.shape[1])
    block_ids = jnp.arange(piece_blocks, dtype=jnp.int32)

    def walk_block(carried, packed):
        block_keys, block_id = packed
        is_live = jnp.sum(jnp.where(block_range == block_id, block_mask, 0))
        updated = lax.cond(
            is_live > 0,
            lambda total: score_block(total, query_heads, block_keys),
            lambda total: total,
            carried,
        )
        return (updated, None)

    result, unused = lax.scan(walk_block, zero_sum, (key_blocks, block_ids))
    mixed = (centred_norm(result) * gain_attn[0] * gate_vals).astype(jnp.bfloat16)
    hidden = (residual + jnp.dot(mixed, w_out[0], preferred_element_type=jnp.float32)).astype(
        jnp.bfloat16
    )
    returned = lax.all_to_all(
        hidden.reshape(owner_count, slot_cap, feat_width),
        "users",
        split_axis=0,
        concat_axis=0,
        tiled=True,
    )
    return returned.reshape(slot_rows, feat_width)[send_slot]


def solution(mesh):
    in_specs = (
        P(("users", "ctx"), None),
        P(("users", "ctx"), None),
        P(None, "users", "ctx", None),
        P("users", None),
        P(),
        P(),
        P(),
        P(),
    )
    out_specs = P(("users", "ctx"), None)
    return jax.shard_map(
        on_device, mesh=mesh, in_specs=in_specs, out_specs=out_specs, check_vma=False
    )
```

profile of v0, /device:TPU:0, one launch (start us, length us, event | category | flops | bytes accessed | tf_op | source)
XLA Modules:
  0.0 180.5 jit_solution(16282595997286634961)
XLA Ops:
  10.4 4.0 %scatter_custom_fusion = bf16[768,1024]{1,0:T(8,128)(2,1)} fusion(s32[384]{0:T(512)S(1)} %fusion.24, bf16[384,1024]{1,0:T(8,128)(2,1)} %param.12, bf16[]{:T(256)} %constant.41.clone.1), kind=kCustom, calls=%fused_computation.31 | custom fusion | bytes 1573376 | tf_op jit(solution)/shard_map/scatter | solution.py:45
  14.4 5.3 %all-to-all-start = ((bf16[4,192,1024]{2,1,0:T(8,128)(2,1)}), bf16[4,192,1024]{2,1,0:T(8,128)(2,1)}, u32[]{:S(2)}, u32[]{:S(2)}) async-start(bf16[4,192,1024]{2,1,0:T(8,128)(2,1)} %bitcast.77), calls=%async_computation | async-start | bytes 3145728 | tf_op jit(solution)/shard_map/all_to_all | solution.py:46
  19.7 20.2 %all-to-all-done = bf16[4,192,1024]{2,1,0:T(8,128)(2,1)} async-done(((bf16[4,192,1024]{2,1,0:T(8,128)(2,1)}), bf16[4,192,1024]{2,1,0:T(8,128)(2,1)}, u32[]{:S(2)}, u32[]{:S(2)}) %all-to-all-start) | async-done | bytes 1572896 | tf_op jit(solution)/shard_map/all_to_all | solution.py:46
  39.9 1.8 %convert_reduce_fusion = f32[4,192]{1,0:T(4,128)S(1)} fusion(bf16[4,192,1024]{2,1,0:T(8,128)(2,1)} %all-to-all-done), kind=kLoop, calls=%fused_computation.26 | loop fusion | flops 1572096 | bytes 1575936 | tf_op jit(solution)/shard_map/reduce_sum | solution.py:11
  41.7 2.0 %multiply_reduce_fusion.1 = f32[4,192]{1,0:T(4,128)S(1)} fusion(bf16[4,192,1024]{2,1,0:T(8,128)(2,1)} %all-to-all-done, f32[4,192]{1,0:T(4,128)S(1)} %broadcast_multiply_fusion.1), kind=kLoop, calls=%fused_computation.25 | loop fusion | flops 3144960 | bytes 1579008 | tf_op jit(solution)/shard_map/reduce_sum | solution.py:13
  43.8 2.0 %multiply_convert_fusion.2 = bf16[4,192,1024]{2,1,0:T(8,128)(2,1)S(1)} fusion(bf16[4,192,1024]{2,1,0:T(8,128)(2,1)} %all-to-all-done, f32[1024]{0:T(1024)S(1)} %bitcast.84, f32[4,192]{1,0:T(4,128)S(1)} %add_rsqrt_fusion.1, f32[4,192]{1,0:T(4,128)S(1)} %broadcast_multiply_fusion.1), kind=kLoop, calls=%fused_computation.24 | loop fusion | flops 3932160 | bytes 3155968 | tf_op jit(solution)/shard_map/convert_element_type | solution.py:58
  45.7 3.4 %fusion.10 = f32[768,2048]{1,0:T(8,128)S(1)} fusion(bf16[768,1024]{1,0:T(8,128)(2,1)S(1)} %bitcast.80, bf16[1,1024,2048]{2,1,0:T(8,128)(2,1)S(1)} %copy-done.5), kind=kOutput, calls=%fused_computation.17 | convolution fusion | flops 3221225472 | bytes 12058624 | tf_op jit(solution)/shard_map/dot_general | solution.py:59
  49.2 2.7 %copy-done.2 = f32[768,2048]{1,0:T(8,128)} copy-done((f32[768,2048]{1,0:T(8,128)}, f32[768,2048]{1,0:T(8,128)S(1)}, u32[]{:S(2)}) %copy-start.2) | copy-done | bytes 6291480
  51.8 2.0 %copy_bitcast_fusion = bf16[768,8,128]{2,0,1:T(8,128)(2,1)} fusion(f32[768,2048]{1,0:T(8,128)S(1)} %fusion.10), kind=kLoop, calls=%fused_computation.29 | loop fusion | flops 3932160 | bytes 4718592
  53.8 5.0 %all-gather.3.cloned.1.call-done = bf16[1,1,1024,2048]{3,2,1,0:T(8,128)(2,1)} async-done(((bf16[1,1,128,2048]{3,2,1,0:T(8,128)(2,1)}), bf16[1,1,1024,2048]{3,2,1,0:T(8,128)(2,1)}) %all-gather.3.cloned.1.call-update) | async-done | bytes 4194320 | tf_op jit(solution)/shard_map/all_gather | solution.py:65
  58.8 6.5 %copy.14 = bf16[8,128,2048]{1,2,0:T(8,128)(2,1)} copy(bf16[8,128,2048]{2,1,0:T(8,128)(2,1)} %bitcast.78) | data formatting | bytes 8388608
  65.4 1.8 %broadcast_in_dim.10 = f32[768,1024]{0,1:T(8,128)} broadcast(f32[]{:T(128)} %constant.45.clone.1), dimensions={} | broadcast | bytes 3145732 | tf_op jit(solution)/shard_map/broadcast_in_dim | solution.py:64
  67.2 62.9 %while.15 = (s32[]{:T(128)}, f32[768,1024]{0,1:T(8,128)}, s32[8]{0:T(128)S(1)}, s32[8]{0:T(128)S(1)}, bf16[8,128,2048]{1,2,0:T(8,128)(2,1)}, /*index=5*/bf16[768,8,128]{2,0,1:T(8,128)(2,1)}, s32[]{:T(128)}, s32[]{:T(128)}) while((s32[]{:T(128)}, f32[768,1024]{0,1:T(8,128)}, s32[8]{0:T(128)S(1)}, s32[8]{0:T(128)S(1)}, ...), condition=%wide.region_10.11_spmd.clone, body=%wide.region_6.10_spmd.clone.sunk | while | flops 408158240 | bytes 16777444 | solution.py:81
  72.2 10.7 %conditional.3 = (f32[768,1024]{0,1:T(8,128)}) conditional(s32[]{:T(128)} %convert_element_type.73, f32[768,1024]{0,1:T(8,128)} %get-tuple-element.175, (bf16[8,128,2048]{1,2,0:T(8,128)(2,1)}, s32[]{:T(128)}, bf16[768,8,128]{2,0,1:T(8,128)(2,1)}, f32[768,1024]{0,1:T(8,128)}) %tuple.38), branch_computations={%region_8.8_spmd, %region_9.9_spmd} | conditional | flops 408158208 | bytes 16777228 | solution.py:73
  73.3 4.7 %fusion.4 = f32[8,768,128]{1,2,0:T(8,128)} fusion(bf16[128,8,128]{0,2,1:T(8,128)(2,1)S(1)} %bitcast.76, bf16[128,8,128]{0,2,1:T(8,128)(2,1)S(1)} %bitcast.75, bf16[768,8,128]{2,0,1:T(8,128)(2,1)} %get-tuple-element.76), kind=kOutput, calls=%fused_computation.9 | convolution fusion | flops 407371776 | bytes 5242880 | tf_op jit(solution)/shard_map/while/body/eval_jaxpr/cond/branch_1_fun/hsk,khd->shd/dot_general | solution.py:28
  78.0 4.9 %bitcast_add_fusion = f32[768,1024]{0,1:T(8,128)} fusion(f32[768,1024]{0,1:T(8,128)} %get-tuple-element.73, f32[8,768,128]{1,2,0:T(8,128)} %fusion.4), kind=kLoop, calls=%fused_computation.2 | loop fusion | flops 786432 | bytes 9437184 | tf_op jit(solution)/shard_map/while/body/eval_jaxpr/cond/branch_1_fun/add | solution.py:31
  85.4 10.7 %conditional.3 = (f32[768,1024]{0,1:T(8,128)}) conditional(s32[]{:T(128)} %convert_element_type.73, f32[768,1024]{0,1:T(8,128)} %get-tuple-element.175, (bf16[8,128,2048]{1,2,0:T(8,128)(2,1)}, s32[]{:T(128)}, bf16[768,8,128]{2,0,1:T(8,128)(2,1)}, f32[768,1024]{0,1:T(8,128)}) %tuple.38), branch_computations={%region_8.8_spmd, %region_9.9_spmd} | conditional | flops 408158208 | bytes 16777228 | solution.py:73
  86.5 4.7 %fusion.4 = f32[8,768,128]{1,2,0:T(8,128)} fusion(bf16[128,8,128]{0,2,1:T(8,128)(2,1)S(1)} %bitcast.76, bf16[128,8,128]{0,2,1:T(8,128)(2,1)S(1)} %bitcast.75, bf16[768,8,128]{2,0,1:T(8,128)(2,1)} %get-tuple-element.76), kind=kOutput, calls=%fused_computation.9 | convolution fusion | flops 407371776 | bytes 5242880 | tf_op jit(solution)/shard_map/while/body/eval_jaxpr/cond/branch_1_fun/hsk,khd->shd/dot_general | solution.py:28
  91.3 4.9 %bitcast_add_fusion = f32[768,1024]{0,1:T(8,128)} fusion(f32[768,1024]{0,1:T(8,128)} %get-tuple-element.73, f32[8,768,128]{1,2,0:T(8,128)} %fusion.4), kind=kLoop, calls=%fused_computation.2 | loop fusion | flops 786432 | bytes 9437184 | tf_op jit(solution)/shard_map/while/body/eval_jaxpr/cond/branch_1_fun/add | solution.py:31
  98.6 10.7 %conditional.3 = (f32[768,1024]{0,1:T(8,128)}) conditional(s32[]{:T(128)} %convert_element_type.73, f32[768,1024]{0,1:T(8,128)} %get-tuple-element.175, (bf16[8,128,2048]{1,2,0:T(8,128)(2,1)}, s32[]{:T(128)}, bf16[768,8,128]{2,0,1:T(8,128)(2,1)}, f32[768,1024]{0,1:T(8,128)}) %tuple.38), branch_computations={%region_8.8_spmd, %region_9.9_spmd} | conditional | flops 408158208 | bytes 16777228 | solution.py:73
  99.7 4.7 %fusion.4 = f32[8,768,128]{1,2,0:T(8,128)} fusion(bf16[128,8,128]{0,2,1:T(8,128)(2,1)S(1)} %bitcast.76, bf16[128,8,128]{0,2,1:T(8,128)(2,1)S(1)} %bitcast.75, bf16[768,8,128]{2,0,1:T(8,128)(2,1)} %get-tuple-element.76), kind=kOutput, calls=%fused_computation.9 | convolution fusion | flops 407371776 | bytes 5242880 | tf_op jit(solution)/shard_map/while/body/eval_jaxpr/cond/branch_1_fun/hsk,khd->shd/dot_general | solution.py:28
  104.5 4.9 %bitcast_add_fusion = f32[768,1024]{0,1:T(8,128)} fusion(f32[768,1024]{0,1:T(8,128)} %get-tuple-element.73, f32[8,768,128]{1,2,0:T(8,128)} %fusion.4), kind=kLoop, calls=%fused_computation.2 | loop fusion | flops 786432 | bytes 9437184 | tf_op jit(solution)/shard_map/while/body/eval_jaxpr/cond/branch_1_fun/add | solution.py:31
  114.3 10.7 %conditional.3 = (f32[768,1024]{0,1:T(8,128)}) conditional(s32[]{:T(128)} %convert_element_type.73, f32[768,1024]{0,1:T(8,128)} %get-tuple-element.175, (bf16[8,128,2048]{1,2,0:T(8,128)(2,1)}, s32[]{:T(128)}, bf16[768,8,128]{2,0,1:T(8,128)(2,1)}, f32[768,1024]{0,1:T(8,128)}) %tuple.38), branch_computations={%region_8.8_spmd, %region_9.9_spmd} | conditional | flops 408158208 | bytes 16777228 | solution.py:73
  115.5 4.7 %fusion.4 = f32[8,768,128]{1,2,0:T(8,128)} fusion(bf16[128,8,128]{0,2,1:T(8,128)(2,1)S(1)} %bitcast.76, bf16[128,8,128]{0,2,1:T(8,128)(2,1)S(1)} %bitcast.75, bf16[768,8,128]{2,0,1:T(8,128)(2,1)} %get-tuple-element.76), kind=kOutput, calls=%fused_computation.9 | convolution fusion | flops 407371776 | bytes 5242880 | tf_op jit(solution)/shard_map/while/body/eval_jaxpr/cond/branch_1_fun/hsk,khd->shd/dot_general | solution.py:28
  120.2 4.9 %bitcast_add_fusion = f32[768,1024]{0,1:T(8,128)} fusion(f32[768,1024]{0,1:T(8,128)} %get-tuple-element.73, f32[8,768,128]{1,2,0:T(8,128)} %fusion.4), kind=kLoop, calls=%fused_computation.2 | loop fusion | flops 786432 | bytes 9437184 | tf_op jit(solution)/shard_map/while/body/eval_jaxpr/cond/branch_1_fun/add | solution.py:31
  130.1 3.6 %copy.16 = f32[768,1024]{1,0:T(8,128)} copy(f32[768,1024]{0,1:T(8,128)} %get-tuple-element.86) | data formatting | bytes 6291456 | tf_op jit(solution)/shard_map/while | solution.py:81
  133.7 2.1 %reduce_sum.61 = f32[768]{0:T(1024)S(1)} reduce(f32[768,1024]{0,1:T(8,128)} %get-tuple-element.86, f32[]{:T(128)} %constant.45.clone.1), dimensions={1}, to_apply=%region_11.12 | reduce | flops 785664 | bytes 3148804 | tf_op jit(solution)/shard_map/reduce_sum | solution.py:11
  135.8 2.5 %multiply_reduce_fusion = f32[768]{0:T(1024)S(1)} fusion(f32[768,1024]{1,0:T(8,128)} %copy.16, f32[768]{0:T(1024)S(1)} %broadcast_multiply_fusion), kind=kLoop, calls=%fused_computation.22 | loop fusion | flops 2358528 | bytes 3151872 | tf_op jit(solution)/shard_map/reduce_sum | solution.py:13
  138.7 5.6 %fusion.12 = bf16[768,1024]{1,0:T(8,128)(2,1)} fusion(bf16[4,192,1024]{2,1,0:T(8,128)(2,1)} %all-to-all-done, bf16[1,1024,1024]{2,1,0:T(8,128)(2,1)S(1)} %copy-done, f32[768,2048]{1,0:T(8,128)} %copy-done.2, f32[768,1024]{1,0:T(8,128)S(1)} %copy-done.1, f32[1024]{0:T(1024)S(1)} %bitcast.85, f32[768]{0:T(1024)S(1)} %add_rsqrt_fusion, ...), kind=kOutput, calls=%fused_computation.20 | convolution fusion | flops 1620049920 | bytes 11544576 | tf_op jit(solution)/shard_map/dot_general | solution.py:83
  144.3 4.3 %all-to-all-start.1 = ((bf16[4,192,1024]{2,1,0:T(8,128)(2,1)}), bf16[4,192,1024]{2,1,0:T(8,128)(2,1)}, u32[]{:S(2)}, u32[]{:S(2)}) async-start(bf16[4,192,1024]{2,1,0:T(8,128)(2,1)} %bitcast.79), calls=%async_computation.1 | async-start | bytes 3145728 | tf_op jit(solution)/shard_map/all_to_all | solution.py:86
  148.6 20.0 %all-to-all-done.1 = bf16[4,192,1024]{2,1,0:T(8,128)(2,1)} async-done(((bf16[4,192,1024]{2,1,0:T(8,128)(2,1)}), bf16[4,192,1024]{2,1,0:T(8,128)(2,1)}, u32[]{:S(2)}, u32[]{:S(2)}) %all-to-all-start.1) | async-done | bytes 1572896 | tf_op jit(solution)/shard_map/all_to_all | solution.py:86
  168.6 5.0 %gather_fusion = bf16[384,1024]{1,0:T(8,128)(2,1)} fusion(bf16[768,1024]{1,0:T(8,128)(2,1)} %bitcast.17, s32[1024]{0:T(1024)S(1)} %pad_clamp_fusion), kind=kCustom, calls=%fused_computation | custom fusion | bytes 1574400 | tf_op jit(solution)/shard_map/gather | solution.py:93
  (57 shorter events, 24.1 us)
Async XLA Ops:
  6.5 131.8 %copy-start = (bf16[1,1024,1024]{2,1,0:T(8,128)(2,1)S(1)}, bf16[1,1024,1024]{2,1,0:T(8,128)(2,1)}, u32[]{:S(2)}) copy-start(bf16[1,1024,1024]{2,1,0:T(8,128)(2,1)} %param.19) | copy-start | bytes 6291460
  6.5 52.3 %all-gather.3.cloned.1.call-start = ((), (), s32[]{:S(2)}) async-start(), calls=%async_computation.2 | async-start | bytes 4718592 | tf_op jit(solution)/shard_map/all_gather | solution.py:65
  14.4 29.3 %copy-start.4 = (f32[1,1024]{1,0:T(1,128)S(1)}, f32[1,1024]{1,0:T(1,128)}, u32[]{:S(2)}) copy-start(f32[1,1024]{1,0:T(1,128)} %param.16) | copy-start | bytes 12292
  14.4 25.5 %all-to-all-start = ((bf16[4,192,1024]{2,1,0:T(8,128)(2,1)}), bf16[4,192,1024]{2,1,0:T(8,128)(2,1)}, u32[]{:S(2)}, u32[]{:S(2)}) async-start(bf16[4,192,1024]{2,1,0:T(8,128)(2,1)} %bitcast.77), calls=%async_computation | async-start | bytes 3145728 | tf_op jit(solution)/shard_map/all_to_all | solution.py:46
  39.9 5.9 %copy-start.5 = (bf16[1,1024,2048]{2,1,0:T(8,128)(2,1)S(1)}, bf16[1,1024,2048]{2,1,0:T(8,128)(2,1)}, u32[]{:S(2)}) copy-start(bf16[1,1024,2048]{2,1,0:T(8,128)(2,1)} %param.17) | copy-start | bytes 12582916
  49.2 2.7 %copy-start.2 = (f32[768,2048]{1,0:T(8,128)}, f32[768,2048]{1,0:T(8,128)S(1)}, u32[]{:S(2)}) copy-start(f32[768,2048]{1,0:T(8,128)S(1)} %fusion.10) | copy-start | bytes 18874372
  65.3 1.9 %copy-start.3 = (s32[1,8]{1,0:T(1,128)S(1)}, s32[1,8]{1,0:T(1,128)}, u32[]{:S(2)}) copy-start(s32[1,8]{1,0:T(1,128)} %param.15) | copy-start | bytes 100
  133.7 4.7 %copy-start.6 = (f32[1,1024]{1,0:T(1,128)S(1)}, f32[1,1024]{1,0:T(1,128)}, u32[]{:S(2)}) copy-start(f32[1,1024]{1,0:T(1,128)} %param.18) | copy-start | bytes 12292
  135.8 2.8 %copy-start.1 = (f32[768,1024]{1,0:T(8,128)S(1)}, f32[768,1024]{1,0:T(8,128)}, u32[]{:S(2)}) copy-start(f32[768,1024]{1,0:T(8,128)} %copy.16) | copy-start | bytes 9437188
  144.3 24.3 %all-to-all-start.1 = ((bf16[4,192,1024]{2,1,0:T(8,128)(2,1)}), bf16[4,192,1024]{2,1,0:T(8,128)(2,1)}, u32[]{:S(2)}, u32[]{:S(2)}) async-start(bf16[4,192,1024]{2,1,0:T(8,128)(2,1)} %bitcast.79), calls=%async_computation.1 | async-start | bytes 3145728 | tf_op jit(solution)/shard_map/all_to_all | solution.py:86
Sparse Core Ops, SparseCore 0:
  9.0 49.8 all-gather.2
where the time goes:
time: 181 us; the launch traced here: 180 us
  waiting for transfers between devices  45.9 us (25%)
  other arithmetic  45 us (25%)
  local copies, waits for them, and re-layouts  33.8 us (19%)
  matrix products  27.9 us (15%)
  between operations  13.5 us (7%)
  starting transfers between devices  9.63 us (5%)
  loops' own time  4.69 us (3%)
    all_to_all x1, waiting for transfers between devices, on_device(): lax.all_to_all(outgoing.reshape(owner_count, slot_cap, feat_width), 'user...  20.2 us
    all_to_all x1, waiting for transfers between devices, on_device(): lax.all_to_all(hidden.reshape(owner_count, slot_cap, feat_width), 'users'...  20 us
    add x4, other arithmetic, score_block(): return running + combined.reshape(running.shape)  19.5 us
    dot_general x4, matrix products, score_block(): jnp.einsum('hsk,khd->shd', attn_weights, value_heads, preferred_element_t...  18.9 us
    reduce_sum x8, other arithmetic, walk_block(): is_live = jnp.sum(jnp.where(block_range == block_id, block_mask, 0))  10.2 us
    unnamed x15, local copies, waits for them, and re-layouts  9.48 us
    dot_general x1, matrix products, on_device(): jnp.dot(mixed, w_out[0], preferred_element_type=jnp.float32)  5.62 us
    all_to_all x1, starting transfers between devices, on_device(): lax.all_to_all(outgoing.reshape(owner_count, slot_cap, feat_width), 'user...  5.3 us
  transfers between devices with their start and end apart: 3, of which 3 were waited for; matrix products, arithmetic and copies ran while one was open for 10% of the time, Pallas kernels for 0%

commit v1 on v0

v1 whole, which is shorter than its diff:
```python
import functools

import jax
import jax.numpy as jnp
from jax import lax
from jax.experimental import pallas as pl
from jax.experimental.pallas import tpu as pltpu
from jax.sharding import PartitionSpec as P

BLK = 128
HEAD = 128
CHUNKS = 2
VMEM_LIMIT = 56 * 1024 * 1024


def silu_halved(t):
    return t + t * jnp.tanh(t)


def centred_norm(x):
    middle = jnp.mean(x, axis=-1, keepdims=True)
    shifted = x - middle
    spread = jnp.mean(shifted * shifted, axis=-1, keepdims=True)
    return shifted * lax.rsqrt(spread + 1e-05)


def slots_of(user, me, cap):
    rows = user.shape[0]
    rel = user ^ me
    lanes = lax.broadcasted_iota(jnp.int32, (rows, 128), 1)
    one_hot = (rel == lanes).astype(jnp.float32)
    above = lax.broadcasted_iota(jnp.int32, (rows, rows), 0)
    below = lax.broadcasted_iota(jnp.int32, (rows, rows), 1)
    earlier = (below < above).astype(jnp.bfloat16)
    rank = jnp.dot(earlier, one_hot.astype(jnp.bfloat16), preferred_element_type=jnp.float32)
    rank = jnp.sum(rank * one_hot, axis=1, keepdims=True)
    return rel.astype(jnp.float32) * cap + rank


def kv_split_kernel(chunks, ids, kv, *outs):
    core = ids[1]
    half = kv.shape[1] // 4
    wide = half // chunks
    for chunk in range(chunks):
        for swap in range(2):
            side = core if swap == 0 else 1 - core
            out = outs[2 * chunk + swap]
            for part in range(2):
                at = pl.multiple_of(part * 2 * half + side * half + chunk * wide, 128)
                out[:, part * wide:(part + 1) * wide] = kv[:, pl.ds(at, wide)]


def query_kernel(chunks, cap, ids, feat, user, gain, wq, normed_out, *rest):
    outs, halves = rest[:-1], rest[-1]
    me, core = ids[0], ids[1]
    rows, width = feat.shape
    half = width // 2
    wide = half // chunks
    users = rows * 2 // cap
    normed = (centred_norm(feat[...].astype(jnp.float32)) * gain[...]).astype(jnp.bfloat16)
    normed_out[...] = normed
    slot = slots_of(user[...], me, cap)
    slot_row = jnp.transpose(jnp.broadcast_to(slot, (rows, 128)))[0:1, :]
    places = lax.broadcasted_iota(jnp.int32, (users * cap, rows), 0).astype(jnp.float32)
    pick = (places == slot_row).astype(jnp.bfloat16)
    for side in range(2):
        part = jnp.dot(
            normed, wq[:, side * half:(side + 1) * half], preferred_element_type=jnp.float32
        )
        halves[side] = silu_halved(part * 0.5).astype(jnp.bfloat16)
    for swap in range(2):
        side = core if swap == 0 else 1 - core
        sent = jnp.dot(pick, halves[side], preferred_element_type=jnp.float32).astype(jnp.bfloat16)
        for chunk in range(chunks):
            for d in range(users):
                outs[(chunk * 2 + swap) * users + d][...] = sent[
                    d * cap:(d + 1) * cap, chunk * wide:(chunk + 1) * wide
                ]


def gate_kernel(normed, wg, out):
    part = jnp.dot(normed[...], wg[...], preferred_element_type=jnp.float32)
    out[...] = silu_halved(part * 0.5)


def attend_kernel(offsets, count_q, ids, mask, *rest):
    count_kv = len(offsets)
    queries = rest[:count_q]
    pairs = rest[count_q:count_q + count_kv]
    outs = rest[count_q + count_kv:count_q + count_kv + count_q]
    live_kv, all_q, all_out = rest[count_q + count_kv + count_q:]
    core, z = ids[1], ids[2]
    blocks = mask.shape[1]
    cap, wide = queries[0].shape
    taken = jnp.int32(0)
    for offset, pair in zip(offsets, pairs):
        there = z + offset
        inside = (there >= 0) & (there < blocks // 2)
        there = jnp.clip(there, 0, blocks // 2 - 1)
        for b in range(2):
            side = core if b == 0 else 1 - core
            live = inside & (mask[0, 2 * there + side] > 0)

            def take(pair=pair, b=b, taken=taken):
                at = pl.multiple_of(taken * BLK, BLK)
                live_kv[pl.ds(at, BLK), :] = pair[b * BLK:(b + 1) * BLK, :]

            pl.when(live)(take)
            taken = jnp.minimum(taken + live.astype(jnp.int32), blocks // 2 - 1)
    for i, q in enumerate(queries):
        all_q[i * cap:(i + 1) * cap, :] = q[...]
    scale = 0.5 * HEAD ** (-0.5)
    total = count_q * cap
    tile = 256 if total % 256 == 0 else cap
    for head in range(wide // HEAD):
        cols = slice(head * HEAD, (head + 1) * HEAD)
        keys = live_kv[:, cols]
        values = live_kv[:, wide + head * HEAD:wide + (head + 1) * HEAD]
        for first in range(0, total, tile):
            scores = lax.dot_general(
                all_q[first:first + tile, cols], keys, (((1,), (1,)), ((), ())),
                preferred_element_type=jnp.float32,
            )
            weight = silu_halved(scores * scale).astype(jnp.bfloat16)
            got = jnp.dot(weight, values, preferred_element_type=jnp.float32)
            all_out[first:first + tile, cols] = got.astype(jnp.bfloat16)
    for i, out in enumerate(outs):
        out[...] = all_out[i * cap:(i + 1) * cap, :]


def finish_kernel(chunks, cap, ids, feat, user, gate, gain, w_out, *rest):
    parts, out, back, attended = rest[:-3], rest[-3], rest[-2], rest[-1]
    me, core = ids[0], ids[1]
    rows, width = feat.shape
    half = width // 2
    wide = half // chunks
    users = rows * 2 // cap
    slot = slots_of(user[...], me, cap)
    places = lax.broadcasted_iota(jnp.int32, (rows, users * cap), 1).astype(jnp.float32)
    pick = (places == slot).astype(jnp.bfloat16)
    for swap in range(2):
        side = core if swap == 0 else 1 - core
        for chunk in range(chunks):
            for d in range(users):
                back[d * cap:(d + 1) * cap, :] = parts[(chunk * 2 + swap) * users + d][...]
            got = jnp.dot(pick, back[...], preferred_element_type=jnp.float32)
            at = pl.multiple_of(side * half + chunk * wide, 128)
            attended[:, pl.ds(at, wide)] = got
    mixed = (centred_norm(attended[...]) * gain[...] * gate[...]).astype(jnp.bfloat16)
    grown = jnp.dot(mixed, w_out[...], preferred_element_type=jnp.float32)
    out[...] = (feat[...].astype(jnp.float32) + grown).astype(jnp.bfloat16)


SMEM = pl.BlockSpec(memory_space=pltpu.SMEM)
VMEM = pl.BlockSpec(memory_space=pltpu.VMEM)


def call(kernel, name, in_specs, out_shape, scratch, flops, *args):
    moved = sum(a.size * a.dtype.itemsize for a in args)
    return pl.pallas_call(
        kernel,
        name=name,
        in_specs=in_specs,
        out_specs=jax.tree.map(lambda s: VMEM, out_shape),
        out_shape=out_shape,
        scratch_shapes=scratch,
        cost_estimate=pl.CostEstimate(flops=flops, bytes_accessed=moved, transcendentals=0),
        compiler_params=pltpu.CompilerParams(vmem_limit_bytes=VMEM_LIMIT),
    )(*args)


def on_device(cand_feat, cand_user, hist_kv, hist_mask, gain_in, w_uq, gain_attn, w_out):
    users = lax.axis_size("users")
    ctx = lax.axis_size("ctx")
    chips = ctx // 2
    rows, width = cand_feat.shape
    cap = 2 * rows // users
    half = width // 2
    wide = half // CHUNKS
    me = lax.axis_index("users")
    place = lax.axis_index("ctx")
    ids = jnp.stack([me, place % 2, place // 2]).astype(jnp.int32)
    bf16 = jnp.bfloat16

    def shape(*dims, dtype=bf16):
        return jax.ShapeDtypeStruct(dims, dtype)

    halves = call(
        functools.partial(kv_split_kernel, CHUNKS), "kv_split", [SMEM, VMEM],
        [shape(BLK, 2 * wide)] * (2 * CHUNKS), [], 0, ids, hist_kv[0, 0],
    )
    core_swap = [(c, c ^ 1) for c in range(ctx)]
    pairs = []
    for chunk in range(CHUNKS):
        other = lax.ppermute(halves[2 * chunk + 1], "ctx", core_swap)
        pairs.append(jnp.concatenate([halves[2 * chunk], other], axis=0))

    def along(value, step, sign):
        moves = []
        for c in range(ctx):
            z = c // 2
            goal = z + sign
            origin = z - sign * (step - 1)
            if 0 <= goal < chips and 0 <= origin < chips:
                moves.append((c, c + 2 * sign))
        return lax.ppermute(value, "ctx", moves)

    def route(value, d, k):
        moves = [(u * ctx + c, (u ^ d) * ctx + (c ^ k)) for u in range(users) for c in range(ctx)]
        return lax.ppermute(value, ("users", "ctx"), moves)

    def exchange(values):
        got = []
        for k in range(2):
            for d in range(users):
                value = values[k * users + d]
                got.append(value if k == 0 and d == 0 else route(value, d, k))
        return got

    normed, *queries = pl.pallas_call(
        functools.partial(query_kernel, CHUNKS, cap),
        name="query",
        grid=(1,),
        in_specs=[
            SMEM,
            pl.BlockSpec((rows, width), lambda i: (0, 0)),
            pl.BlockSpec((rows, 1), lambda i: (0, 0)),
            pl.BlockSpec((1, width), lambda i: (0, 0)),
            pl.BlockSpec((width, width), lambda i: (0, 1)),
        ],
        out_specs=[pl.BlockSpec((rows, width), lambda i: (0, 0))]
        + [pl.BlockSpec((cap, wide), lambda i: (0, 0))] * (CHUNKS * 2 * users),
        out_shape=[shape(rows, width)] + [shape(cap, wide)] * (CHUNKS * 2 * users),
        scratch_shapes=[pltpu.VMEM((2, rows, half), bf16)],
        cost_estimate=pl.CostEstimate(
            flops=4 * rows * width * width, bytes_accessed=2 * width * width, transcendentals=0
        ),
        compiler_params=pltpu.CompilerParams(vmem_limit_bytes=VMEM_LIMIT),
    )(ids, cand_feat, cand_user, gain_in, w_uq[0])

    per_chunk = 2 * users
    arrived = [
        exchange(queries[chunk * per_chunk:(chunk + 1) * per_chunk]) for chunk in range(CHUNKS)
    ]
    offsets = [0]
    for step in range(1, chips):
        offsets += [-step, step]
    gathered = []
    for chunk in range(CHUNKS):
        right = left = pairs[chunk]
        held = [pairs[chunk]]
        for step in range(1, chips):
            right = along(right, step, 1)
            left = along(left, step, -1)
            held += [right, left]
        gathered.append(held)

    gate = pl.pallas_call(
        gate_kernel,
        name="gate",
        grid=(1,),
        in_specs=[
            pl.BlockSpec((rows, width), lambda i: (0, 0)),
            pl.BlockSpec((width, width), lambda i: (0, 0)),
        ],
        out_specs=pl.BlockSpec((rows, width), lambda i: (0, 0)),
        out_shape=shape(rows, width, dtype=jnp.float32),
        cost_estimate=pl.CostEstimate(
            flops=2 * rows * width * width, bytes_accessed=2 * width * width, transcendentals=0
        ),
        compiler_params=pltpu.CompilerParams(vmem_limit_bytes=VMEM_LIMIT),
    )(normed, w_uq[0])

    live_rows = hist_mask.shape[1] // 2 * BLK
    returned = []
    for chunk in range(CHUNKS):
        scored = call(
            functools.partial(attend_kernel, tuple(offsets), per_chunk), "attend",
            [SMEM, SMEM] + [VMEM] * (per_chunk + len(offsets)),
            [shape(cap, wide)] * per_chunk,
            [
                pltpu.VMEM((live_rows, 2 * wide), bf16),
                pltpu.VMEM((per_chunk * cap, wide), bf16),
                pltpu.VMEM((per_chunk * cap, wide), bf16),
            ],
            8 * per_chunk * cap * live_rows * wide,
            ids, hist_mask, *arrived[chunk], *gathered[chunk],
        )
        returned += exchange(scored)

    return call(
        functools.partial(finish_kernel, CHUNKS, cap), "finish",
        [SMEM] + [VMEM] * (5 + len(returned)),
        shape(rows, width),
        [pltpu.VMEM((users * cap, wide), bf16), pltpu.VMEM((rows, width), jnp.float32)],
        4 * rows * width * width,
        ids, cand_feat, cand_user, gate, gain_attn, w_out[0], *returned,
    )


def solution(mesh):
    in_specs = (
        P(("users", "ctx"), None),
        P(("users", "ctx"), None),
        P(None, "users", "ctx", None),
        P("users", None),
        P(),
        P(),
        P(),
        P(),
    )
    out_specs = P(("users", "ctx"), None)
    return jax.shard_map(
        on_device, mesh=mesh, in_specs=in_specs, out_specs=out_specs, check_vma=False
    )
```

time: 181 us -> 108 us (0.60)
  other arithmetic: 45 us -> 0.65 us
  starting transfers between devices: 9.63 us -> 43.7 us
  local copies, waits for them, and re-layouts: 33.8 us -> 2.5 us
  Pallas kernels: 0 us -> 29.1 us
  matrix products: 27.9 us -> 0 us
  waiting for transfers between devices: 45.9 us -> 30.6 us
  between operations: 13.5 us -> 0.7 us
  loops' own time: 4.69 us -> 0 us
    ppermute x0 -> x42, starting transfers between devices: none -> 43.7 us  [the longest x28 24.8 us: route(): return lax.ppermute(value, ('users', 'ctx'), moves)]
    all_to_all x2 -> x0, waiting for transfers between devices: 40.2 us -> none  [the longest x1 20.2 us: on_device(): lax.all_to_all(outgoing.reshape(owner_count, slot_cap, feat_width), 'user...]
    ppermute x0 -> x42, waiting for transfers between devices: none -> 30.6 us  [the longest x28 24.1 us: route(): return lax.ppermute(value, ('users', 'ctx'), moves)]
    pallas_call x0 -> x6, Pallas kernels: none -> 29.1 us  [the longest x4 19.7 us: call(): pl.pallas_call(kernel, name=name, in_specs=in_specs, out_specs=jax.tree.m...]
    dot_general x6 -> x0, matrix products: 27.9 us -> none  [the longest x4 18.9 us: score_block(): jnp.einsum('hsk,khd->shd', attn_weights, value_heads, preferred_element_t...]
    add x4 -> x0, other arithmetic: 19.5 us -> none  [score_block(): return running + combined.reshape(running.shape)]
    reduce_sum x13 -> x0, other arithmetic: 18.6 us -> none  [the longest x8 10.2 us: walk_block(): is_live = jnp.sum(jnp.where(block_range == block_id, block_mask, 0))]
    all_to_all x2 -> x0, starting transfers between devices: 9.63 us -> none  [the longest x1 5.3 us: on_device(): lax.all_to_all(outgoing.reshape(owner_count, slot_cap, feat_width), 'user...]
  transfers between devices with their start and end apart: 3 -> 42, of which waited for: 3 -> 12; matrix products, arithmetic and copies ran while one was open for 10% -> 1% of each run, Pallas kernels for 0% -> 19%
where the time goes in v1:
time: 108 us; the launch traced here: 107 us
  starting transfers between devices  43.7 us (40%)
  waiting for transfers between devices  30.6 us (28%)
  Pallas kernels  29.1 us (27%)
  local copies, waits for them, and re-layouts  2.5 us (2%)
    ppermute x28, starting transfers between devices, route(): return lax.ppermute(value, ('users', 'ctx'), moves)  24.8 us
    ppermute x28, waiting for transfers between devices, route(): return lax.ppermute(value, ('users', 'ctx'), moves)  24.1 us
    pallas_call x4, Pallas kernels, call(): pl.pallas_call(kernel, name=name, in_specs=in_specs, out_specs=jax.tree.m...  19.7 us
    ppermute x12, starting transfers between devices, along(): return lax.ppermute(value, 'ctx', moves)  18.5 us
    ppermute x12, waiting for transfers between devices, along(): return lax.ppermute(value, 'ctx', moves)  6.48 us
    pallas_call x1, Pallas kernels, on_device(): pl.pallas_call(functools.partial(query_kernel, CHUNKS, cap), name='query'...  5.37 us
    pallas_call x1, Pallas kernels, on_device(): pl.pallas_call(gate_kernel, name='gate', grid=(1,), in_specs=[pl.BlockSpe...  4 us
    unnamed x97, local copies, waits for them, and re-layouts  2.48 us
  transfers between devices with their start and end apart: 42, of which 12 were waited for; matrix products, arithmetic and copies ran while one was open for 1% of the time, Pallas kernels for 19%

profile of v1, /device:TPU:0, one launch (start us, length us, event | category | flops | bytes accessed | tf_op | source)
XLA Modules:
  0.0 107.2 jit_solution(11067377400163720315)
XLA Ops:
  0.7 1.9 %kv_split.1 = (bf16[128,512]{1,0:T(8,128)(2,1)}, bf16[128,512]{1,0:T(8,128)(2,1)}, bf16[128,512]{1,0:T(8,128)(2,1)}, bf16[128,512]{1,0:T(8,128)(2,1)}) custom-call(s32[3]{0:T(128)} %pad_add_fusion.ids, bf16[128,2048]{1,0:T(8,128)(2,1)} %bitcast.9), custom_call_target="tpu_custom_call" | custom-call | bytes 524300 | tf_op jit(solution)/shard_map/kv_split/pallas_call | solution.py:160
  3.0 1.5 %copy.10.user = s32[384,1]{1,0:T(8,128)} copy(s32[384,1]{0,1:T(1,128)} %param.9) | data formatting | bytes 3072 | tf_op args[1]
  4.6 5.4 %query.1 = (bf16[384,1024]{1,0:T(8,128)(2,1)}, bf16[192,256]{1,0:T(8,128)(2,1)}, bf16[192,256]{1,0:T(8,128)(2,1)}, bf16[192,256]{1,0:T(8,128)(2,1)}, bf16[192,25...) custom-call(s32[3]{0:T(128)} %pad_add_fusion.ids, ...), custom_call_target="tpu_custom_call" | custom-call | flops 1610612736 | bytes 2097152 | tf_op jit(solution)/shard_map/query/pallas_call | solution.py:220
  9.9 2.5 %collective-permute-start.21 = (bf16[192,256]{1,0:T(8,128)(2,1)}, bf16[192,256]{1,0:T(8,128)(2,1)S(1)}, u32[]{:S(2)}, u32[]{:S(2)}) collective-permute-start(bf16[192,256]{1,0:T(8,128)(2,1)} %get-tuple-element.62), channel_id=1, source_target_pairs={{0,8},{1,9},{2,10},{3,11},{4,12},{5,13},{6,14},{7,15},{8,0},{9,1},... | collective-permute-start | bytes 294920 | tf_op jit(solution)/shard_map/ppermute | solution.py:210
  12.5 1.5 %collective-permute-start.22 = (bf16[192,256]{1,0:T(8,128)(2,1)}, bf16[192,256]{1,0:T(8,128)(2,1)S(1)}, u32[]{:S(2)}, u32[]{:S(2)}) collective-permute-start(bf16[192,256]{1,0:T(8,128)(2,1)} %get-tuple-element.63), channel_id=1, source_target_pairs={{0,16},{1,17},{2,18},{3,19},{4,20},{5,21},{6,22},{7,23},{8,24},{9,... | collective-permute-start | bytes 294920 | tf_op jit(solution)/shard_map/ppermute | solution.py:210
  14.1 3.5 %collective-permute-start.29 = (bf16[256,512]{1,0:T(8,128)(2,1)S(1)}, bf16[256,512]{1,0:T(8,128)(2,1)S(1)}, u32[]{:S(2)}, u32[]{:S(2)}) collective-permute-start(bf16[256,512]{1,0:T(8,128)(2,1)S(1)} %constant_dynamic-update-slice_fusion.2.rest_8_), channel_id=1, source_target_pairs={{0,2},{1,3},{2,4},{3,5},{4,6},{5,7},{8,10},{9,11},{10,12},{11,13},... | collective-permute-start | bytes 786440 | tf_op jit(solution)/shard_map/ppermute | solution.py:206
  17.6 1.3 %collective-permute-start.30 = (bf16[256,512]{1,0:T(8,128)(2,1)S(1)}, bf16[256,512]{1,0:T(8,128)(2,1)S(1)}, u32[]{:S(2)}, u32[]{:S(2)}) collective-permute-start(bf16[256,512]{1,0:T(8,128)(2,1)S(1)} %constant_dynamic-update-slice_fusion.2.rest_8_), channel_id=1, source_target_pairs={{2,0},{3,1},{4,2},{5,3},{6,4},{7,5},{10,8},{11,9},{12,10},{13,11},... | collective-permute-start | bytes 786440 | tf_op jit(solution)/shard_map/ppermute | solution.py:206
  19.5 1.6 %collective-permute-start.25 = (bf16[192,256]{1,0:T(8,128)(2,1)}, bf16[192,256]{1,0:T(8,128)(2,1)S(1)}, u32[]{:S(2)}, u32[]{:S(2)}) collective-permute-start(bf16[192,256]{1,0:T(8,128)(2,1)} %get-tuple-element.66), channel_id=1, source_target_pairs={{0,9},{1,8},{2,11},{3,10},{4,13},{5,12},{6,15},{7,14},{8,1},{9,0},... | collective-permute-start | bytes 294920 | tf_op jit(solution)/shard_map/ppermute | solution.py:210
  21.1 4.6 %collective-permute-done.23.rest_3_ = bf16[192,256]{1,0:T(8,128)(2,1)S(1)} collective-permute-done((bf16[192,256]{1,0:T(8,128)(2,1)}, bf16[192,256]{1,0:T(8,128)(2,1)S(1)}, u32[]{:S(2)}, u32[]{:S(2)}) %collective-permute-start.23) | collective-permute-done | bytes 98336 | tf_op jit(solution)/shard_map/ppermute | solution.py:210
  25.7 4.6 %collective-permute-start.8 = (bf16[256,512]{1,0:T(8,128)(2,1)S(1)}, bf16[256,512]{1,0:T(8,128)(2,1)S(1)}, u32[]{:S(2)}, u32[]{:S(2)}) collective-permute-start(bf16[256,512]{1,0:T(8,128)(2,1)S(1)} %constant_dynamic-update-slice_fusion.rest_8_), channel_id=1, source_target_pairs={{0,2},{1,3},{2,4},{3,5},{4,6},{5,7},{8,10},{9,11},{10,12},{11,13},... | collective-permute-start | bytes 786440 | tf_op jit(solution)/shard_map/ppermute | solution.py:206
  33.8 2.3 %collective-permute-done.26.rest_6_ = bf16[192,256]{1,0:T(8,128)(2,1)S(1)} collective-permute-done((bf16[192,256]{1,0:T(8,128)(2,1)}, bf16[192,256]{1,0:T(8,128)(2,1)S(1)}, u32[]{:S(2)}, u32[]{:S(2)}) %collective-permute-start.26) | collective-permute-done | bytes 98336 | tf_op jit(solution)/shard_map/ppermute | solution.py:210
  36.3 5.4 %collective-permute-done.27.rest_7_ = bf16[192,256]{1,0:T(8,128)(2,1)S(1)} collective-permute-done((bf16[192,256]{1,0:T(8,128)(2,1)}, bf16[192,256]{1,0:T(8,128)(2,1)S(1)}, u32[]{:S(2)}, u32[]{:S(2)}) %collective-permute-start.27) | collective-permute-done | bytes 98336 | tf_op jit(solution)/shard_map/ppermute | solution.py:210
  43.9 2.6 %collective-permute-done.rest_1_ = bf16[192,256]{1,0:T(8,128)(2,1)S(1)} collective-permute-done((bf16[192,256]{1,0:T(8,128)(2,1)}, bf16[192,256]{1,0:T(8,128)(2,1)S(1)}, u32[]{:S(2)}, u32[]{:S(2)}) %collective-permute-start) | collective-permute-done | bytes 98336 | tf_op jit(solution)/shard_map/ppermute | solution.py:210
  46.5 1.9 %collective-permute-start.1 = (bf16[192,256]{1,0:T(8,128)(2,1)}, bf16[192,256]{1,0:T(8,128)(2,1)S(1)}, u32[]{:S(2)}, u32[]{:S(2)}) collective-permute-start(bf16[192,256]{1,0:T(8,128)(2,1)} %get-tuple-element.45), channel_id=1, source_target_pairs={{0,16},{1,17},{2,18},{3,19},{4,20},{5,21},{6,22},{7,23},{8,24},{9,... | collective-permute-start | bytes 294920 | tf_op jit(solution)/shard_map/ppermute | solution.py:210
  51.3 1.6 %collective-permute-start.2 = (bf16[192,256]{1,0:T(8,128)(2,1)}, bf16[192,256]{1,0:T(8,128)(2,1)S(1)}, u32[]{:S(2)}, u32[]{:S(2)}) collective-permute-start(bf16[192,256]{1,0:T(8,128)(2,1)} %get-tuple-element.46), channel_id=1, source_target_pairs={{0,24},{1,25},{2,26},{3,27},{4,28},{5,29},{6,30},{7,31},{8,16},{9,... | collective-permute-start | bytes 294920 | tf_op jit(solution)/shard_map/ppermute | solution.py:210
  53.6 5.4 %collective-permute-done.11.rest_12_ = bf16[256,512]{1,0:T(8,128)(2,1)S(1)} collective-permute-done((bf16[256,512]{1,0:T(8,128)(2,1)S(1)}, bf16[256,512]{1,0:T(8,128)(2,1)S(1)}, u32[]{:S(2)}, u32[]{:S(2)}) %collective-permute-start.11) | collective-permute-done | bytes 262176 | tf_op jit(solution)/shard_map/ppermute | solution.py:206
  60.4 1.5 %collective-permute-done.3.rest_4_ = bf16[192,256]{1,0:T(8,128)(2,1)S(1)} collective-permute-done((bf16[192,256]{1,0:T(8,128)(2,1)}, bf16[192,256]{1,0:T(8,128)(2,1)S(1)}, u32[]{:S(2)}, u32[]{:S(2)}) %collective-permute-start.3) | collective-permute-done | bytes 98336 | tf_op jit(solution)/shard_map/ppermute | solution.py:210
  61.9 1.7 %collective-permute-start.4 = (bf16[192,256]{1,0:T(8,128)(2,1)}, bf16[192,256]{1,0:T(8,128)(2,1)S(1)}, u32[]{:S(2)}, u32[]{:S(2)}) collective-permute-start(bf16[192,256]{1,0:T(8,128)(2,1)} %get-tuple-element.48), channel_id=1, source_target_pairs={{0,9},{1,8},{2,11},{3,10},{4,13},{5,12},{6,15},{7,14},{8,1},{9,0},... | collective-permute-start | bytes 294920 | tf_op jit(solution)/shard_map/ppermute | solution.py:210
  65.4 5.6 %attend.3 = (bf16[192,256]{1,0:T(8,128)(2,1)}, bf16[192,256]{1,0:T(8,128)(2,1)}, bf16[192,256]{1,0:T(8,128)(2,1)}, bf16[192,256]{1,0:T(8,128)(2,1)}, bf16[192,25...) custom-call(s32[3]{0:T(128)} %pad_add_fusion.ids, ...), custom_call_target="tpu_custom_call" | custom-call | flops 1610612736 | bytes 2621484 | tf_op jit(solution)/shard_map/attend/pallas_call | solution.py:160
  71.1 2.0 %collective-permute-start.35 = (bf16[192,256]{1,0:T(8,128)(2,1)}, bf16[192,256]{1,0:T(8,128)(2,1)S(1)}, u32[]{:S(2)}, u32[]{:S(2)}) collective-permute-start(bf16[192,256]{1,0:T(8,128)(2,1)} %get-tuple-element.72), channel_id=1, source_target_pairs={{0,8},{1,9},{2,10},{3,11},{4,12},{5,13},{6,14},{7,15},{8,0},{9,1},... | collective-permute-start | bytes 294920 | tf_op jit(solution)/shard_map/ppermute | solution.py:210
  73.1 1.5 %collective-permute-start.37 = (bf16[192,256]{1,0:T(8,128)(2,1)}, bf16[192,256]{1,0:T(8,128)(2,1)S(1)}, u32[]{:S(2)}, u32[]{:S(2)}) collective-permute-start(bf16[192,256]{1,0:T(8,128)(2,1)} %get-tuple-element.74), channel_id=1, source_target_pairs={{0,24},{1,25},{2,26},{3,27},{4,28},{5,29},{6,30},{7,31},{8,16},{9,... | collective-permute-start | bytes 294920 | tf_op jit(solution)/shard_map/ppermute | solution.py:210
  75.1 1.6 %collective-permute-start.39 = (bf16[192,256]{1,0:T(8,128)(2,1)}, bf16[192,256]{1,0:T(8,128)(2,1)S(1)}, u32[]{:S(2)}, u32[]{:S(2)}) collective-permute-start(bf16[192,256]{1,0:T(8,128)(2,1)} %get-tuple-element.76), channel_id=1, source_target_pairs={{0,9},{1,8},{2,11},{3,10},{4,13},{5,12},{6,15},{7,14},{8,1},{9,0},... | collective-permute-start | bytes 294920 | tf_op jit(solution)/shard_map/ppermute | solution.py:210
  76.8 5.8 %attend.2 = (bf16[192,256]{1,0:T(8,128)(2,1)}, bf16[192,256]{1,0:T(8,128)(2,1)}, bf16[192,256]{1,0:T(8,128)(2,1)}, bf16[192,256]{1,0:T(8,128)(2,1)}, bf16[192,25...) custom-call(s32[3]{0:T(128)} %pad_add_fusion.ids, ...), custom_call_target="tpu_custom_call" | custom-call | flops 1610612736 | bytes 2621484 | tf_op jit(solution)/shard_map/attend/pallas_call | solution.py:160
  83.0 1.5 %collective-permute-start.41 = (bf16[192,256]{1,0:T(8,128)(2,1)S(1)}, bf16[192,256]{1,0:T(8,128)(2,1)S(1)}, u32[]{:S(2)}, u32[]{:S(2)}) collective-permute-start(bf16[192,256]{1,0:T(8,128)(2,1)S(1)} %copy-done.39), channel_id=1, source_target_pairs={{0,25},{1,24},{2,27},{3,26},{4,29},{5,28},{6,31},{7,30},{8,17},{9,... | collective-permute-start | bytes 294920 | tf_op jit(solution)/shard_map/ppermute | solution.py:210
  84.5 1.5 %collective-permute-start.14 = (bf16[192,256]{1,0:T(8,128)(2,1)}, bf16[192,256]{1,0:T(8,128)(2,1)S(1)}, u32[]{:S(2)}, u32[]{:S(2)}) collective-permute-start(bf16[192,256]{1,0:T(8,128)(2,1)} %get-tuple-element.54), channel_id=1, source_target_pairs={{0,8},{1,9},{2,10},{3,11},{4,12},{5,13},{6,14},{7,15},{8,0},{9,1},... | collective-permute-start | bytes 294920 | tf_op jit(solution)/shard_map/ppermute | solution.py:210
  86.7 1.4 %collective-permute-start.16 = (bf16[192,256]{1,0:T(8,128)(2,1)}, bf16[192,256]{1,0:T(8,128)(2,1)S(1)}, u32[]{:S(2)}, u32[]{:S(2)}) collective-permute-start(bf16[192,256]{1,0:T(8,128)(2,1)} %get-tuple-element.56), channel_id=1, source_target_pairs={{0,24},{1,25},{2,26},{3,27},{4,28},{5,29},{6,30},{7,31},{8,16},{9,... | collective-permute-start | bytes 294920 | tf_op jit(solution)/shard_map/ppermute | solution.py:210
  88.0 1.5 %collective-permute-done.40.rest_14_ = bf16[192,256]{1,0:T(8,128)(2,1)S(1)} collective-permute-done((bf16[192,256]{1,0:T(8,128)(2,1)S(1)}, bf16[192,256]{1,0:T(8,128)(2,1)S(1)}, u32[]{:S(2)}, u32[]{:S(2)}) %collective-permute-start.40) | collective-permute-done | bytes 98336 | tf_op jit(solution)/shard_map/ppermute | solution.py:210
  90.3 1.4 %collective-permute-done.14.rest_1_ = bf16[192,256]{1,0:T(8,128)(2,1)S(1)} collective-permute-done((bf16[192,256]{1,0:T(8,128)(2,1)}, bf16[192,256]{1,0:T(8,128)(2,1)S(1)}, u32[]{:S(2)}, u32[]{:S(2)}) %collective-permute-start.14) | collective-permute-done | bytes 98336 | tf_op jit(solution)/shard_map/ppermute | solution.py:210
  91.7 2.4 %collective-permute-done.15.rest_2_ = bf16[192,256]{1,0:T(8,128)(2,1)S(1)} collective-permute-done((bf16[192,256]{1,0:T(8,128)(2,1)}, bf16[192,256]{1,0:T(8,128)(2,1)S(1)}, u32[]{:S(2)}, u32[]{:S(2)}) %collective-permute-start.15) | collective-permute-done | bytes 98336 | tf_op jit(solution)/shard_map/ppermute | solution.py:210
  94.8 4.0 %gate.1 = f32[384,1024]{1,0:T(8,128)} custom-call(bf16[384,1024]{1,0:T(8,128)(2,1)} %get-tuple-element.42.normed, bf16[1024,2048]{1,0:T(8,128)(2,1)} %bitcast.7), custom_call_target="tpu_custom_call" | custom-call | flops 805306368 | bytes 2097152 | tf_op jit(solution)/shard_map/gate/pallas_call | solution.py:258
  98.9 1.3 %collective-permute-done.20.rest_7_ = bf16[192,256]{1,0:T(8,128)(2,1)S(1)} collective-permute-done((bf16[192,256]{1,0:T(8,128)(2,1)}, bf16[192,256]{1,0:T(8,128)(2,1)S(1)}, u32[]{:S(2)}, u32[]{:S(2)}) %collective-permute-start.20) | collective-permute-done | bytes 98336 | tf_op jit(solution)/shard_map/ppermute | solution.py:210
  100.9 6.3 %finish.1 = bf16[384,1024]{1,0:T(8,128)(2,1)} custom-call(s32[3]{0:T(128)} %pad_add_fusion.ids, bf16[384,1024]{1,0:T(8,128)(2,1)} %feat.3, s32[384,1]{1,0:T(8,128)} %copy.10.user, f32[384,1024]{1,0:T(8,128)} %gate.1, f32[1,1024]{1,0:T(1,128)} %gain.3, bf16[1024,1024]{1,0:T(8,128)(2,1)} %bitcast.8, bf16[192,256]{1,0:T(8,128)(2,1)} %get-tuple-element.53.rest_0_, ...), custom_call_target="tpu_custom_call" | custom-call | flops 1610612736 | bytes 6034956 | tf_op jit(solution)/shard_map/finish/pallas_call | solution.py:160
  (158 shorter events, 17.7 us)
Async XLA Ops:
  2.6 11.5 %collective-permute-start.28 = (bf16[128,512]{1,0:T(8,128)(2,1)}, bf16[128,512]{1,0:T(8,128)(2,1)S(1)}, u32[]{:S(2)}, u32[]{:S(2)}) collective-permute-start(bf16[128,512]{1,0:T(8,128)(2,1)} %get-tuple-element.70), channel_id=1, source_target_pairs={{0,1},{1,0},{2,3},{3,2},{4,5},{5,4},{6,7},{7,6},{8,9},{9,8},{10,11... | collective-permute-start | bytes 393224 | tf_op jit(solution)/shard_map/ppermute | solution.py:195
  9.9 9.0 %collective-permute-start.21 = (bf16[192,256]{1,0:T(8,128)(2,1)}, bf16[192,256]{1,0:T(8,128)(2,1)S(1)}, u32[]{:S(2)}, u32[]{:S(2)}) collective-permute-start(bf16[192,256]{1,0:T(8,128)(2,1)} %get-tuple-element.62), channel_id=1, source_target_pairs={{0,8},{1,9},{2,10},{3,11},{4,12},{5,13},{6,14},{7,15},{8,0},{9,1},... | collective-permute-start | bytes 294920 | tf_op jit(solution)/shard_map/ppermute | solution.py:210
  14.1 17.7 %collective-permute-start.29 = (bf16[256,512]{1,0:T(8,128)(2,1)S(1)}, bf16[256,512]{1,0:T(8,128)(2,1)S(1)}, u32[]{:S(2)}, u32[]{:S(2)}) collective-permute-start(bf16[256,512]{1,0:T(8,128)(2,1)S(1)} %constant_dynamic-update-slice_fusion.2.rest_8_), channel_id=1, source_target_pairs={{0,2},{1,3},{2,4},{3,5},{4,6},{5,7},{8,10},{9,11},{10,12},{11,13},... | collective-permute-start | bytes 786440 | tf_op jit(solution)/shard_map/ppermute | solution.py:206
  17.6 14.9 %collective-permute-start.30 = (bf16[256,512]{1,0:T(8,128)(2,1)S(1)}, bf16[256,512]{1,0:T(8,128)(2,1)S(1)}, u32[]{:S(2)}, u32[]{:S(2)}) collective-permute-start(bf16[256,512]{1,0:T(8,128)(2,1)S(1)} %constant_dynamic-update-slice_fusion.2.rest_8_), channel_id=1, source_target_pairs={{2,0},{3,1},{4,2},{5,3},{6,4},{7,5},{10,8},{11,9},{12,10},{13,11},... | collective-permute-start | bytes 786440 | tf_op jit(solution)/shard_map/ppermute | solution.py:206
  19.5 10.9 %collective-permute-start.24 = (bf16[192,256]{1,0:T(8,128)(2,1)}, bf16[192,256]{1,0:T(8,128)(2,1)S(1)}, u32[]{:S(2)}, u32[]{:S(2)}) collective-permute-start(bf16[192,256]{1,0:T(8,128)(2,1)} %get-tuple-element.65), channel_id=1, source_target_pairs={{0,1},{1,0},{2,3},{3,2},{4,5},{5,4},{6,7},{7,6},{8,9},{9,8},{10,11... | collective-permute-start | bytes 294920 | tf_op jit(solution)/shard_map/ppermute | solution.py:210
  19.5 12.2 %collective-permute-start.25 = (bf16[192,256]{1,0:T(8,128)(2,1)}, bf16[192,256]{1,0:T(8,128)(2,1)S(1)}, u32[]{:S(2)}, u32[]{:S(2)}) collective-permute-start(bf16[192,256]{1,0:T(8,128)(2,1)} %get-tuple-element.66), channel_id=1, source_target_pairs={{0,9},{1,8},{2,11},{3,10},{4,13},{5,12},{6,15},{7,14},{8,1},{9,0},... | collective-permute-start | bytes 294920 | tf_op jit(solution)/shard_map/ppermute | solution.py:210
  25.7 16.1 %collective-permute-start.8 = (bf16[256,512]{1,0:T(8,128)(2,1)S(1)}, bf16[256,512]{1,0:T(8,128)(2,1)S(1)}, u32[]{:S(2)}, u32[]{:S(2)}) collective-permute-start(bf16[256,512]{1,0:T(8,128)(2,1)S(1)} %constant_dynamic-update-slice_fusion.rest_8_), channel_id=1, source_target_pairs={{0,2},{1,3},{2,4},{3,5},{4,6},{5,7},{8,10},{9,11},{10,12},{11,13},... | collective-permute-start | bytes 786440 | tf_op jit(solution)/shard_map/ppermute | solution.py:206
  30.3 12.2 %collective-permute-start.9 = (bf16[256,512]{1,0:T(8,128)(2,1)S(1)}, bf16[256,512]{1,0:T(8,128)(2,1)S(1)}, u32[]{:S(2)}, u32[]{:S(2)}) collective-permute-start(bf16[256,512]{1,0:T(8,128)(2,1)S(1)} %constant_dynamic-update-slice_fusion.rest_8_), channel_id=1, source_target_pairs={{2,0},{3,1},{4,2},{5,3},{6,4},{7,5},{10,8},{11,9},{12,10},{13,11},... | collective-permute-start | bytes 786440 | tf_op jit(solution)/shard_map/ppermute | solution.py:206
  31.8 16.7 %collective-permute-start.31 = (bf16[256,512]{1,0:T(8,128)(2,1)S(1)}, bf16[256,512]{1,0:T(8,128)(2,1)S(1)}, u32[]{:S(2)}, u32[]{:S(2)}) collective-permute-start(bf16[256,512]{1,0:T(8,128)(2,1)S(1)} %collective-permute-done.29.rest_9_), channel_id=1, source_target_pairs={{2,4},{3,5},{4,6},{5,7},{10,12},{11,13},{12,14},{13,15},{18,20},{1... | collective-permute-start | bytes 786440 | tf_op jit(solution)/shard_map/ppermute | solution.py:206
  32.5 16.6 %collective-permute-start.32 = (bf16[256,512]{1,0:T(8,128)(2,1)S(1)}, bf16[256,512]{1,0:T(8,128)(2,1)S(1)}, u32[]{:S(2)}, u32[]{:S(2)}) collective-permute-start(bf16[256,512]{1,0:T(8,128)(2,1)S(1)} %collective-permute-done.30.rest_10_), channel_id=1, source_target_pairs={{2,0},{3,1},{4,2},{5,3},{10,8},{11,9},{12,10},{13,11},{18,16},{19,... | collective-permute-start | bytes 786440 | tf_op jit(solution)/shard_map/ppermute | solution.py:206
  41.9 11.1 %collective-permute-start.10 = (bf16[256,512]{1,0:T(8,128)(2,1)S(1)}, bf16[256,512]{1,0:T(8,128)(2,1)S(1)}, u32[]{:S(2)}, u32[]{:S(2)}) collective-permute-start(bf16[256,512]{1,0:T(8,128)(2,1)S(1)} %collective-permute-done.8.rest_9_), channel_id=1, source_target_pairs={{2,4},{3,5},{4,6},{5,7},{10,12},{11,13},{12,14},{13,15},{18,20},{1... | collective-permute-start | bytes 786440 | tf_op jit(solution)/shard_map/ppermute | solution.py:206
  42.6 16.5 %collective-permute-start.11 = (bf16[256,512]{1,0:T(8,128)(2,1)S(1)}, bf16[256,512]{1,0:T(8,128)(2,1)S(1)}, u32[]{:S(2)}, u32[]{:S(2)}) collective-permute-start(bf16[256,512]{1,0:T(8,128)(2,1)S(1)} %collective-permute-done.9.rest_10_), channel_id=1, source_target_pairs={{2,0},{3,1},{4,2},{5,3},{10,8},{11,9},{12,10},{13,11},{18,16},{19,... | collective-permute-start | bytes 786440 | tf_op jit(solution)/shard_map/ppermute | solution.py:206
  48.4 15.2 %collective-permute-start.33 = (bf16[256,512]{1,0:T(8,128)(2,1)S(1)}, bf16[256,512]{1,0:T(8,128)(2,1)S(1)}, u32[]{:S(2)}, u32[]{:S(2)}) collective-permute-start(bf16[256,512]{1,0:T(8,128)(2,1)S(1)} %collective-permute-done.31.rest_11_), channel_id=1, source_target_pairs={{4,6},{5,7},{12,14},{13,15},{20,22},{21,23},{28,30},{29,31}} | collective-permute-start | bytes 786440 | tf_op jit(solution)/shard_map/ppermute | solution.py:206
  49.1 15.6 %collective-permute-start.34 = (bf16[256,512]{1,0:T(8,128)(2,1)S(1)}, bf16[256,512]{1,0:T(8,128)(2,1)S(1)}, u32[]{:S(2)}, u32[]{:S(2)}) collective-permute-start(bf16[256,512]{1,0:T(8,128)(2,1)S(1)} %collective-permute-done.32.rest_12_), channel_id=1, source_target_pairs={{2,0},{3,1},{10,8},{11,9},{18,16},{19,17},{26,24},{27,25}} | collective-permute-start | bytes 786440 | tf_op jit(solution)/shard_map/ppermute | solution.py:206
  51.3 9.0 %collective-permute-start.2 = (bf16[192,256]{1,0:T(8,128)(2,1)}, bf16[192,256]{1,0:T(8,128)(2,1)S(1)}, u32[]{:S(2)}, u32[]{:S(2)}) collective-permute-start(bf16[192,256]{1,0:T(8,128)(2,1)} %get-tuple-element.46), channel_id=1, source_target_pairs={{0,24},{1,25},{2,26},{3,27},{4,28},{5,29},{6,30},{7,31},{8,16},{9,... | collective-permute-start | bytes 294920 | tf_op jit(solution)/shard_map/ppermute | solution.py:210
  53.0 21.7 %collective-permute-start.12 = (bf16[256,512]{1,0:T(8,128)(2,1)S(1)}, bf16[256,512]{1,0:T(8,128)(2,1)S(1)}, u32[]{:S(2)}, u32[]{:S(2)}) collective-permute-start(bf16[256,512]{1,0:T(8,128)(2,1)S(1)} %collective-permute-done.10.rest_11_), channel_id=1, source_target_pairs={{4,6},{5,7},{12,14},{13,15},{20,22},{21,23},{28,30},{29,31}} | collective-permute-start | bytes 786440 | tf_op jit(solution)/shard_map/ppermute | solution.py:206
  59.1 16.0 %collective-permute-start.13 = (bf16[256,512]{1,0:T(8,128)(2,1)S(1)}, bf16[256,512]{1,0:T(8,128)(2,1)S(1)}, u32[]{:S(2)}, u32[]{:S(2)}) collective-permute-start(bf16[256,512]{1,0:T(8,128)(2,1)S(1)} %collective-permute-done.11.rest_12_), channel_id=1, source_target_pairs={{2,0},{3,1},{10,8},{11,9},{18,16},{19,17},{26,24},{27,25}} | collective-permute-start | bytes 786440 | tf_op jit(solution)/shard_map/ppermute | solution.py:206
  61.9 9.1 %collective-permute-start.4 = (bf16[192,256]{1,0:T(8,128)(2,1)}, bf16[192,256]{1,0:T(8,128)(2,1)S(1)}, u32[]{:S(2)}, u32[]{:S(2)}) collective-permute-start(bf16[192,256]{1,0:T(8,128)(2,1)} %get-tuple-element.48), channel_id=1, source_target_pairs={{0,9},{1,8},{2,11},{3,10},{4,13},{5,12},{6,15},{7,14},{8,1},{9,0},... | collective-permute-start | bytes 294920 | tf_op jit(solution)/shard_map/ppermute | solution.py:210
  63.6 9.4 %collective-permute-start.5 = (bf16[192,256]{1,0:T(8,128)(2,1)}, bf16[192,256]{1,0:T(8,128)(2,1)S(1)}, u32[]{:S(2)}, u32[]{:S(2)}) collective-permute-start(bf16[192,256]{1,0:T(8,128)(2,1)} %get-tuple-element.49), channel_id=1, source_target_pairs={{0,17},{1,16},{2,19},{3,18},{4,21},{5,20},{6,23},{7,22},{8,25},{9,... | collective-permute-start | bytes 294920 | tf_op jit(solution)/shard_map/ppermute | solution.py:210
  64.7 8.4 %collective-permute-start.6 = (bf16[192,256]{1,0:T(8,128)(2,1)}, bf16[192,256]{1,0:T(8,128)(2,1)S(1)}, u32[]{:S(2)}, u32[]{:S(2)}) collective-permute-start(bf16[192,256]{1,0:T(8,128)(2,1)} %get-tuple-element.50), channel_id=1, source_target_pairs={{0,25},{1,24},{2,27},{3,26},{4,29},{5,28},{6,31},{7,30},{8,17},{9,... | collective-permute-start | bytes 294920 | tf_op jit(solution)/shard_map/ppermute | solution.py:210
  71.1 11.6 %collective-permute-start.35 = (bf16[192,256]{1,0:T(8,128)(2,1)}, bf16[192,256]{1,0:T(8,128)(2,1)S(1)}, u32[]{:S(2)}, u32[]{:S(2)}) collective-permute-start(bf16[192,256]{1,0:T(8,128)(2,1)} %get-tuple-element.72), channel_id=1, source_target_pairs={{0,8},{1,9},{2,10},{3,11},{4,12},{5,13},{6,14},{7,15},{8,0},{9,1},... | collective-permute-start | bytes 294920 | tf_op jit(solution)/shard_map/ppermute | solution.py:210
  73.0 10.0 %collective-permute-start.36 = (bf16[192,256]{1,0:T(8,128)(2,1)}, bf16[192,256]{1,0:T(8,128)(2,1)S(1)}, u32[]{:S(2)}, u32[]{:S(2)}) collective-permute-start(bf16[192,256]{1,0:T(8,128)(2,1)} %get-tuple-element.73), channel_id=1, source_target_pairs={{0,16},{1,17},{2,18},{3,19},{4,20},{5,21},{6,22},{7,23},{8,24},{9,... | collective-permute-start | bytes 294920 | tf_op jit(solution)/shard_map/ppermute | solution.py:210
  73.1 11.4 %collective-permute-start.37 = (bf16[192,256]{1,0:T(8,128)(2,1)}, bf16[192,256]{1,0:T(8,128)(2,1)S(1)}, u32[]{:S(2)}, u32[]{:S(2)}) collective-permute-start(bf16[192,256]{1,0:T(8,128)(2,1)} %get-tuple-element.74), channel_id=1, source_target_pairs={{0,24},{1,25},{2,26},{3,27},{4,28},{5,29},{6,30},{7,31},{8,16},{9,... | collective-permute-start | bytes 294920 | tf_op jit(solution)/shard_map/ppermute | solution.py:210
  74.6 11.4 %collective-permute-start.38 = (bf16[192,256]{1,0:T(8,128)(2,1)}, bf16[192,256]{1,0:T(8,128)(2,1)S(1)}, u32[]{:S(2)}, u32[]{:S(2)}) collective-permute-start(bf16[192,256]{1,0:T(8,128)(2,1)} %get-tuple-element.75), channel_id=1, source_target_pairs={{0,1},{1,0},{2,3},{3,2},{4,5},{5,4},{6,7},{7,6},{8,9},{9,8},{10,11... | collective-permute-start | bytes 294920 | tf_op jit(solution)/shard_map/ppermute | solution.py:210
  75.1 11.6 %collective-permute-start.39 = (bf16[192,256]{1,0:T(8,128)(2,1)}, bf16[192,256]{1,0:T(8,128)(2,1)S(1)}, u32[]{:S(2)}, u32[]{:S(2)}) collective-permute-start(bf16[192,256]{1,0:T(8,128)(2,1)} %get-tuple-element.76), channel_id=1, source_target_pairs={{0,9},{1,8},{2,11},{3,10},{4,13},{5,12},{6,15},{7,14},{8,1},{9,0},... | collective-permute-start | bytes 294920 | tf_op jit(solution)/shard_map/ppermute | solution.py:210
  83.0 7.2 %collective-permute-start.41 = (bf16[192,256]{1,0:T(8,128)(2,1)S(1)}, bf16[192,256]{1,0:T(8,128)(2,1)S(1)}, u32[]{:S(2)}, u32[]{:S(2)}) collective-permute-start(bf16[192,256]{1,0:T(8,128)(2,1)S(1)} %copy-done.39), channel_id=1, source_target_pairs={{0,25},{1,24},{2,27},{3,26},{4,29},{5,28},{6,31},{7,30},{8,17},{9,... | collective-permute-start | bytes 294920 | tf_op jit(solution)/shard_map/ppermute | solution.py:210
  84.5 7.2 %collective-permute-start.14 = (bf16[192,256]{1,0:T(8,128)(2,1)}, bf16[192,256]{1,0:T(8,128)(2,1)S(1)}, u32[]{:S(2)}, u32[]{:S(2)}) collective-permute-start(bf16[192,256]{1,0:T(8,128)(2,1)} %get-tuple-element.54), channel_id=1, source_target_pairs={{0,8},{1,9},{2,10},{3,11},{4,12},{5,13},{6,14},{7,15},{8,0},{9,1},... | collective-permute-start | bytes 294920 | tf_op jit(solution)/shard_map/ppermute | solution.py:210
  86.0 8.1 %collective-permute-start.15 = (bf16[192,256]{1,0:T(8,128)(2,1)}, bf16[192,256]{1,0:T(8,128)(2,1)S(1)}, u32[]{:S(2)}, u32[]{:S(2)}) collective-permute-start(bf16[192,256]{1,0:T(8,128)(2,1)} %get-tuple-element.55), channel_id=1, source_target_pairs={{0,16},{1,17},{2,18},{3,19},{4,20},{5,21},{6,22},{7,23},{8,24},{9,... | collective-permute-start | bytes 294920 | tf_op jit(solution)/shard_map/ppermute | solution.py:210
  86.7 12.2 %collective-permute-start.16 = (bf16[192,256]{1,0:T(8,128)(2,1)}, bf16[192,256]{1,0:T(8,128)(2,1)S(1)}, u32[]{:S(2)}, u32[]{:S(2)}) collective-permute-start(bf16[192,256]{1,0:T(8,128)(2,1)} %get-tuple-element.56), channel_id=1, source_target_pairs={{0,24},{1,25},{2,26},{3,27},{4,28},{5,29},{6,30},{7,31},{8,16},{9,... | collective-permute-start | bytes 294920 | tf_op jit(solution)/shard_map/ppermute | solution.py:210
  89.6 9.3 %collective-permute-start.17 = (bf16[192,256]{1,0:T(8,128)(2,1)}, bf16[192,256]{1,0:T(8,128)(2,1)S(1)}, u32[]{:S(2)}, u32[]{:S(2)}) collective-permute-start(bf16[192,256]{1,0:T(8,128)(2,1)} %get-tuple-element.57), channel_id=1, source_target_pairs={{0,1},{1,0},{2,3},{3,2},{4,5},{5,4},{6,7},{7,6},{8,9},{9,8},{10,11... | collective-permute-start | bytes 294920 | tf_op jit(solution)/shard_map/ppermute | solution.py:210
  90.3 8.6 %collective-permute-start.18 = (bf16[192,256]{1,0:T(8,128)(2,1)}, bf16[192,256]{1,0:T(8,128)(2,1)S(1)}, u32[]{:S(2)}, u32[]{:S(2)}) collective-permute-start(bf16[192,256]{1,0:T(8,128)(2,1)} %get-tuple-element.58), channel_id=1, source_target_pairs={{0,9},{1,8},{2,11},{3,10},{4,13},{5,12},{6,15},{7,14},{8,1},{9,0},... | collective-permute-start | bytes 294920 | tf_op jit(solution)/shard_map/ppermute | solution.py:210
  91.7 7.2 %collective-permute-start.19 = (bf16[192,256]{1,0:T(8,128)(2,1)}, bf16[192,256]{1,0:T(8,128)(2,1)S(1)}, u32[]{:S(2)}, u32[]{:S(2)}) collective-permute-start(bf16[192,256]{1,0:T(8,128)(2,1)} %get-tuple-element.59), channel_id=1, source_target_pairs={{0,17},{1,16},{2,19},{3,18},{4,21},{5,20},{6,23},{7,22},{8,25},{9,... | collective-permute-start | bytes 294920 | tf_op jit(solution)/shard_map/ppermute | solution.py:210
  (57 other events, 851.6 us)

commit v2 on v0

v2 whole, which is shorter than its diff:
```python
import functools

import jax
import jax.numpy as jnp
from jax import lax
from jax.experimental import pallas as pl
from jax.experimental.pallas import tpu as pltpu
from jax.sharding import PartitionSpec as P

BLK = 128
HEAD = 128
CHUNKS = 2
VMEM_LIMIT = 32 * 1024 * 1024


def silu_halved(t):
    return t + t * jnp.tanh(t)


def centred_norm(x):
    middle = jnp.mean(x, axis=-1, keepdims=True)
    shifted = x - middle
    spread = jnp.mean(shifted * shifted, axis=-1, keepdims=True)
    return shifted * lax.rsqrt(spread + 1e-05)


def slots_of(user, me, cap, users):
    rows = user.shape[1]
    rel = user ^ me
    places = max(8, users)
    one_hot = rel == lax.broadcasted_iota(jnp.int32, (places, rows), 0)
    one_hot = one_hot.astype(jnp.float32)
    first = lax.broadcasted_iota(jnp.int32, (rows, rows), 0)
    second = lax.broadcasted_iota(jnp.int32, (rows, rows), 1)
    earlier = (first < second).astype(jnp.bfloat16)
    rank = jnp.dot(one_hot.astype(jnp.bfloat16), earlier, preferred_element_type=jnp.float32)
    rank = jnp.sum(rank * one_hot, axis=0, keepdims=True)
    return rel.astype(jnp.float32) * cap + rank


def kv_split_kernel(chunks, kv, *outs):
    half = kv.shape[1] // 2
    wide = half // chunks
    for chunk in range(chunks):
        for part in range(2):
            outs[chunk][:, part * wide:(part + 1) * wide] = kv[
                :, part * half + chunk * wide:part * half + (chunk + 1) * wide
            ]


def query_kernel(cap, users, ids, feat, user, gain, wq, normed_out, *outs):
    rows, width = feat.shape
    normed = (centred_norm(feat[...].astype(jnp.float32)) * gain[...]).astype(jnp.bfloat16)
    normed_out[...] = normed
    slot = slots_of(user[...], ids[0], cap, users)
    places = lax.broadcasted_iota(jnp.int32, (users * cap, rows), 0).astype(jnp.float32)
    pick = (places == slot).astype(jnp.bfloat16)
    part = jnp.dot(normed, wq[...], preferred_element_type=jnp.float32)
    query = silu_halved(part * 0.5).astype(jnp.bfloat16)
    sent = jnp.dot(pick, query, preferred_element_type=jnp.float32).astype(jnp.bfloat16)
    for d in range(users):
        outs[d][...] = sent[d * cap:(d + 1) * cap, :]


def gate_kernel(cap, users, ids, normed, user, wg, gate, pick):
    rows = user.shape[1]
    part = jnp.dot(normed[...], wg[...], preferred_element_type=jnp.float32)
    gate[...] = silu_halved(part * 0.5)
    slot = slots_of(user[...], ids[0], cap, users)
    slot = jnp.transpose(jnp.broadcast_to(slot, (128, rows)))[:, 0:1]
    places = lax.broadcasted_iota(jnp.int32, (rows, users * cap), 1).astype(jnp.float32)
    pick[...] = (places == slot).astype(jnp.bfloat16)


def attend_kernel(users, chips, ids, mask, *rest):
    queries = rest[:users]
    blocks = rest[users:users + 2 * chips]
    outs, (live_kv, all_q) = rest[-2 - users:-2], rest[-2:]
    core, z = ids[1], ids[2]
    cap, wide = queries[0].shape
    taken = jnp.int32(0)
    for d in range(chips):
        for swap in range(2):
            live = mask[0, 2 * (z ^ d) + (core ^ swap)] > 0

            def take(block=blocks[2 * d + swap], taken=taken):
                at = pl.multiple_of(taken * BLK, BLK)
                live_kv[pl.ds(at, BLK), :] = block[...]

            pl.when(live)(take)
            taken = jnp.minimum(taken + live.astype(jnp.int32), chips - 1)
    for i, q in enumerate(queries):
        all_q[i * cap:(i + 1) * cap, :] = q[...]
    scale = 0.5 * HEAD ** (-0.5)
    for head in range(wide // HEAD):
        cols = slice(head * HEAD, (head + 1) * HEAD)
        keys = live_kv[:, cols]
        values = live_kv[:, wide + head * HEAD:wide + (head + 1) * HEAD]
        scores = lax.dot_general(
            all_q[:, cols], keys, (((1,), (1,)), ((), ())), preferred_element_type=jnp.float32
        )
        weight = silu_halved(scores * scale).astype(jnp.bfloat16)
        got = jnp.dot(weight, values, preferred_element_type=jnp.float32).astype(jnp.bfloat16)
        for i, out in enumerate(outs):
            out[:, cols] = got[i * cap:(i + 1) * cap, :]


def finish_kernel(users, feat, gate, pick, gain, w_out, *rest):
    parts, out, back = rest[:-2], rest[-2], rest[-1]
    cap, wide = parts[0].shape
    for i, part in enumerate(parts):
        chunk, d = i // users, i % users
        back[d * cap:(d + 1) * cap, chunk * wide:(chunk + 1) * wide] = part[...]
    attended = jnp.dot(pick[...], back[...], preferred_element_type=jnp.float32)
    mixed = (centred_norm(attended) * gain[...] * gate[...]).astype(jnp.bfloat16)
    grown = jnp.dot(mixed, w_out[...], preferred_element_type=jnp.float32)
    out[...] = (feat[...].astype(jnp.float32) + grown).astype(jnp.bfloat16)


SMEM = pl.BlockSpec(memory_space=pltpu.SMEM)
ANY = pl.BlockSpec(memory_space=pl.ANY)


def whole(*dims, at=None):
    return pl.BlockSpec(dims, lambda i: at or (0,) * len(dims))


def call(kernel, name, in_specs, out_shape, scratch, flops, *args):
    moved = sum(a.size * a.dtype.itemsize for a in args)
    return pl.pallas_call(
        kernel,
        name=name,
        grid=(1,),
        in_specs=in_specs,
        out_specs=[whole(*s.shape) for s in out_shape],
        out_shape=out_shape,
        scratch_shapes=scratch,
        cost_estimate=pl.CostEstimate(flops=flops, bytes_accessed=moved, transcendentals=0),
        compiler_params=pltpu.CompilerParams(vmem_limit_bytes=VMEM_LIMIT),
    )(*args)


def on_device(cand_feat, cand_user, hist_kv, hist_mask, gain_in, w_uq, gain_attn, w_out):
    users = lax.axis_size("users")
    ctx = lax.axis_size("ctx")
    chips = ctx // 2
    rows, width = cand_feat.shape
    cap = 2 * rows // users
    wide = width // CHUNKS
    me = lax.axis_index("users")
    place = lax.axis_index("ctx")
    ids = jnp.stack([me, place % 2, place // 2]).astype(jnp.int32)
    bf16 = jnp.bfloat16
    user_row = cand_user.reshape(1, rows)

    def shape(*dims, dtype=bf16):
        return jax.ShapeDtypeStruct(dims, dtype)

    def over_z(value, d):
        return lax.ppermute(value, "ctx", [(c, c ^ (2 * d)) for c in range(ctx)])

    def over_cores(value):
        return lax.ppermute(value, "ctx", [(c, c ^ 1) for c in range(ctx)])

    def over_users(values):
        return [values[0]] + [
            lax.ppermute(values[d], "users", [(u, u ^ d) for u in range(users)])
            for d in range(1, users)
        ]

    kv = hist_kv[0, 0]
    split = call(
        functools.partial(kv_split_kernel, CHUNKS), "kv_split", [whole(*kv.shape)],
        [shape(BLK, 2 * wide)] * CHUNKS, [], 0, kv,
    )
    gathered = []
    for own in split:
        held = {0: own}
        for d in [3, 1, 2] + list(range(4, chips)):
            held[d] = over_z(held[3], 1) if d == 2 else over_z(own, d)
        blocks = []
        for d in range(chips):
            blocks += [held[d], over_cores(held[d])]
        gathered.append(blocks)

    normed, *queries = call(
        functools.partial(query_kernel, cap, users), "query",
        [SMEM, whole(rows, width), whole(1, rows), whole(1, width), whole(width, width, at=(0, 1))],
        [shape(rows, width)] + [shape(cap, width)] * users,
        [], 4 * rows * width * width,
        ids, cand_feat, user_row, gain_in, w_uq[0],
    )
    arrived = over_users(queries)

    gate, pick = call(
        functools.partial(gate_kernel, cap, users), "gate",
        [SMEM, whole(rows, width), whole(1, rows), whole(width, width)],
        [shape(rows, width, dtype=jnp.float32), shape(rows, users * cap)],
        [], 2 * rows * width * width,
        ids, normed, user_row, w_uq[0],
    )

    returned = []
    for chunk in range(CHUNKS):
        scored = call(
            functools.partial(attend_kernel, users, chips), "attend",
            [SMEM, SMEM]
            + [whole(cap, wide, at=(0, chunk))] * users
            + [whole(BLK, 2 * wide)] * (2 * chips)
            + [ANY],
            [shape(cap, wide)] * users,
            [pltpu.VMEM((chips * BLK, 2 * wide), bf16), pltpu.VMEM((users * cap, wide), bf16)],
            8 * users * cap * chips * BLK * wide,
            ids, hist_mask, *arrived, *gathered[chunk], gate,
        )
        returned += over_users(scored)

    return call(
        functools.partial(finish_kernel, users), "finish",
        [
            whole(rows, width), whole(rows, width), whole(rows, users * cap), whole(1, width),
            whole(width, width),
        ]
        + [whole(cap, wide)] * len(returned),
        [shape(rows, width)],
        [pltpu.VMEM((users * cap, width), bf16)],
        4 * rows * width * width,
        cand_feat, gate, pick, gain_attn, w_out[0], *returned,
    )[0]


def solution(mesh):
    in_specs = (
        P(("users", "ctx"), None),
        P(("users", "ctx"), None),
        P(None, "users", "ctx", None),
        P("users", None),
        P(),
        P(),
        P(),
        P(),
    )
    out_specs = P(("users", "ctx"), None)
    return jax.shard_map(
        on_device, mesh=mesh, in_specs=in_specs, out_specs=out_specs, check_vma=False
    )
```

time: 181 us -> 70.5 us (0.39)
  other arithmetic: 45 us -> 0.08 us
  local copies, waits for them, and re-layouts: 33.8 us -> 5.75 us
  matrix products: 27.9 us -> 0 us
  waiting for transfers between devices: 45.9 us -> 26.3 us
  starting transfers between devices: 9.63 us -> 25.1 us
  between operations: 13.5 us -> 0.1 us
  Pallas kernels: 0 us -> 12.9 us
  loops' own time: 4.69 us -> 0 us
    all_to_all x2 -> x0, waiting for transfers between devices: 40.2 us -> none  [the longest x1 20.2 us: on_device(): lax.all_to_all(outgoing.reshape(owner_count, slot_cap, feat_width), 'user...]
    dot_general x6 -> x0, matrix products: 27.9 us -> none  [the longest x4 18.9 us: score_block(): jnp.einsum('hsk,khd->shd', attn_weights, value_heads, preferred_element_t...]
    ppermute x0 -> x23, waiting for transfers between devices: none -> 26.3 us  [the longest x9 15.3 us: over_users(): lax.ppermute(values[d], 'users', [(u, u ^ d) for u in range(users)])]
    ppermute x0 -> x23, starting transfers between devices: none -> 25.1 us  [the longest x9 13.1 us: over_users(): lax.ppermute(values[d], 'users', [(u, u ^ d) for u in range(users)])]
    add x4 -> x0, other arithmetic: 19.5 us -> none  [score_block(): return running + combined.reshape(running.shape)]
    reduce_sum x13 -> x0, other arithmetic: 18.6 us -> none  [the longest x8 10.2 us: walk_block(): is_live = jnp.sum(jnp.where(block_range == block_id, block_mask, 0))]
    pallas_call x0 -> x6, Pallas kernels: none -> 12.9 us  [call(): pl.pallas_call(kernel, name=name, grid=(1,), in_specs=in_specs, out_specs...]
    all_to_all x2 -> x0, starting transfers between devices: 9.63 us -> none  [the longest x1 5.3 us: on_device(): lax.all_to_all(outgoing.reshape(owner_count, slot_cap, feat_width), 'user...]
  transfers between devices with their start and end apart: 3 -> 23, of which waited for: 3 -> 9; matrix products, arithmetic and copies ran while one was open for 10% -> 0% of each run, Pallas kernels for 0% -> 14%
where the time goes in v2:
time: 70.5 us; the launch traced here: 70.2 us
  waiting for transfers between devices  26.3 us (37%)
  starting transfers between devices  25.1 us (36%)
  Pallas kernels  12.9 us (18%)
  local copies, waits for them, and re-layouts  5.75 us (8%)
    ppermute x9, waiting for transfers between devices, over_users(): lax.ppermute(values[d], 'users', [(u, u ^ d) for u in range(users)])  15.3 us
    ppermute x9, starting transfers between devices, over_users(): lax.ppermute(values[d], 'users', [(u, u ^ d) for u in range(users)])  13.1 us
    pallas_call x6, Pallas kernels, call(): pl.pallas_call(kernel, name=name, grid=(1,), in_specs=in_specs, out_specs...  12.9 us
    ppermute x6, waiting for transfers between devices, over_z(): return lax.ppermute(value, 'ctx', [(c, c ^ 2 * d) for c in range(ctx)])  10.9 us
    ppermute x6, starting transfers between devices, over_z(): return lax.ppermute(value, 'ctx', [(c, c ^ 2 * d) for c in range(ctx)])  10 us
    unnamed x20, local copies, waits for them, and re-layouts  5.75 us
    ppermute x8, starting transfers between devices, over_cores(): return lax.ppermute(value, 'ctx', [(c, c ^ 1) for c in range(ctx)])  2.05 us
  transfers between devices with their start and end apart: 23, of which 9 were waited for; matrix products, arithmetic and copies ran while one was open for 0% of the time, Pallas kernels for 14%

profile of v2, /device:TPU:0, one launch (start us, length us, event | category | flops | bytes accessed | tf_op | source)
XLA Modules:
  0.0 70.2 jit_solution(1215974465518172344)
XLA Ops:
  0.0 1.0 %copy-done.5 = bf16[1,1,128,2048]{3,2,1,0:T(8,128)(2,1)S(1)} copy-done((bf16[1,1,128,2048]{3,2,1,0:T(8,128)(2,1)S(1)}, bf16[1,1,128,2048]{3,2,1,0:T(8,128)(2,1)}, u32[]{:S(2)}) %copy-start.5) | copy-done | bytes 524312
  1.1 0.5 collective-permute-start.3
  1.6 2.6 %collective-permute-start.4 = (bf16[128,1024]{1,0:T(8,128)(2,1)S(1)}, bf16[128,1024]{1,0:T(8,128)(2,1)S(1)}, u32[]{:S(2)}, u32[]{:S(2)}) collective-permute-start(bf16[128,1024]{1,0:T(8,128)(2,1)S(1)} %get-tuple-element.29.rest_4_), channel_id=1, source_target_pairs={{0,2},{1,3},{2,0},{3,1},{4,6},{5,7},{6,4},{7,5},{8,10},{9,11},{10,... | collective-permute-start | bytes 786440 | tf_op jit(solution)/shard_map/ppermute | solution.py:160
  4.3 2.5 %collective-permute-start.6 = (bf16[128,1024]{1,0:T(8,128)(2,1)S(1)}, bf16[128,1024]{1,0:T(8,128)(2,1)S(1)}, u32[]{:S(2)}, u32[]{:S(2)}) collective-permute-start(bf16[128,1024]{1,0:T(8,128)(2,1)S(1)} %get-tuple-element.29.rest_4_), channel_id=1, source_target_pairs={{0,6},{1,7},{2,4},{3,5},{4,2},{5,3},{6,0},{7,1},{8,14},{9,15},{10,... | collective-permute-start | bytes 786440 | tf_op jit(solution)/shard_map/ppermute | solution.py:160
  6.7 0.7 collective-permute-start.14
  7.5 2.2 %copy-done = bf16[1,1024,2048]{2,1,0:T(8,128)(2,1)S(1)} copy-done((bf16[1,1024,2048]{2,1,0:T(8,128)(2,1)S(1)}, bf16[1,1024,2048]{2,1,0:T(8,128)(2,1)}, u32[]{:S(2)}) %copy-start) | copy-done | bytes 4194328
  9.7 1.1 %copy-done.3 = bf16[384,1024]{1,0:T(8,128)(2,1)S(1)} copy-done((bf16[384,1024]{1,0:T(8,128)(2,1)S(1)}, bf16[384,1024]{1,0:T(8,128)(2,1)}, u32[]{:S(2)}) %copy-start.3) | copy-done | bytes 786456
  10.8 0.7 copy-done.7
  11.5 0.7 copy-done.8
  12.2 2.9 %query.1 = (bf16[384,1024]{1,0:T(8,128)(2,1)S(1)}, bf16[192,1024]{1,0:T(8,128)(2,1)S(1)}, bf16[192,1024]{1,0:T(8,128)(2,1)S(1)}, bf16[192,1024]{1,0:T(8,128)(2,1)S(1)}, bf16[192,1024]{1,0:T(8,128)(2,1)S(1)}) custom-call(s32[3]{0:T(128)S(1)} %pad_add_fusion.ids, bf16[384,1024]{1,0:T(8,128)(2,1)S(1)} %copy-done.3, s32[1,384]{1,0:T(1,128)S(1)} %bitcast.11, ...), custom_call_target="tpu_custom_call" | custom-call | flops 1610612736 | bytes 4986380 | tf_op jit(solution)/shard_map/query/pallas_call | solution.py:130
  15.1 1.6 %collective-permute-start = (bf16[192,1024]{1,0:T(8,128)(2,1)S(1)}, bf16[192,1024]{1,0:T(8,128)(2,1)S(1)}, u32[]{:S(2)}, u32[]{:S(2)}) collective-permute-start(bf16[192,1024]{1,0:T(8,128)(2,1)S(1)} %get-tuple-element.26), channel_id=1, source_target_pairs={{0,8},{8,0},{16,24},{24,16},{1,9},{9,1},{17,25},{25,17},{2,10},{10... | collective-permute-start | bytes 1179656 | tf_op jit(solution)/shard_map/ppermute | solution.py:167
  16.6 1.5 %collective-permute-start.1 = (bf16[192,1024]{1,0:T(8,128)(2,1)S(1)}, bf16[192,1024]{1,0:T(8,128)(2,1)S(1)}, u32[]{:S(2)}, u32[]{:S(2)}) collective-permute-start(bf16[192,1024]{1,0:T(8,128)(2,1)S(1)} %get-tuple-element.27), channel_id=1, source_target_pairs={{0,16},{8,24},{16,0},{24,8},{1,17},{9,25},{17,1},{25,9},{2,18},{10... | collective-permute-start | bytes 1179656 | tf_op jit(solution)/shard_map/ppermute | solution.py:167
  18.1 2.9 %collective-permute-start.16 = (bf16[128,1024]{1,0:T(8,128)(2,1)S(1)}, bf16[128,1024]{1,0:T(8,128)(2,1)S(1)}, u32[]{:S(2)}, u32[]{:S(2)}) collective-permute-start(bf16[128,1024]{1,0:T(8,128)(2,1)S(1)} %get-tuple-element.34.rest_4_), channel_id=1, source_target_pairs={{0,6},{1,7},{2,4},{3,5},{4,2},{5,3},{6,0},{7,1},{8,14},{9,15},{10,... | collective-permute-start | bytes 786440 | tf_op jit(solution)/shard_map/ppermute | solution.py:160
  21.0 1.6 %collective-permute-done.14.rest_6_ = bf16[128,1024]{1,0:T(8,128)(2,1)S(1)} collective-permute-done((bf16[128,1024]{1,0:T(8,128)(2,1)S(1)}, bf16[128,1024]{1,0:T(8,128)(2,1)S(1)}, u32[]{:S(2)}, u32[]{:S(2)}) %collective-permute-start.14) | collective-permute-done | bytes 262176 | tf_op jit(solution)/shard_map/ppermute | solution.py:160
  22.6 2.8 %collective-permute-start.2 = (bf16[192,1024]{1,0:T(8,128)(2,1)S(1)}, bf16[192,1024]{1,0:T(8,128)(2,1)S(1)}, u32[]{:S(2)}, u32[]{:S(2)}) collective-permute-start(bf16[192,1024]{1,0:T(8,128)(2,1)S(1)} %get-tuple-element.28), channel_id=1, source_target_pairs={{0,24},{8,16},{16,8},{24,0},{1,25},{9,17},{17,9},{25,1},{2,26},{10... | collective-permute-start | bytes 1179656 | tf_op jit(solution)/shard_map/ppermute | solution.py:167
  25.5 5.3 %collective-permute-done.16.rest_10_ = bf16[128,1024]{1,0:T(8,128)(2,1)S(1)} collective-permute-done((bf16[128,1024]{1,0:T(8,128)(2,1)S(1)}, bf16[128,1024]{1,0:T(8,128)(2,1)S(1)}, u32[]{:S(2)}, u32[]{:S(2)}) %collective-permute-start.16) | collective-permute-done | bytes 262176 | tf_op jit(solution)/shard_map/ppermute | solution.py:160
  31.3 4.1 %collective-permute-done.1.rest_2_ = bf16[192,1024]{1,0:T(8,128)(2,1)S(1)} collective-permute-done((bf16[192,1024]{1,0:T(8,128)(2,1)S(1)}, bf16[192,1024]{1,0:T(8,128)(2,1)S(1)}, u32[]{:S(2)}, u32[]{:S(2)}) %collective-permute-start.1) | collective-permute-done | bytes 393248 | tf_op jit(solution)/shard_map/ppermute | solution.py:167
  35.4 1.3 %collective-permute-start.17 = (bf16[128,1024]{1,0:T(8,128)(2,1)S(1)}, bf16[128,1024]{1,0:T(8,128)(2,1)S(1)}, u32[]{:S(2)}, u32[]{:S(2)}) collective-permute-start(bf16[128,1024]{1,0:T(8,128)(2,1)S(1)} %collective-permute-done.16.rest_10_), channel_id=1, source_target_pairs={{0,2},{1,3},{2,0},{3,1},{4,6},{5,7},{6,4},{7,5},{8,10},{9,11},{10,... | collective-permute-start | bytes 786440 | tf_op jit(solution)/shard_map/ppermute | solution.py:160
  37.8 4.0 %collective-permute-done.17.rest_8_ = bf16[128,1024]{1,0:T(8,128)(2,1)S(1)} collective-permute-done((bf16[128,1024]{1,0:T(8,128)(2,1)S(1)}, bf16[128,1024]{1,0:T(8,128)(2,1)S(1)}, u32[]{:S(2)}, u32[]{:S(2)}) %collective-permute-start.17) | collective-permute-done | bytes 262176 | tf_op jit(solution)/shard_map/ppermute | solution.py:160
  41.8 1.8 %gate.1 = (f32[384,1024]{1,0:T(8,128)S(1)}, bf16[384,768]{1,0:T(8,128)(2,1)S(1)}) custom-call(s32[3]{0:T(128)S(1)} %pad_add_fusion.ids, bf16[384,1024]{1,0:T(8,128)(2,1)S(1)} %get-tuple-element.22.normed, s32[1,384]{1,0:T(1,128)S(1)} %bitcast.12, bf16[1024,2048]{1,0:T(8,128)(2,1)S(1)} %bitcast.8), custom_call_target="tpu_custom_call" | custom-call | flops 805306368 | bytes 4982284 | tf_op jit(solution)/shard_map/gate/pallas_call | solution.py:130
  43.6 2.6 %attend.2 = (bf16[192,512]{1,0:T(8,128)(2,1)S(1)}, bf16[192,512]{1,0:T(8,128)(2,1)S(1)}, bf16[192,512]{1,0:T(8,128)(2,1)S(1)}, bf16[192,512]{1,0:T(8,128)(2,1)S(1)}) custom-call(s32[3]{0:T(128)S(1)} %pad_add_fusion.ids, s32[1,8]{1,0:T(1,128)S(1)} %copy-done.9, bf16[192,1024]{1,0:T(8,128)(2,1)S(1)} %get-tuple-element.25.rest_0_, ...), custom_call_target="tpu_custom_call" | custom-call | flops 1610612736 | bytes 5242924 | tf_op jit(solution)/shard_map/attend/pallas_call | solution.py:130
  46.3 2.0 %collective-permute-start.11 = (bf16[192,512]{1,0:T(8,128)(2,1)S(1)}, bf16[192,512]{1,0:T(8,128)(2,1)S(1)}, u32[]{:S(2)}, u32[]{:S(2)}) collective-permute-start(bf16[192,512]{1,0:T(8,128)(2,1)S(1)} %get-tuple-element.32), channel_id=1, source_target_pairs={{0,16},{8,24},{16,0},{24,8},{1,17},{9,25},{17,1},{25,9},{2,18},{10... | collective-permute-start | bytes 589832 | tf_op jit(solution)/shard_map/ppermute | solution.py:167
  48.4 1.5 %collective-permute-start.12 = (bf16[192,512]{1,0:T(8,128)(2,1)S(1)}, bf16[192,512]{1,0:T(8,128)(2,1)S(1)}, u32[]{:S(2)}, u32[]{:S(2)}) collective-permute-start(bf16[192,512]{1,0:T(8,128)(2,1)S(1)} %get-tuple-element.33), channel_id=1, source_target_pairs={{0,24},{8,16},{16,8},{24,0},{1,25},{9,17},{17,9},{25,1},{2,26},{10... | collective-permute-start | bytes 589832 | tf_op jit(solution)/shard_map/ppermute | solution.py:167
  49.9 2.6 %attend.3 = (bf16[192,512]{1,0:T(8,128)(2,1)S(1)}, bf16[192,512]{1,0:T(8,128)(2,1)S(1)}, bf16[192,512]{1,0:T(8,128)(2,1)S(1)}, bf16[192,512]{1,0:T(8,128)(2,1)S(1)}) custom-call(s32[3]{0:T(128)S(1)} %pad_add_fusion.ids, s32[1,8]{1,0:T(1,128)S(1)} %copy-done.9, bf16[192,1024]{1,0:T(8,128)(2,1)S(1)} %get-tuple-element.25.rest_0_, ...), custom_call_target="tpu_custom_call" | custom-call | flops 1610612736 | bytes 5242924 | tf_op jit(solution)/shard_map/attend/pallas_call | solution.py:130
  52.6 2.0 %collective-permute-start.21 = (bf16[192,512]{1,0:T(8,128)(2,1)S(1)}, bf16[192,512]{1,0:T(8,128)(2,1)S(1)}, u32[]{:S(2)}, u32[]{:S(2)}) collective-permute-start(bf16[192,512]{1,0:T(8,128)(2,1)S(1)} %get-tuple-element.37), channel_id=1, source_target_pairs={{0,16},{8,24},{16,0},{24,8},{1,17},{9,25},{17,1},{25,9},{2,18},{10... | collective-permute-start | bytes 589832 | tf_op jit(solution)/shard_map/ppermute | solution.py:167
  54.6 1.4 %collective-permute-start.22 = (bf16[192,512]{1,0:T(8,128)(2,1)S(1)}, bf16[192,512]{1,0:T(8,128)(2,1)S(1)}, u32[]{:S(2)}, u32[]{:S(2)}) collective-permute-start(bf16[192,512]{1,0:T(8,128)(2,1)S(1)} %get-tuple-element.38), channel_id=1, source_target_pairs={{0,24},{8,16},{16,8},{24,0},{1,25},{9,17},{17,9},{25,1},{2,26},{10... | collective-permute-start | bytes 589832 | tf_op jit(solution)/shard_map/ppermute | solution.py:167
  56.0 0.8 %collective-permute-done.11.rest_2_ = bf16[192,512]{1,0:T(8,128)(2,1)S(1)} collective-permute-done((bf16[192,512]{1,0:T(8,128)(2,1)S(1)}, bf16[192,512]{1,0:T(8,128)(2,1)S(1)}, u32[]{:S(2)}, u32[]{:S(2)}) %collective-permute-start.11) | collective-permute-done | bytes 196640 | tf_op jit(solution)/shard_map/ppermute | solution.py:167
  56.9 2.3 %collective-permute-done.12.rest_3_ = bf16[192,512]{1,0:T(8,128)(2,1)S(1)} collective-permute-done((bf16[192,512]{1,0:T(8,128)(2,1)S(1)}, bf16[192,512]{1,0:T(8,128)(2,1)S(1)}, u32[]{:S(2)}, u32[]{:S(2)}) %collective-permute-start.12) | collective-permute-done | bytes 196640 | tf_op jit(solution)/shard_map/ppermute | solution.py:167
  59.2 3.3 %collective-permute-done.20.rest_5_ = bf16[192,512]{1,0:T(8,128)(2,1)S(1)} collective-permute-done((bf16[192,512]{1,0:T(8,128)(2,1)S(1)}, bf16[192,512]{1,0:T(8,128)(2,1)S(1)}, u32[]{:S(2)}, u32[]{:S(2)}) %collective-permute-start.20) | collective-permute-done | bytes 196640 | tf_op jit(solution)/shard_map/ppermute | solution.py:167
  62.5 0.8 %collective-permute-done.21.rest_6_ = bf16[192,512]{1,0:T(8,128)(2,1)S(1)} collective-permute-done((bf16[192,512]{1,0:T(8,128)(2,1)S(1)}, bf16[192,512]{1,0:T(8,128)(2,1)S(1)}, u32[]{:S(2)}, u32[]{:S(2)}) %collective-permute-start.21) | collective-permute-done | bytes 196640 | tf_op jit(solution)/shard_map/ppermute | solution.py:167
  63.3 4.0 %collective-permute-done.22.rest_7_ = bf16[192,512]{1,0:T(8,128)(2,1)S(1)} collective-permute-done((bf16[192,512]{1,0:T(8,128)(2,1)S(1)}, bf16[192,512]{1,0:T(8,128)(2,1)S(1)}, u32[]{:S(2)}, u32[]{:S(2)}) %collective-permute-start.22) | collective-permute-done | bytes 196640 | tf_op jit(solution)/shard_map/ppermute | solution.py:167
  67.3 2.9 %finish.1 = bf16[384,1024]{1,0:T(8,128)(2,1)} custom-call(bf16[384,1024]{1,0:T(8,128)(2,1)S(1)} %copy-done.4, f32[384,1024]{1,0:T(8,128)S(1)} %get-tuple-element.23.rest_12_.gate, bf16[384,768]{1,0:T(8,128)(2,1)S(1)} %get-tuple-element.24.pick, f32[1,1024]{1,0:T(1,128)S(1)} %copy-done.6, bf16[1024,1024]{1,0:T(8,128)(2,1)S(1)} %bitcast.9, ...), custom_call_target="tpu_custom_call" | custom-call | flops 1610612736 | bytes 6623232 | tf_op jit(solution)/shard_map/finish/pallas_call | solution.py:130
  (41 shorter events, 1.9 us)
Async XLA Ops:
  0.0 1.0 %copy-start.5 = (bf16[1,1,128,2048]{3,2,1,0:T(8,128)(2,1)S(1)}, bf16[1,1,128,2048]{3,2,1,0:T(8,128)(2,1)}, u32[]{:S(2)}) copy-start(bf16[1,1,128,2048]{3,2,1,0:T(8,128)(2,1)} %param.10) | copy-start | bytes 1572868
  1.1 15.5 %collective-permute-start.3 = (bf16[128,1024]{1,0:T(8,128)(2,1)S(1)}, bf16[128,1024]{1,0:T(8,128)(2,1)S(1)}, u32[]{:S(2)}, u32[]{:S(2)}) collective-permute-start(bf16[128,1024]{1,0:T(8,128)(2,1)S(1)} %get-tuple-element.29.rest_4_), channel_id=1, source_target_pairs={{0,1},{1,0},{2,3},{3,2},{4,5},{5,4},{6,7},{7,6},{8,9},{9,8},{10,11... | collective-permute-start | bytes 786440 | tf_op jit(solution)/shard_map/ppermute | solution.py:163
  1.6 16.5 %collective-permute-start.4 = (bf16[128,1024]{1,0:T(8,128)(2,1)S(1)}, bf16[128,1024]{1,0:T(8,128)(2,1)S(1)}, u32[]{:S(2)}, u32[]{:S(2)}) collective-permute-start(bf16[128,1024]{1,0:T(8,128)(2,1)S(1)} %get-tuple-element.29.rest_4_), channel_id=1, source_target_pairs={{0,2},{1,3},{2,0},{3,1},{4,6},{5,7},{6,4},{7,5},{8,10},{9,11},{10,... | collective-permute-start | bytes 786440 | tf_op jit(solution)/shard_map/ppermute | solution.py:160
  4.3 16.8 %collective-permute-start.6 = (bf16[128,1024]{1,0:T(8,128)(2,1)S(1)}, bf16[128,1024]{1,0:T(8,128)(2,1)S(1)}, u32[]{:S(2)}, u32[]{:S(2)}) collective-permute-start(bf16[128,1024]{1,0:T(8,128)(2,1)S(1)} %get-tuple-element.29.rest_4_), channel_id=1, source_target_pairs={{0,6},{1,7},{2,4},{3,5},{4,2},{5,3},{6,0},{7,1},{8,14},{9,15},{10,... | collective-permute-start | bytes 786440 | tf_op jit(solution)/shard_map/ppermute | solution.py:160
  6.7 15.9 %collective-permute-start.14 = (bf16[128,1024]{1,0:T(8,128)(2,1)S(1)}, bf16[128,1024]{1,0:T(8,128)(2,1)S(1)}, u32[]{:S(2)}, u32[]{:S(2)}) collective-permute-start(bf16[128,1024]{1,0:T(8,128)(2,1)S(1)} %get-tuple-element.34.rest_4_), channel_id=1, source_target_pairs={{0,2},{1,3},{2,0},{3,1},{4,6},{5,7},{6,4},{7,5},{8,10},{9,11},{10,... | collective-permute-start | bytes 786440 | tf_op jit(solution)/shard_map/ppermute | solution.py:160
  7.5 2.2 %copy-start = (bf16[1,1024,2048]{2,1,0:T(8,128)(2,1)S(1)}, bf16[1,1024,2048]{2,1,0:T(8,128)(2,1)}, u32[]{:S(2)}) copy-start(bf16[1,1024,2048]{2,1,0:T(8,128)(2,1)} %param.13) | copy-start | bytes 12582916
  9.7 1.1 %copy-start.3 = (bf16[384,1024]{1,0:T(8,128)(2,1)S(1)}, bf16[384,1024]{1,0:T(8,128)(2,1)}, u32[]{:S(2)}) copy-start(bf16[384,1024]{1,0:T(8,128)(2,1)} %feat.3) | copy-start | bytes 2359300
  11.5 0.7 copy-start.8
  12.2 29.6 %copy-start.1 = (bf16[1,1024,2048]{2,1,0:T(8,128)(2,1)S(1)}, bf16[1,1024,2048]{2,1,0:T(8,128)(2,1)}, u32[]{:S(2)}) copy-start(bf16[1,1024,2048]{2,1,0:T(8,128)(2,1)} %param.13) | copy-start | bytes 12582916
  15.1 15.7 %collective-permute-start = (bf16[192,1024]{1,0:T(8,128)(2,1)S(1)}, bf16[192,1024]{1,0:T(8,128)(2,1)S(1)}, u32[]{:S(2)}, u32[]{:S(2)}) collective-permute-start(bf16[192,1024]{1,0:T(8,128)(2,1)S(1)} %get-tuple-element.26), channel_id=1, source_target_pairs={{0,8},{8,0},{16,24},{24,16},{1,9},{9,1},{17,25},{25,17},{2,10},{10... | collective-permute-start | bytes 1179656 | tf_op jit(solution)/shard_map/ppermute | solution.py:167
  16.6 18.8 %collective-permute-start.1 = (bf16[192,1024]{1,0:T(8,128)(2,1)S(1)}, bf16[192,1024]{1,0:T(8,128)(2,1)S(1)}, u32[]{:S(2)}, u32[]{:S(2)}) collective-permute-start(bf16[192,1024]{1,0:T(8,128)(2,1)S(1)} %get-tuple-element.27), channel_id=1, source_target_pairs={{0,16},{8,24},{16,0},{24,8},{1,17},{9,25},{17,1},{25,9},{2,18},{10... | collective-permute-start | bytes 1179656 | tf_op jit(solution)/shard_map/ppermute | solution.py:167
  18.1 12.6 %collective-permute-start.16 = (bf16[128,1024]{1,0:T(8,128)(2,1)S(1)}, bf16[128,1024]{1,0:T(8,128)(2,1)S(1)}, u32[]{:S(2)}, u32[]{:S(2)}) collective-permute-start(bf16[128,1024]{1,0:T(8,128)(2,1)S(1)} %get-tuple-element.34.rest_4_), channel_id=1, source_target_pairs={{0,6},{1,7},{2,4},{3,5},{4,2},{5,3},{6,0},{7,1},{8,14},{9,15},{10,... | collective-permute-start | bytes 786440 | tf_op jit(solution)/shard_map/ppermute | solution.py:160
  21.0 15.7 %collective-permute-start.7 = (bf16[128,1024]{1,0:T(8,128)(2,1)S(1)}, bf16[128,1024]{1,0:T(8,128)(2,1)S(1)}, u32[]{:S(2)}, u32[]{:S(2)}) collective-permute-start(bf16[128,1024]{1,0:T(8,128)(2,1)S(1)} %collective-permute-done.6.rest_10_), channel_id=1, source_target_pairs={{0,2},{1,3},{2,0},{3,1},{4,6},{5,7},{6,4},{7,5},{8,10},{9,11},{10,... | collective-permute-start | bytes 786440 | tf_op jit(solution)/shard_map/ppermute | solution.py:160
  22.6 14.1 %collective-permute-start.2 = (bf16[192,1024]{1,0:T(8,128)(2,1)S(1)}, bf16[192,1024]{1,0:T(8,128)(2,1)S(1)}, u32[]{:S(2)}, u32[]{:S(2)}) collective-permute-start(bf16[192,1024]{1,0:T(8,128)(2,1)S(1)} %get-tuple-element.28), channel_id=1, source_target_pairs={{0,24},{8,16},{16,8},{24,0},{1,25},{9,17},{17,9},{25,1},{2,26},{10... | collective-permute-start | bytes 1179656 | tf_op jit(solution)/shard_map/ppermute | solution.py:167
  30.8 6.5 %collective-permute-start.5 = (bf16[128,1024]{1,0:T(8,128)(2,1)S(1)}, bf16[128,1024]{1,0:T(8,128)(2,1)S(1)}, u32[]{:S(2)}, u32[]{:S(2)}) collective-permute-start(bf16[128,1024]{1,0:T(8,128)(2,1)S(1)} %collective-permute-done.4.rest_6_), channel_id=1, source_target_pairs={{0,1},{1,0},{2,3},{3,2},{4,5},{5,4},{6,7},{7,6},{8,9},{9,8},{10,11... | collective-permute-start | bytes 786440 | tf_op jit(solution)/shard_map/ppermute | solution.py:163
  30.8 6.6 %collective-permute-start.9 = (bf16[128,1024]{1,0:T(8,128)(2,1)S(1)}, bf16[128,1024]{1,0:T(8,128)(2,1)S(1)}, u32[]{:S(2)}, u32[]{:S(2)}) collective-permute-start(bf16[128,1024]{1,0:T(8,128)(2,1)S(1)} %collective-permute-done.6.rest_10_), channel_id=1, source_target_pairs={{0,1},{1,0},{2,3},{3,2},{4,5},{5,4},{6,7},{7,6},{8,9},{9,8},{10,11... | collective-permute-start | bytes 786440 | tf_op jit(solution)/shard_map/ppermute | solution.py:163
  35.4 6.4 %collective-permute-start.17 = (bf16[128,1024]{1,0:T(8,128)(2,1)S(1)}, bf16[128,1024]{1,0:T(8,128)(2,1)S(1)}, u32[]{:S(2)}, u32[]{:S(2)}) collective-permute-start(bf16[128,1024]{1,0:T(8,128)(2,1)S(1)} %collective-permute-done.16.rest_10_), channel_id=1, source_target_pairs={{0,2},{1,3},{2,0},{3,1},{4,6},{5,7},{6,4},{7,5},{8,10},{9,11},{10,... | collective-permute-start | bytes 786440 | tf_op jit(solution)/shard_map/ppermute | solution.py:160
  36.7 6.9 %collective-permute-start.8 = (bf16[128,1024]{1,0:T(8,128)(2,1)S(1)}, bf16[128,1024]{1,0:T(8,128)(2,1)S(1)}, u32[]{:S(2)}, u32[]{:S(2)}) collective-permute-start(bf16[128,1024]{1,0:T(8,128)(2,1)S(1)} %collective-permute-done.7.rest_8_), channel_id=1, source_target_pairs={{0,1},{1,0},{2,3},{3,2},{4,5},{5,4},{6,7},{7,6},{8,9},{9,8},{10,11... | collective-permute-start | bytes 786440 | tf_op jit(solution)/shard_map/ppermute | solution.py:163
  36.8 9.6 %collective-permute-start.13 = (bf16[128,1024]{1,0:T(8,128)(2,1)S(1)}, bf16[128,1024]{1,0:T(8,128)(2,1)S(1)}, u32[]{:S(2)}, u32[]{:S(2)}) collective-permute-start(bf16[128,1024]{1,0:T(8,128)(2,1)S(1)} %get-tuple-element.34.rest_4_), channel_id=1, source_target_pairs={{0,1},{1,0},{2,3},{3,2},{4,5},{5,4},{6,7},{7,6},{8,9},{9,8},{10,11... | collective-permute-start | bytes 786440 | tf_op jit(solution)/shard_map/ppermute | solution.py:163
  37.3 12.6 %collective-permute-start.19 = (bf16[128,1024]{1,0:T(8,128)(2,1)S(1)}, bf16[128,1024]{1,0:T(8,128)(2,1)S(1)}, u32[]{:S(2)}, u32[]{:S(2)}) collective-permute-start(bf16[128,1024]{1,0:T(8,128)(2,1)S(1)} %collective-permute-done.16.rest_10_), channel_id=1, source_target_pairs={{0,1},{1,0},{2,3},{3,2},{4,5},{5,4},{6,7},{7,6},{8,9},{9,8},{10,11... | collective-permute-start | bytes 786440 | tf_op jit(solution)/shard_map/ppermute | solution.py:163
  37.3 11.0 %collective-permute-start.15 = (bf16[128,1024]{1,0:T(8,128)(2,1)S(1)}, bf16[128,1024]{1,0:T(8,128)(2,1)S(1)}, u32[]{:S(2)}, u32[]{:S(2)}) collective-permute-start(bf16[128,1024]{1,0:T(8,128)(2,1)S(1)} %collective-permute-done.14.rest_6_), channel_id=1, source_target_pairs={{0,1},{1,0},{2,3},{3,2},{4,5},{5,4},{6,7},{7,6},{8,9},{9,8},{10,11... | collective-permute-start | bytes 786440 | tf_op jit(solution)/shard_map/ppermute | solution.py:163
  41.8 8.1 %collective-permute-start.18 = (bf16[128,1024]{1,0:T(8,128)(2,1)S(1)}, bf16[128,1024]{1,0:T(8,128)(2,1)S(1)}, u32[]{:S(2)}, u32[]{:S(2)}) collective-permute-start(bf16[128,1024]{1,0:T(8,128)(2,1)S(1)} %collective-permute-done.17.rest_8_), channel_id=1, source_target_pairs={{0,1},{1,0},{2,3},{3,2},{4,5},{5,4},{6,7},{7,6},{8,9},{9,8},{10,11... | collective-permute-start | bytes 786440 | tf_op jit(solution)/shard_map/ppermute | solution.py:163
  41.8 1.8 %copy-start.9 = (s32[1,8]{1,0:T(1,128)S(1)}, s32[1,8]{1,0:T(1,128)}, u32[]{:S(2)}) copy-start(s32[1,8]{1,0:T(1,128)} %mask.3) | copy-start | bytes 100
  46.2 8.4 %collective-permute-start.10 = (bf16[192,512]{1,0:T(8,128)(2,1)S(1)}, bf16[192,512]{1,0:T(8,128)(2,1)S(1)}, u32[]{:S(2)}, u32[]{:S(2)}) collective-permute-start(bf16[192,512]{1,0:T(8,128)(2,1)S(1)} %get-tuple-element.31), channel_id=1, source_target_pairs={{0,8},{8,0},{16,24},{24,16},{1,9},{9,1},{17,25},{25,17},{2,10},{10... | collective-permute-start | bytes 589832 | tf_op jit(solution)/shard_map/ppermute | solution.py:167
  46.3 10.5 %collective-permute-start.11 = (bf16[192,512]{1,0:T(8,128)(2,1)S(1)}, bf16[192,512]{1,0:T(8,128)(2,1)S(1)}, u32[]{:S(2)}, u32[]{:S(2)}) collective-permute-start(bf16[192,512]{1,0:T(8,128)(2,1)S(1)} %get-tuple-element.32), channel_id=1, source_target_pairs={{0,16},{8,24},{16,0},{24,8},{1,17},{9,25},{17,1},{25,9},{2,18},{10... | collective-permute-start | bytes 589832 | tf_op jit(solution)/shard_map/ppermute | solution.py:167
  48.4 18.9 %copy-start.2 = (bf16[1,1024,1024]{2,1,0:T(8,128)(2,1)S(1)}, bf16[1,1024,1024]{2,1,0:T(8,128)(2,1)}, u32[]{:S(2)}) copy-start(bf16[1,1024,1024]{2,1,0:T(8,128)(2,1)} %param.15) | copy-start | bytes 6291460
  48.4 18.9 %copy-start.4 = (bf16[384,1024]{1,0:T(8,128)(2,1)S(1)}, bf16[384,1024]{1,0:T(8,128)(2,1)}, u32[]{:S(2)}) copy-start(bf16[384,1024]{1,0:T(8,128)(2,1)} %feat.3) | copy-start | bytes 2359300
  48.4 18.9 %copy-start.6 = (f32[1,1024]{1,0:T(1,128)S(1)}, f32[1,1024]{1,0:T(1,128)}, u32[]{:S(2)}) copy-start(f32[1,1024]{1,0:T(1,128)} %gain.3) | copy-start | bytes 12292
  48.4 10.8 %collective-permute-start.12 = (bf16[192,512]{1,0:T(8,128)(2,1)S(1)}, bf16[192,512]{1,0:T(8,128)(2,1)S(1)}, u32[]{:S(2)}, u32[]{:S(2)}) collective-permute-start(bf16[192,512]{1,0:T(8,128)(2,1)S(1)} %get-tuple-element.33), channel_id=1, source_target_pairs={{0,24},{8,16},{16,8},{24,0},{1,25},{9,17},{17,9},{25,1},{2,26},{10... | collective-permute-start | bytes 589832 | tf_op jit(solution)/shard_map/ppermute | solution.py:167
  52.5 10.0 %collective-permute-start.20 = (bf16[192,512]{1,0:T(8,128)(2,1)S(1)}, bf16[192,512]{1,0:T(8,128)(2,1)S(1)}, u32[]{:S(2)}, u32[]{:S(2)}) collective-permute-start(bf16[192,512]{1,0:T(8,128)(2,1)S(1)} %get-tuple-element.36), channel_id=1, source_target_pairs={{0,8},{8,0},{16,24},{24,16},{1,9},{9,1},{17,25},{25,17},{2,10},{10... | collective-permute-start | bytes 589832 | tf_op jit(solution)/shard_map/ppermute | solution.py:167
  52.6 10.6 %collective-permute-start.21 = (bf16[192,512]{1,0:T(8,128)(2,1)S(1)}, bf16[192,512]{1,0:T(8,128)(2,1)S(1)}, u32[]{:S(2)}, u32[]{:S(2)}) collective-permute-start(bf16[192,512]{1,0:T(8,128)(2,1)S(1)} %get-tuple-element.37), channel_id=1, source_target_pairs={{0,16},{8,24},{16,0},{24,8},{1,17},{9,25},{17,1},{25,9},{2,18},{10... | collective-permute-start | bytes 589832 | tf_op jit(solution)/shard_map/ppermute | solution.py:167
  54.6 12.6 %collective-permute-start.22 = (bf16[192,512]{1,0:T(8,128)(2,1)S(1)}, bf16[192,512]{1,0:T(8,128)(2,1)S(1)}, u32[]{:S(2)}, u32[]{:S(2)}) collective-permute-start(bf16[192,512]{1,0:T(8,128)(2,1)S(1)} %get-tuple-element.38), channel_id=1, source_target_pairs={{0,24},{8,16},{16,8},{24,0},{1,25},{9,17},{17,9},{25,1},{2,26},{10... | collective-permute-start | bytes 589832 | tf_op jit(solution)/shard_map/ppermute | solution.py:167
  (1 other events, 0.7 us)

commit v3 on v2

--- a/solution.py
+++ b/solution.py
@@ -11,6 +11,8 @@
 HEAD = 128
 CHUNKS = 2
 VMEM_LIMIT = 32 * 1024 * 1024
+VMEM_MOST = 60 * 1024 * 1024
+HEAVY = 4 * 10**11
 
 
 def silu_halved(t):
@@ -48,35 +50,73 @@
             ]
 
 
-def query_kernel(cap, users, ids, feat, user, gain, wq, normed_out, *outs):
+def query_kernel(cap, users, feat_in, user_in, gain_in, w_in, normed_out, *rest):
+    outs, (feat, user, gain, wq, sems) = rest[:users], rest[users:]
     rows, width = feat.shape
+    half = width // 2
+    copies = [
+        pltpu.make_async_copy(feat_in, feat, sems.at[0]),
+        pltpu.make_async_copy(user_in, user, sems.at[1]),
+        pltpu.make_async_copy(gain_in, gain, sems.at[2]),
+    ]
+    for side in range(2):
+        copies.append(
+            pltpu.make_async_copy(
+                w_in.at[:, pl.ds(width + side * half, half)], wq.at[side], sems.at[3 + side]
+            )
+        )
+    for copy in copies:
+        copy.start()
+    copies[1].wait()
+    slot = slots_of(user[...], lax.axis_index("users"), cap, users)
+    places = lax.broadcasted_iota(jnp.int32, (users * cap, rows), 0).astype(jnp.float32)
+    pick = (places == slot).astype(jnp.bfloat16)
+    copies[0].wait()
+    copies[2].wait()
     normed = (centred_norm(feat[...].astype(jnp.float32)) * gain[...]).astype(jnp.bfloat16)
     normed_out[...] = normed
-    slot = slots_of(user[...], ids[0], cap, users)
-    places = lax.broadcasted_iota(jnp.int32, (users * cap, rows), 0).astype(jnp.float32)
-    pick = (places == slot).astype(jnp.bfloat16)
-    part = jnp.dot(normed, wq[...], preferred_element_type=jnp.float32)
-    query = silu_halved(part * 0.5).astype(jnp.bfloat16)
-    sent = jnp.dot(pick, query, preferred_element_type=jnp.float32).astype(jnp.bfloat16)
-    for d in range(users):
-        outs[d][...] = sent[d * cap:(d + 1) * cap, :]
-
-
-def gate_kernel(cap, users, ids, normed, user, wg, gate, pick):
-    rows = user.shape[1]
-    part = jnp.dot(normed[...], wg[...], preferred_element_type=jnp.float32)
-    gate[...] = silu_halved(part * 0.5)
-    slot = slots_of(user[...], ids[0], cap, users)
+    for side in range(2):
+        copies[3 + side].wait()
+        part = jnp.dot(normed, wq[side], preferred_element_type=jnp.float32)
+        query = silu_halved(part * 0.5).astype(jnp.bfloat16)
+        sent = jnp.dot(pick, query, preferred_element_type=jnp.float32).astype(jnp.bfloat16)
+        for d in range(users):
+            outs[d][:, side * half:(side + 1) * half] = sent[d * cap:(d + 1) * cap, :]
+
+
+def gate_kernel(cap, users, normed_in, user_in, w_in, gate, pick, normed, user, wg, sems):
+    rows, width = normed.shape
+    half = width // 2
+    copies = [
+        pltpu.make_async_copy(user_in, user, sems.at[0]),
+        pltpu.make_async_copy(normed_in, normed, sems.at[1]),
+    ]
+    for side in range(2):
+        copies.append(
+            pltpu.make_async_copy(
+                w_in.at[:, pl.ds(side * half, half)], wg.at[side], sems.at[2 + side]
+            )
+        )
+    for copy in copies:
+        copy.start()
+    copies[0].wait()
+    slot = slots_of(user[...], lax.axis_index("users"), cap, users)
     slot = jnp.transpose(jnp.broadcast_to(slot, (128, rows)))[:, 0:1]
     places = lax.broadcasted_iota(jnp.int32, (rows, users * cap), 1).astype(jnp.float32)
     pick[...] = (places == slot).astype(jnp.bfloat16)
-
-
-def attend_kernel(users, chips, ids, mask, *rest):
+    copies[1].wait()
+    for side in range(2):
+        copies[2 + side].wait()
+        part = jnp.dot(normed[...], wg[side], preferred_element_type=jnp.float32)
+        gate[:, side * half:(side + 1) * half] = silu_halved(part * 0.5)
+
+
+def attend_kernel(users, chips, mask, *rest):
     queries = rest[:users]
     blocks = rest[users:users + 2 * chips]
     outs, (live_kv, all_q) = rest[-2 - users:-2], rest[-2:]
-    core, z = ids[1], ids[2]
+    place = lax.axis_index("ctx")
+    core, z = place % 2, place // 2
     cap, wide = queries[0].shape
     taken = jnp.int32(0)
     for d in range(chips):
@@ -118,14 +158,14 @@
 
 
 SMEM = pl.BlockSpec(memory_space=pltpu.SMEM)
-ANY = pl.BlockSpec(memory_space=pl.ANY)
+HBM = pl.BlockSpec(memory_space=pltpu.HBM)
 
 
 def whole(*dims, at=None):
     return pl.BlockSpec(dims, lambda i: at or (0,) * len(dims))
 
 
-def call(kernel, name, in_specs, out_shape, scratch, flops, *args):
+def call(kernel, name, in_specs, out_shape, scratch, flops, *args, vmem=VMEM_LIMIT):
     moved = sum(a.size * a.dtype.itemsize for a in args)
     return pl.pallas_call(
         kernel,
@@ -136,7 +176,7 @@
         out_shape=out_shape,
         scratch_shapes=scratch,
         cost_estimate=pl.CostEstimate(flops=flops, bytes_accessed=moved, transcendentals=0),
-        compiler_params=pltpu.CompilerParams(vmem_limit_bytes=VMEM_LIMIT),
+        compiler_params=pltpu.CompilerParams(vmem_limit_bytes=vmem),
     )(*args)
 
 
@@ -147,9 +187,6 @@
     rows, width = cand_feat.shape
     cap = 2 * rows // users
     wide = width // CHUNKS
-    me = lax.axis_index("users")
-    place = lax.axis_index("ctx")
-    ids = jnp.stack([me, place % 2, place // 2]).astype(jnp.int32)
     bf16 = jnp.bfloat16
     user_row = cand_user.reshape(1, rows)
 
@@ -168,50 +205,69 @@
             for d in range(1, users)
         ]
 
+    def after(value, *others):
+        return lax.optimization_barrier((value, *others))[0]
+
     kv = hist_kv[0, 0]
     split = call(
         functools.partial(kv_split_kernel, CHUNKS), "kv_split", [whole(*kv.shape)],
         [shape(BLK, 2 * wide)] * CHUNKS, [], 0, kv,
     )
-    gathered = []
-    for own in split:
-        held = {0: own}
+
+    normed, *queries = call(
+        functools.partial(query_kernel, cap, users), "query",
+        [HBM] * 4,
+        [shape(rows, width)] + [shape(cap, width)] * users,
+        [
+            pltpu.VMEM((rows, width), bf16),
+            pltpu.VMEM((1, rows), jnp.int32),
+            pltpu.VMEM((1, width), jnp.float32),
+            pltpu.VMEM((2, width, width // 2), bf16),
+            pltpu.SemaphoreType.DMA((5,)),
+        ],
+        HEAVY,
+        after(cand_feat, split[0]), user_row, gain_in, w_uq[0], vmem=VMEM_MOST,
+    )
+    arrived = over_users(queries)
+
+    gate, pick = call(
+        functools.partial(gate_kernel, cap, users), "gate",
+        [HBM] * 3,
+        [shape(rows, width, dtype=jnp.float32), shape(rows, users * cap)],
+        [
+            pltpu.VMEM((rows, width), bf16),
+            pltpu.VMEM((1, rows), jnp.int32),
+            pltpu.VMEM((2, width, width // 2), bf16),
+            pltpu.SemaphoreType.DMA((4,)),
+        ],
+        HEAVY,
+        normed, user_row, w_uq[0], vmem=VMEM_MOST,
+    )
+
+    returned, earlier = [], None
+    for chunk in range(CHUNKS):
+        held = {0: split[chunk]}
+        far, near = split[chunk], split[chunk]
+        if chunk:
+            far = after(far, earlier[3], gate)
+            near = after(near, earlier[1], gate)
         for d in [3, 1, 2] + list(range(4, chips)):
-            held[d] = over_z(held[3], 1) if d == 2 else over_z(own, d)
+            held[d] = over_z(held[3], 1) if d == 2 else over_z(near if d == 1 else far, d)
         blocks = []
         for d in range(chips):
-            blocks += [held[d], over_cores(held[d])]
-        gathered.append(blocks)
-
-    normed, *queries = call(
-        functools.partial(query_kernel, cap, users), "query",
-        [SMEM, whole(rows, width), whole(1, rows), whole(1, width), whole(width, width, at=(0, 1))],
-        [shape(rows, width)] + [shape(cap, width)] * users,
-        [], 4 * rows * width * width,
-        ids, cand_feat, user_row, gain_in, w_uq[0],
-    )
-    arrived = over_users(queries)
-
-    gate, pick = call(
-        functools.partial(gate_kernel, cap, users), "gate",
-        [SMEM, whole(rows, width), whole(1, rows), whole(width, width)],
-        [shape(rows, width, dtype=jnp.float32), shape(rows, users * cap)],
-        [], 2 * rows * width * width,
-        ids, normed, user_row, w_uq[0],
-    )
-
-    returned = []
-    for chunk in range(CHUNKS):
+            if chunk == 0:
+                ready = arrived[1:2] if d != 2 else []
+            else:
+                ready = returned[-users + 1:] if d in (1, 2) else []
+            blocks += [held[d], over_cores(after(held[d], *ready) if ready else held[d])]
+        earlier = held
         scored = call(
             functools.partial(attend_kernel, users, chips), "attend",
-            [SMEM, SMEM]
-            + [whole(cap, wide, at=(0, chunk))] * users
-            + [whole(BLK, 2 * wide)] * (2 * chips)
-            + [ANY],
+            [SMEM] + [whole(cap, wide, at=(0, chunk))] * users + [whole(BLK, 2 * wide)] * (2 * chips),
             [shape(cap, wide)] * users,
             [pltpu.VMEM((chips * BLK, 2 * wide), bf16), pltpu.VMEM((users * cap, wide), bf16)],
             8 * users * cap * chips * BLK * wide,
-            ids, hist_mask, *arrived, *gathered[chunk], gate,
+            hist_mask, *arrived, *blocks,
         )
         returned += over_users(scored)
 

time: 70.5 us -> 71 us (level)
  Pallas kernels: 12.9 us -> 19.2 us
  local copies, waits for them, and re-layouts: 5.75 us -> 1.07 us
  waiting for transfers between devices: 26.3 us -> 25.3 us
    ppermute x6, waiting for transfers between devices: 10.9 us -> 0.03 us  [over_z(): return lax.ppermute(value, 'ctx', [(c, c ^ 2 * d) for c in range(ctx)])]
    ppermute x9, waiting for transfers between devices: 15.3 us -> 23.9 us  [over_users(): lax.ppermute(values[d], 'users', [(u, u ^ d) for u in range(users)])]
    pallas_call x6, Pallas kernels: 12.9 us -> 19.2 us  [call(): pl.pallas_call(kernel, name=name, grid=(1,), in_specs=in_specs, out_specs...]
    unnamed x20 -> x16, local copies, waits for them, and re-layouts: 5.75 us -> 1.07 us
    ppermute x6, starting transfers between devices: 10 us -> 13.2 us  [over_z(): return lax.ppermute(value, 'ctx', [(c, c ^ 2 * d) for c in range(ctx)])]
    ppermute x9, starting transfers between devices: 13.1 us -> 10.7 us  [over_users(): lax.ppermute(values[d], 'users', [(u, u ^ d) for u in range(users)])]
    ppermute x8, waiting for transfers between devices: 0.02 us -> 1.4 us  [over_cores(): return lax.ppermute(value, 'ctx', [(c, c ^ 1) for c in range(ctx)])]
    ppermute x8, starting transfers between devices: 2.05 us -> 1.1 us  [over_cores(): return lax.ppermute(value, 'ctx', [(c, c ^ 1) for c in range(ctx)])]
  transfers between devices with their start and end apart: 23 -> 23, of which waited for: 9 -> 9; matrix products, arithmetic and copies ran while one was open for 0% -> 0% of each run, Pallas kernels for 14% -> 17%
where the time goes in v3:
time: 71 us; the launch traced here: 70.8 us
  waiting for transfers between devices  25.3 us (36%)
  starting transfers between devices  25 us (35%)
  Pallas kernels  19.2 us (27%)
  local copies, waits for them, and re-layouts  1.07 us (2%)
    ppermute x9, waiting for transfers between devices, over_users(): lax.ppermute(values[d], 'users', [(u, u ^ d) for u in range(users)])  23.9 us
    pallas_call x6, Pallas kernels, call(): pl.pallas_call(kernel, name=name, grid=(1,), in_specs=in_specs, out_specs...  19.2 us
    ppermute x6, starting transfers between devices, over_z(): return lax.ppermute(value, 'ctx', [(c, c ^ 2 * d) for c in range(ctx)])  13.2 us
    ppermute x9, starting transfers between devices, over_users(): lax.ppermute(values[d], 'users', [(u, u ^ d) for u in range(users)])  10.7 us
  transfers between devices with their start and end apart: 23, of which 9 were waited for; matrix products, arithmetic and copies ran while one was open for 0% of the time, Pallas kernels for 17%

profile of v3, /device:TPU:0, one launch (start us, length us, event | category | flops | bytes accessed | tf_op | source)
XLA Modules:
  0.0 70.8 jit_solution(7832327566883602489)
XLA Ops:
  0.0 1.0 %copy-done.4 = bf16[1,1,128,2048]{3,2,1,0:T(8,128)(2,1)S(1)} copy-done((bf16[1,1,128,2048]{3,2,1,0:T(8,128)(2,1)S(1)}, bf16[1,1,128,2048]{3,2,1,0:T(8,128)(2,1)}, u32[]{:S(2)}) %copy-start.4) | copy-done | bytes 524312
  1.0 0.8 %kv_split.1 = (bf16[128,1024]{1,0:T(8,128)(2,1)}, bf16[128,1024]{1,0:T(8,128)(2,1)S(1)}) custom-call(bf16[128,2048]{1,0:T(8,128)(2,1)S(1)} %bitcast.5), custom_call_target="tpu_custom_call" | custom-call | bytes 524288 | tf_op jit(solution)/shard_map/kv_split/pallas_call | solution.py:170
  1.8 5.0 %collective-permute-start.6 = (bf16[128,1024]{1,0:T(8,128)(2,1)}, bf16[128,1024]{1,0:T(8,128)(2,1)}, u32[]{:S(2)}, u32[]{:S(2)}) collective-permute-start(bf16[128,1024]{1,0:T(8,128)(2,1)} %get-tuple-element.39.rest_4_), channel_id=1, source_target_pairs={{0,6},{1,7},{2,4},{3,5},{4,2},{5,3},{6,0},{7,1},{8,14},{9,15},{10,... | collective-permute-start | bytes 786440 | tf_op jit(solution)/shard_map/ppermute | solution.py:197
  6.9 5.0 %query.1 = (bf16[384,1024]{1,0:T(8,128)(2,1)}, bf16[192,1024]{1,0:T(8,128)(2,1)}, bf16[192,1024]{1,0:T(8,128)(2,1)}, bf16[192,1024]{1,0:T(8,128)(2,1)}, bf16[192,1024]{1,0:T(8,128)(2,1)}) custom-call(bf16[384,1024]{1,0:T(8,128)(2,1)} %feat.1, s32[1,384]{1,0:T(1,128)} %bitcast.8, f32[1,1024]{1,0:T(1,128)} %gain_in.1, bf16[1024,2048]{1,0:T(8,128)(2,1)} %bitcast.6), custom_call_target="tpu_custom_call" | custom-call | flops 399999991808 | bytes 4986368 | tf_op jit(solution)/shard_map/query/pallas_call | solution.py:170
  11.8 1.6 %collective-permute-start = (bf16[192,1024]{1,0:T(8,128)(2,1)}, bf16[192,1024]{1,0:T(8,128)(2,1)}, u32[]{:S(2)}, u32[]{:S(2)}) collective-permute-start(bf16[192,1024]{1,0:T(8,128)(2,1)} %get-tuple-element.36), channel_id=1, source_target_pairs={{0,8},{8,0},{16,24},{24,16},{1,9},{9,1},{17,25},{25,17},{2,10},{10... | collective-permute-start | bytes 1179656 | tf_op jit(solution)/shard_map/ppermute | solution.py:204
  13.4 1.5 %collective-permute-start.1 = (bf16[192,1024]{1,0:T(8,128)(2,1)}, bf16[192,1024]{1,0:T(8,128)(2,1)}, u32[]{:S(2)}, u32[]{:S(2)}) collective-permute-start(bf16[192,1024]{1,0:T(8,128)(2,1)} %get-tuple-element.37), channel_id=1, source_target_pairs={{0,16},{8,24},{16,0},{24,8},{1,17},{9,25},{17,1},{25,9},{2,18},{10... | collective-permute-start | bytes 1179656 | tf_op jit(solution)/shard_map/ppermute | solution.py:204
  14.9 0.5 collective-permute-start.2
  15.4 3.4 %collective-permute-start.7 = (bf16[128,1024]{1,0:T(8,128)(2,1)}, bf16[128,1024]{1,0:T(8,128)(2,1)}, u32[]{:S(2)}, u32[]{:S(2)}) collective-permute-start(bf16[128,1024]{1,0:T(8,128)(2,1)} %collective-permute-done.6.rest_10_), channel_id=1, source_target_pairs={{0,2},{1,3},{2,0},{3,1},{4,6},{5,7},{6,4},{7,5},{8,10},{9,11},{10,... | collective-permute-start | bytes 786440 | tf_op jit(solution)/shard_map/ppermute | solution.py:197
  18.8 3.9 %gate.1 = (f32[384,1024]{1,0:T(8,128)}, bf16[384,768]{1,0:T(8,128)(2,1)}) custom-call(bf16[384,1024]{1,0:T(8,128)(2,1)} %get-tuple-element.32.normed_in, s32[1,384]{1,0:T(1,128)} %bitcast.9, bf16[1024,2048]{1,0:T(8,128)(2,1)} %bitcast.7), custom_call_target="tpu_custom_call" | custom-call | flops 399999991808 | bytes 4982272 | tf_op jit(solution)/shard_map/gate/pallas_call | solution.py:170
  22.7 1.5 %collective-permute-done.rest_1_ = bf16[192,1024]{1,0:T(8,128)(2,1)} collective-permute-done((bf16[192,1024]{1,0:T(8,128)(2,1)}, bf16[192,1024]{1,0:T(8,128)(2,1)}, u32[]{:S(2)}, u32[]{:S(2)}) %collective-permute-start) | collective-permute-done | bytes 393248 | tf_op jit(solution)/shard_map/ppermute | solution.py:204
  24.3 1.0 %collective-permute-start.16 = (bf16[128,1024]{1,0:T(8,128)(2,1)S(1)}, bf16[128,1024]{1,0:T(8,128)(2,1)S(1)}, u32[]{:S(2)}, u32[]{:S(2)}) collective-permute-start(bf16[128,1024]{1,0:T(8,128)(2,1)S(1)} %get-tuple-element.49.rest_4_), channel_id=1, source_target_pairs={{0,6},{1,7},{2,4},{3,5},{4,2},{5,3},{6,0},{7,1},{8,14},{9,15},{10,... | collective-permute-start | bytes 786440 | tf_op jit(solution)/shard_map/ppermute | solution.py:197
  25.3 7.1 %collective-permute-done.1.rest_2_ = bf16[192,1024]{1,0:T(8,128)(2,1)} collective-permute-done((bf16[192,1024]{1,0:T(8,128)(2,1)}, bf16[192,1024]{1,0:T(8,128)(2,1)}, u32[]{:S(2)}, u32[]{:S(2)}) %collective-permute-start.1) | collective-permute-done | bytes 393248 | tf_op jit(solution)/shard_map/ppermute | solution.py:204
  32.4 0.5 collective-permute-start.9
  32.9 0.1 collective-permute-start.8
  33.0 3.7 %collective-permute-start.14 = (bf16[128,1024]{1,0:T(8,128)(2,1)S(1)}, bf16[128,1024]{1,0:T(8,128)(2,1)S(1)}, u32[]{:S(2)}, u32[]{:S(2)}) collective-permute-start(bf16[128,1024]{1,0:T(8,128)(2,1)S(1)} %get-tuple-element.49.rest_4_), channel_id=1, source_target_pairs={{0,2},{1,3},{2,0},{3,1},{4,6},{5,7},{6,4},{7,5},{8,10},{9,11},{10,... | collective-permute-start | bytes 786440 | tf_op jit(solution)/shard_map/ppermute | solution.py:197
  36.8 3.5 %attend.2 = (bf16[192,512]{1,0:T(8,128)(2,1)S(1)}, bf16[192,512]{1,0:T(8,128)(2,1)S(1)}, bf16[192,512]{1,0:T(8,128)(2,1)S(1)}, bf16[192,512]{1,0:T(8,128)(2,1)S(1)}) custom-call(s32[1,8]{1,0:T(1,128)S(1)} %copy-done.6, bf16[192,1024]{1,0:T(8,128)(2,1)S(1)} %copy-done.7, bf16[192,1024]{1,0:T(8,128)(2,1)} %collective-permute-done.rest_1_, ...), custom_call_target="tpu_custom_call" | custom-call | flops 1610612736 | bytes 3670048 | tf_op jit(solution)/shard_map/attend/pallas_call | solution.py:170
  40.3 1.6 %collective-permute-start.10 = (bf16[192,512]{1,0:T(8,128)(2,1)S(1)}, bf16[192,512]{1,0:T(8,128)(2,1)S(1)}, u32[]{:S(2)}, u32[]{:S(2)}) collective-permute-start(bf16[192,512]{1,0:T(8,128)(2,1)S(1)} %get-tuple-element.43), channel_id=1, source_target_pairs={{0,8},{8,0},{16,24},{24,16},{1,9},{9,1},{17,25},{25,17},{2,10},{10... | collective-permute-start | bytes 589832 | tf_op jit(solution)/shard_map/ppermute | solution.py:204
  41.8 1.5 %collective-permute-start.11 = (bf16[192,512]{1,0:T(8,128)(2,1)S(1)}, bf16[192,512]{1,0:T(8,128)(2,1)S(1)}, u32[]{:S(2)}, u32[]{:S(2)}) collective-permute-start(bf16[192,512]{1,0:T(8,128)(2,1)S(1)} %get-tuple-element.44), channel_id=1, source_target_pairs={{0,16},{8,24},{16,0},{24,8},{1,17},{9,25},{17,1},{25,9},{2,18},{10... | collective-permute-start | bytes 589832 | tf_op jit(solution)/shard_map/ppermute | solution.py:204
  43.4 0.5 collective-permute-start.12
  43.9 3.6 %collective-permute-done.10.rest_1_ = bf16[192,512]{1,0:T(8,128)(2,1)S(1)} collective-permute-done((bf16[192,512]{1,0:T(8,128)(2,1)S(1)}, bf16[192,512]{1,0:T(8,128)(2,1)S(1)}, u32[]{:S(2)}, u32[]{:S(2)}) %collective-permute-start.10) | collective-permute-done | bytes 196640 | tf_op jit(solution)/shard_map/ppermute | solution.py:204
  47.6 3.4 %collective-permute-done.11.rest_2_ = bf16[192,512]{1,0:T(8,128)(2,1)S(1)} collective-permute-done((bf16[192,512]{1,0:T(8,128)(2,1)S(1)}, bf16[192,512]{1,0:T(8,128)(2,1)S(1)}, u32[]{:S(2)}, u32[]{:S(2)}) %collective-permute-start.11) | collective-permute-done | bytes 196640 | tf_op jit(solution)/shard_map/ppermute | solution.py:204
  51.0 0.5 collective-permute-start.18
  51.5 1.0 %collective-permute-done.15.rest_7_ = bf16[128,1024]{1,0:T(8,128)(2,1)S(1)} collective-permute-done((bf16[128,1024]{1,0:T(8,128)(2,1)S(1)}, bf16[128,1024]{1,0:T(8,128)(2,1)S(1)}, u32[]{:S(2)}, u32[]{:S(2)}) %collective-permute-start.15) | collective-permute-done | bytes 262176 | tf_op jit(solution)/shard_map/ppermute | solution.py:200
  52.5 0.4 collective-permute-done.18.rest_9_
  52.9 3.2 %attend.3 = (bf16[192,512]{1,0:T(8,128)(2,1)S(1)}, bf16[192,512]{1,0:T(8,128)(2,1)S(1)}, bf16[192,512]{1,0:T(8,128)(2,1)S(1)}, bf16[192,512]{1,0:T(8,128)(2,1)S(1)}) custom-call(s32[1,8]{1,0:T(1,128)S(1)} %copy-done.6, bf16[192,1024]{1,0:T(8,128)(2,1)S(1)} %copy-done.7, bf16[192,1024]{1,0:T(8,128)(2,1)} %collective-permute-done.rest_1_, ...), custom_call_target="tpu_custom_call" | custom-call | flops 1610612736 | bytes 3670048 | tf_op jit(solution)/shard_map/attend/pallas_call | solution.py:170
  56.1 0.9 %collective-permute-start.20 = (bf16[192,512]{1,0:T(8,128)(2,1)S(1)}, bf16[192,512]{1,0:T(8,128)(2,1)S(1)}, u32[]{:S(2)}, u32[]{:S(2)}) collective-permute-start(bf16[192,512]{1,0:T(8,128)(2,1)S(1)} %get-tuple-element.52), channel_id=1, source_target_pairs={{0,8},{8,0},{16,24},{24,16},{1,9},{9,1},{17,25},{25,17},{2,10},{10... | collective-permute-start | bytes 589832 | tf_op jit(solution)/shard_map/ppermute | solution.py:204
  56.9 1.2 %collective-permute-start.21 = (bf16[192,512]{1,0:T(8,128)(2,1)S(1)}, bf16[192,512]{1,0:T(8,128)(2,1)S(1)}, u32[]{:S(2)}, u32[]{:S(2)}) collective-permute-start(bf16[192,512]{1,0:T(8,128)(2,1)S(1)} %get-tuple-element.53), channel_id=1, source_target_pairs={{0,16},{8,24},{16,0},{24,8},{1,17},{9,25},{17,1},{25,9},{2,18},{10... | collective-permute-start | bytes 589832 | tf_op jit(solution)/shard_map/ppermute | solution.py:204
  58.1 1.5 %collective-permute-start.22 = (bf16[192,512]{1,0:T(8,128)(2,1)S(1)}, bf16[192,512]{1,0:T(8,128)(2,1)S(1)}, u32[]{:S(2)}, u32[]{:S(2)}) collective-permute-start(bf16[192,512]{1,0:T(8,128)(2,1)S(1)} %get-tuple-element.54), channel_id=1, source_target_pairs={{0,24},{8,16},{16,8},{24,0},{1,25},{9,17},{17,9},{25,1},{2,26},{10... | collective-permute-start | bytes 589832 | tf_op jit(solution)/shard_map/ppermute | solution.py:204
  59.6 4.3 %collective-permute-done.20.rest_5_ = bf16[192,512]{1,0:T(8,128)(2,1)S(1)} collective-permute-done((bf16[192,512]{1,0:T(8,128)(2,1)S(1)}, bf16[192,512]{1,0:T(8,128)(2,1)S(1)}, u32[]{:S(2)}, u32[]{:S(2)}) %collective-permute-start.20) | collective-permute-done | bytes 196640 | tf_op jit(solution)/shard_map/ppermute | solution.py:204
  63.9 0.5 collective-permute-done.21.rest_6_
  64.4 3.4 %collective-permute-done.22.rest_7_ = bf16[192,512]{1,0:T(8,128)(2,1)S(1)} collective-permute-done((bf16[192,512]{1,0:T(8,128)(2,1)S(1)}, bf16[192,512]{1,0:T(8,128)(2,1)S(1)}, u32[]{:S(2)}, u32[]{:S(2)}) %collective-permute-start.22) | collective-permute-done | bytes 196640 | tf_op jit(solution)/shard_map/ppermute | solution.py:204
  67.8 2.9 %finish.1 = bf16[384,1024]{1,0:T(8,128)(2,1)} custom-call(bf16[384,1024]{1,0:T(8,128)(2,1)S(1)} %copy-done.2, f32[384,1024]{1,0:T(8,128)S(1)} %copy-done.1, bf16[384,768]{1,0:T(8,128)(2,1)S(1)} %copy-done.3, f32[1,1024]{1,0:T(1,128)S(1)} %copy-done.5, bf16[1024,1024]{1,0:T(8,128)(2,1)S(1)} %bitcast.4, bf16[192,512]{1,0:T(8,128)(2,1)S(1)} %get-tuple-element.42.rest_0_, ...), custom_call_target="tpu_custom_call" | custom-call | flops 1610612736 | bytes 6623232 | tf_op jit(solution)/shard_map/finish/pallas_call | solution.py:170
  (36 shorter events, 0.1 us)
Async XLA Ops:
  0.0 1.0 %copy-start.4 = (bf16[1,1,128,2048]{3,2,1,0:T(8,128)(2,1)S(1)}, bf16[1,1,128,2048]{3,2,1,0:T(8,128)(2,1)}, u32[]{:S(2)}) copy-start(bf16[1,1,128,2048]{3,2,1,0:T(8,128)(2,1)} %param.10) | copy-start | bytes 1572868
  1.8 13.6 %collective-permute-start.6 = (bf16[128,1024]{1,0:T(8,128)(2,1)}, bf16[128,1024]{1,0:T(8,128)(2,1)}, u32[]{:S(2)}, u32[]{:S(2)}) collective-permute-start(bf16[128,1024]{1,0:T(8,128)(2,1)} %get-tuple-element.39.rest_4_), channel_id=1, source_target_pairs={{0,6},{1,7},{2,4},{3,5},{4,2},{5,3},{6,0},{7,1},{8,14},{9,15},{10,... | collective-permute-start | bytes 786440 | tf_op jit(solution)/shard_map/ppermute | solution.py:197
  6.9 18.4 %collective-permute-start.4 = (bf16[128,1024]{1,0:T(8,128)(2,1)}, bf16[128,1024]{1,0:T(8,128)(2,1)}, u32[]{:S(2)}, u32[]{:S(2)}) collective-permute-start(bf16[128,1024]{1,0:T(8,128)(2,1)} %get-tuple-element.39.rest_4_), channel_id=1, source_target_pairs={{0,2},{1,3},{2,0},{3,1},{4,6},{5,7},{6,4},{7,5},{8,10},{9,11},{10,... | collective-permute-start | bytes 786440 | tf_op jit(solution)/shard_map/ppermute | solution.py:197
  11.8 12.4 %collective-permute-start = (bf16[192,1024]{1,0:T(8,128)(2,1)}, bf16[192,1024]{1,0:T(8,128)(2,1)}, u32[]{:S(2)}, u32[]{:S(2)}) collective-permute-start(bf16[192,1024]{1,0:T(8,128)(2,1)} %get-tuple-element.36), channel_id=1, source_target_pairs={{0,8},{8,0},{16,24},{24,16},{1,9},{9,1},{17,25},{25,17},{2,10},{10... | collective-permute-start | bytes 1179656 | tf_op jit(solution)/shard_map/ppermute | solution.py:204
  13.4 19.0 %collective-permute-start.1 = (bf16[192,1024]{1,0:T(8,128)(2,1)}, bf16[192,1024]{1,0:T(8,128)(2,1)}, u32[]{:S(2)}, u32[]{:S(2)}) collective-permute-start(bf16[192,1024]{1,0:T(8,128)(2,1)} %get-tuple-element.37), channel_id=1, source_target_pairs={{0,16},{8,24},{16,0},{24,8},{1,17},{9,25},{17,1},{25,9},{2,18},{10... | collective-permute-start | bytes 1179656 | tf_op jit(solution)/shard_map/ppermute | solution.py:204
  14.9 17.5 %collective-permute-start.2 = (bf16[192,1024]{1,0:T(8,128)(2,1)}, bf16[192,1024]{1,0:T(8,128)(2,1)}, u32[]{:S(2)}, u32[]{:S(2)}) collective-permute-start(bf16[192,1024]{1,0:T(8,128)(2,1)} %get-tuple-element.38), channel_id=1, source_target_pairs={{0,24},{8,16},{16,8},{24,0},{1,25},{9,17},{17,9},{25,1},{2,26},{10... | collective-permute-start | bytes 1179656 | tf_op jit(solution)/shard_map/ppermute | solution.py:204
  15.4 17.6 %collective-permute-start.7 = (bf16[128,1024]{1,0:T(8,128)(2,1)}, bf16[128,1024]{1,0:T(8,128)(2,1)}, u32[]{:S(2)}, u32[]{:S(2)}) collective-permute-start(bf16[128,1024]{1,0:T(8,128)(2,1)} %collective-permute-done.6.rest_10_), channel_id=1, source_target_pairs={{0,2},{1,3},{2,0},{3,1},{4,6},{5,7},{6,4},{7,5},{8,10},{9,11},{10,... | collective-permute-start | bytes 786440 | tf_op jit(solution)/shard_map/ppermute | solution.py:197
  18.8 18.0 %copy-start.6 = (s32[1,8]{1,0:T(1,128)S(1)}, s32[1,8]{1,0:T(1,128)}, u32[]{:S(2)}) copy-start(s32[1,8]{1,0:T(1,128)} %mask.3) | copy-start | bytes 100
  18.8 18.0 %copy-start.7 = (bf16[192,1024]{1,0:T(8,128)(2,1)S(1)}, bf16[192,1024]{1,0:T(8,128)(2,1)}, u32[]{:S(2)}) copy-start(bf16[192,1024]{1,0:T(8,128)(2,1)} %get-tuple-element.35.rest_0_) | copy-start | bytes 1179652
  24.3 8.8 %collective-permute-start.16 = (bf16[128,1024]{1,0:T(8,128)(2,1)S(1)}, bf16[128,1024]{1,0:T(8,128)(2,1)S(1)}, u32[]{:S(2)}, u32[]{:S(2)}) collective-permute-start(bf16[128,1024]{1,0:T(8,128)(2,1)S(1)} %get-tuple-element.49.rest_4_), channel_id=1, source_target_pairs={{0,6},{1,7},{2,4},{3,5},{4,2},{5,3},{6,0},{7,1},{8,14},{9,15},{10,... | collective-permute-start | bytes 786440 | tf_op jit(solution)/shard_map/ppermute | solution.py:197
  25.3 11.4 %collective-permute-start.3 = (bf16[128,1024]{1,0:T(8,128)(2,1)}, bf16[128,1024]{1,0:T(8,128)(2,1)S(1)}, u32[]{:S(2)}, u32[]{:S(2)}) collective-permute-start(bf16[128,1024]{1,0:T(8,128)(2,1)} %get-tuple-element.39.rest_4_), channel_id=1, source_target_pairs={{0,1},{1,0},{2,3},{3,2},{4,5},{5,4},{6,7},{7,6},{8,9},{9,8},{10,11... | collective-permute-start | bytes 786440 | tf_op jit(solution)/shard_map/ppermute | solution.py:200
  32.4 4.3 %collective-permute-start.5 = (bf16[128,1024]{1,0:T(8,128)(2,1)}, bf16[128,1024]{1,0:T(8,128)(2,1)S(1)}, u32[]{:S(2)}, u32[]{:S(2)}) collective-permute-start(bf16[128,1024]{1,0:T(8,128)(2,1)} %collective-permute-done.4.rest_6_), channel_id=1, source_target_pairs={{0,1},{1,0},{2,3},{3,2},{4,5},{5,4},{6,7},{7,6},{8,9},{9,8},{10,11... | collective-permute-start | bytes 786440 | tf_op jit(solution)/shard_map/ppermute | solution.py:200
  32.4 4.3 %collective-permute-start.9 = (bf16[128,1024]{1,0:T(8,128)(2,1)}, bf16[128,1024]{1,0:T(8,128)(2,1)S(1)}, u32[]{:S(2)}, u32[]{:S(2)}) collective-permute-start(bf16[128,1024]{1,0:T(8,128)(2,1)} %collective-permute-done.6.rest_10_), channel_id=1, source_target_pairs={{0,1},{1,0},{2,3},{3,2},{4,5},{5,4},{6,7},{7,6},{8,9},{9,8},{10,11... | collective-permute-start | bytes 786440 | tf_op jit(solution)/shard_map/ppermute | solution.py:200
  32.9 3.8 %collective-permute-start.8 = (bf16[128,1024]{1,0:T(8,128)(2,1)}, bf16[128,1024]{1,0:T(8,128)(2,1)S(1)}, u32[]{:S(2)}, u32[]{:S(2)}) collective-permute-start(bf16[128,1024]{1,0:T(8,128)(2,1)} %collective-permute-done.7.rest_8_), channel_id=1, source_target_pairs={{0,1},{1,0},{2,3},{3,2},{4,5},{5,4},{6,7},{7,6},{8,9},{9,8},{10,11... | collective-permute-start | bytes 786440 | tf_op jit(solution)/shard_map/ppermute | solution.py:200
  33.0 10.9 %collective-permute-start.14 = (bf16[128,1024]{1,0:T(8,128)(2,1)S(1)}, bf16[128,1024]{1,0:T(8,128)(2,1)S(1)}, u32[]{:S(2)}, u32[]{:S(2)}) collective-permute-start(bf16[128,1024]{1,0:T(8,128)(2,1)S(1)} %get-tuple-element.49.rest_4_), channel_id=1, source_target_pairs={{0,2},{1,3},{2,0},{3,1},{4,6},{5,7},{6,4},{7,5},{8,10},{9,11},{10,... | collective-permute-start | bytes 786440 | tf_op jit(solution)/shard_map/ppermute | solution.py:197
  36.7 14.2 %collective-permute-start.17 = (bf16[128,1024]{1,0:T(8,128)(2,1)S(1)}, bf16[128,1024]{1,0:T(8,128)(2,1)S(1)}, u32[]{:S(2)}, u32[]{:S(2)}) collective-permute-start(bf16[128,1024]{1,0:T(8,128)(2,1)S(1)} %collective-permute-done.16.rest_10_), channel_id=1, source_target_pairs={{0,2},{1,3},{2,0},{3,1},{4,6},{5,7},{6,4},{7,5},{8,10},{9,11},{10,... | collective-permute-start | bytes 786440 | tf_op jit(solution)/shard_map/ppermute | solution.py:197
  40.3 7.3 %collective-permute-start.10 = (bf16[192,512]{1,0:T(8,128)(2,1)S(1)}, bf16[192,512]{1,0:T(8,128)(2,1)S(1)}, u32[]{:S(2)}, u32[]{:S(2)}) collective-permute-start(bf16[192,512]{1,0:T(8,128)(2,1)S(1)} %get-tuple-element.43), channel_id=1, source_target_pairs={{0,8},{8,0},{16,24},{24,16},{1,9},{9,1},{17,25},{25,17},{2,10},{10... | collective-permute-start | bytes 589832 | tf_op jit(solution)/shard_map/ppermute | solution.py:204
  41.8 9.1 %collective-permute-start.11 = (bf16[192,512]{1,0:T(8,128)(2,1)S(1)}, bf16[192,512]{1,0:T(8,128)(2,1)S(1)}, u32[]{:S(2)}, u32[]{:S(2)}) collective-permute-start(bf16[192,512]{1,0:T(8,128)(2,1)S(1)} %get-tuple-element.44), channel_id=1, source_target_pairs={{0,16},{8,24},{16,0},{24,8},{1,17},{9,25},{17,1},{25,9},{2,18},{10... | collective-permute-start | bytes 589832 | tf_op jit(solution)/shard_map/ppermute | solution.py:204
  43.4 24.5 %copy-start = (bf16[1,1024,1024]{2,1,0:T(8,128)(2,1)S(1)}, bf16[1,1024,1024]{2,1,0:T(8,128)(2,1)}, u32[]{:S(2)}) copy-start(bf16[1,1024,1024]{2,1,0:T(8,128)(2,1)} %param.15) | copy-start | bytes 6291460
  43.4 24.5 %copy-start.1 = (f32[384,1024]{1,0:T(8,128)S(1)}, f32[384,1024]{1,0:T(8,128)}, u32[]{:S(2)}) copy-start(f32[384,1024]{1,0:T(8,128)} %get-tuple-element.33.gate) | copy-start | bytes 4718596
  43.4 24.5 %copy-start.2 = (bf16[384,1024]{1,0:T(8,128)(2,1)S(1)}, bf16[384,1024]{1,0:T(8,128)(2,1)}, u32[]{:S(2)}) copy-start(bf16[384,1024]{1,0:T(8,128)(2,1)} %feat.1) | copy-start | bytes 2359300
  43.4 24.5 %copy-start.3 = (bf16[384,768]{1,0:T(8,128)(2,1)S(1)}, bf16[384,768]{1,0:T(8,128)(2,1)}, u32[]{:S(2)}) copy-start(bf16[384,768]{1,0:T(8,128)(2,1)} %get-tuple-element.34.pick) | copy-start | bytes 1769476
  43.4 24.5 %copy-start.5 = (f32[1,1024]{1,0:T(1,128)S(1)}, f32[1,1024]{1,0:T(1,128)}, u32[]{:S(2)}) copy-start(f32[1,1024]{1,0:T(1,128)} %gain.1) | copy-start | bytes 12292
  43.4 7.6 %collective-permute-start.12 = (bf16[192,512]{1,0:T(8,128)(2,1)S(1)}, bf16[192,512]{1,0:T(8,128)(2,1)S(1)}, u32[]{:S(2)}, u32[]{:S(2)}) collective-permute-start(bf16[192,512]{1,0:T(8,128)(2,1)S(1)} %get-tuple-element.45), channel_id=1, source_target_pairs={{0,24},{8,16},{16,8},{24,0},{1,25},{9,17},{17,9},{25,1},{2,26},{10... | collective-permute-start | bytes 589832 | tf_op jit(solution)/shard_map/ppermute | solution.py:204
  43.9 7.5 %collective-permute-start.13 = (bf16[128,1024]{1,0:T(8,128)(2,1)S(1)}, bf16[128,1024]{1,0:T(8,128)(2,1)S(1)}, u32[]{:S(2)}, u32[]{:S(2)}) collective-permute-start(bf16[128,1024]{1,0:T(8,128)(2,1)S(1)} %get-tuple-element.49.rest_4_), channel_id=1, source_target_pairs={{0,1},{1,0},{2,3},{3,2},{4,5},{5,4},{6,7},{7,6},{8,9},{9,8},{10,11... | collective-permute-start | bytes 786440 | tf_op jit(solution)/shard_map/ppermute | solution.py:200
  47.6 3.9 %collective-permute-start.19 = (bf16[128,1024]{1,0:T(8,128)(2,1)S(1)}, bf16[128,1024]{1,0:T(8,128)(2,1)S(1)}, u32[]{:S(2)}, u32[]{:S(2)}) collective-permute-start(bf16[128,1024]{1,0:T(8,128)(2,1)S(1)} %collective-permute-done.16.rest_10_), channel_id=1, source_target_pairs={{0,1},{1,0},{2,3},{3,2},{4,5},{5,4},{6,7},{7,6},{8,9},{9,8},{10,11... | collective-permute-start | bytes 786440 | tf_op jit(solution)/shard_map/ppermute | solution.py:200
  50.9 1.5 %collective-permute-start.15 = (bf16[128,1024]{1,0:T(8,128)(2,1)S(1)}, bf16[128,1024]{1,0:T(8,128)(2,1)S(1)}, u32[]{:S(2)}, u32[]{:S(2)}) collective-permute-start(bf16[128,1024]{1,0:T(8,128)(2,1)S(1)} %collective-permute-done.14.rest_6_), channel_id=1, source_target_pairs={{0,1},{1,0},{2,3},{3,2},{4,5},{5,4},{6,7},{7,6},{8,9},{9,8},{10,11... | collective-permute-start | bytes 786440 | tf_op jit(solution)/shard_map/ppermute | solution.py:200
  51.0 1.9 %collective-permute-start.18 = (bf16[128,1024]{1,0:T(8,128)(2,1)S(1)}, bf16[128,1024]{1,0:T(8,128)(2,1)S(1)}, u32[]{:S(2)}, u32[]{:S(2)}) collective-permute-start(bf16[128,1024]{1,0:T(8,128)(2,1)S(1)} %collective-permute-done.17.rest_8_), channel_id=1, source_target_pairs={{0,1},{1,0},{2,3},{3,2},{4,5},{5,4},{6,7},{7,6},{8,9},{9,8},{10,11... | collective-permute-start | bytes 786440 | tf_op jit(solution)/shard_map/ppermute | solution.py:200
  56.1 7.8 %collective-permute-start.20 = (bf16[192,512]{1,0:T(8,128)(2,1)S(1)}, bf16[192,512]{1,0:T(8,128)(2,1)S(1)}, u32[]{:S(2)}, u32[]{:S(2)}) collective-permute-start(bf16[192,512]{1,0:T(8,128)(2,1)S(1)} %get-tuple-element.52), channel_id=1, source_target_pairs={{0,8},{8,0},{16,24},{24,16},{1,9},{9,1},{17,25},{25,17},{2,10},{10... | collective-permute-start | bytes 589832 | tf_op jit(solution)/shard_map/ppermute | solution.py:204
  56.9 7.5 %collective-permute-start.21 = (bf16[192,512]{1,0:T(8,128)(2,1)S(1)}, bf16[192,512]{1,0:T(8,128)(2,1)S(1)}, u32[]{:S(2)}, u32[]{:S(2)}) collective-permute-start(bf16[192,512]{1,0:T(8,128)(2,1)S(1)} %get-tuple-element.53), channel_id=1, source_target_pairs={{0,16},{8,24},{16,0},{24,8},{1,17},{9,25},{17,1},{25,9},{2,18},{10... | collective-permute-start | bytes 589832 | tf_op jit(solution)/shard_map/ppermute | solution.py:204
  58.1 9.7 %collective-permute-start.22 = (bf16[192,512]{1,0:T(8,128)(2,1)S(1)}, bf16[192,512]{1,0:T(8,128)(2,1)S(1)}, u32[]{:S(2)}, u32[]{:S(2)}) collective-permute-start(bf16[192,512]{1,0:T(8,128)(2,1)S(1)} %get-tuple-element.54), channel_id=1, source_target_pairs={{0,24},{8,16},{16,8},{24,0},{1,25},{9,17},{17,9},{25,1},{2,26},{10... | collective-permute-start | bytes 589832 | tf_op jit(solution)/shard_map/ppermute | solution.py:204

commit v4 on v3

v4 whole, which is shorter than its diff:
```python
import functools

import jax
import jax.numpy as jnp
from jax import lax
from jax.experimental import pallas as pl
from jax.experimental.pallas import tpu as pltpu
from jax.sharding import PartitionSpec as P

BLK = 128
HEAD = 128
OPTS = {'chunks': [4, 4], 'order': 0, 'qs': 0, 'cq': 10000000000, 'cg': 0, 'ca': 1000000000, 'cf': 10000000000, 'm1': [], 'a1': [], 'g': ['m0'], 's0': [['qx'], ['g', 'qy'], ['g'], []], 's1': [['s', 'rx'], ['ry'], [], []]}
CHUNKS = OPTS['chunks']
SIDES = 4
VMEM_LIMIT = 32 * 1024 * 1024
VMEM_MOST = 60 * 1024 * 1024
HEAVY = 4 * 10**11


def silu_halved(t):
    return t + t * jnp.tanh(t)


def centred_norm(x):
    middle = jnp.mean(x, axis=-1, keepdims=True)
    shifted = x - middle
    spread = jnp.mean(shifted * shifted, axis=-1, keepdims=True)
    return shifted * lax.rsqrt(spread + 1e-05)


def slots_of(user, me, cap, users):
    rows = user.shape[1]
    rel = user ^ me
    places = max(8, users)
    one_hot = rel == lax.broadcasted_iota(jnp.int32, (places, rows), 0)
    one_hot = one_hot.astype(jnp.float32)
    first = lax.broadcasted_iota(jnp.int32, (rows, rows), 0)
    second = lax.broadcasted_iota(jnp.int32, (rows, rows), 1)
    earlier = (first < second).astype(jnp.bfloat16)
    rank = jnp.dot(one_hot.astype(jnp.bfloat16), earlier, preferred_element_type=jnp.float32)
    rank = jnp.sum(rank * one_hot, axis=0, keepdims=True)
    return rel.astype(jnp.float32) * cap + rank


def kv_split_kernel(kv, *rest):
    outs, sems = rest[:-1], rest[-1]
    half = kv.shape[1] // 2
    copies, first = [], 0
    for out in outs:
        wide = out.shape[1] // 2
        for part in range(2):
            copies.append(
                pltpu.make_async_copy(
                    kv.at[:, pl.ds(part * half + first, wide)],
                    out.at[:, pl.ds(part * wide, wide)],
                    sems.at[len(copies)],
                )
            )
        first += wide
    for copy in copies:
        copy.start()
    for copy in copies:
        copy.wait()


def query_kernel(cap, users, feat_in, user_in, gain_in, w_in, *rest):
    outs, (feat, user, gain, wq, sent, sems, out_sems) = rest[:users], rest[users:]
    rows, width = feat.shape
    sides, _, part_width = wq.shape
    copies = [
        pltpu.make_async_copy(user_in, user, sems.at[0]),
        pltpu.make_async_copy(feat_in, feat, sems.at[1]),
        pltpu.make_async_copy(gain_in, gain, sems.at[2]),
    ]
    for side in range(sides):
        copies.append(
            pltpu.make_async_copy(
                w_in.at[:, pl.ds(width + side * part_width, part_width)],
                wq.at[side],
                sems.at[3 + side],
            )
        )
    for copy in copies:
        copy.start()
    copies[0].wait()
    slot = slots_of(user[...], lax.axis_index("users"), cap, users)
    places = lax.broadcasted_iota(jnp.int32, (users * cap, rows), 0).astype(jnp.float32)
    pick = (places == slot).astype(jnp.bfloat16)
    copies[1].wait()
    copies[2].wait()
    normed = (centred_norm(feat[...].astype(jnp.float32)) * gain[...]).astype(jnp.bfloat16)
    writes = []
    for side in range(sides):
        copies[3 + side].wait()
        cols = slice(side * part_width, (side + 1) * part_width)
        part = jnp.dot(normed, wq[side], preferred_element_type=jnp.float32)
        query = silu_halved(part * 0.5).astype(jnp.bfloat16)
        sent[:, cols] = jnp.dot(pick, query, preferred_element_type=jnp.float32).astype(
            jnp.bfloat16
        )
        for d in range(users):
            write = pltpu.make_async_copy(
                sent.at[pl.ds(d * cap, cap), pl.ds(side * part_width, part_width)],
                outs[d].at[:, pl.ds(side * part_width, part_width)],
                out_sems.at[side * users + d],
            )
            write.start()
            writes.append(write)
    for write in writes:
        write.wait()


def gate_kernel(cap, users, feat_in, user_in, gain_in, w_in, gate, pick, feat, user, gain, wg, sems):
    rows, width = feat.shape
    sides, _, part_width = wg.shape
    copies = [
        pltpu.make_async_copy(user_in, user, sems.at[0]),
        pltpu.make_async_copy(feat_in, feat, sems.at[1]),
        pltpu.make_async_copy(gain_in, gain, sems.at[2]),
    ]
    for side in range(sides):
        copies.append(
            pltpu.make_async_copy(
                w_in.at[:, pl.ds(side * part_width, part_width)], wg.at[side], sems.at[3 + side]
            )
        )
    for copy in copies:
        copy.start()
    copies[0].wait()
    slot = slots_of(user[...], lax.axis_index("users"), cap, users)
    slot = jnp.transpose(jnp.broadcast_to(slot, (128, rows)))[:, 0:1]
    places = lax.broadcasted_iota(jnp.int32, (rows, users * cap), 1).astype(jnp.float32)
    pick[...] = (places == slot).astype(jnp.bfloat16)
    copies[1].wait()
    copies[2].wait()
    normed = (centred_norm(feat[...].astype(jnp.float32)) * gain[...]).astype(jnp.bfloat16)
    for side in range(sides):
        copies[3 + side].wait()
        part = jnp.dot(normed, wg[side], preferred_element_type=jnp.float32)
        gate[:, side * part_width:(side + 1) * part_width] = silu_halved(part * 0.5)


def attend_kernel(users, chips, first, mask, *rest):
    queries = rest[:users]
    blocks = rest[users:users + 2 * chips]
    outs, (live_kv, all_q) = rest[-2 - users:-2], rest[-2:]
    place = lax.axis_index("ctx")
    core, z = place % 2, place // 2
    cap, wide = outs[0].shape
    taken = jnp.int32(0)
    for d in range(chips):
        for swap in range(2):
            live = mask[0, 2 * (z ^ d) + (core ^ swap)] > 0

            def take(block=blocks[2 * d + swap], taken=taken):
                at = pl.multiple_of(taken * BLK, BLK)
                live_kv[pl.ds(at, BLK), :] = block[...]

            pl.when(live)(take)
            taken = jnp.minimum(taken + live.astype(jnp.int32), chips - 1)
    for i, q in enumerate(queries):
        all_q[i * cap:(i + 1) * cap, :] = q[:, first:first + wide]
    scale = 0.5 * HEAD ** (-0.5)
    for head in range(wide // HEAD):
        cols = slice(head * HEAD, (head + 1) * HEAD)
        keys = live_kv[:, cols]
        values = live_kv[:, wide + head * HEAD:wide + (head + 1) * HEAD]
        scores = lax.dot_general(
            all_q[:, cols], keys, (((1,), (1,)), ((), ())), preferred_element_type=jnp.float32
        )
        weight = silu_halved(scores * scale).astype(jnp.bfloat16)
        got = jnp.dot(weight, values, preferred_element_type=jnp.float32).astype(jnp.bfloat16)
        for i, out in enumerate(outs):
            out[:, cols] = got[i * cap:(i + 1) * cap, :]


def finish_kernel(users, feat, gate, pick, gain, w_out, *rest):
    parts, out, back = rest[:-2], rest[-2], rest[-1]
    first = 0
    for chunk in range(len(parts) // users):
        cap, wide = parts[chunk * users].shape
        for d in range(users):
            part = parts[chunk * users + d]
            back[d * cap:(d + 1) * cap, first:first + wide] = part[...]
        first += wide
    attended = jnp.dot(pick[...], back[...], preferred_element_type=jnp.float32)
    mixed = (centred_norm(attended) * gain[...] * gate[...]).astype(jnp.bfloat16)
    grown = jnp.dot(mixed, w_out[...], preferred_element_type=jnp.float32)
    out[...] = (feat[...].astype(jnp.float32) + grown).astype(jnp.bfloat16)


SMEM = pl.BlockSpec(memory_space=pltpu.SMEM)
HBM = pl.BlockSpec(memory_space=pltpu.HBM)


def whole(*dims, at=None):
    return pl.BlockSpec(dims, lambda i: at or (0,) * len(dims))


def call(kernel, name, in_specs, out_shape, scratch, flops, *args, vmem=VMEM_LIMIT):
    moved = sum(a.size * a.dtype.itemsize for a in args)
    return pl.pallas_call(
        kernel,
        name=name,
        grid=(1,),
        in_specs=in_specs,
        out_specs=[whole(*s.shape) for s in out_shape],
        out_shape=out_shape,
        scratch_shapes=scratch,
        cost_estimate=pl.CostEstimate(flops=flops, bytes_accessed=moved if flops else 0, transcendentals=0),
        compiler_params=pltpu.CompilerParams(vmem_limit_bytes=vmem),
    )(*args)


def on_device(cand_feat, cand_user, hist_kv, hist_mask, gain_in, w_uq, gain_attn, w_out):
    users = lax.axis_size("users")
    ctx = lax.axis_size("ctx")
    chips = ctx // 2
    rows, width = cand_feat.shape
    cap = 2 * rows // users
    wides = [heads * HEAD for heads in CHUNKS]
    bf16 = jnp.bfloat16
    user_row = cand_user.reshape(1, rows)

    def shape(*dims, dtype=bf16):
        return jax.ShapeDtypeStruct(dims, dtype)

    def over_z(value, d):
        return lax.ppermute(value, "ctx", [(c, c ^ (2 * d)) for c in range(ctx)])

    def over_cores(value):
        return lax.ppermute(value, "ctx", [(c, c ^ 1) for c in range(ctx)])

    def to_user(value, d):
        return lax.ppermute(value, "users", [(u, u ^ d) for u in range(users)])

    def after(value, *others):
        return lax.optimization_barrier((value, *others))[0]

    def over_users(values):
        if OPTS['order'] == 0:
            got = [to_user(values[d], d) for d in range(users - 1, 0, -1)]
            return [values[0]] + got[::-1]
        return [values[0]] + [to_user(values[d], d) for d in range(1, users)]

    kv = hist_kv[0, 0]
    split = pl.pallas_call(
        kv_split_kernel,
        name="kv_split",
        in_specs=[HBM],
        out_specs=[HBM] * len(wides),
        out_shape=[shape(BLK, 2 * wide) for wide in wides],
        scratch_shapes=[pltpu.SemaphoreType.DMA((2 * len(wides),))],
        cost_estimate=pl.CostEstimate(flops=0, bytes_accessed=4 * kv.size, transcendentals=0),
        compiler_params=pltpu.CompilerParams(vmem_limit_bytes=VMEM_MOST),
    )(kv)

    operands = [
        pltpu.VMEM((rows, width), bf16),
        pltpu.VMEM((1, rows), jnp.int32),
        pltpu.VMEM((1, width), jnp.float32),
        pltpu.VMEM((SIDES, width, width // SIDES), bf16),
    ]
    queries = pl.pallas_call(
        functools.partial(query_kernel, cap, users),
        name="query",
        in_specs=[HBM] * 4,
        out_specs=[HBM] * users,
        out_shape=[shape(cap, width)] * users,
        scratch_shapes=operands + [
            pltpu.VMEM((users * cap, width), bf16),
            pltpu.SemaphoreType.DMA((3 + SIDES,)),
            pltpu.SemaphoreType.DMA((SIDES * users,)),
        ],
        cost_estimate=pl.CostEstimate(flops=OPTS['cq'], bytes_accessed=0, transcendentals=0),
        compiler_params=pltpu.CompilerParams(vmem_limit_bytes=VMEM_MOST),
    )((after(cand_feat, split[0]) if OPTS['qs'] else cand_feat), user_row, gain_in, w_uq[0])
    arrived = over_users(queries)

    returned, first, env = [], 0, {}
    env.update({'qx': arrived[1], 'qy': arrived[2], 'qd': arrived[3], 'q': queries[0]})

    def gated(value, keys):
        ready = [env[k] for k in keys]
        return after(value, *ready) if ready else value

    for chunk, wide in enumerate(wides):
        held = {0: split[chunk]}
        far = near = split[chunk]
        if chunk:
            c = str(chunk - 1)
            far = gated(far, [k + c if k in 'maf' else k for k in OPTS['m1']])
            near = gated(near, [k + c if k in 'maf' else k for k in OPTS['a1']])
        for d in [3, 1, 2] + list(range(4, chips)):
            held[d] = over_z(held[3], 1) if d == 2 else over_z(near if d == 1 else far, d)
        env.update({'a' + str(chunk): held[1], 'm' + str(chunk): held[3], 'f' + str(chunk): held[2]})
        if chunk == 0:
            gate, pick = call(
                functools.partial(gate_kernel, cap, users), "gate",
                [HBM] * 4,
                [shape(rows, width, dtype=jnp.float32), shape(rows, users * cap)],
                operands + [pltpu.SemaphoreType.DMA((3 + SIDES,))],
                OPTS['cg'],
                gated(cand_feat, ['q'] + OPTS['g']), user_row, gain_in, w_uq[0], vmem=VMEM_MOST,
            )
            env['g'] = gate
        blocks = []
        for d in range(chips):
            if chunk == 0:
                keys = OPTS['s0'][d % 4]
            else:
                keys = OPTS['s1'][d % 4]
            blocks += [held[d], over_cores(gated(held[d], keys))]
        scored = call(
            functools.partial(attend_kernel, users, chips, first), "attend",
            [SMEM] + [whole(cap, width)] * users + [whole(BLK, 2 * wide)] * (2 * chips),
            [shape(cap, wide)] * users,
            [pltpu.VMEM((chips * BLK, 2 * wide), bf16), pltpu.VMEM((users * cap, wide), bf16)],
            OPTS['ca'],
            hist_mask, *arrived, *blocks,
        )
        back = over_users(scored)
        env.update({'s': scored[0], 'rx': back[1], 'ry': back[2], 'rd': back[3]})
        returned += back
        first += wide

    return call(
        functools.partial(finish_kernel, users), "finish",
        [
            whole(rows, width), whole(rows, width), whole(rows, users * cap), whole(1, width),
            whole(width, width),
        ]
        + [whole(*part.shape) for part in returned],
        [shape(rows, width)],
        [pltpu.VMEM((users * cap, width), bf16)],
        OPTS["cf"],
        cand_feat, gate, pick, gain_attn, w_out[0], *returned,
    )[0]


def solution(mesh):
    in_specs = (
        P(("users", "ctx"), None),
        P(("users", "ctx"), None),
        P(None, "users", "ctx", None),
        P("users", None),
        P(),
        P(),
        P(),
        P(),
    )
    out_specs = P(("users", "ctx"), None)
    return jax.shard_map(
        on_device, mesh=mesh, in_specs=in_specs, out_specs=out_specs, check_vma=False
    )
```

time: 71 us -> 89.8 us (1.26)
  Pallas kernels: 19.2 us -> 37.3 us
  starting transfers between devices: 25 us -> 26.6 us
  local copies, waits for them, and re-layouts: 1.07 us -> 0.04 us
    pallas_call x0 -> x2, Pallas kernels: none -> 23.8 us  [the longest x1 17 us: on_device(): pl.pallas_call(kv_split_kernel, name='kv_split', in_specs=[HBM], out_spec...]
    ppermute x6, waiting for transfers between devices: 0.03 us -> 16.6 us  [over_z(): return lax.ppermute(value, 'ctx', [(c, c ^ 2 * d) for c in range(ctx)])]
    ppermute x9, waiting for transfers between devices: 23.9 us -> 8.77 us  [to_user(): return lax.ppermute(value, 'users', [(u, u ^ d) for u in range(users)])]
    pallas_call x6 -> x4, Pallas kernels: 19.2 us -> 13.5 us  [call(): pl.pallas_call(kernel, name=name, grid=(1,), in_specs=in_specs, out_specs...]
    ppermute x9, starting transfers between devices: 10.7 us -> 13.2 us  [to_user(): return lax.ppermute(value, 'users', [(u, u ^ d) for u in range(users)])]
    ppermute x8, waiting for transfers between devices: 1.4 us -> 0.2 us  [over_cores(): return lax.ppermute(value, 'ctx', [(c, c ^ 1) for c in range(ctx)])]
    ppermute x6, starting transfers between devices: 13.2 us -> 12.2 us  [over_z(): return lax.ppermute(value, 'ctx', [(c, c ^ 2 * d) for c in range(ctx)])]
    unnamed x16 -> x18, local copies, waits for them, and re-layouts: 1.07 us -> 0.04 us
  transfers between devices with their start and end apart: 23 -> 23, of which waited for: 9 -> 7; matrix products, arithmetic and copies ran while one was open for 0% -> 0% of each run, Pallas kernels for 17% -> 31%
where the time goes in v4:
time: 89.8 us; the launch traced here: 89.7 us
  Pallas kernels  37.3 us (42%)
  starting transfers between devices  26.6 us (30%)
  waiting for transfers between devices  25.5 us (28%)
    pallas_call x1, Pallas kernels, on_device(): pl.pallas_call(kv_split_kernel, name='kv_split', in_specs=[HBM], out_spec...  17 us
    ppermute x6, waiting for transfers between devices, over_z(): return lax.ppermute(value, 'ctx', [(c, c ^ 2 * d) for c in range(ctx)])  16.6 us
    pallas_call x4, Pallas kernels, call(): pl.pallas_call(kernel, name=name, grid=(1,), in_specs=in_specs, out_specs...  13.5 us
    ppermute x9, starting transfers between devices, to_user(): return lax.ppermute(value, 'users', [(u, u ^ d) for u in range(users)])  13.2 us
    ppermute x6, starting transfers between devices, over_z(): return lax.ppermute(value, 'ctx', [(c, c ^ 2 * d) for c in range(ctx)])  12.2 us
    ppermute x9, waiting for transfers between devices, to_user(): return lax.ppermute(value, 'users', [(u, u ^ d) for u in range(users)])  8.77 us
    pallas_call x1, Pallas kernels, on_device(): pl.pallas_call(functools.partial(query_kernel, cap, users), name='query',...  6.81 us
  transfers between devices with their start and end apart: 23, of which 7 were waited for; matrix products, arithmetic and copies ran while one was open for 0% of the time, Pallas kernels for 31%

profile of v4, /device:TPU:0, one launch (start us, length us, event | category | flops | bytes accessed | tf_op | source)
XLA Modules:
  0.0 89.7 jit_solution(1488283747813237898)
XLA Ops:
  0.0 6.8 %query.1 = (bf16[192,1024]{1,0:T(8,128)(2,1)}, bf16[192,1024]{1,0:T(8,128)(2,1)}, bf16[192,1024]{1,0:T(8,128)(2,1)}, bf16[192,1024]{1,0:T(8,128)(2,1)}) custom-call(bf16[384,1024]{1,0:T(8,128)(2,1)} %feat.1, s32[1,384]{1,0:T(1,128)} %bitcast.8, f32[1,1024]{1,0:T(1,128)} %gain_in.3, bf16[1024,2048]{1,0:T(8,128)(2,1)} %bitcast.5), custom_call_target="tpu_custom_call" | custom-call | flops 10000000000 | tf_op jit(solution)/shard_map/query/pallas_call | solution.py:264
  6.8 3.0 %collective-permute-start.1 = (bf16[192,1024]{1,0:T(8,128)(2,1)}, bf16[192,1024]{1,0:T(8,128)(2,1)S(1)}, u32[]{:S(2)}, u32[]{:S(2)}) collective-permute-start(bf16[192,1024]{1,0:T(8,128)(2,1)} %get-tuple-element.32), channel_id=1, source_target_pairs={{0,8},{8,0},{16,24},{24,16},{1,9},{9,1},{17,25},{25,17},{2,10},{10... | collective-permute-start | bytes 1179656 | tf_op jit(solution)/shard_map/ppermute | solution.py:235
  9.8 17.0 %kv_split.1 = (bf16[128,1024]{1,0:T(8,128)(2,1)}, bf16[128,1024]{1,0:T(8,128)(2,1)}) custom-call(bf16[128,2048]{1,0:T(8,128)(2,1)} %bitcast.7), custom_call_target="tpu_custom_call" | custom-call | bytes 1048576 | tf_op jit(solution)/shard_map/kv_split/pallas_call | solution.py:247
  26.8 3.7 %collective-permute-start = (bf16[128,1024]{1,0:T(8,128)(2,1)}, bf16[128,1024]{1,0:T(8,128)(2,1)S(1)}, u32[]{:S(2)}, u32[]{:S(2)}) collective-permute-start(bf16[128,1024]{1,0:T(8,128)(2,1)} %get-tuple-element.35.rest_4_), channel_id=1, source_target_pairs={{0,6},{1,7},{2,4},{3,5},{4,2},{5,3},{6,0},{7,1},{8,14},{9,15},{10,... | collective-permute-start | bytes 786440 | tf_op jit(solution)/shard_map/ppermute | solution.py:229
  30.5 1.5 %collective-permute-start.2 = (bf16[192,1024]{1,0:T(8,128)(2,1)}, bf16[192,1024]{1,0:T(8,128)(2,1)S(1)}, u32[]{:S(2)}, u32[]{:S(2)}) collective-permute-start(bf16[192,1024]{1,0:T(8,128)(2,1)} %get-tuple-element.33), channel_id=1, source_target_pairs={{0,16},{8,24},{16,0},{24,8},{1,17},{9,25},{17,1},{25,9},{2,18},{10... | collective-permute-start | bytes 1179656 | tf_op jit(solution)/shard_map/ppermute | solution.py:235
  32.0 6.1 %collective-permute-done.rest_10_ = bf16[128,1024]{1,0:T(8,128)(2,1)S(1)} collective-permute-done((bf16[128,1024]{1,0:T(8,128)(2,1)}, bf16[128,1024]{1,0:T(8,128)(2,1)S(1)}, u32[]{:S(2)}, u32[]{:S(2)}) %collective-permute-start) | collective-permute-done | bytes 262176 | tf_op jit(solution)/shard_map/ppermute | solution.py:229
  38.1 3.9 %collective-permute-start.7 = (bf16[128,1024]{1,0:T(8,128)(2,1)S(1)}, bf16[128,1024]{1,0:T(8,128)(2,1)S(1)}, u32[]{:S(2)}, u32[]{:S(2)}) collective-permute-start(bf16[128,1024]{1,0:T(8,128)(2,1)S(1)} %collective-permute-done.rest_10_), channel_id=1, source_target_pairs={{0,2},{1,3},{2,0},{3,1},{4,6},{5,7},{6,4},{7,5},{8,10},{9,11},{10,... | collective-permute-start | bytes 786440 | tf_op jit(solution)/shard_map/ppermute | solution.py:229
  42.1 2.5 %collective-permute-start.16 = (bf16[128,1024]{1,0:T(8,128)(2,1)}, bf16[128,1024]{1,0:T(8,128)(2,1)S(1)}, u32[]{:S(2)}, u32[]{:S(2)}) collective-permute-start(bf16[128,1024]{1,0:T(8,128)(2,1)} %get-tuple-element.43.rest_4_), channel_id=1, source_target_pairs={{0,6},{1,7},{2,4},{3,5},{4,2},{5,3},{6,0},{7,1},{8,14},{9,15},{10,... | collective-permute-start | bytes 786440 | tf_op jit(solution)/shard_map/ppermute | solution.py:229
  44.6 1.5 %collective-permute-start.3 = (bf16[192,1024]{1,0:T(8,128)(2,1)}, bf16[192,1024]{1,0:T(8,128)(2,1)S(1)}, u32[]{:S(2)}, u32[]{:S(2)}) collective-permute-start(bf16[192,1024]{1,0:T(8,128)(2,1)} %get-tuple-element.34), channel_id=1, source_target_pairs={{0,24},{8,16},{16,8},{24,0},{1,25},{9,17},{17,9},{25,1},{2,26},{10... | collective-permute-start | bytes 1179656 | tf_op jit(solution)/shard_map/ppermute | solution.py:235
  46.1 5.2 %gate.1 = (f32[384,1024]{1,0:T(8,128)}, bf16[384,768]{1,0:T(8,128)(2,1)}) custom-call(bf16[384,1024]{1,0:T(8,128)(2,1)} %feat.1, s32[1,384]{1,0:T(1,128)} %bitcast.9, f32[1,1024]{1,0:T(1,128)} %gain_in.3, bf16[1024,2048]{1,0:T(8,128)(2,1)} %bitcast.6), custom_call_target="tpu_custom_call" | custom-call | tf_op jit(solution)/shard_map/gate/pallas_call | solution.py:202
  51.3 0.1 collective-permute-start.9
  51.4 0.5 collective-permute-start.4
  51.9 0.1 collective-permute-start.6
  51.9 3.0 %collective-permute-done.16.rest_10_ = bf16[128,1024]{1,0:T(8,128)(2,1)S(1)} collective-permute-done((bf16[128,1024]{1,0:T(8,128)(2,1)}, bf16[128,1024]{1,0:T(8,128)(2,1)S(1)}, u32[]{:S(2)}, u32[]{:S(2)}) %collective-permute-start.16) | collective-permute-done | bytes 262176 | tf_op jit(solution)/shard_map/ppermute | solution.py:229
  55.0 0.1 collective-permute-start.14
  55.1 2.0 %collective-permute-start.17 = (bf16[128,1024]{1,0:T(8,128)(2,1)S(1)}, bf16[128,1024]{1,0:T(8,128)(2,1)S(1)}, u32[]{:S(2)}, u32[]{:S(2)}) collective-permute-start(bf16[128,1024]{1,0:T(8,128)(2,1)S(1)} %collective-permute-done.16.rest_10_), channel_id=1, source_target_pairs={{0,2},{1,3},{2,0},{3,1},{4,6},{5,7},{6,4},{7,5},{8,10},{9,11},{10,... | collective-permute-start | bytes 786440 | tf_op jit(solution)/shard_map/ppermute | solution.py:229
  57.1 2.6 %attend.2 = (bf16[192,512]{1,0:T(8,128)(2,1)S(1)}, bf16[192,512]{1,0:T(8,128)(2,1)S(1)}, bf16[192,512]{1,0:T(8,128)(2,1)S(1)}, bf16[192,512]{1,0:T(8,128)(2,1)S(1)}) custom-call(s32[1,8]{1,0:T(1,128)S(1)} %copy-done.7, bf16[192,1024]{1,0:T(8,128)(2,1)S(1)} %copy-done.8, bf16[192,1024]{1,0:T(8,128)(2,1)S(1)} %collective-permute-done.1.rest_1_, ...), custom_call_target="tpu_custom_call" | custom-call | flops 1000000000 | bytes 3670048 | tf_op jit(solution)/shard_map/attend/pallas_call | solution.py:202
  59.8 0.6 collective-permute-start.10
  60.4 1.5 %collective-permute-start.11 = (bf16[192,512]{1,0:T(8,128)(2,1)S(1)}, bf16[192,512]{1,0:T(8,128)(2,1)S(1)}, u32[]{:S(2)}, u32[]{:S(2)}) collective-permute-start(bf16[192,512]{1,0:T(8,128)(2,1)S(1)} %get-tuple-element.40), channel_id=1, source_target_pairs={{0,16},{8,24},{16,0},{24,8},{1,17},{9,25},{17,1},{25,9},{2,18},{10... | collective-permute-start | bytes 589832 | tf_op jit(solution)/shard_map/ppermute | solution.py:235
  61.9 7.4 %collective-permute-done.17.rest_8_ = bf16[128,1024]{1,0:T(8,128)(2,1)S(1)} collective-permute-done((bf16[128,1024]{1,0:T(8,128)(2,1)S(1)}, bf16[128,1024]{1,0:T(8,128)(2,1)S(1)}, u32[]{:S(2)}, u32[]{:S(2)}) %collective-permute-start.17) | collective-permute-done | bytes 262176 | tf_op jit(solution)/shard_map/ppermute | solution.py:229
  69.3 0.5 collective-permute-start.13
  69.9 0.1 collective-permute-start.15
  69.9 1.5 %collective-permute-start.12 = (bf16[192,512]{1,0:T(8,128)(2,1)S(1)}, bf16[192,512]{1,0:T(8,128)(2,1)S(1)}, u32[]{:S(2)}, u32[]{:S(2)}) collective-permute-start(bf16[192,512]{1,0:T(8,128)(2,1)S(1)} %get-tuple-element.41), channel_id=1, source_target_pairs={{0,24},{8,16},{16,8},{24,0},{1,25},{9,17},{17,9},{25,1},{2,26},{10... | collective-permute-start | bytes 589832 | tf_op jit(solution)/shard_map/ppermute | solution.py:235
  71.4 0.2 collective-permute-done.15.rest_7_
  71.6 2.8 %attend.3 = (bf16[192,512]{1,0:T(8,128)(2,1)S(1)}, bf16[192,512]{1,0:T(8,128)(2,1)S(1)}, bf16[192,512]{1,0:T(8,128)(2,1)S(1)}, bf16[192,512]{1,0:T(8,128)(2,1)S(1)}) custom-call(s32[1,8]{1,0:T(1,128)S(1)} %copy-done.7, bf16[192,1024]{1,0:T(8,128)(2,1)S(1)} %copy-done.8, bf16[192,1024]{1,0:T(8,128)(2,1)S(1)} %collective-permute-done.1.rest_1_, ...), custom_call_target="tpu_custom_call" | custom-call | flops 1000000000 | bytes 3670048 | tf_op jit(solution)/shard_map/attend/pallas_call | solution.py:202
  74.4 1.4 %collective-permute-start.20 = (bf16[192,512]{1,0:T(8,128)(2,1)S(1)}, bf16[192,512]{1,0:T(8,128)(2,1)S(1)}, u32[]{:S(2)}, u32[]{:S(2)}) collective-permute-start(bf16[192,512]{1,0:T(8,128)(2,1)S(1)} %get-tuple-element.46), channel_id=1, source_target_pairs={{0,8},{8,0},{16,24},{24,16},{1,9},{9,1},{17,25},{25,17},{2,10},{10... | collective-permute-start | bytes 589832 | tf_op jit(solution)/shard_map/ppermute | solution.py:235
  75.8 0.7 collective-permute-start.21
  76.5 1.4 %collective-permute-start.22 = (bf16[192,512]{1,0:T(8,128)(2,1)S(1)}, bf16[192,512]{1,0:T(8,128)(2,1)S(1)}, u32[]{:S(2)}, u32[]{:S(2)}) collective-permute-start(bf16[192,512]{1,0:T(8,128)(2,1)S(1)} %get-tuple-element.48), channel_id=1, source_target_pairs={{0,24},{8,16},{16,8},{24,0},{1,25},{9,17},{17,9},{25,1},{2,26},{10... | collective-permute-start | bytes 589832 | tf_op jit(solution)/shard_map/ppermute | solution.py:235
  78.0 0.1 collective-permute-done.12.rest_3_
  78.1 4.7 %collective-permute-done.20.rest_5_ = bf16[192,512]{1,0:T(8,128)(2,1)S(1)} collective-permute-done((bf16[192,512]{1,0:T(8,128)(2,1)S(1)}, bf16[192,512]{1,0:T(8,128)(2,1)S(1)}, u32[]{:S(2)}, u32[]{:S(2)}) %collective-permute-start.20) | collective-permute-done | bytes 196640 | tf_op jit(solution)/shard_map/ppermute | solution.py:235
  82.8 3.9 %collective-permute-done.21.rest_6_ = bf16[192,512]{1,0:T(8,128)(2,1)S(1)} collective-permute-done((bf16[192,512]{1,0:T(8,128)(2,1)S(1)}, bf16[192,512]{1,0:T(8,128)(2,1)S(1)}, u32[]{:S(2)}, u32[]{:S(2)}) %collective-permute-start.21) | collective-permute-done | bytes 196640 | tf_op jit(solution)/shard_map/ppermute | solution.py:235
  86.8 2.9 %finish.1 = bf16[384,1024]{1,0:T(8,128)(2,1)} custom-call(bf16[384,1024]{1,0:T(8,128)(2,1)S(1)} %copy-done, f32[384,1024]{1,0:T(8,128)S(1)} %copy-done.2, bf16[384,768]{1,0:T(8,128)(2,1)S(1)} %copy-done.3, f32[1,1024]{1,0:T(1,128)S(1)} %copy-done.6, bf16[1024,1024]{1,0:T(8,128)(2,1)S(1)} %bitcast.4, bf16[192,512]{1,0:T(8,128)(2,1)S(1)} %get-tuple-element.38.rest_0_, ...), custom_call_target="tpu_custom_call" | custom-call | flops 10000000000 | bytes 6623232 | tf_op jit(solution)/shard_map/finish/pallas_call | solution.py:202
  (38 shorter events, 0.1 us)
Async XLA Ops:
  6.8 37.7 %collective-permute-start.1 = (bf16[192,1024]{1,0:T(8,128)(2,1)}, bf16[192,1024]{1,0:T(8,128)(2,1)S(1)}, u32[]{:S(2)}, u32[]{:S(2)}) collective-permute-start(bf16[192,1024]{1,0:T(8,128)(2,1)} %get-tuple-element.32), channel_id=1, source_target_pairs={{0,8},{8,0},{16,24},{24,16},{1,9},{9,1},{17,25},{25,17},{2,10},{10... | collective-permute-start | bytes 1179656 | tf_op jit(solution)/shard_map/ppermute | solution.py:235
  26.8 11.3 %collective-permute-start = (bf16[128,1024]{1,0:T(8,128)(2,1)}, bf16[128,1024]{1,0:T(8,128)(2,1)S(1)}, u32[]{:S(2)}, u32[]{:S(2)}) collective-permute-start(bf16[128,1024]{1,0:T(8,128)(2,1)} %get-tuple-element.35.rest_4_), channel_id=1, source_target_pairs={{0,6},{1,7},{2,4},{3,5},{4,2},{5,3},{6,0},{7,1},{8,14},{9,15},{10,... | collective-permute-start | bytes 786440 | tf_op jit(solution)/shard_map/ppermute | solution.py:229
  30.5 20.8 %collective-permute-start.2 = (bf16[192,1024]{1,0:T(8,128)(2,1)}, bf16[192,1024]{1,0:T(8,128)(2,1)S(1)}, u32[]{:S(2)}, u32[]{:S(2)}) collective-permute-start(bf16[192,1024]{1,0:T(8,128)(2,1)} %get-tuple-element.33), channel_id=1, source_target_pairs={{0,16},{8,24},{16,0},{24,8},{1,17},{9,25},{17,1},{25,9},{2,18},{10... | collective-permute-start | bytes 1179656 | tf_op jit(solution)/shard_map/ppermute | solution.py:235
  32.0 19.2 %collective-permute-start.5 = (bf16[128,1024]{1,0:T(8,128)(2,1)}, bf16[128,1024]{1,0:T(8,128)(2,1)S(1)}, u32[]{:S(2)}, u32[]{:S(2)}) collective-permute-start(bf16[128,1024]{1,0:T(8,128)(2,1)} %get-tuple-element.35.rest_4_), channel_id=1, source_target_pairs={{0,2},{1,3},{2,0},{3,1},{4,6},{5,7},{6,4},{7,5},{8,10},{9,11},{10,... | collective-permute-start | bytes 786440 | tf_op jit(solution)/shard_map/ppermute | solution.py:229
  38.1 13.7 %collective-permute-start.7 = (bf16[128,1024]{1,0:T(8,128)(2,1)S(1)}, bf16[128,1024]{1,0:T(8,128)(2,1)S(1)}, u32[]{:S(2)}, u32[]{:S(2)}) collective-permute-start(bf16[128,1024]{1,0:T(8,128)(2,1)S(1)} %collective-permute-done.rest_10_), channel_id=1, source_target_pairs={{0,2},{1,3},{2,0},{3,1},{4,6},{5,7},{6,4},{7,5},{8,10},{9,11},{10,... | collective-permute-start | bytes 786440 | tf_op jit(solution)/shard_map/ppermute | solution.py:229
  42.1 12.9 %collective-permute-start.16 = (bf16[128,1024]{1,0:T(8,128)(2,1)}, bf16[128,1024]{1,0:T(8,128)(2,1)S(1)}, u32[]{:S(2)}, u32[]{:S(2)}) collective-permute-start(bf16[128,1024]{1,0:T(8,128)(2,1)} %get-tuple-element.43.rest_4_), channel_id=1, source_target_pairs={{0,6},{1,7},{2,4},{3,5},{4,2},{5,3},{6,0},{7,1},{8,14},{9,15},{10,... | collective-permute-start | bytes 786440 | tf_op jit(solution)/shard_map/ppermute | solution.py:229
  44.6 10.4 %collective-permute-start.3 = (bf16[192,1024]{1,0:T(8,128)(2,1)}, bf16[192,1024]{1,0:T(8,128)(2,1)S(1)}, u32[]{:S(2)}, u32[]{:S(2)}) collective-permute-start(bf16[192,1024]{1,0:T(8,128)(2,1)} %get-tuple-element.34), channel_id=1, source_target_pairs={{0,24},{8,16},{16,8},{24,0},{1,25},{9,17},{17,9},{25,1},{2,26},{10... | collective-permute-start | bytes 1179656 | tf_op jit(solution)/shard_map/ppermute | solution.py:235
  46.0 5.3 %copy-start.5 = (bf16[128,1024]{1,0:T(8,128)(2,1)S(1)}, bf16[128,1024]{1,0:T(8,128)(2,1)}, u32[]{:S(2)}) copy-start(bf16[128,1024]{1,0:T(8,128)(2,1)} %get-tuple-element.35.rest_4_) | copy-start | bytes 786436
  46.1 9.0 %copy-start.4 = (bf16[128,1024]{1,0:T(8,128)(2,1)S(1)}, bf16[128,1024]{1,0:T(8,128)(2,1)}, u32[]{:S(2)}) copy-start(bf16[128,1024]{1,0:T(8,128)(2,1)} %get-tuple-element.43.rest_4_) | copy-start | bytes 786436
  46.1 11.1 %copy-start.7 = (s32[1,8]{1,0:T(1,128)S(1)}, s32[1,8]{1,0:T(1,128)}, u32[]{:S(2)}) copy-start(s32[1,8]{1,0:T(1,128)} %mask.3) | copy-start | bytes 100
  46.1 11.1 %copy-start.8 = (bf16[192,1024]{1,0:T(8,128)(2,1)S(1)}, bf16[192,1024]{1,0:T(8,128)(2,1)}, u32[]{:S(2)}) copy-start(bf16[192,1024]{1,0:T(8,128)(2,1)} %get-tuple-element.27.rest_0_) | copy-start | bytes 1179652
  51.3 3.8 %collective-permute-start.9 = (bf16[128,1024]{1,0:T(8,128)(2,1)S(1)}, bf16[128,1024]{1,0:T(8,128)(2,1)S(1)}, u32[]{:S(2)}, u32[]{:S(2)}) collective-permute-start(bf16[128,1024]{1,0:T(8,128)(2,1)S(1)} %collective-permute-done.rest_10_), channel_id=1, source_target_pairs={{0,1},{1,0},{2,3},{3,2},{4,5},{5,4},{6,7},{7,6},{8,9},{9,8},{10,11... | collective-permute-start | bytes 786440 | tf_op jit(solution)/shard_map/ppermute | solution.py:232
  51.4 5.7 %collective-permute-start.4 = (bf16[128,1024]{1,0:T(8,128)(2,1)S(1)}, bf16[128,1024]{1,0:T(8,128)(2,1)S(1)}, u32[]{:S(2)}, u32[]{:S(2)}) collective-permute-start(bf16[128,1024]{1,0:T(8,128)(2,1)S(1)} %copy-done.5), channel_id=1, source_target_pairs={{0,1},{1,0},{2,3},{3,2},{4,5},{5,4},{6,7},{7,6},{8,9},{9,8},{10,11... | collective-permute-start | bytes 786440 | tf_op jit(solution)/shard_map/ppermute | solution.py:232
  51.9 5.3 %collective-permute-start.6 = (bf16[128,1024]{1,0:T(8,128)(2,1)S(1)}, bf16[128,1024]{1,0:T(8,128)(2,1)S(1)}, u32[]{:S(2)}, u32[]{:S(2)}) collective-permute-start(bf16[128,1024]{1,0:T(8,128)(2,1)S(1)} %collective-permute-done.5.rest_6_), channel_id=1, source_target_pairs={{0,1},{1,0},{2,3},{3,2},{4,5},{5,4},{6,7},{7,6},{8,9},{9,8},{10,11... | collective-permute-start | bytes 786440 | tf_op jit(solution)/shard_map/ppermute | solution.py:232
  55.0 2.1 %collective-permute-start.8 = (bf16[128,1024]{1,0:T(8,128)(2,1)S(1)}, bf16[128,1024]{1,0:T(8,128)(2,1)S(1)}, u32[]{:S(2)}, u32[]{:S(2)}) collective-permute-start(bf16[128,1024]{1,0:T(8,128)(2,1)S(1)} %collective-permute-done.7.rest_8_), channel_id=1, source_target_pairs={{0,1},{1,0},{2,3},{3,2},{4,5},{5,4},{6,7},{7,6},{8,9},{9,8},{10,11... | collective-permute-start | bytes 786440 | tf_op jit(solution)/shard_map/ppermute | solution.py:232
  55.0 14.9 %collective-permute-start.14 = (bf16[128,1024]{1,0:T(8,128)(2,1)S(1)}, bf16[128,1024]{1,0:T(8,128)(2,1)S(1)}, u32[]{:S(2)}, u32[]{:S(2)}) collective-permute-start(bf16[128,1024]{1,0:T(8,128)(2,1)S(1)} %copy-done.4), channel_id=1, source_target_pairs={{0,2},{1,3},{2,0},{3,1},{4,6},{5,7},{6,4},{7,5},{8,10},{9,11},{10,... | collective-permute-start | bytes 786440 | tf_op jit(solution)/shard_map/ppermute | solution.py:229
  55.1 14.2 %collective-permute-start.17 = (bf16[128,1024]{1,0:T(8,128)(2,1)S(1)}, bf16[128,1024]{1,0:T(8,128)(2,1)S(1)}, u32[]{:S(2)}, u32[]{:S(2)}) collective-permute-start(bf16[128,1024]{1,0:T(8,128)(2,1)S(1)} %collective-permute-done.16.rest_10_), channel_id=1, source_target_pairs={{0,2},{1,3},{2,0},{3,1},{4,6},{5,7},{6,4},{7,5},{8,10},{9,11},{10,... | collective-permute-start | bytes 786440 | tf_op jit(solution)/shard_map/ppermute | solution.py:229
  57.1 29.6 %copy-start.2 = (f32[384,1024]{1,0:T(8,128)S(1)}, f32[384,1024]{1,0:T(8,128)}, u32[]{:S(2)}) copy-start(f32[384,1024]{1,0:T(8,128)} %get-tuple-element.30.gate) | copy-start | bytes 4718596
  59.8 27.0 %copy-start = (bf16[384,1024]{1,0:T(8,128)(2,1)S(1)}, bf16[384,1024]{1,0:T(8,128)(2,1)}, u32[]{:S(2)}) copy-start(bf16[384,1024]{1,0:T(8,128)(2,1)} %feat.1) | copy-start | bytes 2359300
  59.8 27.0 %copy-start.1 = (bf16[1,1024,1024]{2,1,0:T(8,128)(2,1)S(1)}, bf16[1,1024,1024]{2,1,0:T(8,128)(2,1)}, u32[]{:S(2)}) copy-start(bf16[1,1024,1024]{2,1,0:T(8,128)(2,1)} %param.15) | copy-start | bytes 6291460
  59.8 27.0 %copy-start.3 = (bf16[384,768]{1,0:T(8,128)(2,1)S(1)}, bf16[384,768]{1,0:T(8,128)(2,1)}, u32[]{:S(2)}) copy-start(bf16[384,768]{1,0:T(8,128)(2,1)} %get-tuple-element.31.pick) | copy-start | bytes 1769476
  59.8 27.0 %copy-start.6 = (f32[1,1024]{1,0:T(1,128)S(1)}, f32[1,1024]{1,0:T(1,128)}, u32[]{:S(2)}) copy-start(f32[1,1024]{1,0:T(1,128)} %gain.1) | copy-start | bytes 12292
  59.8 9.5 %collective-permute-start.10 = (bf16[192,512]{1,0:T(8,128)(2,1)S(1)}, bf16[192,512]{1,0:T(8,128)(2,1)S(1)}, u32[]{:S(2)}, u32[]{:S(2)}) collective-permute-start(bf16[192,512]{1,0:T(8,128)(2,1)S(1)} %get-tuple-element.39), channel_id=1, source_target_pairs={{0,8},{8,0},{16,24},{24,16},{1,9},{9,1},{17,25},{25,17},{2,10},{10... | collective-permute-start | bytes 589832 | tf_op jit(solution)/shard_map/ppermute | solution.py:235
  60.4 9.4 %collective-permute-start.11 = (bf16[192,512]{1,0:T(8,128)(2,1)S(1)}, bf16[192,512]{1,0:T(8,128)(2,1)S(1)}, u32[]{:S(2)}, u32[]{:S(2)}) collective-permute-start(bf16[192,512]{1,0:T(8,128)(2,1)S(1)} %get-tuple-element.40), channel_id=1, source_target_pairs={{0,16},{8,24},{16,0},{24,8},{1,17},{9,25},{17,1},{25,9},{2,18},{10... | collective-permute-start | bytes 589832 | tf_op jit(solution)/shard_map/ppermute | solution.py:235
  61.9 9.5 %collective-permute-start.19 = (bf16[128,1024]{1,0:T(8,128)(2,1)S(1)}, bf16[128,1024]{1,0:T(8,128)(2,1)S(1)}, u32[]{:S(2)}, u32[]{:S(2)}) collective-permute-start(bf16[128,1024]{1,0:T(8,128)(2,1)S(1)} %collective-permute-done.16.rest_10_), channel_id=1, source_target_pairs={{0,1},{1,0},{2,3},{3,2},{4,5},{5,4},{6,7},{7,6},{8,9},{9,8},{10,11... | collective-permute-start | bytes 786440 | tf_op jit(solution)/shard_map/ppermute | solution.py:232
  69.3 2.1 %collective-permute-start.18 = (bf16[128,1024]{1,0:T(8,128)(2,1)S(1)}, bf16[128,1024]{1,0:T(8,128)(2,1)S(1)}, u32[]{:S(2)}, u32[]{:S(2)}) collective-permute-start(bf16[128,1024]{1,0:T(8,128)(2,1)S(1)} %collective-permute-done.17.rest_8_), channel_id=1, source_target_pairs={{0,1},{1,0},{2,3},{3,2},{4,5},{5,4},{6,7},{7,6},{8,9},{9,8},{10,11... | collective-permute-start | bytes 786440 | tf_op jit(solution)/shard_map/ppermute | solution.py:232
  69.3 2.1 %collective-permute-start.13 = (bf16[128,1024]{1,0:T(8,128)(2,1)S(1)}, bf16[128,1024]{1,0:T(8,128)(2,1)S(1)}, u32[]{:S(2)}, u32[]{:S(2)}) collective-permute-start(bf16[128,1024]{1,0:T(8,128)(2,1)S(1)} %copy-done.4), channel_id=1, source_target_pairs={{0,1},{1,0},{2,3},{3,2},{4,5},{5,4},{6,7},{7,6},{8,9},{9,8},{10,11... | collective-permute-start | bytes 786440 | tf_op jit(solution)/shard_map/ppermute | solution.py:232
  69.9 1.8 %collective-permute-start.15 = (bf16[128,1024]{1,0:T(8,128)(2,1)S(1)}, bf16[128,1024]{1,0:T(8,128)(2,1)S(1)}, u32[]{:S(2)}, u32[]{:S(2)}) collective-permute-start(bf16[128,1024]{1,0:T(8,128)(2,1)S(1)} %collective-permute-done.14.rest_6_), channel_id=1, source_target_pairs={{0,1},{1,0},{2,3},{3,2},{4,5},{5,4},{6,7},{7,6},{8,9},{9,8},{10,11... | collective-permute-start | bytes 786440 | tf_op jit(solution)/shard_map/ppermute | solution.py:232
  69.9 8.2 %collective-permute-start.12 = (bf16[192,512]{1,0:T(8,128)(2,1)S(1)}, bf16[192,512]{1,0:T(8,128)(2,1)S(1)}, u32[]{:S(2)}, u32[]{:S(2)}) collective-permute-start(bf16[192,512]{1,0:T(8,128)(2,1)S(1)} %get-tuple-element.41), channel_id=1, source_target_pairs={{0,24},{8,16},{16,8},{24,0},{1,25},{9,17},{17,9},{25,1},{2,26},{10... | collective-permute-start | bytes 589832 | tf_op jit(solution)/shard_map/ppermute | solution.py:235
  74.4 8.4 %collective-permute-start.20 = (bf16[192,512]{1,0:T(8,128)(2,1)S(1)}, bf16[192,512]{1,0:T(8,128)(2,1)S(1)}, u32[]{:S(2)}, u32[]{:S(2)}) collective-permute-start(bf16[192,512]{1,0:T(8,128)(2,1)S(1)} %get-tuple-element.46), channel_id=1, source_target_pairs={{0,8},{8,0},{16,24},{24,16},{1,9},{9,1},{17,25},{25,17},{2,10},{10... | collective-permute-start | bytes 589832 | tf_op jit(solution)/shard_map/ppermute | solution.py:235
  75.8 10.9 %collective-permute-start.21 = (bf16[192,512]{1,0:T(8,128)(2,1)S(1)}, bf16[192,512]{1,0:T(8,128)(2,1)S(1)}, u32[]{:S(2)}, u32[]{:S(2)}) collective-permute-start(bf16[192,512]{1,0:T(8,128)(2,1)S(1)} %get-tuple-element.47), channel_id=1, source_target_pairs={{0,16},{8,24},{16,0},{24,8},{1,17},{9,25},{17,1},{25,9},{2,18},{10... | collective-permute-start | bytes 589832 | tf_op jit(solution)/shard_map/ppermute | solution.py:235
  76.5 10.2 %collective-permute-start.22 = (bf16[192,512]{1,0:T(8,128)(2,1)S(1)}, bf16[192,512]{1,0:T(8,128)(2,1)S(1)}, u32[]{:S(2)}, u32[]{:S(2)}) collective-permute-start(bf16[192,512]{1,0:T(8,128)(2,1)S(1)} %get-tuple-element.48), channel_id=1, source_target_pairs={{0,24},{8,16},{16,8},{24,0},{1,25},{9,17},{17,9},{25,1},{2,26},{10... | collective-permute-start | bytes 589832 | tf_op jit(solution)/shard_map/ppermute | solution.py:235

commit v5 on v4

v5 whole, which is shorter than its diff:
```python
import functools

import jax
import jax.numpy as jnp
from jax import lax
from jax.experimental import pallas as pl
from jax.experimental.pallas import tpu as pltpu
from jax.sharding import PartitionSpec as P

BLK = 128
HEAD = 128
OPTS = {'chunks': [4, 4], 'order': 0, 'cq': 400000000000, 'cg': 400000000000, 'ca': 0, 'cf': 0, 'cp': 0, 'cs': 0, 'a': [], 'g': ['a', 'qx'], 'f0': ['g'], 'f1': ['g', 'a'], 'pk': ['f', 'g'], 'p': ['g', 'qx', 'qy', 'f'], 's0': ['p'], 's1': ['s']}
CHUNKS = OPTS['chunks']
SLICES = 2
VMEM_LIMIT = 32 * 1024 * 1024
VMEM_MOST = 60 * 1024 * 1024
HEAVY = 4 * 10**11


def silu_halved(t):
    return t + t * jnp.tanh(t)


def centred_norm(x):
    middle = jnp.mean(x, axis=-1, keepdims=True)
    shifted = x - middle
    spread = jnp.mean(shifted * shifted, axis=-1, keepdims=True)
    return shifted * lax.rsqrt(spread + 1e-05)


def slots_of(user, me, cap, users):
    rows = user.shape[1]
    rel = user ^ me
    places = max(8, users)
    one_hot = rel == lax.broadcasted_iota(jnp.int32, (places, rows), 0)
    one_hot = one_hot.astype(jnp.float32)
    first = lax.broadcasted_iota(jnp.int32, (rows, rows), 0)
    second = lax.broadcasted_iota(jnp.int32, (rows, rows), 1)
    earlier = (first < second).astype(jnp.bfloat16)
    rank = jnp.dot(one_hot.astype(jnp.bfloat16), earlier, preferred_element_type=jnp.float32)
    rank = jnp.sum(rank * one_hot, axis=0, keepdims=True)
    return rel.astype(jnp.float32) * cap + rank


def kv_split_kernel(kv, *outs):
    half = kv.shape[1] // 2
    first = 0
    for out in outs:
        wide = out.shape[1] // 2
        for part in range(2):
            out[:, part * wide:(part + 1) * wide] = kv[
                :, part * half + first:part * half + first + wide
            ]
        first += wide


def load_operands(first_col, feat_in, user_in, gain_in, w_in, feat, user, gain, weights, sems):
    slices, depth, width = weights.shape
    copies = [
        pltpu.make_async_copy(user_in, user, sems.at[0]),
        pltpu.make_async_copy(feat_in, feat, sems.at[1]),
        pltpu.make_async_copy(gain_in, gain, sems.at[2]),
    ]
    for k in range(slices):
        copies.append(
            pltpu.make_async_copy(
                w_in.at[pl.ds(k * depth, depth), pl.ds(first_col, width)],
                weights.at[k],
                sems.at[3 + k],
            )
        )
    for copy in copies:
        copy.start()
    return copies


def project(copies, feat, gain, weights):
    slices, depth, _ = weights.shape
    copies[1].wait()
    copies[2].wait()
    normed = (centred_norm(feat[...].astype(jnp.float32)) * gain[...]).astype(jnp.bfloat16)
    total = None
    for k in range(slices):
        copies[3 + k].wait()
        part = jnp.dot(
            normed[:, k * depth:(k + 1) * depth], weights[k], preferred_element_type=jnp.float32
        )
        total = part if total is None else total + part
    return silu_halved(total * 0.5)


def query_kernel(cap, users, feat_in, user_in, gain_in, w_in, *rest):
    outs, (feat, user, gain, weights, sent, sems, out_sems) = rest[:users], rest[users:]
    rows, width = feat.shape
    copies = load_operands(width, feat_in, user_in, gain_in, w_in, feat, user, gain, weights, sems)
    copies[0].wait()
    slot = slots_of(user[...], lax.axis_index("users"), cap, users)
    places = lax.broadcasted_iota(jnp.int32, (users * cap, rows), 0).astype(jnp.float32)
    pick = (places == slot).astype(jnp.bfloat16)
    query = project(copies, feat, gain, weights).astype(jnp.bfloat16)
    writes = []
    for d in range(users):
        at = slice(d * cap, (d + 1) * cap)
        sent[at, :] = jnp.dot(pick[at, :], query, preferred_element_type=jnp.float32).astype(
            jnp.bfloat16
        )
        writes.append(
            pltpu.make_async_copy(sent.at[pl.ds(d * cap, cap), :], outs[d], out_sems.at[d])
        )
        writes[-1].start()
    for write in writes:
        write.wait()


def gate_kernel(cap, users, feat_in, user_in, gain_in, w_in, gate, pick, feat, user, gain, weights, sems):
    rows, _ = feat.shape
    copies = load_operands(0, feat_in, user_in, gain_in, w_in, feat, user, gain, weights, sems)
    copies[0].wait()
    slot = slots_of(user[...], lax.axis_index("users"), cap, users)
    slot = jnp.transpose(jnp.broadcast_to(slot, (128, rows)))[:, 0:1]
    places = lax.broadcasted_iota(jnp.int32, (rows, users * cap), 1).astype(jnp.float32)
    pick[...] = (places == slot).astype(jnp.bfloat16)
    gate[...] = project(copies, feat, gain, weights)


def early_chips(chips):
    return [d for d in range(chips) if d != 2]


def pack_kernel(chips, mask, *rest):
    blocks, out = rest[:-1], rest[-1]
    place = lax.axis_index("ctx")
    core, z = place % 2, place // 2
    taken = jnp.int32(0)
    for d, block in zip(early_chips(chips), blocks):
        live = mask[0, 2 * (z ^ d) + core] > 0

        def take(block=block, taken=taken):
            at = pl.multiple_of(taken * BLK, BLK)
            out[pl.ds(at, BLK), :] = block[...]

        pl.when(live)(take)
        taken = taken + live.astype(jnp.int32)


def attend_kernel(users, chips, first, mask, *rest):
    queries, packs, lasts = rest[:users], rest[users:users + 2], rest[users + 2:users + 4]
    outs, (all_q, live_kv) = rest[users + 4:2 * users + 4], rest[2 * users + 4:]
    cap, wide = outs[0].shape
    width = packs[0].shape[1] // 2
    place = lax.axis_index("ctx")
    core, z = place % 2, place // 2
    taken = jnp.int32(0)

    def take(live, block, parts, taken):
        def copy():
            at = pl.multiple_of(jnp.minimum(taken, chips - 1) * BLK, BLK)
            for part, cols in enumerate(parts):
                live_kv[pl.ds(at, BLK), part * wide:(part + 1) * wide] = block[:, cols]

        pl.when(live)(copy)
        return taken + live.astype(jnp.int32)

    for swap, pack in enumerate(packs):
        count = jnp.int32(0)
        for d in early_chips(chips):
            count = count + (mask[0, 2 * (z ^ d) + (core ^ swap)] > 0).astype(jnp.int32)
        parts = [slice(part * width + first, part * width + first + wide) for part in range(2)]
        for slot in range(chips - 1):
            taken = take(slot < count, pack.at[slot * BLK:(slot + 1) * BLK, :], parts, taken)
    for swap, last in enumerate(lasts):
        live = mask[0, 2 * (z ^ 2) + (core ^ swap)] > 0
        parts = [slice(part * wide, (part + 1) * wide) for part in range(2)]
        taken = take(live, last, parts, taken)
    for i, q in enumerate(queries):
        all_q[i * cap:(i + 1) * cap, :] = q[:, first:first + wide]
    scale = 0.5 * HEAD ** (-0.5)
    for head in range(wide // HEAD):
        cols = slice(head * HEAD, (head + 1) * HEAD)
        keys = live_kv[:, cols]
        values = live_kv[:, wide + head * HEAD:wide + (head + 1) * HEAD]
        scores = lax.dot_general(
            all_q[:, cols], keys, (((1,), (1,)), ((), ())), preferred_element_type=jnp.float32
        )
        weight = silu_halved(scores * scale).astype(jnp.bfloat16)
        got = jnp.dot(weight, values, preferred_element_type=jnp.float32).astype(jnp.bfloat16)
        for i, out in enumerate(outs):
            out[:, cols] = got[i * cap:(i + 1) * cap, :]


def finish_kernel(users, feat, gate, pick, gain, w_out, *rest):
    parts, out, back = rest[:-2], rest[-2], rest[-1]
    first = 0
    for chunk in range(len(parts) // users):
        cap, wide = parts[chunk * users].shape
        for d in range(users):
            part = parts[chunk * users + d]
            back[d * cap:(d + 1) * cap, first:first + wide] = part[...]
        first += wide
    attended = jnp.dot(pick[...], back[...], preferred_element_type=jnp.float32)
    mixed = (centred_norm(attended) * gain[...] * gate[...]).astype(jnp.bfloat16)
    grown = jnp.dot(mixed, w_out[...], preferred_element_type=jnp.float32)
    out[...] = (feat[...].astype(jnp.float32) + grown).astype(jnp.bfloat16)


SMEM = pl.BlockSpec(memory_space=pltpu.SMEM)
HBM = pl.BlockSpec(memory_space=pltpu.HBM)


def whole(*dims, at=None):
    return pl.BlockSpec(dims, lambda i: at or (0,) * len(dims))


def call(kernel, name, in_specs, out_shape, scratch, flops, *args, vmem=VMEM_LIMIT):
    moved = sum(a.size * a.dtype.itemsize for a in args)
    return pl.pallas_call(
        kernel,
        name=name,
        grid=(1,),
        in_specs=in_specs,
        out_specs=[whole(*s.shape) for s in out_shape],
        out_shape=out_shape,
        scratch_shapes=scratch,
        cost_estimate=pl.CostEstimate(flops=flops, bytes_accessed=moved if flops else 0, transcendentals=0),
        compiler_params=pltpu.CompilerParams(vmem_limit_bytes=vmem),
    )(*args)


def on_device(cand_feat, cand_user, hist_kv, hist_mask, gain_in, w_uq, gain_attn, w_out):
    users = lax.axis_size("users")
    ctx = lax.axis_size("ctx")
    chips = ctx // 2
    rows, width = cand_feat.shape
    cap = 2 * rows // users
    wides = [heads * HEAD for heads in CHUNKS]
    bf16 = jnp.bfloat16
    user_row = cand_user.reshape(1, rows)

    def shape(*dims, dtype=bf16):
        return jax.ShapeDtypeStruct(dims, dtype)

    def over_z(value, d):
        return lax.ppermute(value, "ctx", [(c, c ^ (2 * d)) for c in range(ctx)])

    def over_cores(value):
        return lax.ppermute(value, "ctx", [(c, c ^ 1) for c in range(ctx)])

    def to_user(value, d):
        return lax.ppermute(value, "users", [(u, u ^ d) for u in range(users)])

    def after(value, *others):
        return lax.optimization_barrier((value, *others))[0]

    def over_users(values):
        if OPTS['order'] == 0:
            got = [to_user(values[d], d) for d in range(users - 1, 0, -1)]
            return [values[0]] + got[::-1]
        return [values[0]] + [to_user(values[d], d) for d in range(1, users)]

    kv = hist_kv[0, 0]
    operands = [
        pltpu.VMEM((rows, width), bf16),
        pltpu.VMEM((1, rows), jnp.int32),
        pltpu.VMEM((1, width), jnp.float32),
        pltpu.VMEM((SLICES, width // SLICES, width), bf16),
    ]
    queries = pl.pallas_call(
        functools.partial(query_kernel, cap, users),
        name="query",
        in_specs=[HBM] * 4,
        out_specs=[HBM] * users,
        out_shape=[shape(cap, width)] * users,
        scratch_shapes=operands + [
            pltpu.VMEM((users * cap, width), bf16),
            pltpu.SemaphoreType.DMA((3 + SLICES,)),
            pltpu.SemaphoreType.DMA((users,)),
        ],
        cost_estimate=pl.CostEstimate(flops=OPTS['cq'], bytes_accessed=0, transcendentals=0),
        compiler_params=pltpu.CompilerParams(vmem_limit_bytes=VMEM_MOST),
    )(cand_feat, user_row, gain_in, w_uq[0])
    arrived = over_users(queries)

    env = {'q': queries[0], 'qx': arrived[1], 'qy': arrived[2], 'qd': arrived[3]}

    def gated(value, keys):
        ready = [env[k] for k in keys]
        return after(value, *ready) if ready else value

    held = {0: kv}
    for d in [3, 1] + list(range(4, chips)):
        held[d] = over_z(gated(kv, OPTS['a']) if d == 1 else kv, d)
    env.update(m=held[3], a=held[1])
    gate, pick = call(
        functools.partial(gate_kernel, cap, users), "gate",
        [HBM] * 4,
        [shape(rows, width, dtype=jnp.float32), shape(rows, users * cap)],
        operands + [pltpu.SemaphoreType.DMA((3 + SLICES,))],
        OPTS['cg'],
        gated(cand_feat, ['q'] + OPTS['g']), user_row, gain_in, w_uq[0], vmem=VMEM_MOST,
    )
    env['g'] = gate
    split = call(
        kv_split_kernel, "kv_split", [whole(*kv.shape)],
        [shape(BLK, 2 * wide) for wide in wides], [], OPTS['cs'], held[3],
    )
    env['f'] = split[0]
    last = [over_z(gated(part, OPTS['f' + str(i)]), 1) for i, part in enumerate(split)]
    packed, = call(
        functools.partial(pack_kernel, chips), "pack",
        [SMEM] + [whole(*kv.shape)] * (chips - 1),
        [shape((chips - 1) * BLK, 2 * width)], [], OPTS['cp'],
        hist_mask, gated(kv, OPTS['pk']), *[held[d] for d in early_chips(chips)[1:]],
    )
    packs = [packed, over_cores(gated(packed, OPTS['p']))]
    env['p'] = packs[1]
    returned, first = [], 0
    for chunk, wide in enumerate(wides):
        blocks = [*packs, last[chunk], over_cores(gated(last[chunk], OPTS['s' + str(chunk)]))]
        scored = call(
            functools.partial(attend_kernel, users, chips, first), "attend",
            [SMEM] + [whole(cap, width)] * users + [whole(*block.shape) for block in blocks],
            [shape(cap, wide)] * users,
            [pltpu.VMEM((users * cap, wide), bf16), pltpu.VMEM((chips * BLK, 2 * wide), bf16)],
            OPTS['ca'],
            hist_mask, *arrived, *blocks,
        )
        back = over_users(scored)
        env.update({'s': scored[0], 'rx': back[1], 'ry': back[2], 'rd': back[3]})
        returned += back
        first += wide

    return call(
        functools.partial(finish_kernel, users), "finish",
        [
            whole(rows, width), whole(rows, width), whole(rows, users * cap), whole(1, width),
            whole(width, width),
        ]
        + [whole(*part.shape) for part in returned],
        [shape(rows, width)],
        [pltpu.VMEM((users * cap, width), bf16)],
        OPTS["cf"],
        cand_feat, gate, pick, gain_attn, w_out[0], *returned,
    )[0]


def solution(mesh):
    in_specs = (
        P(("users", "ctx"), None),
        P(("users", "ctx"), None),
        P(None, "users", "ctx", None),
        P("users", None),
        P(),
        P(),
        P(),
        P(),
    )
    out_specs = P(("users", "ctx"), None)
    return jax.shard_map(
        on_device, mesh=mesh, in_specs=in_specs, out_specs=out_specs, check_vma=False
    )
```

time: 89.8 us -> 77.9 us (0.87)
  Pallas kernels: 37.3 us -> 20.4 us
  waiting for transfers between devices: 25.5 us -> 30.8 us
  starting transfers between devices: 26.6 us -> 25.5 us
    pallas_call x1 -> x0, Pallas kernels: 17 us -> none  [on_device(): pl.pallas_call(kv_split_kernel, name='kv_split', in_specs=[HBM], out_spec...]
    ppermute x9, waiting for transfers between devices: 8.77 us -> 19.4 us  [to_user(): return lax.ppermute(value, 'users', [(u, u ^ d) for u in range(users)])]
    ppermute x6 -> x4, waiting for transfers between devices: 16.6 us -> 11.3 us  [over_z(): return lax.ppermute(value, 'ctx', [(c, c ^ 2 * d) for c in range(ctx)])]
    pallas_call x4 -> x6, Pallas kernels: 13.5 us -> 15.8 us  [call(): pl.pallas_call(kernel, name=name, grid=(1,), in_specs=in_specs, out_specs...]
    pallas_call x1, Pallas kernels: 6.81 us -> 4.6 us  [on_device(): pl.pallas_call(functools.partial(query_kernel, cap, users), name='query',...]
    ppermute x6 -> x4, starting transfers between devices: 12.2 us -> 13.8 us  [over_z(): return lax.ppermute(value, 'ctx', [(c, c ^ 2 * d) for c in range(ctx)])]
    ppermute x9, starting transfers between devices: 13.2 us -> 11.7 us  [to_user(): return lax.ppermute(value, 'users', [(u, u ^ d) for u in range(users)])]
    ppermute x8 -> x3, starting transfers between devices: 1.24 us -> 0.08 us  [over_cores(): return lax.ppermute(value, 'ctx', [(c, c ^ 1) for c in range(ctx)])]
  transfers between devices with their start and end apart: 23 -> 16, of which waited for: 7 -> 10; matrix products, arithmetic and copies ran while one was open for 0% -> 0% of each run, Pallas kernels for 31% -> 22%
where the time goes in v5:
time: 77.9 us; the launch traced here: 77.6 us
  waiting for transfers between devices  30.8 us (40%)
  starting transfers between devices  25.5 us (33%)
  Pallas kernels  20.4 us (26%)
  local copies, waits for them, and re-layouts  0.81 us (1%)
    ppermute x9, waiting for transfers between devices, to_user(): return lax.ppermute(value, 'users', [(u, u ^ d) for u in range(users)])  19.4 us
    pallas_call x6, Pallas kernels, call(): pl.pallas_call(kernel, name=name, grid=(1,), in_specs=in_specs, out_specs...  15.8 us
    ppermute x4, starting transfers between devices, over_z(): return lax.ppermute(value, 'ctx', [(c, c ^ 2 * d) for c in range(ctx)])  13.8 us
    ppermute x9, starting transfers between devices, to_user(): return lax.ppermute(value, 'users', [(u, u ^ d) for u in range(users)])  11.7 us
    ppermute x4, waiting for transfers between devices, over_z(): return lax.ppermute(value, 'ctx', [(c, c ^ 2 * d) for c in range(ctx)])  11.3 us
    pallas_call x1, Pallas kernels, on_device(): pl.pallas_call(functools.partial(query_kernel, cap, users), name='query',...  4.6 us
  transfers between devices with their start and end apart: 16, of which 10 were waited for; matrix products, arithmetic and copies ran while one was open for 0% of the time, Pallas kernels for 22%

profile of v5, /device:TPU:0, one launch (start us, length us, event | category | flops | bytes accessed | tf_op | source)
XLA Modules:
  0.0 77.6 jit_solution(13647396874831769635)
XLA Ops:
  0.0 3.0 %collective-permute-start = (bf16[128,2048]{1,0:T(8,128)(2,1)}, bf16[128,2048]{1,0:T(8,128)(2,1)}, u32[]{:S(2)}, u32[]{:S(2)}) collective-permute-start(bf16[128,2048]{1,0:T(8,128)(2,1)} %bitcast.2.rest_0_), channel_id=1, source_target_pairs={{0,2},{1,3},{2,0},{3,1},{4,6},{5,7},{6,4},{7,5},{8,10},{9,11},{10,... | collective-permute-start | bytes 1572872 | tf_op jit(solution)/shard_map/ppermute | solution.py:243
  3.0 4.6 %query.1 = (bf16[192,1024]{1,0:T(8,128)(2,1)}, bf16[192,1024]{1,0:T(8,128)(2,1)}, bf16[192,1024]{1,0:T(8,128)(2,1)}, bf16[192,1024]{1,0:T(8,128)(2,1)}) custom-call(bf16[384,1024]{1,0:T(8,128)(2,1)} %feat.1, s32[1,384]{1,0:T(1,128)} %bitcast.7, f32[1,1024]{1,0:T(1,128)} %gain_in.3, bf16[1024,2048]{1,0:T(8,128)(2,1)} %bitcast.5), custom_call_target="tpu_custom_call" | custom-call | flops 399999991808 | tf_op jit(solution)/shard_map/query/pallas_call | solution.py:267
  7.6 1.6 %collective-permute-start.1 = (bf16[192,1024]{1,0:T(8,128)(2,1)}, bf16[192,1024]{1,0:T(8,128)(2,1)S(1)}, u32[]{:S(2)}, u32[]{:S(2)}) collective-permute-start(bf16[192,1024]{1,0:T(8,128)(2,1)} %get-tuple-element.29), channel_id=1, source_target_pairs={{0,8},{8,0},{16,24},{24,16},{1,9},{9,1},{17,25},{25,17},{2,10},{10... | collective-permute-start | bytes 1179656 | tf_op jit(solution)/shard_map/ppermute | solution.py:249
  9.2 2.5 %collective-permute-start.4 = (bf16[128,2048]{1,0:T(8,128)(2,1)}, bf16[128,2048]{1,0:T(8,128)(2,1)}, u32[]{:S(2)}, u32[]{:S(2)}) collective-permute-start(bf16[128,2048]{1,0:T(8,128)(2,1)} %bitcast.2.rest_0_), channel_id=1, source_target_pairs={{0,6},{1,7},{2,4},{3,5},{4,2},{5,3},{6,0},{7,1},{8,14},{9,15},{10,... | collective-permute-start | bytes 1572872 | tf_op jit(solution)/shard_map/ppermute | solution.py:243
  11.7 1.5 %collective-permute-start.2 = (bf16[192,1024]{1,0:T(8,128)(2,1)}, bf16[192,1024]{1,0:T(8,128)(2,1)}, u32[]{:S(2)}, u32[]{:S(2)}) collective-permute-start(bf16[192,1024]{1,0:T(8,128)(2,1)} %get-tuple-element.33), channel_id=1, source_target_pairs={{0,16},{8,24},{16,0},{24,8},{1,17},{9,25},{17,1},{25,9},{2,18},{10... | collective-permute-start | bytes 1179656 | tf_op jit(solution)/shard_map/ppermute | solution.py:249
  13.2 5.3 %collective-permute-done.1.rest_1_ = bf16[192,1024]{1,0:T(8,128)(2,1)S(1)} collective-permute-done((bf16[192,1024]{1,0:T(8,128)(2,1)}, bf16[192,1024]{1,0:T(8,128)(2,1)S(1)}, u32[]{:S(2)}, u32[]{:S(2)}) %collective-permute-start.1) | collective-permute-done | bytes 393248 | tf_op jit(solution)/shard_map/ppermute | solution.py:249
  18.5 0.8 copy-done.3
  19.3 4.1 %gate.1 = (f32[384,1024]{1,0:T(8,128)}, bf16[384,768]{1,0:T(8,128)(2,1)}) custom-call(bf16[384,1024]{1,0:T(8,128)(2,1)} %feat.1, s32[1,384]{1,0:T(1,128)} %bitcast.8, f32[1,1024]{1,0:T(1,128)} %gain_in.3, bf16[1024,2048]{1,0:T(8,128)(2,1)} %bitcast.6), custom_call_target="tpu_custom_call" | custom-call | flops 399999991808 | bytes 4986368 | tf_op jit(solution)/shard_map/gate/pallas_call | solution.py:216
  23.4 5.4 %collective-permute-done.4.kv.rest_2_ = bf16[128,2048]{1,0:T(8,128)(2,1)} collective-permute-done((bf16[128,2048]{1,0:T(8,128)(2,1)}, bf16[128,2048]{1,0:T(8,128)(2,1)}, u32[]{:S(2)}, u32[]{:S(2)}) %collective-permute-start.4) | collective-permute-done | bytes 524320 | tf_op jit(solution)/shard_map/ppermute | solution.py:243
  28.8 1.1 %kv_split.1 = (bf16[128,1024]{1,0:T(8,128)(2,1)S(1)}, bf16[128,1024]{1,0:T(8,128)(2,1)S(1)}) custom-call(bf16[128,2048]{1,0:T(8,128)(2,1)} %collective-permute-done.4.kv.rest_2_), custom_call_target="tpu_custom_call" | custom-call | tf_op jit(solution)/shard_map/kv_split/pallas_call | solution.py:216
  29.9 1.5 %pack.1.rest_4_ = bf16[384,2048]{1,0:T(8,128)(2,1)S(1)} custom-call(s32[1,8]{1,0:T(1,128)S(1)} %copy-done.7, bf16[128,2048]{1,0:T(8,128)(2,1)} %bitcast.2.rest_0_, bf16[128,2048]{1,0:T(8,128)(2,1)} %collective-permute-done.rest_1_, bf16[128,2048]{1,0:T(8,128)(2,1)} %collective-permute-done.4.kv.rest_2_), custom_call_target="tpu_custom_call" | custom-call | tf_op jit(solution)/shard_map/pack/pallas_call | solution.py:216
  31.5 0.1 collective-permute-start.5
  31.6 6.6 %collective-permute-start.6 = (bf16[128,1024]{1,0:T(8,128)(2,1)S(1)}, bf16[128,1024]{1,0:T(8,128)(2,1)S(1)}, u32[]{:S(2)}, u32[]{:S(2)}) collective-permute-start(bf16[128,1024]{1,0:T(8,128)(2,1)S(1)} %get-tuple-element.38), channel_id=1, source_target_pairs={{0,2},{1,3},{2,0},{3,1},{4,6},{5,7},{6,4},{7,5},{8,10},{9,11},{10,... | collective-permute-start | bytes 786440 | tf_op jit(solution)/shard_map/ppermute | solution.py:243
  38.1 1.5 %collective-permute-start.3 = (bf16[192,1024]{1,0:T(8,128)(2,1)S(1)}, bf16[192,1024]{1,0:T(8,128)(2,1)S(1)}, u32[]{:S(2)}, u32[]{:S(2)}) collective-permute-start(bf16[192,1024]{1,0:T(8,128)(2,1)S(1)} %copy-done.9), channel_id=1, source_target_pairs={{0,24},{8,16},{16,8},{24,0},{1,25},{9,17},{17,9},{25,1},{2,26},{10... | collective-permute-start | bytes 1179656 | tf_op jit(solution)/shard_map/ppermute | solution.py:249
  39.6 5.4 %collective-permute-done.6.rest_6_ = bf16[128,1024]{1,0:T(8,128)(2,1)S(1)} collective-permute-done((bf16[128,1024]{1,0:T(8,128)(2,1)S(1)}, bf16[128,1024]{1,0:T(8,128)(2,1)S(1)}, u32[]{:S(2)}, u32[]{:S(2)}) %collective-permute-start.6) | collective-permute-done | bytes 262176 | tf_op jit(solution)/shard_map/ppermute | solution.py:243
  45.0 1.8 %collective-permute-start.11 = (bf16[128,1024]{1,0:T(8,128)(2,1)S(1)}, bf16[128,1024]{1,0:T(8,128)(2,1)S(1)}, u32[]{:S(2)}, u32[]{:S(2)}) collective-permute-start(bf16[128,1024]{1,0:T(8,128)(2,1)S(1)} %get-tuple-element.45), channel_id=1, source_target_pairs={{0,2},{1,3},{2,0},{3,1},{4,6},{5,7},{6,4},{7,5},{8,10},{9,11},{10,... | collective-permute-start | bytes 786440 | tf_op jit(solution)/shard_map/ppermute | solution.py:243
  46.8 3.4 %collective-permute-done.3.rest_3_ = bf16[192,1024]{1,0:T(8,128)(2,1)S(1)} collective-permute-done((bf16[192,1024]{1,0:T(8,128)(2,1)S(1)}, bf16[192,1024]{1,0:T(8,128)(2,1)S(1)}, u32[]{:S(2)}, u32[]{:S(2)}) %collective-permute-start.3) | collective-permute-done | bytes 393248 | tf_op jit(solution)/shard_map/ppermute | solution.py:249
  50.2 3.1 %attend.2 = (bf16[192,512]{1,0:T(8,128)(2,1)S(1)}, bf16[192,512]{1,0:T(8,128)(2,1)S(1)}, bf16[192,512]{1,0:T(8,128)(2,1)S(1)}, bf16[192,512]{1,0:T(8,128)(2,1)S(1)}) custom-call(s32[1,8]{1,0:T(1,128)S(1)} %copy-done.7, bf16[192,1024]{1,0:T(8,128)(2,1)S(1)} %copy-done.2, bf16[192,1024]{1,0:T(8,128)(2,1)S(1)} %copy-done.4, ...), custom_call_target="tpu_custom_call" | custom-call | tf_op jit(solution)/shard_map/attend/pallas_call | solution.py:216
  53.3 0.5 collective-permute-done.11.rest_6_
  53.8 0.5 collective-permute-start.8
  54.3 1.5 %collective-permute-start.9 = (bf16[192,512]{1,0:T(8,128)(2,1)S(1)}, bf16[192,512]{1,0:T(8,128)(2,1)S(1)}, u32[]{:S(2)}, u32[]{:S(2)}) collective-permute-start(bf16[192,512]{1,0:T(8,128)(2,1)S(1)} %get-tuple-element.42), channel_id=1, source_target_pairs={{0,16},{8,24},{16,0},{24,8},{1,17},{9,25},{17,1},{25,9},{2,18},{10... | collective-permute-start | bytes 589832 | tf_op jit(solution)/shard_map/ppermute | solution.py:249
  55.8 1.5 %collective-permute-start.10 = (bf16[192,512]{1,0:T(8,128)(2,1)S(1)}, bf16[192,512]{1,0:T(8,128)(2,1)S(1)}, u32[]{:S(2)}, u32[]{:S(2)}) collective-permute-start(bf16[192,512]{1,0:T(8,128)(2,1)S(1)} %get-tuple-element.43), channel_id=1, source_target_pairs={{0,24},{8,16},{16,8},{24,0},{1,25},{9,17},{17,9},{25,1},{2,26},{10... | collective-permute-start | bytes 589832 | tf_op jit(solution)/shard_map/ppermute | solution.py:249
  57.3 3.1 %attend.3 = (bf16[192,512]{1,0:T(8,128)(2,1)S(1)}, bf16[192,512]{1,0:T(8,128)(2,1)S(1)}, bf16[192,512]{1,0:T(8,128)(2,1)S(1)}, bf16[192,512]{1,0:T(8,128)(2,1)S(1)}) custom-call(s32[1,8]{1,0:T(1,128)S(1)} %copy-done.7, bf16[192,1024]{1,0:T(8,128)(2,1)S(1)} %copy-done.2, bf16[192,1024]{1,0:T(8,128)(2,1)S(1)} %copy-done.4, ...), custom_call_target="tpu_custom_call" | custom-call | tf_op jit(solution)/shard_map/attend/pallas_call | solution.py:216
  60.4 0.8 %collective-permute-start.13 = (bf16[192,512]{1,0:T(8,128)(2,1)S(1)}, bf16[192,512]{1,0:T(8,128)(2,1)S(1)}, u32[]{:S(2)}, u32[]{:S(2)}) collective-permute-start(bf16[192,512]{1,0:T(8,128)(2,1)S(1)} %get-tuple-element.48), channel_id=1, source_target_pairs={{0,8},{8,0},{16,24},{24,16},{1,9},{9,1},{17,25},{25,17},{2,10},{10... | collective-permute-start | bytes 589832 | tf_op jit(solution)/shard_map/ppermute | solution.py:249
  61.3 1.2 %collective-permute-start.14 = (bf16[192,512]{1,0:T(8,128)(2,1)S(1)}, bf16[192,512]{1,0:T(8,128)(2,1)S(1)}, u32[]{:S(2)}, u32[]{:S(2)}) collective-permute-start(bf16[192,512]{1,0:T(8,128)(2,1)S(1)} %get-tuple-element.49), channel_id=1, source_target_pairs={{0,16},{8,24},{16,0},{24,8},{1,17},{9,25},{17,1},{25,9},{2,18},{10... | collective-permute-start | bytes 589832 | tf_op jit(solution)/shard_map/ppermute | solution.py:249
  62.5 1.5 %collective-permute-start.15 = (bf16[192,512]{1,0:T(8,128)(2,1)S(1)}, bf16[192,512]{1,0:T(8,128)(2,1)S(1)}, u32[]{:S(2)}, u32[]{:S(2)}) collective-permute-start(bf16[192,512]{1,0:T(8,128)(2,1)S(1)} %get-tuple-element.50), channel_id=1, source_target_pairs={{0,24},{8,16},{16,8},{24,0},{1,25},{9,17},{17,9},{25,1},{2,26},{10... | collective-permute-start | bytes 589832 | tf_op jit(solution)/shard_map/ppermute | solution.py:249
  64.0 0.2 collective-permute-done.9.rest_2_
  64.2 2.4 %collective-permute-done.10.rest_3_ = bf16[192,512]{1,0:T(8,128)(2,1)S(1)} collective-permute-done((bf16[192,512]{1,0:T(8,128)(2,1)S(1)}, bf16[192,512]{1,0:T(8,128)(2,1)S(1)}, u32[]{:S(2)}, u32[]{:S(2)}) %collective-permute-start.10) | collective-permute-done | bytes 196640 | tf_op jit(solution)/shard_map/ppermute | solution.py:249
  66.6 3.3 %collective-permute-done.13.rest_5_ = bf16[192,512]{1,0:T(8,128)(2,1)S(1)} collective-permute-done((bf16[192,512]{1,0:T(8,128)(2,1)S(1)}, bf16[192,512]{1,0:T(8,128)(2,1)S(1)}, u32[]{:S(2)}, u32[]{:S(2)}) %collective-permute-start.13) | collective-permute-done | bytes 196640 | tf_op jit(solution)/shard_map/ppermute | solution.py:249
  69.9 0.8 %collective-permute-done.14.rest_6_ = bf16[192,512]{1,0:T(8,128)(2,1)S(1)} collective-permute-done((bf16[192,512]{1,0:T(8,128)(2,1)S(1)}, bf16[192,512]{1,0:T(8,128)(2,1)S(1)}, u32[]{:S(2)}, u32[]{:S(2)}) %collective-permute-start.14) | collective-permute-done | bytes 196640 | tf_op jit(solution)/shard_map/ppermute | solution.py:249
  70.8 3.9 %collective-permute-done.15.rest_7_ = bf16[192,512]{1,0:T(8,128)(2,1)S(1)} collective-permute-done((bf16[192,512]{1,0:T(8,128)(2,1)S(1)}, bf16[192,512]{1,0:T(8,128)(2,1)S(1)}, u32[]{:S(2)}, u32[]{:S(2)}) %collective-permute-start.15) | collective-permute-done | bytes 196640 | tf_op jit(solution)/shard_map/ppermute | solution.py:249
  74.7 2.9 %finish.1 = bf16[384,1024]{1,0:T(8,128)(2,1)} custom-call(bf16[384,1024]{1,0:T(8,128)(2,1)S(1)} %copy-done.5, f32[384,1024]{1,0:T(8,128)S(1)} %copy-done.1, bf16[384,768]{1,0:T(8,128)(2,1)S(1)} %copy-done.6, f32[1,1024]{1,0:T(1,128)S(1)} %copy-done.8, bf16[1024,1024]{1,0:T(8,128)(2,1)S(1)} %bitcast.4, bf16[192,512]{1,0:T(8,128)(2,1)S(1)} %get-tuple-element.40.rest_0_, ...), custom_call_target="tpu_custom_call" | custom-call | tf_op jit(solution)/shard_map/finish/pallas_call | solution.py:216
  (27 shorter events, 0.1 us)
Async XLA Ops:
  0.0 19.3 %collective-permute-start = (bf16[128,2048]{1,0:T(8,128)(2,1)}, bf16[128,2048]{1,0:T(8,128)(2,1)}, u32[]{:S(2)}, u32[]{:S(2)}) collective-permute-start(bf16[128,2048]{1,0:T(8,128)(2,1)} %bitcast.2.rest_0_), channel_id=1, source_target_pairs={{0,2},{1,3},{2,0},{3,1},{4,6},{5,7},{6,4},{7,5},{8,10},{9,11},{10,... | collective-permute-start | bytes 1572872 | tf_op jit(solution)/shard_map/ppermute | solution.py:243
  7.6 10.9 %collective-permute-start.1 = (bf16[192,1024]{1,0:T(8,128)(2,1)}, bf16[192,1024]{1,0:T(8,128)(2,1)S(1)}, u32[]{:S(2)}, u32[]{:S(2)}) collective-permute-start(bf16[192,1024]{1,0:T(8,128)(2,1)} %get-tuple-element.29), channel_id=1, source_target_pairs={{0,8},{8,0},{16,24},{24,16},{1,9},{9,1},{17,25},{25,17},{2,10},{10... | collective-permute-start | bytes 1179656 | tf_op jit(solution)/shard_map/ppermute | solution.py:249
  9.2 19.6 %collective-permute-start.4 = (bf16[128,2048]{1,0:T(8,128)(2,1)}, bf16[128,2048]{1,0:T(8,128)(2,1)}, u32[]{:S(2)}, u32[]{:S(2)}) collective-permute-start(bf16[128,2048]{1,0:T(8,128)(2,1)} %bitcast.2.rest_0_), channel_id=1, source_target_pairs={{0,6},{1,7},{2,4},{3,5},{4,2},{5,3},{6,0},{7,1},{8,14},{9,15},{10,... | collective-permute-start | bytes 1572872 | tf_op jit(solution)/shard_map/ppermute | solution.py:243
  11.7 19.8 %collective-permute-start.2 = (bf16[192,1024]{1,0:T(8,128)(2,1)}, bf16[192,1024]{1,0:T(8,128)(2,1)}, u32[]{:S(2)}, u32[]{:S(2)}) collective-permute-start(bf16[192,1024]{1,0:T(8,128)(2,1)} %get-tuple-element.33), channel_id=1, source_target_pairs={{0,16},{8,24},{16,0},{24,8},{1,17},{9,25},{17,1},{25,9},{2,18},{10... | collective-permute-start | bytes 1179656 | tf_op jit(solution)/shard_map/ppermute | solution.py:249
  18.5 0.8 copy-start.3
  19.3 10.6 %copy-start.7 = (s32[1,8]{1,0:T(1,128)S(1)}, s32[1,8]{1,0:T(1,128)}, u32[]{:S(2)}) copy-start(s32[1,8]{1,0:T(1,128)} %mask.5) | copy-start | bytes 100
  29.9 8.2 %copy-start.9 = (bf16[192,1024]{1,0:T(8,128)(2,1)S(1)}, bf16[192,1024]{1,0:T(8,128)(2,1)}, u32[]{:S(2)}) copy-start(bf16[192,1024]{1,0:T(8,128)(2,1)} %get-tuple-element.34) | copy-start | bytes 1179652
  29.9 20.3 %copy-start.2 = (bf16[192,1024]{1,0:T(8,128)(2,1)S(1)}, bf16[192,1024]{1,0:T(8,128)(2,1)}, u32[]{:S(2)}) copy-start(bf16[192,1024]{1,0:T(8,128)(2,1)} %get-tuple-element.28.rest_0_) | copy-start | bytes 1179652
  29.9 20.3 %copy-start.4 = (bf16[192,1024]{1,0:T(8,128)(2,1)S(1)}, bf16[192,1024]{1,0:T(8,128)(2,1)}, u32[]{:S(2)}) copy-start(bf16[192,1024]{1,0:T(8,128)(2,1)} %copy-done.3) | copy-start | bytes 1179652
  31.5 13.5 %collective-permute-start.5 = (bf16[384,2048]{1,0:T(8,128)(2,1)S(1)}, bf16[384,2048]{1,0:T(8,128)(2,1)S(1)}, u32[]{:S(2)}, u32[]{:S(2)}) collective-permute-start(bf16[384,2048]{1,0:T(8,128)(2,1)S(1)} %pack.1.rest_4_), channel_id=1, source_target_pairs={{0,1},{1,0},{2,3},{3,2},{4,5},{5,4},{6,7},{7,6},{8,9},{9,8},{10,11... | collective-permute-start | bytes 4718600 | tf_op jit(solution)/shard_map/ppermute | solution.py:246
  31.6 13.5 %collective-permute-start.6 = (bf16[128,1024]{1,0:T(8,128)(2,1)S(1)}, bf16[128,1024]{1,0:T(8,128)(2,1)S(1)}, u32[]{:S(2)}, u32[]{:S(2)}) collective-permute-start(bf16[128,1024]{1,0:T(8,128)(2,1)S(1)} %get-tuple-element.38), channel_id=1, source_target_pairs={{0,2},{1,3},{2,0},{3,1},{4,6},{5,7},{6,4},{7,5},{8,10},{9,11},{10,... | collective-permute-start | bytes 786440 | tf_op jit(solution)/shard_map/ppermute | solution.py:243
  38.1 12.1 %collective-permute-start.3 = (bf16[192,1024]{1,0:T(8,128)(2,1)S(1)}, bf16[192,1024]{1,0:T(8,128)(2,1)S(1)}, u32[]{:S(2)}, u32[]{:S(2)}) collective-permute-start(bf16[192,1024]{1,0:T(8,128)(2,1)S(1)} %copy-done.9), channel_id=1, source_target_pairs={{0,24},{8,16},{16,8},{24,0},{1,25},{9,17},{17,9},{25,1},{2,26},{10... | collective-permute-start | bytes 1179656 | tf_op jit(solution)/shard_map/ppermute | solution.py:249
  45.0 5.2 %collective-permute-start.7 = (bf16[128,1024]{1,0:T(8,128)(2,1)S(1)}, bf16[128,1024]{1,0:T(8,128)(2,1)S(1)}, u32[]{:S(2)}, u32[]{:S(2)}) collective-permute-start(bf16[128,1024]{1,0:T(8,128)(2,1)S(1)} %collective-permute-done.6.rest_6_), channel_id=1, source_target_pairs={{0,1},{1,0},{2,3},{3,2},{4,5},{5,4},{6,7},{7,6},{8,9},{9,8},{10,11... | collective-permute-start | bytes 786440 | tf_op jit(solution)/shard_map/ppermute | solution.py:246
  45.0 8.7 %collective-permute-start.11 = (bf16[128,1024]{1,0:T(8,128)(2,1)S(1)}, bf16[128,1024]{1,0:T(8,128)(2,1)S(1)}, u32[]{:S(2)}, u32[]{:S(2)}) collective-permute-start(bf16[128,1024]{1,0:T(8,128)(2,1)S(1)} %get-tuple-element.45), channel_id=1, source_target_pairs={{0,2},{1,3},{2,0},{3,1},{4,6},{5,7},{6,4},{7,5},{8,10},{9,11},{10,... | collective-permute-start | bytes 786440 | tf_op jit(solution)/shard_map/ppermute | solution.py:243
  53.8 3.6 %collective-permute-start.12 = (bf16[128,1024]{1,0:T(8,128)(2,1)S(1)}, bf16[128,1024]{1,0:T(8,128)(2,1)S(1)}, u32[]{:S(2)}, u32[]{:S(2)}) collective-permute-start(bf16[128,1024]{1,0:T(8,128)(2,1)S(1)} %collective-permute-done.11.rest_6_), channel_id=1, source_target_pairs={{0,1},{1,0},{2,3},{3,2},{4,5},{5,4},{6,7},{7,6},{8,9},{9,8},{10,11... | collective-permute-start | bytes 786440 | tf_op jit(solution)/shard_map/ppermute | solution.py:246
  53.8 8.7 %collective-permute-start.8 = (bf16[192,512]{1,0:T(8,128)(2,1)S(1)}, bf16[192,512]{1,0:T(8,128)(2,1)S(1)}, u32[]{:S(2)}, u32[]{:S(2)}) collective-permute-start(bf16[192,512]{1,0:T(8,128)(2,1)S(1)} %get-tuple-element.41), channel_id=1, source_target_pairs={{0,8},{8,0},{16,24},{24,16},{1,9},{9,1},{17,25},{25,17},{2,10},{10... | collective-permute-start | bytes 589832 | tf_op jit(solution)/shard_map/ppermute | solution.py:249
  54.3 9.9 %collective-permute-start.9 = (bf16[192,512]{1,0:T(8,128)(2,1)S(1)}, bf16[192,512]{1,0:T(8,128)(2,1)S(1)}, u32[]{:S(2)}, u32[]{:S(2)}) collective-permute-start(bf16[192,512]{1,0:T(8,128)(2,1)S(1)} %get-tuple-element.42), channel_id=1, source_target_pairs={{0,16},{8,24},{16,0},{24,8},{1,17},{9,25},{17,1},{25,9},{2,18},{10... | collective-permute-start | bytes 589832 | tf_op jit(solution)/shard_map/ppermute | solution.py:249
  55.8 18.9 %copy-start = (bf16[1,1024,1024]{2,1,0:T(8,128)(2,1)S(1)}, bf16[1,1024,1024]{2,1,0:T(8,128)(2,1)}, u32[]{:S(2)}) copy-start(bf16[1,1024,1024]{2,1,0:T(8,128)(2,1)} %param.15) | copy-start | bytes 6291460
  55.8 18.9 %copy-start.1 = (f32[384,1024]{1,0:T(8,128)S(1)}, f32[384,1024]{1,0:T(8,128)}, u32[]{:S(2)}) copy-start(f32[384,1024]{1,0:T(8,128)} %get-tuple-element.31.gate) | copy-start | bytes 4718596
  55.8 18.9 %copy-start.5 = (bf16[384,1024]{1,0:T(8,128)(2,1)S(1)}, bf16[384,1024]{1,0:T(8,128)(2,1)}, u32[]{:S(2)}) copy-start(bf16[384,1024]{1,0:T(8,128)(2,1)} %feat.1) | copy-start | bytes 2359300
  55.8 18.9 %copy-start.6 = (bf16[384,768]{1,0:T(8,128)(2,1)S(1)}, bf16[384,768]{1,0:T(8,128)(2,1)}, u32[]{:S(2)}) copy-start(bf16[384,768]{1,0:T(8,128)(2,1)} %get-tuple-element.32.pick) | copy-start | bytes 1769476
  55.8 18.9 %copy-start.8 = (f32[1,1024]{1,0:T(1,128)S(1)}, f32[1,1024]{1,0:T(1,128)}, u32[]{:S(2)}) copy-start(f32[1,1024]{1,0:T(1,128)} %gain.1) | copy-start | bytes 12292
  55.8 10.8 %collective-permute-start.10 = (bf16[192,512]{1,0:T(8,128)(2,1)S(1)}, bf16[192,512]{1,0:T(8,128)(2,1)S(1)}, u32[]{:S(2)}, u32[]{:S(2)}) collective-permute-start(bf16[192,512]{1,0:T(8,128)(2,1)S(1)} %get-tuple-element.43), channel_id=1, source_target_pairs={{0,24},{8,16},{16,8},{24,0},{1,25},{9,17},{17,9},{25,1},{2,26},{10... | collective-permute-start | bytes 589832 | tf_op jit(solution)/shard_map/ppermute | solution.py:249
  60.4 9.5 %collective-permute-start.13 = (bf16[192,512]{1,0:T(8,128)(2,1)S(1)}, bf16[192,512]{1,0:T(8,128)(2,1)S(1)}, u32[]{:S(2)}, u32[]{:S(2)}) collective-permute-start(bf16[192,512]{1,0:T(8,128)(2,1)S(1)} %get-tuple-element.48), channel_id=1, source_target_pairs={{0,8},{8,0},{16,24},{24,16},{1,9},{9,1},{17,25},{25,17},{2,10},{10... | collective-permute-start | bytes 589832 | tf_op jit(solution)/shard_map/ppermute | solution.py:249
  61.3 9.5 %collective-permute-start.14 = (bf16[192,512]{1,0:T(8,128)(2,1)S(1)}, bf16[192,512]{1,0:T(8,128)(2,1)S(1)}, u32[]{:S(2)}, u32[]{:S(2)}) collective-permute-start(bf16[192,512]{1,0:T(8,128)(2,1)S(1)} %get-tuple-element.49), channel_id=1, source_target_pairs={{0,16},{8,24},{16,0},{24,8},{1,17},{9,25},{17,1},{25,9},{2,18},{10... | collective-permute-start | bytes 589832 | tf_op jit(solution)/shard_map/ppermute | solution.py:249
  62.5 12.2 %collective-permute-start.15 = (bf16[192,512]{1,0:T(8,128)(2,1)S(1)}, bf16[192,512]{1,0:T(8,128)(2,1)S(1)}, u32[]{:S(2)}, u32[]{:S(2)}) collective-permute-start(bf16[192,512]{1,0:T(8,128)(2,1)S(1)} %get-tuple-element.50), channel_id=1, source_target_pairs={{0,24},{8,16},{16,8},{24,0},{1,25},{9,17},{17,9},{25,1},{2,26},{10... | collective-permute-start | bytes 589832 | tf_op jit(solution)/shard_map/ppermute | solution.py:249

commit v6 on v5

--- a/solution.py
+++ b/solution.py
@@ -9,7 +9,7 @@
 
 BLK = 128
 HEAD = 128
-OPTS = {'chunks': [4, 4], 'order': 0, 'cq': 400000000000, 'cg': 400000000000, 'ca': 0, 'cf': 0, 'cp': 0, 'cs': 0, 'a': [], 'g': ['a', 'qx'], 'f0': ['g'], 'f1': ['g', 'a'], 'pk': ['f', 'g'], 'p': ['g', 'qx', 'qy', 'f'], 's0': ['p'], 's1': ['s']}
+OPTS = {'chunks': [4, 4], 'order': 0, 'qs': 0, 'cq': 400000000000, 'cg': 400000000000, 'ca': 1000000000, 'cf': 10000000000, 'm1': [], 'a1': ['f'], 'g': ['a0', 'qx'], 's0': [['qx'], ['g', 'qy'], ['g'], []], 's1': [['s', 'rx'], ['ry'], [], []], 'cp': 0, 'sw': [0, 0], 'p0': [], 'p1': []}
 CHUNKS = OPTS['chunks']
 SLICES = 2
 VMEM_LIMIT = 32 * 1024 * 1024
@@ -123,16 +123,12 @@
     gate[...] = project(copies, feat, gain, weights)
 
 
-def early_chips(chips):
-    return [d for d in range(chips) if d != 2]
-
-
 def pack_kernel(chips, mask, *rest):
     blocks, out = rest[:-1], rest[-1]
     place = lax.axis_index("ctx")
     core, z = place % 2, place // 2
     taken = jnp.int32(0)
-    for d, block in zip(early_chips(chips), blocks):
+    for d, block in enumerate(blocks):
         live = mask[0, 2 * (z ^ d) + core] > 0
 
         def take(block=block, taken=taken):
@@ -144,34 +140,59 @@
 
 
 def attend_kernel(users, chips, first, mask, *rest):
-    queries, packs, lasts = rest[:users], rest[users:users + 2], rest[users + 2:users + 4]
-    outs, (all_q, live_kv) = rest[users + 4:2 * users + 4], rest[2 * users + 4:]
+    queries, (mine, other) = rest[:users], rest[users:users + 2]
+    outs, (all_q, live_kv) = rest[users + 2:2 * users + 2], rest[2 * users + 2:]
     cap, wide = outs[0].shape
-    width = packs[0].shape[1] // 2
+    core = lax.axis_index("ctx") % 2
+    count = jnp.int32(0)
+    for z in range(chips):
+        count = count + (mask[0, 2 * z + core] > 0).astype(jnp.int32)
+    for slot in range(chips):
+        at = slice(slot * BLK, (slot + 1) * BLK)
+
+        def from_mine(at=at):
+            live_kv[at, :] = mine[at, :]
+
+        def from_other(at=at, slot=slot):
+            source = pl.multiple_of(jnp.maximum(slot - count, 0) * BLK, BLK)
+            live_kv[at, :] = other[pl.ds(source, BLK), :]
+
+        pl.when(slot < count)(from_mine)
+        pl.when(slot >= count)(from_other)
+    for i, q in enumerate(queries):
+        all_q[i * cap:(i + 1) * cap, :] = q[:, first:first + wide]
+    scale = 0.5 * HEAD ** (-0.5)
+    for head in range(wide // HEAD):
+        cols = slice(head * HEAD, (head + 1) * HEAD)
+        keys = live_kv[:, cols]
+        values = live_kv[:, wide + head * HEAD:wide + (head + 1) * HEAD]
+        scores = lax.dot_general(
+            all_q[:, cols], keys, (((1,), (1,)), ((), ())), preferred_element_type=jnp.float32
+        )
+        weight = silu_halved(scores * scale).astype(jnp.bfloat16)
+        got = jnp.dot(weight, values, preferred_element_type=jnp.float32).astype(jnp.bfloat16)
+        for i, out in enumerate(outs):
+            out[:, cols] = got[i * cap:(i + 1) * cap, :]
+
+
+def attend_blocks_kernel(users, chips, first, mask, *rest):
+    queries = rest[:users]
+    blocks = rest[users:users + 2 * chips]
+    outs, (all_q, live_kv) = rest[-2 - users:-2], rest[-2:]
     place = lax.axis_index("ctx")
     core, z = place % 2, place // 2
+    cap, wide = outs[0].shape
     taken = jnp.int32(0)
-
-    def take(live, block, parts, taken):
-        def copy():
-            at = pl.multiple_of(jnp.minimum(taken, chips - 1) * BLK, BLK)
-            for part, cols in enumerate(parts):
-                live_kv[pl.ds(at, BLK), part * wide:(part + 1) * wide] = block[:, cols]
-
-        pl.when(live)(copy)
-        return taken + live.astype(jnp.int32)
-
-    for swap, pack in enumerate(packs):
-        count = jnp.int32(0)
-        for d in early_chips(chips):
-            count = count + (mask[0, 2 * (z ^ d) + (core ^ swap)] > 0).astype(jnp.int32)
-        parts = [slice(part * width + first, part * width + first + wide) for part in range(2)]
-        for slot in range(chips - 1):
-            taken = take(slot < count, pack.at[slot * BLK:(slot + 1) * BLK, :], parts, taken)
-    for swap, last in enumerate(lasts):
-        live = mask[0, 2 * (z ^ 2) + (core ^ swap)] > 0
-        parts = [slice(part * wide, (part + 1) * wide) for part in range(2)]
-        taken = take(live, last, parts, taken)
+    for d in range(chips):
+        for swap in range(2):
+            live = mask[0, 2 * (z ^ d) + (core ^ swap)] > 0
+
+            def take(block=blocks[2 * d + swap], taken=taken):
+                at = pl.multiple_of(taken * BLK, BLK)
+                live_kv[pl.ds(at, BLK), :] = block[...]
+
+            pl.when(live)(take)
+            taken = jnp.minimum(taken + live.astype(jnp.int32), chips - 1)
     for i, q in enumerate(queries):
         all_q[i * cap:(i + 1) * cap, :] = q[:, first:first + wide]
     scale = 0.5 * HEAD ** (-0.5)
@@ -258,6 +279,11 @@
         return [values[0]] + [to_user(values[d], d) for d in range(1, users)]
 
     kv = hist_kv[0, 0]
+    split = call(
+        kv_split_kernel, "kv_split", [whole(*kv.shape)],
+        [shape(BLK, 2 * wide) for wide in wides], [], 0, kv,
+    )
+
     operands = [
         pltpu.VMEM((rows, width), bf16),
         pltpu.VMEM((1, rows), jnp.int32),
@@ -277,47 +303,52 @@
         ],
         cost_estimate=pl.CostEstimate(flops=OPTS['cq'], bytes_accessed=0, transcendentals=0),
         compiler_params=pltpu.CompilerParams(vmem_limit_bytes=VMEM_MOST),
-    )(cand_feat, user_row, gain_in, w_uq[0])
+    )(*([after(cand_feat, split[0])] if OPTS['qs'] else [cand_feat]), user_row, gain_in, w_uq[0])
     arrived = over_users(queries)
 
-    env = {'q': queries[0], 'qx': arrived[1], 'qy': arrived[2], 'qd': arrived[3]}
+    returned, first, env = [], 0, {}
+    env.update({'qx': arrived[1], 'qy': arrived[2], 'qd': arrived[3], 'q': queries[0]})
 
     def gated(value, keys):
         ready = [env[k] for k in keys]
         return after(value, *ready) if ready else value
 
-    held = {0: kv}
-    for d in [3, 1] + list(range(4, chips)):
-        held[d] = over_z(gated(kv, OPTS['a']) if d == 1 else kv, d)
-    env.update(m=held[3], a=held[1])
-    gate, pick = call(
-        functools.partial(gate_kernel, cap, users), "gate",
-        [HBM] * 4,
-        [shape(rows, width, dtype=jnp.float32), shape(rows, users * cap)],
-        operands + [pltpu.SemaphoreType.DMA((3 + SLICES,))],
-        OPTS['cg'],
-        gated(cand_feat, ['q'] + OPTS['g']), user_row, gain_in, w_uq[0], vmem=VMEM_MOST,
-    )
-    env['g'] = gate
-    split = call(
-        kv_split_kernel, "kv_split", [whole(*kv.shape)],
-        [shape(BLK, 2 * wide) for wide in wides], [], OPTS['cs'], held[3],
-    )
-    env['f'] = split[0]
-    last = [over_z(gated(part, OPTS['f' + str(i)]), 1) for i, part in enumerate(split)]
-    packed, = call(
-        functools.partial(pack_kernel, chips), "pack",
-        [SMEM] + [whole(*kv.shape)] * (chips - 1),
-        [shape((chips - 1) * BLK, 2 * width)], [], OPTS['cp'],
-        hist_mask, gated(kv, OPTS['pk']), *[held[d] for d in early_chips(chips)[1:]],
-    )
-    packs = [packed, over_cores(gated(packed, OPTS['p']))]
-    env['p'] = packs[1]
-    returned, first = [], 0
     for chunk, wide in enumerate(wides):
-        blocks = [*packs, last[chunk], over_cores(gated(last[chunk], OPTS['s' + str(chunk)]))]
+        held = {0: split[chunk]}
+        far = near = split[chunk]
+        if chunk:
+            c = str(chunk - 1)
+            far = gated(far, [k + c if k in 'maf' else k for k in OPTS['m1']])
+            near = gated(near, [k + c if k in 'maf' else k for k in OPTS['a1']])
+        for d in [3, 1, 2] + list(range(4, chips)):
+            held[d] = over_z(held[3], 1) if d == 2 else over_z(near if d == 1 else far, d)
+        env.update({'a' + str(chunk): held[1], 'm' + str(chunk): held[3], 'f' + str(chunk): held[2]})
+        if chunk == 0:
+            gate, pick = call(
+                functools.partial(gate_kernel, cap, users), "gate",
+                [HBM] * 4,
+                [shape(rows, width, dtype=jnp.float32), shape(rows, users * cap)],
+                operands + [pltpu.SemaphoreType.DMA((3 + SLICES,))],
+                OPTS['cg'],
+                gated(cand_feat, ['q'] + OPTS['g']), user_row, gain_in, w_uq[0], vmem=VMEM_MOST,
+            )
+            env['g'] = gate
+        if OPTS['sw'][chunk]:
+            keys = OPTS['p0'] if chunk == 0 else OPTS['p1']
+            packed, = call(
+                functools.partial(pack_kernel, chips), "pack",
+                [SMEM] + [whole(BLK, 2 * wide)] * chips,
+                [shape(chips * BLK, 2 * wide)], [], OPTS['cp'],
+                hist_mask, gated(held[0], keys), *[held[d] for d in range(1, chips)],
+            )
+            blocks, kernel = [packed, over_cores(packed)], attend_kernel
+        else:
+            blocks, kernel = [], attend_blocks_kernel
+            for d in range(chips):
+                keys = OPTS['s0' if chunk == 0 else 's1'][d % 4]
+                blocks += [held[d], over_cores(gated(held[d], keys))]
         scored = call(
-            functools.partial(attend_kernel, users, chips, first), "attend",
+            functools.partial(kernel, users, chips, first), "attend",
             [SMEM] + [whole(cap, width)] * users + [whole(*block.shape) for block in blocks],
             [shape(cap, wide)] * users,
             [pltpu.VMEM((users * cap, wide), bf16), pltpu.VMEM((chips * BLK, 2 * wide), bf16)],

time: 77.9 us -> 71.2 us (0.914)
  waiting for transfers between devices: 30.8 us -> 19.8 us
  starting transfers between devices: 25.5 us -> 30.8 us
  Pallas kernels: 20.4 us -> 19.4 us
    ppermute x9, waiting for transfers between devices: 19.4 us -> 12 us  [to_user(): return lax.ppermute(value, 'users', [(u, u ^ d) for u in range(users)])]
    ppermute x4 -> x6, starting transfers between devices: 13.8 us -> 17.6 us  [over_z(): return lax.ppermute(value, 'ctx', [(c, c ^ 2 * d) for c in range(ctx)])]
    ppermute x4 -> x6, waiting for transfers between devices: 11.3 us -> 7.8 us  [over_z(): return lax.ppermute(value, 'ctx', [(c, c ^ 2 * d) for c in range(ctx)])]
    pallas_call x6 -> x5, Pallas kernels: 15.8 us -> 14.7 us  [call(): pl.pallas_call(kernel, name=name, grid=(1,), in_specs=in_specs, out_specs...]
    ppermute x3 -> x8, starting transfers between devices: 0.08 us -> 1.08 us  [over_cores(): return lax.ppermute(value, 'ctx', [(c, c ^ 1) for c in range(ctx)])]
  transfers between devices with their start and end apart: 16 -> 23, of which waited for: 10 -> 7; matrix products, arithmetic and copies ran while one was open for 0% -> 0% of each run, Pallas kernels for 22% -> 17%
where the time goes in v6:
time: 71.2 us; the launch traced here: 71 us
  starting transfers between devices  30.8 us (43%)
  waiting for transfers between devices  19.8 us (28%)
  Pallas kernels  19.4 us (27%)
  local copies, waits for them, and re-layouts  0.8 us (1%)
    ppermute x6, starting transfers between devices, over_z(): return lax.ppermute(value, 'ctx', [(c, c ^ 2 * d) for c in range(ctx)])  17.6 us
    pallas_call x5, Pallas kernels, call(): pl.pallas_call(kernel, name=name, grid=(1,), in_specs=in_specs, out_specs...  14.7 us
    ppermute x9, starting transfers between devices, to_user(): return lax.ppermute(value, 'users', [(u, u ^ d) for u in range(users)])  12.2 us
    ppermute x9, waiting for transfers between devices, to_user(): return lax.ppermute(value, 'users', [(u, u ^ d) for u in range(users)])  12 us
    ppermute x6, waiting for transfers between devices, over_z(): return lax.ppermute(value, 'ctx', [(c, c ^ 2 * d) for c in range(ctx)])  7.8 us
    pallas_call x1, Pallas kernels, on_device(): pl.pallas_call(functools.partial(query_kernel, cap, users), name='query',...  4.67 us
  transfers between devices with their start and end apart: 23, of which 7 were waited for; matrix products, arithmetic and copies ran while one was open for 0% of the time, Pallas kernels for 17%

profile of v6, /device:TPU:0, one launch (start us, length us, event | category | flops | bytes accessed | tf_op | source)
XLA Modules:
  0.0 71.0 jit_solution(6813931199126109904)
XLA Ops:
  0.0 4.7 %query.1 = (bf16[192,1024]{1,0:T(8,128)(2,1)}, bf16[192,1024]{1,0:T(8,128)(2,1)}, bf16[192,1024]{1,0:T(8,128)(2,1)}, bf16[192,1024]{1,0:T(8,128)(2,1)}) custom-call(bf16[384,1024]{1,0:T(8,128)(2,1)} %feat.1, s32[1,384]{1,0:T(1,128)} %bitcast.8, f32[1,1024]{1,0:T(1,128)} %gain_in.3, bf16[1024,2048]{1,0:T(8,128)(2,1)} %bitcast.6), custom_call_target="tpu_custom_call" | custom-call | flops 399999991808 | tf_op jit(solution)/shard_map/query/pallas_call | solution.py:293
  4.7 3.0 %collective-permute-start.1 = (bf16[192,1024]{1,0:T(8,128)(2,1)}, bf16[192,1024]{1,0:T(8,128)(2,1)S(1)}, u32[]{:S(2)}, u32[]{:S(2)}) collective-permute-start(bf16[192,1024]{1,0:T(8,128)(2,1)} %get-tuple-element.30), channel_id=1, source_target_pairs={{0,8},{8,0},{16,24},{24,16},{1,9},{9,1},{17,25},{25,17},{2,10},{10... | collective-permute-start | bytes 1179656 | tf_op jit(solution)/shard_map/ppermute | solution.py:270
  7.7 0.8 %kv_split.1 = (bf16[128,1024]{1,0:T(8,128)(2,1)S(1)}, bf16[128,1024]{1,0:T(8,128)(2,1)}) custom-call(bf16[128,2048]{1,0:T(8,128)(2,1)S(1)} %bitcast.4), custom_call_target="tpu_custom_call" | custom-call | tf_op jit(solution)/shard_map/kv_split/pallas_call | solution.py:237
  8.4 1.6 %collective-permute-start = (bf16[128,1024]{1,0:T(8,128)(2,1)S(1)}, bf16[128,1024]{1,0:T(8,128)(2,1)S(1)}, u32[]{:S(2)}, u32[]{:S(2)}) collective-permute-start(bf16[128,1024]{1,0:T(8,128)(2,1)S(1)} %get-tuple-element.36.rest_4_), channel_id=1, source_target_pairs={{0,2},{1,3},{2,0},{3,1},{4,6},{5,7},{6,4},{7,5},{8,10},{9,11},{10,... | collective-permute-start | bytes 786440 | tf_op jit(solution)/shard_map/ppermute | solution.py:264
  10.0 2.5 %collective-permute-start.6 = (bf16[128,1024]{1,0:T(8,128)(2,1)S(1)}, bf16[128,1024]{1,0:T(8,128)(2,1)}, u32[]{:S(2)}, u32[]{:S(2)}) collective-permute-start(bf16[128,1024]{1,0:T(8,128)(2,1)S(1)} %get-tuple-element.36.rest_4_), channel_id=1, source_target_pairs={{0,6},{1,7},{2,4},{3,5},{4,2},{5,3},{6,0},{7,1},{8,14},{9,15},{10,... | collective-permute-start | bytes 786440 | tf_op jit(solution)/shard_map/ppermute | solution.py:264
  12.5 1.5 %collective-permute-start.2 = (bf16[192,1024]{1,0:T(8,128)(2,1)}, bf16[192,1024]{1,0:T(8,128)(2,1)}, u32[]{:S(2)}, u32[]{:S(2)}) collective-permute-start(bf16[192,1024]{1,0:T(8,128)(2,1)} %get-tuple-element.34), channel_id=1, source_target_pairs={{0,16},{8,24},{16,0},{24,8},{1,17},{9,25},{17,1},{25,9},{2,18},{10... | collective-permute-start | bytes 1179656 | tf_op jit(solution)/shard_map/ppermute | solution.py:270
  14.0 0.5 collective-permute-start.3
  14.5 2.3 %collective-permute-done.rest_6_ = bf16[128,1024]{1,0:T(8,128)(2,1)S(1)} collective-permute-done((bf16[128,1024]{1,0:T(8,128)(2,1)S(1)}, bf16[128,1024]{1,0:T(8,128)(2,1)S(1)}, u32[]{:S(2)}, u32[]{:S(2)}) %collective-permute-start) | collective-permute-done | bytes 262176 | tf_op jit(solution)/shard_map/ppermute | solution.py:264
  16.8 11.5 %collective-permute-start.16 = (bf16[128,1024]{1,0:T(8,128)(2,1)}, bf16[128,1024]{1,0:T(8,128)(2,1)}, u32[]{:S(2)}, u32[]{:S(2)}) collective-permute-start(bf16[128,1024]{1,0:T(8,128)(2,1)} %get-tuple-element.45.rest_4_), channel_id=1, source_target_pairs={{0,6},{1,7},{2,4},{3,5},{4,2},{5,3},{6,0},{7,1},{8,14},{9,15},{10,... | collective-permute-start | bytes 786440 | tf_op jit(solution)/shard_map/ppermute | solution.py:264
  28.3 0.7 %copy-done.3 = bf16[192,1024]{1,0:T(8,128)(2,1)} copy-done((bf16[192,1024]{1,0:T(8,128)(2,1)}, bf16[192,1024]{1,0:T(8,128)(2,1)S(1)}, u32[]{:S(2)}) %copy-start.3) | copy-done | bytes 393240
  29.1 4.1 %gate.1 = (f32[384,1024]{1,0:T(8,128)}, bf16[384,768]{1,0:T(8,128)(2,1)}) custom-call(bf16[384,1024]{1,0:T(8,128)(2,1)} %feat.1, s32[1,384]{1,0:T(1,128)} %bitcast.9, f32[1,1024]{1,0:T(1,128)} %gain_in.3, bf16[1024,2048]{1,0:T(8,128)(2,1)} %bitcast.7), custom_call_target="tpu_custom_call" | custom-call | flops 399999991808 | bytes 4986368 | tf_op jit(solution)/shard_map/gate/pallas_call | solution.py:237
  33.2 0.6 collective-permute-start.4
  33.8 2.0 %collective-permute-done.7.rest_8_ = bf16[128,1024]{1,0:T(8,128)(2,1)} collective-permute-done((bf16[128,1024]{1,0:T(8,128)(2,1)}, bf16[128,1024]{1,0:T(8,128)(2,1)}, u32[]{:S(2)}, u32[]{:S(2)}) %collective-permute-start.7) | collective-permute-done | bytes 262176 | tf_op jit(solution)/shard_map/ppermute | solution.py:264
  35.8 0.5 collective-permute-start.8
  36.3 2.0 %collective-permute-start.17 = (bf16[128,1024]{1,0:T(8,128)(2,1)}, bf16[128,1024]{1,0:T(8,128)(2,1)S(1)}, u32[]{:S(2)}, u32[]{:S(2)}) collective-permute-start(bf16[128,1024]{1,0:T(8,128)(2,1)} %collective-permute-done.16.rest_10_), channel_id=1, source_target_pairs={{0,2},{1,3},{2,0},{3,1},{4,6},{5,7},{6,4},{7,5},{8,10},{9,11},{10,... | collective-permute-start | bytes 786440 | tf_op jit(solution)/shard_map/ppermute | solution.py:264
  38.3 0.1 collective-permute-start.14
  38.4 3.5 %attend.2 = (bf16[192,512]{1,0:T(8,128)(2,1)S(1)}, bf16[192,512]{1,0:T(8,128)(2,1)S(1)}, bf16[192,512]{1,0:T(8,128)(2,1)S(1)}, bf16[192,512]{1,0:T(8,128)(2,1)S(1)}) custom-call(s32[1,8]{1,0:T(1,128)S(1)} %copy-done.10, bf16[192,1024]{1,0:T(8,128)(2,1)S(1)} %copy-done.11, bf16[192,1024]{1,0:T(8,128)(2,1)S(1)} %copy-done.4, ...), custom_call_target="tpu_custom_call" | custom-call | flops 1000000000 | bytes 3670048 | tf_op jit(solution)/shard_map/attend/pallas_call | solution.py:237
  42.0 0.0 copy-start.2
  42.0 0.6 collective-permute-start.10
  42.6 1.5 %collective-permute-start.11 = (bf16[192,512]{1,0:T(8,128)(2,1)S(1)}, bf16[192,512]{1,0:T(8,128)(2,1)S(1)}, u32[]{:S(2)}, u32[]{:S(2)}) collective-permute-start(bf16[192,512]{1,0:T(8,128)(2,1)S(1)} %get-tuple-element.41), channel_id=1, source_target_pairs={{0,16},{8,24},{16,0},{24,8},{1,17},{9,25},{17,1},{25,9},{2,18},{10... | collective-permute-start | bytes 589832 | tf_op jit(solution)/shard_map/ppermute | solution.py:270
  44.2 1.5 %collective-permute-done.17.rest_8_ = bf16[128,1024]{1,0:T(8,128)(2,1)S(1)} collective-permute-done((bf16[128,1024]{1,0:T(8,128)(2,1)}, bf16[128,1024]{1,0:T(8,128)(2,1)S(1)}, u32[]{:S(2)}, u32[]{:S(2)}) %collective-permute-start.17) | collective-permute-done | bytes 262176 | tf_op jit(solution)/shard_map/ppermute | solution.py:264
  45.7 3.0 %collective-permute-done.10.rest_1_ = bf16[192,512]{1,0:T(8,128)(2,1)S(1)} collective-permute-done((bf16[192,512]{1,0:T(8,128)(2,1)S(1)}, bf16[192,512]{1,0:T(8,128)(2,1)S(1)}, u32[]{:S(2)}, u32[]{:S(2)}) %collective-permute-start.10) | collective-permute-done | bytes 196640 | tf_op jit(solution)/shard_map/ppermute | solution.py:270
  48.7 2.0 %collective-permute-done.14.rest_6_ = bf16[128,1024]{1,0:T(8,128)(2,1)S(1)} collective-permute-done((bf16[128,1024]{1,0:T(8,128)(2,1)}, bf16[128,1024]{1,0:T(8,128)(2,1)S(1)}, u32[]{:S(2)}, u32[]{:S(2)}) %collective-permute-start.14) | collective-permute-done | bytes 262176 | tf_op jit(solution)/shard_map/ppermute | solution.py:264
  50.7 1.5 %collective-permute-start.12 = (bf16[192,512]{1,0:T(8,128)(2,1)S(1)}, bf16[192,512]{1,0:T(8,128)(2,1)S(1)}, u32[]{:S(2)}, u32[]{:S(2)}) collective-permute-start(bf16[192,512]{1,0:T(8,128)(2,1)S(1)} %get-tuple-element.42), channel_id=1, source_target_pairs={{0,24},{8,16},{16,8},{24,0},{1,25},{9,17},{17,9},{25,1},{2,26},{10... | collective-permute-start | bytes 589832 | tf_op jit(solution)/shard_map/ppermute | solution.py:270
  52.2 0.0 collective-permute-done.15.rest_7_
  52.2 3.3 %attend.3 = (bf16[192,512]{1,0:T(8,128)(2,1)S(1)}, bf16[192,512]{1,0:T(8,128)(2,1)S(1)}, bf16[192,512]{1,0:T(8,128)(2,1)S(1)}, bf16[192,512]{1,0:T(8,128)(2,1)S(1)}) custom-call(s32[1,8]{1,0:T(1,128)S(1)} %copy-done.10, bf16[192,1024]{1,0:T(8,128)(2,1)S(1)} %copy-done.11, bf16[192,1024]{1,0:T(8,128)(2,1)S(1)} %copy-done.4, ...), custom_call_target="tpu_custom_call" | custom-call | flops 1000000000 | bytes 3670048 | tf_op jit(solution)/shard_map/attend/pallas_call | solution.py:237
  55.6 1.5 %collective-permute-start.20 = (bf16[192,512]{1,0:T(8,128)(2,1)S(1)}, bf16[192,512]{1,0:T(8,128)(2,1)S(1)}, u32[]{:S(2)}, u32[]{:S(2)}) collective-permute-start(bf16[192,512]{1,0:T(8,128)(2,1)S(1)} %get-tuple-element.48), channel_id=1, source_target_pairs={{0,8},{8,0},{16,24},{24,16},{1,9},{9,1},{17,25},{25,17},{2,10},{10... | collective-permute-start | bytes 589832 | tf_op jit(solution)/shard_map/ppermute | solution.py:270
  57.1 0.6 collective-permute-start.21
  57.7 1.4 %collective-permute-start.22 = (bf16[192,512]{1,0:T(8,128)(2,1)S(1)}, bf16[192,512]{1,0:T(8,128)(2,1)S(1)}, u32[]{:S(2)}, u32[]{:S(2)}) collective-permute-start(bf16[192,512]{1,0:T(8,128)(2,1)S(1)} %get-tuple-element.50), channel_id=1, source_target_pairs={{0,24},{8,16},{16,8},{24,0},{1,25},{9,17},{17,9},{25,1},{2,26},{10... | collective-permute-start | bytes 589832 | tf_op jit(solution)/shard_map/ppermute | solution.py:270
  59.1 4.4 %collective-permute-done.20.rest_5_ = bf16[192,512]{1,0:T(8,128)(2,1)S(1)} collective-permute-done((bf16[192,512]{1,0:T(8,128)(2,1)S(1)}, bf16[192,512]{1,0:T(8,128)(2,1)S(1)}, u32[]{:S(2)}, u32[]{:S(2)}) %collective-permute-start.20) | collective-permute-done | bytes 196640 | tf_op jit(solution)/shard_map/ppermute | solution.py:270
  63.6 4.5 %collective-permute-done.21.rest_6_ = bf16[192,512]{1,0:T(8,128)(2,1)S(1)} collective-permute-done((bf16[192,512]{1,0:T(8,128)(2,1)S(1)}, bf16[192,512]{1,0:T(8,128)(2,1)S(1)}, u32[]{:S(2)}, u32[]{:S(2)}) %collective-permute-start.21) | collective-permute-done | bytes 196640 | tf_op jit(solution)/shard_map/ppermute | solution.py:270
  68.1 2.9 %finish.1 = bf16[384,1024]{1,0:T(8,128)(2,1)} custom-call(bf16[384,1024]{1,0:T(8,128)(2,1)S(1)} %copy-done.2, f32[384,1024]{1,0:T(8,128)S(1)} %copy-done.12, bf16[384,768]{1,0:T(8,128)(2,1)S(1)} %copy-done.13, f32[1,1024]{1,0:T(1,128)S(1)} %copy-done.9, bf16[1024,1024]{1,0:T(8,128)(2,1)S(1)} %bitcast.5, bf16[192,512]{1,0:T(8,128)(2,1)S(1)} %get-tuple-element.39.rest_0_, ...), custom_call_target="tpu_custom_call" | custom-call | flops 10000000000 | bytes 6623232 | tf_op jit(solution)/shard_map/finish/pallas_call | solution.py:237
  (48 shorter events, 0.1 us)
Async XLA Ops:
  4.7 23.6 %collective-permute-start.1 = (bf16[192,1024]{1,0:T(8,128)(2,1)}, bf16[192,1024]{1,0:T(8,128)(2,1)S(1)}, u32[]{:S(2)}, u32[]{:S(2)}) collective-permute-start(bf16[192,1024]{1,0:T(8,128)(2,1)} %get-tuple-element.30), channel_id=1, source_target_pairs={{0,8},{8,0},{16,24},{24,16},{1,9},{9,1},{17,25},{25,17},{2,10},{10... | collective-permute-start | bytes 1179656 | tf_op jit(solution)/shard_map/ppermute | solution.py:270
  8.4 20.6 %copy-start.5 = (bf16[128,1024]{1,0:T(8,128)(2,1)}, bf16[128,1024]{1,0:T(8,128)(2,1)S(1)}, u32[]{:S(2)}) copy-start(bf16[128,1024]{1,0:T(8,128)(2,1)S(1)} %get-tuple-element.36.rest_4_) | copy-start | bytes 786436
  8.4 8.3 %collective-permute-start = (bf16[128,1024]{1,0:T(8,128)(2,1)S(1)}, bf16[128,1024]{1,0:T(8,128)(2,1)S(1)}, u32[]{:S(2)}, u32[]{:S(2)}) collective-permute-start(bf16[128,1024]{1,0:T(8,128)(2,1)S(1)} %get-tuple-element.36.rest_4_), channel_id=1, source_target_pairs={{0,2},{1,3},{2,0},{3,1},{4,6},{5,7},{6,4},{7,5},{8,10},{9,11},{10,... | collective-permute-start | bytes 786440 | tf_op jit(solution)/shard_map/ppermute | solution.py:264
  10.0 18.2 %collective-permute-start.6 = (bf16[128,1024]{1,0:T(8,128)(2,1)S(1)}, bf16[128,1024]{1,0:T(8,128)(2,1)}, u32[]{:S(2)}, u32[]{:S(2)}) collective-permute-start(bf16[128,1024]{1,0:T(8,128)(2,1)S(1)} %get-tuple-element.36.rest_4_), channel_id=1, source_target_pairs={{0,6},{1,7},{2,4},{3,5},{4,2},{5,3},{6,0},{7,1},{8,14},{9,15},{10,... | collective-permute-start | bytes 786440 | tf_op jit(solution)/shard_map/ppermute | solution.py:264
  12.5 20.7 %collective-permute-start.2 = (bf16[192,1024]{1,0:T(8,128)(2,1)}, bf16[192,1024]{1,0:T(8,128)(2,1)}, u32[]{:S(2)}, u32[]{:S(2)}) collective-permute-start(bf16[192,1024]{1,0:T(8,128)(2,1)} %get-tuple-element.34), channel_id=1, source_target_pairs={{0,16},{8,24},{16,0},{24,8},{1,17},{9,25},{17,1},{25,9},{2,18},{10... | collective-permute-start | bytes 1179656 | tf_op jit(solution)/shard_map/ppermute | solution.py:270
  14.0 22.3 %collective-permute-start.3 = (bf16[192,1024]{1,0:T(8,128)(2,1)}, bf16[192,1024]{1,0:T(8,128)(2,1)}, u32[]{:S(2)}, u32[]{:S(2)}) collective-permute-start(bf16[192,1024]{1,0:T(8,128)(2,1)} %get-tuple-element.35), channel_id=1, source_target_pairs={{0,24},{8,16},{16,8},{24,0},{1,25},{9,17},{17,9},{25,1},{2,26},{10... | collective-permute-start | bytes 1179656 | tf_op jit(solution)/shard_map/ppermute | solution.py:270
  16.8 12.2 %copy-start.7 = (bf16[128,1024]{1,0:T(8,128)(2,1)}, bf16[128,1024]{1,0:T(8,128)(2,1)S(1)}, u32[]{:S(2)}) copy-start(bf16[128,1024]{1,0:T(8,128)(2,1)S(1)} %collective-permute-done.rest_6_) | copy-start | bytes 786436
  16.8 19.1 %collective-permute-start.16 = (bf16[128,1024]{1,0:T(8,128)(2,1)}, bf16[128,1024]{1,0:T(8,128)(2,1)}, u32[]{:S(2)}, u32[]{:S(2)}) collective-permute-start(bf16[128,1024]{1,0:T(8,128)(2,1)} %get-tuple-element.45.rest_4_), channel_id=1, source_target_pairs={{0,6},{1,7},{2,4},{3,5},{4,2},{5,3},{6,0},{7,1},{8,14},{9,15},{10,... | collective-permute-start | bytes 786440 | tf_op jit(solution)/shard_map/ppermute | solution.py:264
  28.3 7.6 %collective-permute-start.7 = (bf16[128,1024]{1,0:T(8,128)(2,1)}, bf16[128,1024]{1,0:T(8,128)(2,1)}, u32[]{:S(2)}, u32[]{:S(2)}) collective-permute-start(bf16[128,1024]{1,0:T(8,128)(2,1)} %collective-permute-done.6.rest_10_), channel_id=1, source_target_pairs={{0,2},{1,3},{2,0},{3,1},{4,6},{5,7},{6,4},{7,5},{8,10},{9,11},{10,... | collective-permute-start | bytes 786440 | tf_op jit(solution)/shard_map/ppermute | solution.py:264
  29.0 9.3 %collective-permute-start.9 = (bf16[128,1024]{1,0:T(8,128)(2,1)}, bf16[128,1024]{1,0:T(8,128)(2,1)}, u32[]{:S(2)}, u32[]{:S(2)}) collective-permute-start(bf16[128,1024]{1,0:T(8,128)(2,1)} %collective-permute-done.6.rest_10_), channel_id=1, source_target_pairs={{0,1},{1,0},{2,3},{3,2},{4,5},{5,4},{6,7},{7,6},{8,9},{9,8},{10,11... | collective-permute-start | bytes 786440 | tf_op jit(solution)/shard_map/ppermute | solution.py:267
  29.0 9.4 %copy-start.4 = (bf16[192,1024]{1,0:T(8,128)(2,1)S(1)}, bf16[192,1024]{1,0:T(8,128)(2,1)}, u32[]{:S(2)}) copy-start(bf16[192,1024]{1,0:T(8,128)(2,1)} %copy-done.3) | copy-start | bytes 1179652
  29.0 9.4 %copy-start.10 = (s32[1,8]{1,0:T(1,128)S(1)}, s32[1,8]{1,0:T(1,128)}, u32[]{:S(2)}) copy-start(s32[1,8]{1,0:T(1,128)} %mask.3) | copy-start | bytes 100
  33.2 5.2 %collective-permute-start.4 = (bf16[128,1024]{1,0:T(8,128)(2,1)S(1)}, bf16[128,1024]{1,0:T(8,128)(2,1)S(1)}, u32[]{:S(2)}, u32[]{:S(2)}) collective-permute-start(bf16[128,1024]{1,0:T(8,128)(2,1)S(1)} %copy-done.6), channel_id=1, source_target_pairs={{0,1},{1,0},{2,3},{3,2},{4,5},{5,4},{6,7},{7,6},{8,9},{9,8},{10,11... | collective-permute-start | bytes 786440 | tf_op jit(solution)/shard_map/ppermute | solution.py:267
  35.8 2.6 %collective-permute-start.5 = (bf16[128,1024]{1,0:T(8,128)(2,1)S(1)}, bf16[128,1024]{1,0:T(8,128)(2,1)S(1)}, u32[]{:S(2)}, u32[]{:S(2)}) collective-permute-start(bf16[128,1024]{1,0:T(8,128)(2,1)S(1)} %copy-done.8), channel_id=1, source_target_pairs={{0,1},{1,0},{2,3},{3,2},{4,5},{5,4},{6,7},{7,6},{8,9},{9,8},{10,11... | collective-permute-start | bytes 786440 | tf_op jit(solution)/shard_map/ppermute | solution.py:267
  35.8 2.6 %collective-permute-start.8 = (bf16[128,1024]{1,0:T(8,128)(2,1)}, bf16[128,1024]{1,0:T(8,128)(2,1)S(1)}, u32[]{:S(2)}, u32[]{:S(2)}) collective-permute-start(bf16[128,1024]{1,0:T(8,128)(2,1)} %collective-permute-done.7.rest_8_), channel_id=1, source_target_pairs={{0,1},{1,0},{2,3},{3,2},{4,5},{5,4},{6,7},{7,6},{8,9},{9,8},{10,11... | collective-permute-start | bytes 786440 | tf_op jit(solution)/shard_map/ppermute | solution.py:267
  36.3 9.3 %collective-permute-start.17 = (bf16[128,1024]{1,0:T(8,128)(2,1)}, bf16[128,1024]{1,0:T(8,128)(2,1)S(1)}, u32[]{:S(2)}, u32[]{:S(2)}) collective-permute-start(bf16[128,1024]{1,0:T(8,128)(2,1)} %collective-permute-done.16.rest_10_), channel_id=1, source_target_pairs={{0,2},{1,3},{2,0},{3,1},{4,6},{5,7},{6,4},{7,5},{8,10},{9,11},{10,... | collective-permute-start | bytes 786440 | tf_op jit(solution)/shard_map/ppermute | solution.py:264
  38.3 12.4 %collective-permute-start.14 = (bf16[128,1024]{1,0:T(8,128)(2,1)}, bf16[128,1024]{1,0:T(8,128)(2,1)S(1)}, u32[]{:S(2)}, u32[]{:S(2)}) collective-permute-start(bf16[128,1024]{1,0:T(8,128)(2,1)} %get-tuple-element.45.rest_4_), channel_id=1, source_target_pairs={{0,2},{1,3},{2,0},{3,1},{4,6},{5,7},{6,4},{7,5},{8,10},{9,11},{10,... | collective-permute-start | bytes 786440 | tf_op jit(solution)/shard_map/ppermute | solution.py:264
  38.4 29.7 %copy-start.12 = (f32[384,1024]{1,0:T(8,128)S(1)}, f32[384,1024]{1,0:T(8,128)}, u32[]{:S(2)}) copy-start(f32[384,1024]{1,0:T(8,128)} %get-tuple-element.32.gate) | copy-start | bytes 4718596
  42.0 26.1 %copy-start.1 = (bf16[1,1024,1024]{2,1,0:T(8,128)(2,1)S(1)}, bf16[1,1024,1024]{2,1,0:T(8,128)(2,1)}, u32[]{:S(2)}) copy-start(bf16[1,1024,1024]{2,1,0:T(8,128)(2,1)} %param.15) | copy-start | bytes 6291460
  42.0 26.1 %copy-start.2 = (bf16[384,1024]{1,0:T(8,128)(2,1)S(1)}, bf16[384,1024]{1,0:T(8,128)(2,1)}, u32[]{:S(2)}) copy-start(bf16[384,1024]{1,0:T(8,128)(2,1)} %feat.1) | copy-start | bytes 2359300
  42.0 26.1 %copy-start.9 = (f32[1,1024]{1,0:T(1,128)S(1)}, f32[1,1024]{1,0:T(1,128)}, u32[]{:S(2)}) copy-start(f32[1,1024]{1,0:T(1,128)} %gain.1) | copy-start | bytes 12292
  42.0 26.1 %copy-start.13 = (bf16[384,768]{1,0:T(8,128)(2,1)S(1)}, bf16[384,768]{1,0:T(8,128)(2,1)}, u32[]{:S(2)}) copy-start(bf16[384,768]{1,0:T(8,128)(2,1)} %get-tuple-element.33.pick) | copy-start | bytes 1769476
  42.0 6.7 %collective-permute-start.10 = (bf16[192,512]{1,0:T(8,128)(2,1)S(1)}, bf16[192,512]{1,0:T(8,128)(2,1)S(1)}, u32[]{:S(2)}, u32[]{:S(2)}) collective-permute-start(bf16[192,512]{1,0:T(8,128)(2,1)S(1)} %get-tuple-element.40), channel_id=1, source_target_pairs={{0,8},{8,0},{16,24},{24,16},{1,9},{9,1},{17,25},{25,17},{2,10},{10... | collective-permute-start | bytes 589832 | tf_op jit(solution)/shard_map/ppermute | solution.py:270
  42.6 8.0 %collective-permute-start.11 = (bf16[192,512]{1,0:T(8,128)(2,1)S(1)}, bf16[192,512]{1,0:T(8,128)(2,1)S(1)}, u32[]{:S(2)}, u32[]{:S(2)}) collective-permute-start(bf16[192,512]{1,0:T(8,128)(2,1)S(1)} %get-tuple-element.41), channel_id=1, source_target_pairs={{0,16},{8,24},{16,0},{24,8},{1,17},{9,25},{17,1},{25,9},{2,18},{10... | collective-permute-start | bytes 589832 | tf_op jit(solution)/shard_map/ppermute | solution.py:270
  44.2 8.0 %collective-permute-start.19 = (bf16[128,1024]{1,0:T(8,128)(2,1)}, bf16[128,1024]{1,0:T(8,128)(2,1)S(1)}, u32[]{:S(2)}, u32[]{:S(2)}) collective-permute-start(bf16[128,1024]{1,0:T(8,128)(2,1)} %collective-permute-done.16.rest_10_), channel_id=1, source_target_pairs={{0,1},{1,0},{2,3},{3,2},{4,5},{5,4},{6,7},{7,6},{8,9},{9,8},{10,11... | collective-permute-start | bytes 786440 | tf_op jit(solution)/shard_map/ppermute | solution.py:267
  45.7 6.5 %collective-permute-start.18 = (bf16[128,1024]{1,0:T(8,128)(2,1)S(1)}, bf16[128,1024]{1,0:T(8,128)(2,1)S(1)}, u32[]{:S(2)}, u32[]{:S(2)}) collective-permute-start(bf16[128,1024]{1,0:T(8,128)(2,1)S(1)} %collective-permute-done.17.rest_8_), channel_id=1, source_target_pairs={{0,1},{1,0},{2,3},{3,2},{4,5},{5,4},{6,7},{7,6},{8,9},{9,8},{10,11... | collective-permute-start | bytes 786440 | tf_op jit(solution)/shard_map/ppermute | solution.py:267
  48.7 3.5 %collective-permute-start.13 = (bf16[128,1024]{1,0:T(8,128)(2,1)}, bf16[128,1024]{1,0:T(8,128)(2,1)S(1)}, u32[]{:S(2)}, u32[]{:S(2)}) collective-permute-start(bf16[128,1024]{1,0:T(8,128)(2,1)} %get-tuple-element.45.rest_4_), channel_id=1, source_target_pairs={{0,1},{1,0},{2,3},{3,2},{4,5},{5,4},{6,7},{7,6},{8,9},{9,8},{10,11... | collective-permute-start | bytes 786440 | tf_op jit(solution)/shard_map/ppermute | solution.py:267
  50.7 1.5 %collective-permute-start.15 = (bf16[128,1024]{1,0:T(8,128)(2,1)S(1)}, bf16[128,1024]{1,0:T(8,128)(2,1)S(1)}, u32[]{:S(2)}, u32[]{:S(2)}) collective-permute-start(bf16[128,1024]{1,0:T(8,128)(2,1)S(1)} %collective-permute-done.14.rest_6_), channel_id=1, source_target_pairs={{0,1},{1,0},{2,3},{3,2},{4,5},{5,4},{6,7},{7,6},{8,9},{9,8},{10,11... | collective-permute-start | bytes 786440 | tf_op jit(solution)/shard_map/ppermute | solution.py:267
  50.7 8.4 %collective-permute-start.12 = (bf16[192,512]{1,0:T(8,128)(2,1)S(1)}, bf16[192,512]{1,0:T(8,128)(2,1)S(1)}, u32[]{:S(2)}, u32[]{:S(2)}) collective-permute-start(bf16[192,512]{1,0:T(8,128)(2,1)S(1)} %get-tuple-element.42), channel_id=1, source_target_pairs={{0,24},{8,16},{16,8},{24,0},{1,25},{9,17},{17,9},{25,1},{2,26},{10... | collective-permute-start | bytes 589832 | tf_op jit(solution)/shard_map/ppermute | solution.py:270
  55.6 8.0 %collective-permute-start.20 = (bf16[192,512]{1,0:T(8,128)(2,1)S(1)}, bf16[192,512]{1,0:T(8,128)(2,1)S(1)}, u32[]{:S(2)}, u32[]{:S(2)}) collective-permute-start(bf16[192,512]{1,0:T(8,128)(2,1)S(1)} %get-tuple-element.48), channel_id=1, source_target_pairs={{0,8},{8,0},{16,24},{24,16},{1,9},{9,1},{17,25},{25,17},{2,10},{10... | collective-permute-start | bytes 589832 | tf_op jit(solution)/shard_map/ppermute | solution.py:270
  57.1 11.0 %collective-permute-start.21 = (bf16[192,512]{1,0:T(8,128)(2,1)S(1)}, bf16[192,512]{1,0:T(8,128)(2,1)S(1)}, u32[]{:S(2)}, u32[]{:S(2)}) collective-permute-start(bf16[192,512]{1,0:T(8,128)(2,1)S(1)} %get-tuple-element.49), channel_id=1, source_target_pairs={{0,16},{8,24},{16,0},{24,8},{1,17},{9,25},{17,1},{25,9},{2,18},{10... | collective-permute-start | bytes 589832 | tf_op jit(solution)/shard_map/ppermute | solution.py:270
  57.7 10.4 %collective-permute-start.22 = (bf16[192,512]{1,0:T(8,128)(2,1)S(1)}, bf16[192,512]{1,0:T(8,128)(2,1)S(1)}, u32[]{:S(2)}, u32[]{:S(2)}) collective-permute-start(bf16[192,512]{1,0:T(8,128)(2,1)S(1)} %get-tuple-element.50), channel_id=1, source_target_pairs={{0,24},{8,16},{16,8},{24,0},{1,25},{9,17},{17,9},{25,1},{2,26},{10... | collective-permute-start | bytes 589832 | tf_op jit(solution)/shard_map/ppermute | solution.py:270
  (5 other events, 28.8 us)

commit v7 on v6

--- a/solution.py
+++ b/solution.py
@@ -9,7 +9,7 @@
 
 BLK = 128
 HEAD = 128
-OPTS = {'chunks': [4, 4], 'order': 0, 'qs': 0, 'cq': 400000000000, 'cg': 400000000000, 'ca': 1000000000, 'cf': 10000000000, 'm1': [], 'a1': ['f'], 'g': ['a0', 'qx'], 's0': [['qx'], ['g', 'qy'], ['g'], []], 's1': [['s', 'rx'], ['ry'], [], []], 'cp': 0, 'sw': [0, 0], 'p0': [], 'p1': []}
+OPTS = {'chunks': (4, 4), 'order': 0, 'qs': 1, 'cq': 400000000000, 'cg': 400000000000, 'ca': 2000000000, 'cf': 1000000000, 'cp': 0, 'sw': (0, 0), 'p0': [], 'p1': [], 'm1': ['m', 'g'], 'a1': ['a', 'g'], 'g': [], 's0': [['qx'], ['qx'], [], ['qx']], 's1': [[], ['s'], ['rd'], []]}
 CHUNKS = OPTS['chunks']
 SLICES = 2
 VMEM_LIMIT = 32 * 1024 * 1024
@@ -139,7 +139,7 @@
         taken = taken + live.astype(jnp.int32)
 
 
-def attend_kernel(users, chips, first, mask, *rest):
+def attend_kernel(users, chips, mask, *rest):
     queries, (mine, other) = rest[:users], rest[users:users + 2]
     outs, (all_q, live_kv) = rest[users + 2:2 * users + 2], rest[2 * users + 2:]
     cap, wide = outs[0].shape
@@ -160,7 +160,7 @@
         pl.when(slot < count)(from_mine)
         pl.when(slot >= count)(from_other)
     for i, q in enumerate(queries):
-        all_q[i * cap:(i + 1) * cap, :] = q[:, first:first + wide]
+        all_q[i * cap:(i + 1) * cap, :] = q[...]
     scale = 0.5 * HEAD ** (-0.5)
     for head in range(wide // HEAD):
         cols = slice(head * HEAD, (head + 1) * HEAD)
@@ -175,7 +175,7 @@
             out[:, cols] = got[i * cap:(i + 1) * cap, :]
 
 
-def attend_blocks_kernel(users, chips, first, mask, *rest):
+def attend_blocks_kernel(users, chips, mask, *rest):
     queries = rest[:users]
     blocks = rest[users:users + 2 * chips]
     outs, (all_q, live_kv) = rest[-2 - users:-2], rest[-2:]
@@ -194,7 +194,7 @@
             pl.when(live)(take)
             taken = jnp.minimum(taken + live.astype(jnp.int32), chips - 1)
     for i, q in enumerate(queries):
-        all_q[i * cap:(i + 1) * cap, :] = q[:, first:first + wide]
+        all_q[i * cap:(i + 1) * cap, :] = q[...]
     scale = 0.5 * HEAD ** (-0.5)
     for head in range(wide // HEAD):
         cols = slice(head * HEAD, (head + 1) * HEAD)
@@ -348,8 +348,8 @@
                 keys = OPTS['s0' if chunk == 0 else 's1'][d % 4]
                 blocks += [held[d], over_cores(gated(held[d], keys))]
         scored = call(
-            functools.partial(kernel, users, chips, first), "attend",
-            [SMEM] + [whole(cap, width)] * users + [whole(*block.shape) for block in blocks],
+            functools.partial(kernel, users, chips), "attend",
+            [SMEM] + [whole(cap, wide, at=(0, chunk))] * users + [whole(*block.shape) for block in blocks],
             [shape(cap, wide)] * users,
             [pltpu.VMEM((users * cap, wide), bf16), pltpu.VMEM((chips * BLK, 2 * wide), bf16)],
             OPTS['ca'],

time: 71.2 us -> 67.9 us (0.954)
  starting transfers between devices: 30.8 us -> 27.5 us
    ppermute x9, waiting for transfers between devices: 12 us -> 15.9 us  [to_user(): return lax.ppermute(value, 'users', [(u, u ^ d) for u in range(users)])]
    ppermute x6, waiting for transfers between devices: 7.8 us -> 4 us  [over_z(): return lax.ppermute(value, 'ctx', [(c, c ^ 2 * d) for c in range(ctx)])]
    ppermute x6, starting transfers between devices: 17.6 us -> 14.1 us  [over_z(): return lax.ppermute(value, 'ctx', [(c, c ^ 2 * d) for c in range(ctx)])]
  transfers between devices with their start and end apart: 23 -> 23, of which waited for: 7 -> 6; matrix products, arithmetic and copies ran while one was open for 0% -> 0% of each run, Pallas kernels for 17% -> 23%
where the time goes in v7:
time: 67.9 us; the launch traced here: 67.7 us
  starting transfers between devices  27.5 us (41%)
  waiting for transfers between devices  19.9 us (29%)
  Pallas kernels  19 us (28%)
  local copies, waits for them, and re-layouts  1.07 us (2%)
    ppermute x9, waiting for transfers between devices, to_user(): return lax.ppermute(value, 'users', [(u, u ^ d) for u in range(users)])  15.9 us
    pallas_call x5, Pallas kernels, call(): pl.pallas_call(kernel, name=name, grid=(1,), in_specs=in_specs, out_specs...  14.4 us
    ppermute x6, starting transfers between devices, over_z(): return lax.ppermute(value, 'ctx', [(c, c ^ 2 * d) for c in range(ctx)])  14.1 us
    ppermute x9, starting transfers between devices, to_user(): return lax.ppermute(value, 'users', [(u, u ^ d) for u in range(users)])  12.3 us
    pallas_call x1, Pallas kernels, on_device(): pl.pallas_call(functools.partial(query_kernel, cap, users), name='query',...  4.61 us
    ppermute x6, waiting for transfers between devices, over_z(): return lax.ppermute(value, 'ctx', [(c, c ^ 2 * d) for c in range(ctx)])  4 us
  transfers between devices with their start and end apart: 23, of which 6 were waited for; matrix products, arithmetic and copies ran while one was open for 0% of the time, Pallas kernels for 23%

profile of v7, /device:TPU:0, one launch (start us, length us, event | category | flops | bytes accessed | tf_op | source)
XLA Modules:
  0.0 67.7 jit_solution(11878819286564468822)
XLA Ops:
  0.0 1.0 %copy-done.4 = bf16[1,1,128,2048]{3,2,1,0:T(8,128)(2,1)S(1)} copy-done((bf16[1,1,128,2048]{3,2,1,0:T(8,128)(2,1)S(1)}, bf16[1,1,128,2048]{3,2,1,0:T(8,128)(2,1)}, u32[]{:S(2)}) %copy-start.4) | copy-done | bytes 524312
  1.0 0.7 %kv_split.1 = (bf16[128,1024]{1,0:T(8,128)(2,1)}, bf16[128,1024]{1,0:T(8,128)(2,1)S(1)}) custom-call(bf16[128,2048]{1,0:T(8,128)(2,1)S(1)} %bitcast.5), custom_call_target="tpu_custom_call" | custom-call | tf_op jit(solution)/shard_map/kv_split/pallas_call | solution.py:237
  1.8 5.0 %collective-permute-start.6 = (bf16[128,1024]{1,0:T(8,128)(2,1)}, bf16[128,1024]{1,0:T(8,128)(2,1)}, u32[]{:S(2)}, u32[]{:S(2)}) collective-permute-start(bf16[128,1024]{1,0:T(8,128)(2,1)} %get-tuple-element.39.rest_4_), channel_id=1, source_target_pairs={{0,6},{1,7},{2,4},{3,5},{4,2},{5,3},{6,0},{7,1},{8,14},{9,15},{10,... | collective-permute-start | bytes 786440 | tf_op jit(solution)/shard_map/ppermute | solution.py:264
  6.8 4.6 %query.1 = (bf16[192,1024]{1,0:T(8,128)(2,1)}, bf16[192,1024]{1,0:T(8,128)(2,1)}, bf16[192,1024]{1,0:T(8,128)(2,1)}, bf16[192,1024]{1,0:T(8,128)(2,1)}) custom-call(bf16[384,1024]{1,0:T(8,128)(2,1)} %feat.1, s32[1,384]{1,0:T(1,128)} %bitcast.8, f32[1,1024]{1,0:T(1,128)} %gain_in.3, bf16[1024,2048]{1,0:T(8,128)(2,1)} %bitcast.6), custom_call_target="tpu_custom_call" | custom-call | flops 399999991808 | tf_op jit(solution)/shard_map/query/pallas_call | solution.py:293
  11.5 1.6 %collective-permute-start = (bf16[192,1024]{1,0:T(8,128)(2,1)}, bf16[192,1024]{1,0:T(8,128)(2,1)}, u32[]{:S(2)}, u32[]{:S(2)}) collective-permute-start(bf16[192,1024]{1,0:T(8,128)(2,1)} %get-tuple-element.36), channel_id=1, source_target_pairs={{0,8},{8,0},{16,24},{24,16},{1,9},{9,1},{17,25},{25,17},{2,10},{10... | collective-permute-start | bytes 1179656 | tf_op jit(solution)/shard_map/ppermute | solution.py:270
  13.0 1.5 %collective-permute-start.1 = (bf16[192,1024]{1,0:T(8,128)(2,1)}, bf16[192,1024]{1,0:T(8,128)(2,1)}, u32[]{:S(2)}, u32[]{:S(2)}) collective-permute-start(bf16[192,1024]{1,0:T(8,128)(2,1)} %get-tuple-element.37), channel_id=1, source_target_pairs={{0,16},{8,24},{16,0},{24,8},{1,17},{9,25},{17,1},{25,9},{2,18},{10... | collective-permute-start | bytes 1179656 | tf_op jit(solution)/shard_map/ppermute | solution.py:270
  14.5 0.5 collective-permute-start.2
  15.0 3.8 %collective-permute-start.7 = (bf16[128,1024]{1,0:T(8,128)(2,1)}, bf16[128,1024]{1,0:T(8,128)(2,1)}, u32[]{:S(2)}, u32[]{:S(2)}) collective-permute-start(bf16[128,1024]{1,0:T(8,128)(2,1)} %collective-permute-done.6.rest_10_), channel_id=1, source_target_pairs={{0,2},{1,3},{2,0},{3,1},{4,6},{5,7},{6,4},{7,5},{8,10},{9,11},{10,... | collective-permute-start | bytes 786440 | tf_op jit(solution)/shard_map/ppermute | solution.py:264
  18.8 4.1 %gate.1 = (f32[384,1024]{1,0:T(8,128)}, bf16[384,768]{1,0:T(8,128)(2,1)}) custom-call(bf16[384,1024]{1,0:T(8,128)(2,1)} %feat.1, s32[1,384]{1,0:T(1,128)} %bitcast.9, f32[1,1024]{1,0:T(1,128)} %gain_in.3, bf16[1024,2048]{1,0:T(8,128)(2,1)} %bitcast.7), custom_call_target="tpu_custom_call" | custom-call | flops 399999991808 | bytes 4986368 | tf_op jit(solution)/shard_map/gate/pallas_call | solution.py:237
  22.9 1.0 %collective-permute-done.rest_1_ = bf16[192,1024]{1,0:T(8,128)(2,1)} collective-permute-done((bf16[192,1024]{1,0:T(8,128)(2,1)}, bf16[192,1024]{1,0:T(8,128)(2,1)}, u32[]{:S(2)}, u32[]{:S(2)}) %collective-permute-start) | collective-permute-done | bytes 393248 | tf_op jit(solution)/shard_map/ppermute | solution.py:270
  23.9 1.6 %collective-permute-start.16 = (bf16[128,1024]{1,0:T(8,128)(2,1)S(1)}, bf16[128,1024]{1,0:T(8,128)(2,1)S(1)}, u32[]{:S(2)}, u32[]{:S(2)}) collective-permute-start(bf16[128,1024]{1,0:T(8,128)(2,1)S(1)} %get-tuple-element.49.rest_4_), channel_id=1, source_target_pairs={{0,6},{1,7},{2,4},{3,5},{4,2},{5,3},{6,0},{7,1},{8,14},{9,15},{10,... | collective-permute-start | bytes 786440 | tf_op jit(solution)/shard_map/ppermute | solution.py:264
  25.5 6.6 %collective-permute-done.1.rest_2_ = bf16[192,1024]{1,0:T(8,128)(2,1)} collective-permute-done((bf16[192,1024]{1,0:T(8,128)(2,1)}, bf16[192,1024]{1,0:T(8,128)(2,1)}, u32[]{:S(2)}, u32[]{:S(2)}) %collective-permute-start.1) | collective-permute-done | bytes 393248 | tf_op jit(solution)/shard_map/ppermute | solution.py:270
  32.1 0.5 collective-permute-start.9
  32.6 0.1 collective-permute-start.8
  32.6 3.7 %collective-permute-start.14 = (bf16[128,1024]{1,0:T(8,128)(2,1)S(1)}, bf16[128,1024]{1,0:T(8,128)(2,1)S(1)}, u32[]{:S(2)}, u32[]{:S(2)}) collective-permute-start(bf16[128,1024]{1,0:T(8,128)(2,1)S(1)} %get-tuple-element.49.rest_4_), channel_id=1, source_target_pairs={{0,2},{1,3},{2,0},{3,1},{4,6},{5,7},{6,4},{7,5},{8,10},{9,11},{10,... | collective-permute-start | bytes 786440 | tf_op jit(solution)/shard_map/ppermute | solution.py:264
  36.3 0.0 collective-permute-start.17
  36.4 3.5 %attend.2 = (bf16[192,512]{1,0:T(8,128)(2,1)S(1)}, bf16[192,512]{1,0:T(8,128)(2,1)S(1)}, bf16[192,512]{1,0:T(8,128)(2,1)S(1)}, bf16[192,512]{1,0:T(8,128)(2,1)S(1)}) custom-call(s32[1,8]{1,0:T(1,128)S(1)} %copy-done.6, bf16[192,1024]{1,0:T(8,128)(2,1)S(1)} %copy-done.7, bf16[192,1024]{1,0:T(8,128)(2,1)} %collective-permute-done.rest_1_, ...), custom_call_target="tpu_custom_call" | custom-call | flops 2000000000 | bytes 3670048 | tf_op jit(solution)/shard_map/attend/pallas_call | solution.py:237
  39.9 2.5 %collective-permute-start.12 = (bf16[192,512]{1,0:T(8,128)(2,1)S(1)}, bf16[192,512]{1,0:T(8,128)(2,1)S(1)}, u32[]{:S(2)}, u32[]{:S(2)}) collective-permute-start(bf16[192,512]{1,0:T(8,128)(2,1)S(1)} %get-tuple-element.45), channel_id=1, source_target_pairs={{0,24},{8,16},{16,8},{24,0},{1,25},{9,17},{17,9},{25,1},{2,26},{10... | collective-permute-start | bytes 589832 | tf_op jit(solution)/shard_map/ppermute | solution.py:270
  42.4 0.5 collective-permute-start.19
  42.9 0.6 collective-permute-done.14.rest_6_
  43.6 3.4 %collective-permute-done.17.rest_8_ = bf16[128,1024]{1,0:T(8,128)(2,1)S(1)} collective-permute-done((bf16[128,1024]{1,0:T(8,128)(2,1)S(1)}, bf16[128,1024]{1,0:T(8,128)(2,1)S(1)}, u32[]{:S(2)}, u32[]{:S(2)}) %collective-permute-start.17) | collective-permute-done | bytes 262176 | tf_op jit(solution)/shard_map/ppermute | solution.py:264
  46.9 1.1 %collective-permute-start.10 = (bf16[192,512]{1,0:T(8,128)(2,1)S(1)}, bf16[192,512]{1,0:T(8,128)(2,1)S(1)}, u32[]{:S(2)}, u32[]{:S(2)}) collective-permute-start(bf16[192,512]{1,0:T(8,128)(2,1)S(1)} %get-tuple-element.43), channel_id=1, source_target_pairs={{0,8},{8,0},{16,24},{24,16},{1,9},{9,1},{17,25},{25,17},{2,10},{10... | collective-permute-start | bytes 589832 | tf_op jit(solution)/shard_map/ppermute | solution.py:270
  48.0 0.0 copy-start.3
  48.1 0.0 copy-start.5
  48.1 1.6 %collective-permute-start.11 = (bf16[192,512]{1,0:T(8,128)(2,1)S(1)}, bf16[192,512]{1,0:T(8,128)(2,1)S(1)}, u32[]{:S(2)}, u32[]{:S(2)}) collective-permute-start(bf16[192,512]{1,0:T(8,128)(2,1)S(1)} %get-tuple-element.44), channel_id=1, source_target_pairs={{0,16},{8,24},{16,0},{24,8},{1,17},{9,25},{17,1},{25,9},{2,18},{10... | collective-permute-start | bytes 589832 | tf_op jit(solution)/shard_map/ppermute | solution.py:270
  49.7 3.2 %attend.3 = (bf16[192,512]{1,0:T(8,128)(2,1)S(1)}, bf16[192,512]{1,0:T(8,128)(2,1)S(1)}, bf16[192,512]{1,0:T(8,128)(2,1)S(1)}, bf16[192,512]{1,0:T(8,128)(2,1)S(1)}) custom-call(s32[1,8]{1,0:T(1,128)S(1)} %copy-done.6, bf16[192,1024]{1,0:T(8,128)(2,1)S(1)} %copy-done.7, bf16[192,1024]{1,0:T(8,128)(2,1)} %collective-permute-done.rest_1_, ...), custom_call_target="tpu_custom_call" | custom-call | flops 2000000000 | bytes 3670048 | tf_op jit(solution)/shard_map/attend/pallas_call | solution.py:237
  52.9 1.0 %collective-permute-start.20 = (bf16[192,512]{1,0:T(8,128)(2,1)S(1)}, bf16[192,512]{1,0:T(8,128)(2,1)S(1)}, u32[]{:S(2)}, u32[]{:S(2)}) collective-permute-start(bf16[192,512]{1,0:T(8,128)(2,1)S(1)} %get-tuple-element.52), channel_id=1, source_target_pairs={{0,8},{8,0},{16,24},{24,16},{1,9},{9,1},{17,25},{25,17},{2,10},{10... | collective-permute-start | bytes 589832 | tf_op jit(solution)/shard_map/ppermute | solution.py:270
  53.9 0.8 %collective-permute-start.21 = (bf16[192,512]{1,0:T(8,128)(2,1)S(1)}, bf16[192,512]{1,0:T(8,128)(2,1)S(1)}, u32[]{:S(2)}, u32[]{:S(2)}) collective-permute-start(bf16[192,512]{1,0:T(8,128)(2,1)S(1)} %get-tuple-element.53), channel_id=1, source_target_pairs={{0,16},{8,24},{16,0},{24,8},{1,17},{9,25},{17,1},{25,9},{2,18},{10... | collective-permute-start | bytes 589832 | tf_op jit(solution)/shard_map/ppermute | solution.py:270
  54.7 1.8 %collective-permute-start.22 = (bf16[192,512]{1,0:T(8,128)(2,1)S(1)}, bf16[192,512]{1,0:T(8,128)(2,1)S(1)}, u32[]{:S(2)}, u32[]{:S(2)}) collective-permute-start(bf16[192,512]{1,0:T(8,128)(2,1)S(1)} %get-tuple-element.54), channel_id=1, source_target_pairs={{0,24},{8,16},{16,8},{24,0},{1,25},{9,17},{17,9},{25,1},{2,26},{10... | collective-permute-start | bytes 589832 | tf_op jit(solution)/shard_map/ppermute | solution.py:270
  56.4 4.3 %collective-permute-done.20.rest_5_ = bf16[192,512]{1,0:T(8,128)(2,1)S(1)} collective-permute-done((bf16[192,512]{1,0:T(8,128)(2,1)S(1)}, bf16[192,512]{1,0:T(8,128)(2,1)S(1)}, u32[]{:S(2)}, u32[]{:S(2)}) %collective-permute-start.20) | collective-permute-done | bytes 196640 | tf_op jit(solution)/shard_map/ppermute | solution.py:270
  60.7 4.0 %collective-permute-done.21.rest_6_ = bf16[192,512]{1,0:T(8,128)(2,1)S(1)} collective-permute-done((bf16[192,512]{1,0:T(8,128)(2,1)S(1)}, bf16[192,512]{1,0:T(8,128)(2,1)S(1)}, u32[]{:S(2)}, u32[]{:S(2)}) %collective-permute-start.21) | collective-permute-done | bytes 196640 | tf_op jit(solution)/shard_map/ppermute | solution.py:270
  64.7 2.9 %finish.1 = bf16[384,1024]{1,0:T(8,128)(2,1)} custom-call(bf16[384,1024]{1,0:T(8,128)(2,1)S(1)} %copy-done.2, f32[384,1024]{1,0:T(8,128)S(1)} %copy-done.1, bf16[384,768]{1,0:T(8,128)(2,1)S(1)} %copy-done.3, f32[1,1024]{1,0:T(1,128)S(1)} %copy-done.5, bf16[1024,1024]{1,0:T(8,128)(2,1)S(1)} %bitcast.4, bf16[192,512]{1,0:T(8,128)(2,1)S(1)} %get-tuple-element.42.rest_0_, ...), custom_call_target="tpu_custom_call" | custom-call | flops 1000000000 | bytes 6623232 | tf_op jit(solution)/shard_map/finish/pallas_call | solution.py:237
  (36 shorter events, 0.1 us)
Async XLA Ops:
  0.0 1.0 %copy-start.4 = (bf16[1,1,128,2048]{3,2,1,0:T(8,128)(2,1)S(1)}, bf16[1,1,128,2048]{3,2,1,0:T(8,128)(2,1)}, u32[]{:S(2)}) copy-start(bf16[1,1,128,2048]{3,2,1,0:T(8,128)(2,1)} %param.10) | copy-start | bytes 1572868
  1.8 13.2 %collective-permute-start.6 = (bf16[128,1024]{1,0:T(8,128)(2,1)}, bf16[128,1024]{1,0:T(8,128)(2,1)}, u32[]{:S(2)}, u32[]{:S(2)}) collective-permute-start(bf16[128,1024]{1,0:T(8,128)(2,1)} %get-tuple-element.39.rest_4_), channel_id=1, source_target_pairs={{0,6},{1,7},{2,4},{3,5},{4,2},{5,3},{6,0},{7,1},{8,14},{9,15},{10,... | collective-permute-start | bytes 786440 | tf_op jit(solution)/shard_map/ppermute | solution.py:264
  6.8 18.6 %collective-permute-start.4 = (bf16[128,1024]{1,0:T(8,128)(2,1)}, bf16[128,1024]{1,0:T(8,128)(2,1)}, u32[]{:S(2)}, u32[]{:S(2)}) collective-permute-start(bf16[128,1024]{1,0:T(8,128)(2,1)} %get-tuple-element.39.rest_4_), channel_id=1, source_target_pairs={{0,2},{1,3},{2,0},{3,1},{4,6},{5,7},{6,4},{7,5},{8,10},{9,11},{10,... | collective-permute-start | bytes 786440 | tf_op jit(solution)/shard_map/ppermute | solution.py:264
  11.5 12.4 %collective-permute-start = (bf16[192,1024]{1,0:T(8,128)(2,1)}, bf16[192,1024]{1,0:T(8,128)(2,1)}, u32[]{:S(2)}, u32[]{:S(2)}) collective-permute-start(bf16[192,1024]{1,0:T(8,128)(2,1)} %get-tuple-element.36), channel_id=1, source_target_pairs={{0,8},{8,0},{16,24},{24,16},{1,9},{9,1},{17,25},{25,17},{2,10},{10... | collective-permute-start | bytes 1179656 | tf_op jit(solution)/shard_map/ppermute | solution.py:270
  13.0 19.0 %collective-permute-start.1 = (bf16[192,1024]{1,0:T(8,128)(2,1)}, bf16[192,1024]{1,0:T(8,128)(2,1)}, u32[]{:S(2)}, u32[]{:S(2)}) collective-permute-start(bf16[192,1024]{1,0:T(8,128)(2,1)} %get-tuple-element.37), channel_id=1, source_target_pairs={{0,16},{8,24},{16,0},{24,8},{1,17},{9,25},{17,1},{25,9},{2,18},{10... | collective-permute-start | bytes 1179656 | tf_op jit(solution)/shard_map/ppermute | solution.py:270
  14.5 17.5 %collective-permute-start.2 = (bf16[192,1024]{1,0:T(8,128)(2,1)}, bf16[192,1024]{1,0:T(8,128)(2,1)}, u32[]{:S(2)}, u32[]{:S(2)}) collective-permute-start(bf16[192,1024]{1,0:T(8,128)(2,1)} %get-tuple-element.38), channel_id=1, source_target_pairs={{0,24},{8,16},{16,8},{24,0},{1,25},{9,17},{17,9},{25,1},{2,26},{10... | collective-permute-start | bytes 1179656 | tf_op jit(solution)/shard_map/ppermute | solution.py:270
  15.0 17.6 %collective-permute-start.7 = (bf16[128,1024]{1,0:T(8,128)(2,1)}, bf16[128,1024]{1,0:T(8,128)(2,1)}, u32[]{:S(2)}, u32[]{:S(2)}) collective-permute-start(bf16[128,1024]{1,0:T(8,128)(2,1)} %collective-permute-done.6.rest_10_), channel_id=1, source_target_pairs={{0,2},{1,3},{2,0},{3,1},{4,6},{5,7},{6,4},{7,5},{8,10},{9,11},{10,... | collective-permute-start | bytes 786440 | tf_op jit(solution)/shard_map/ppermute | solution.py:264
  18.8 17.6 %copy-start.6 = (s32[1,8]{1,0:T(1,128)S(1)}, s32[1,8]{1,0:T(1,128)}, u32[]{:S(2)}) copy-start(s32[1,8]{1,0:T(1,128)} %mask.3) | copy-start | bytes 100
  18.8 17.6 %copy-start.7 = (bf16[192,1024]{1,0:T(8,128)(2,1)S(1)}, bf16[192,1024]{1,0:T(8,128)(2,1)}, u32[]{:S(2)}) copy-start(bf16[192,1024]{1,0:T(8,128)(2,1)} %get-tuple-element.32.rest_0_) | copy-start | bytes 1179652
  23.9 8.8 %collective-permute-start.16 = (bf16[128,1024]{1,0:T(8,128)(2,1)S(1)}, bf16[128,1024]{1,0:T(8,128)(2,1)S(1)}, u32[]{:S(2)}, u32[]{:S(2)}) collective-permute-start(bf16[128,1024]{1,0:T(8,128)(2,1)S(1)} %get-tuple-element.49.rest_4_), channel_id=1, source_target_pairs={{0,6},{1,7},{2,4},{3,5},{4,2},{5,3},{6,0},{7,1},{8,14},{9,15},{10,... | collective-permute-start | bytes 786440 | tf_op jit(solution)/shard_map/ppermute | solution.py:264
  25.4 10.9 %collective-permute-start.3 = (bf16[128,1024]{1,0:T(8,128)(2,1)}, bf16[128,1024]{1,0:T(8,128)(2,1)S(1)}, u32[]{:S(2)}, u32[]{:S(2)}) collective-permute-start(bf16[128,1024]{1,0:T(8,128)(2,1)} %get-tuple-element.39.rest_4_), channel_id=1, source_target_pairs={{0,1},{1,0},{2,3},{3,2},{4,5},{5,4},{6,7},{7,6},{8,9},{9,8},{10,11... | collective-permute-start | bytes 786440 | tf_op jit(solution)/shard_map/ppermute | solution.py:267
  32.0 4.3 %collective-permute-start.5 = (bf16[128,1024]{1,0:T(8,128)(2,1)}, bf16[128,1024]{1,0:T(8,128)(2,1)S(1)}, u32[]{:S(2)}, u32[]{:S(2)}) collective-permute-start(bf16[128,1024]{1,0:T(8,128)(2,1)} %collective-permute-done.4.rest_6_), channel_id=1, source_target_pairs={{0,1},{1,0},{2,3},{3,2},{4,5},{5,4},{6,7},{7,6},{8,9},{9,8},{10,11... | collective-permute-start | bytes 786440 | tf_op jit(solution)/shard_map/ppermute | solution.py:267
  32.1 4.3 %collective-permute-start.9 = (bf16[128,1024]{1,0:T(8,128)(2,1)}, bf16[128,1024]{1,0:T(8,128)(2,1)S(1)}, u32[]{:S(2)}, u32[]{:S(2)}) collective-permute-start(bf16[128,1024]{1,0:T(8,128)(2,1)} %collective-permute-done.6.rest_10_), channel_id=1, source_target_pairs={{0,1},{1,0},{2,3},{3,2},{4,5},{5,4},{6,7},{7,6},{8,9},{9,8},{10,11... | collective-permute-start | bytes 786440 | tf_op jit(solution)/shard_map/ppermute | solution.py:267
  32.6 3.8 %collective-permute-start.8 = (bf16[128,1024]{1,0:T(8,128)(2,1)}, bf16[128,1024]{1,0:T(8,128)(2,1)S(1)}, u32[]{:S(2)}, u32[]{:S(2)}) collective-permute-start(bf16[128,1024]{1,0:T(8,128)(2,1)} %collective-permute-done.7.rest_8_), channel_id=1, source_target_pairs={{0,1},{1,0},{2,3},{3,2},{4,5},{5,4},{6,7},{7,6},{8,9},{9,8},{10,11... | collective-permute-start | bytes 786440 | tf_op jit(solution)/shard_map/ppermute | solution.py:267
  32.6 10.9 %collective-permute-start.14 = (bf16[128,1024]{1,0:T(8,128)(2,1)S(1)}, bf16[128,1024]{1,0:T(8,128)(2,1)S(1)}, u32[]{:S(2)}, u32[]{:S(2)}) collective-permute-start(bf16[128,1024]{1,0:T(8,128)(2,1)S(1)} %get-tuple-element.49.rest_4_), channel_id=1, source_target_pairs={{0,2},{1,3},{2,0},{3,1},{4,6},{5,7},{6,4},{7,5},{8,10},{9,11},{10,... | collective-permute-start | bytes 786440 | tf_op jit(solution)/shard_map/ppermute | solution.py:264
  36.3 10.6 %collective-permute-start.17 = (bf16[128,1024]{1,0:T(8,128)(2,1)S(1)}, bf16[128,1024]{1,0:T(8,128)(2,1)S(1)}, u32[]{:S(2)}, u32[]{:S(2)}) collective-permute-start(bf16[128,1024]{1,0:T(8,128)(2,1)S(1)} %collective-permute-done.16.rest_10_), channel_id=1, source_target_pairs={{0,2},{1,3},{2,0},{3,1},{4,6},{5,7},{6,4},{7,5},{8,10},{9,11},{10,... | collective-permute-start | bytes 786440 | tf_op jit(solution)/shard_map/ppermute | solution.py:264
  39.9 7.0 %collective-permute-start.12 = (bf16[192,512]{1,0:T(8,128)(2,1)S(1)}, bf16[192,512]{1,0:T(8,128)(2,1)S(1)}, u32[]{:S(2)}, u32[]{:S(2)}) collective-permute-start(bf16[192,512]{1,0:T(8,128)(2,1)S(1)} %get-tuple-element.45), channel_id=1, source_target_pairs={{0,24},{8,16},{16,8},{24,0},{1,25},{9,17},{17,9},{25,1},{2,26},{10... | collective-permute-start | bytes 589832 | tf_op jit(solution)/shard_map/ppermute | solution.py:270
  42.4 5.6 %collective-permute-start.13 = (bf16[128,1024]{1,0:T(8,128)(2,1)S(1)}, bf16[128,1024]{1,0:T(8,128)(2,1)S(1)}, u32[]{:S(2)}, u32[]{:S(2)}) collective-permute-start(bf16[128,1024]{1,0:T(8,128)(2,1)S(1)} %get-tuple-element.49.rest_4_), channel_id=1, source_target_pairs={{0,1},{1,0},{2,3},{3,2},{4,5},{5,4},{6,7},{7,6},{8,9},{9,8},{10,11... | collective-permute-start | bytes 786440 | tf_op jit(solution)/shard_map/ppermute | solution.py:267
  42.4 7.2 %collective-permute-start.19 = (bf16[128,1024]{1,0:T(8,128)(2,1)S(1)}, bf16[128,1024]{1,0:T(8,128)(2,1)S(1)}, u32[]{:S(2)}, u32[]{:S(2)}) collective-permute-start(bf16[128,1024]{1,0:T(8,128)(2,1)S(1)} %collective-permute-done.16.rest_10_), channel_id=1, source_target_pairs={{0,1},{1,0},{2,3},{3,2},{4,5},{5,4},{6,7},{7,6},{8,9},{9,8},{10,11... | collective-permute-start | bytes 786440 | tf_op jit(solution)/shard_map/ppermute | solution.py:267
  43.6 6.1 %collective-permute-start.15 = (bf16[128,1024]{1,0:T(8,128)(2,1)S(1)}, bf16[128,1024]{1,0:T(8,128)(2,1)S(1)}, u32[]{:S(2)}, u32[]{:S(2)}) collective-permute-start(bf16[128,1024]{1,0:T(8,128)(2,1)S(1)} %collective-permute-done.14.rest_6_), channel_id=1, source_target_pairs={{0,1},{1,0},{2,3},{3,2},{4,5},{5,4},{6,7},{7,6},{8,9},{9,8},{10,11... | collective-permute-start | bytes 786440 | tf_op jit(solution)/shard_map/ppermute | solution.py:267
  46.9 2.7 %collective-permute-start.18 = (bf16[128,1024]{1,0:T(8,128)(2,1)S(1)}, bf16[128,1024]{1,0:T(8,128)(2,1)S(1)}, u32[]{:S(2)}, u32[]{:S(2)}) collective-permute-start(bf16[128,1024]{1,0:T(8,128)(2,1)S(1)} %collective-permute-done.17.rest_8_), channel_id=1, source_target_pairs={{0,1},{1,0},{2,3},{3,2},{4,5},{5,4},{6,7},{7,6},{8,9},{9,8},{10,11... | collective-permute-start | bytes 786440 | tf_op jit(solution)/shard_map/ppermute | solution.py:267
  46.9 9.5 %collective-permute-start.10 = (bf16[192,512]{1,0:T(8,128)(2,1)S(1)}, bf16[192,512]{1,0:T(8,128)(2,1)S(1)}, u32[]{:S(2)}, u32[]{:S(2)}) collective-permute-start(bf16[192,512]{1,0:T(8,128)(2,1)S(1)} %get-tuple-element.43), channel_id=1, source_target_pairs={{0,8},{8,0},{16,24},{24,16},{1,9},{9,1},{17,25},{25,17},{2,10},{10... | collective-permute-start | bytes 589832 | tf_op jit(solution)/shard_map/ppermute | solution.py:270
  48.0 16.7 %copy-start = (bf16[1,1024,1024]{2,1,0:T(8,128)(2,1)S(1)}, bf16[1,1024,1024]{2,1,0:T(8,128)(2,1)}, u32[]{:S(2)}) copy-start(bf16[1,1024,1024]{2,1,0:T(8,128)(2,1)} %param.15) | copy-start | bytes 6291460
  48.0 16.7 %copy-start.1 = (f32[384,1024]{1,0:T(8,128)S(1)}, f32[384,1024]{1,0:T(8,128)}, u32[]{:S(2)}) copy-start(f32[384,1024]{1,0:T(8,128)} %get-tuple-element.34.gate) | copy-start | bytes 4718596
  48.0 16.7 %copy-start.2 = (bf16[384,1024]{1,0:T(8,128)(2,1)S(1)}, bf16[384,1024]{1,0:T(8,128)(2,1)}, u32[]{:S(2)}) copy-start(bf16[384,1024]{1,0:T(8,128)(2,1)} %feat.1) | copy-start | bytes 2359300
  48.0 16.7 %copy-start.3 = (bf16[384,768]{1,0:T(8,128)(2,1)S(1)}, bf16[384,768]{1,0:T(8,128)(2,1)}, u32[]{:S(2)}) copy-start(bf16[384,768]{1,0:T(8,128)(2,1)} %get-tuple-element.35.pick) | copy-start | bytes 1769476
  48.1 16.7 %copy-start.5 = (f32[1,1024]{1,0:T(1,128)S(1)}, f32[1,1024]{1,0:T(1,128)}, u32[]{:S(2)}) copy-start(f32[1,1024]{1,0:T(1,128)} %gain.1) | copy-start | bytes 12292
  48.1 8.4 %collective-permute-start.11 = (bf16[192,512]{1,0:T(8,128)(2,1)S(1)}, bf16[192,512]{1,0:T(8,128)(2,1)S(1)}, u32[]{:S(2)}, u32[]{:S(2)}) collective-permute-start(bf16[192,512]{1,0:T(8,128)(2,1)S(1)} %get-tuple-element.44), channel_id=1, source_target_pairs={{0,16},{8,24},{16,0},{24,8},{1,17},{9,25},{17,1},{25,9},{2,18},{10... | collective-permute-start | bytes 589832 | tf_op jit(solution)/shard_map/ppermute | solution.py:270
  52.9 7.8 %collective-permute-start.20 = (bf16[192,512]{1,0:T(8,128)(2,1)S(1)}, bf16[192,512]{1,0:T(8,128)(2,1)S(1)}, u32[]{:S(2)}, u32[]{:S(2)}) collective-permute-start(bf16[192,512]{1,0:T(8,128)(2,1)S(1)} %get-tuple-element.52), channel_id=1, source_target_pairs={{0,8},{8,0},{16,24},{24,16},{1,9},{9,1},{17,25},{25,17},{2,10},{10... | collective-permute-start | bytes 589832 | tf_op jit(solution)/shard_map/ppermute | solution.py:270
  53.9 10.8 %collective-permute-start.21 = (bf16[192,512]{1,0:T(8,128)(2,1)S(1)}, bf16[192,512]{1,0:T(8,128)(2,1)S(1)}, u32[]{:S(2)}, u32[]{:S(2)}) collective-permute-start(bf16[192,512]{1,0:T(8,128)(2,1)S(1)} %get-tuple-element.53), channel_id=1, source_target_pairs={{0,16},{8,24},{16,0},{24,8},{1,17},{9,25},{17,1},{25,9},{2,18},{10... | collective-permute-start | bytes 589832 | tf_op jit(solution)/shard_map/ppermute | solution.py:270
  54.7 10.0 %collective-permute-start.22 = (bf16[192,512]{1,0:T(8,128)(2,1)S(1)}, bf16[192,512]{1,0:T(8,128)(2,1)S(1)}, u32[]{:S(2)}, u32[]{:S(2)}) collective-permute-start(bf16[192,512]{1,0:T(8,128)(2,1)S(1)} %get-tuple-element.54), channel_id=1, source_target_pairs={{0,24},{8,16},{16,8},{24,0},{1,25},{9,17},{17,9},{25,1},{2,26},{10... | collective-permute-start | bytes 589832 | tf_op jit(solution)/shard_map/ppermute | solution.py:270

commit v8 on v7

--- a/solution.py
+++ b/solution.py
@@ -9,7 +9,7 @@
 
 BLK = 128
 HEAD = 128
-OPTS = {'chunks': (4, 4), 'order': 0, 'qs': 1, 'cq': 400000000000, 'cg': 400000000000, 'ca': 2000000000, 'cf': 1000000000, 'cp': 0, 'sw': (0, 0), 'p0': [], 'p1': [], 'm1': ['m', 'g'], 'a1': ['a', 'g'], 'g': [], 's0': [['qx'], ['qx'], [], ['qx']], 's1': [[], ['s'], ['rd'], []]}
+OPTS = {'chunks': [4, 4], 'order': 0, 'qs': 1, 'cq': 0, 'cg': 400000000000, 'ca': 2000000000, 'cf': 400000000000, 'cp': 0, 'sw': [0, 0], 'p0': [], 'p1': [], 'm1': ['m', 'a'], 'a1': ['f', 'g'], 'g': [], 's0': [['qx'], [], ['g'], ['g', 'qx']], 's1': [[], ['s'], ['rd'], []]}
 CHUNKS = OPTS['chunks']
 SLICES = 2
 VMEM_LIMIT = 32 * 1024 * 1024
@@ -123,44 +123,36 @@
     gate[...] = project(copies, feat, gain, weights)
 
 
-def pack_kernel(chips, mask, *rest):
-    blocks, out = rest[:-1], rest[-1]
+def attend_kernel(users, chips, first, mask, *rest):
+    queries = rest[:users]
+    blocks = rest[users:users + 2 * chips]
+    outs, (all_q, live_kv, q_sems, kv_sems) = rest[-4 - users:-4], rest[-4:]
+    cap, wide = outs[0].shape
     place = lax.axis_index("ctx")
     core, z = place % 2, place // 2
-    taken = jnp.int32(0)
-    for d, block in enumerate(blocks):
-        live = mask[0, 2 * (z ^ d) + core] > 0
-
-        def take(block=block, taken=taken):
+    fetched, taken = [], jnp.int32(0)
+    for d in range(chips):
+        for swap in range(2):
+            live = mask[0, 2 * (z ^ d) + (core ^ swap)] > 0
             at = pl.multiple_of(taken * BLK, BLK)
-            out[pl.ds(at, BLK), :] = block[...]
-
-        pl.when(live)(take)
-        taken = taken + live.astype(jnp.int32)
-
-
-def attend_kernel(users, chips, mask, *rest):
-    queries, (mine, other) = rest[:users], rest[users:users + 2]
-    outs, (all_q, live_kv) = rest[users + 2:2 * users + 2], rest[2 * users + 2:]
-    cap, wide = outs[0].shape
-    core = lax.axis_index("ctx") % 2
-    count = jnp.int32(0)
-    for z in range(chips):
-        count = count + (mask[0, 2 * z + core] > 0).astype(jnp.int32)
-    for slot in range(chips):
-        at = slice(slot * BLK, (slot + 1) * BLK)
-
-        def from_mine(at=at):
-            live_kv[at, :] = mine[at, :]
-
-        def from_other(at=at, slot=slot):
-            source = pl.multiple_of(jnp.maximum(slot - count, 0) * BLK, BLK)
-            live_kv[at, :] = other[pl.ds(source, BLK), :]
-
-        pl.when(slot < count)(from_mine)
-        pl.when(slot >= count)(from_other)
+            copy = pltpu.make_async_copy(
+                blocks[2 * d + swap], live_kv.at[pl.ds(at, BLK), :], kv_sems.at[2 * d + swap]
+            )
+            pl.when(live)(copy.start)
+            fetched.append((live, copy))
+            taken = jnp.minimum(taken + live.astype(jnp.int32), chips - 1)
+    loads = []
     for i, q in enumerate(queries):
-        all_q[i * cap:(i + 1) * cap, :] = q[...]
+        loads.append(
+            pltpu.make_async_copy(
+                q.at[:, pl.ds(first, wide)], all_q.at[pl.ds(i * cap, cap), :], q_sems.at[i]
+            )
+        )
+        loads[-1].start()
+    for live, copy in fetched:
+        pl.when(live)(copy.wait)
+    for load in loads:
+        load.wait()
     scale = 0.5 * HEAD ** (-0.5)
     for head in range(wide // HEAD):
         cols = slice(head * HEAD, (head + 1) * HEAD)
@@ -175,57 +167,48 @@
             out[:, cols] = got[i * cap:(i + 1) * cap, :]
 
 
-def attend_blocks_kernel(users, chips, mask, *rest):
-    queries = rest[:users]
-    blocks = rest[users:users + 2 * chips]
-    outs, (all_q, live_kv) = rest[-2 - users:-2], rest[-2:]
-    place = lax.axis_index("ctx")
-    core, z = place % 2, place // 2
-    cap, wide = outs[0].shape
-    taken = jnp.int32(0)
-    for d in range(chips):
-        for swap in range(2):
-            live = mask[0, 2 * (z ^ d) + (core ^ swap)] > 0
-
-            def take(block=blocks[2 * d + swap], taken=taken):
-                at = pl.multiple_of(taken * BLK, BLK)
-                live_kv[pl.ds(at, BLK), :] = block[...]
-
-            pl.when(live)(take)
-            taken = jnp.minimum(taken + live.astype(jnp.int32), chips - 1)
-    for i, q in enumerate(queries):
-        all_q[i * cap:(i + 1) * cap, :] = q[...]
-    scale = 0.5 * HEAD ** (-0.5)
-    for head in range(wide // HEAD):
-        cols = slice(head * HEAD, (head + 1) * HEAD)
-        keys = live_kv[:, cols]
-        values = live_kv[:, wide + head * HEAD:wide + (head + 1) * HEAD]
-        scores = lax.dot_general(
-            all_q[:, cols], keys, (((1,), (1,)), ((), ())), preferred_element_type=jnp.float32
-        )
-        weight = silu_halved(scores * scale).astype(jnp.bfloat16)
-        got = jnp.dot(weight, values, preferred_element_type=jnp.float32).astype(jnp.bfloat16)
-        for i, out in enumerate(outs):
-            out[:, cols] = got[i * cap:(i + 1) * cap, :]
-
-
-def finish_kernel(users, feat, gate, pick, gain, w_out, *rest):
-    parts, out, back = rest[:-2], rest[-2], rest[-1]
-    first = 0
+def finish_kernel(users, feat_in, gate_in, pick_in, gain_in, w_in, *rest):
+    parts, out = rest[:-8], rest[-8]
+    back, pick, gate, gain, weights, feat, sems = rest[-7:]
+    loads, first = [], 0
     for chunk in range(len(parts) // users):
         cap, wide = parts[chunk * users].shape
         for d in range(users):
-            part = parts[chunk * users + d]
-            back[d * cap:(d + 1) * cap, first:first + wide] = part[...]
+            loads.append(
+                pltpu.make_async_copy(
+                    parts[chunk * users + d],
+                    back.at[pl.ds(d * cap, cap), pl.ds(first, wide)],
+                    sems.at[5 + chunk * users + d],
+                )
+            )
         first += wide
+    loads.append(pltpu.make_async_copy(pick_in, pick, sems.at[0]))
+    gains = [
+        pltpu.make_async_copy(gate_in, gate, sems.at[1]),
+        pltpu.make_async_copy(gain_in, gain, sems.at[2]),
+    ]
+    ends = [
+        pltpu.make_async_copy(w_in, weights, sems.at[3]),
+        pltpu.make_async_copy(feat_in, feat, sems.at[4]),
+    ]
+    for copy in loads + gains + ends:
+        copy.start()
+    for copy in loads:
+        copy.wait()
     attended = jnp.dot(pick[...], back[...], preferred_element_type=jnp.float32)
-    mixed = (centred_norm(attended) * gain[...] * gate[...]).astype(jnp.bfloat16)
-    grown = jnp.dot(mixed, w_out[...], preferred_element_type=jnp.float32)
+    normed = centred_norm(attended)
+    for copy in gains:
+        copy.wait()
+    mixed = (normed * gain[...] * gate[...]).astype(jnp.bfloat16)
+    for copy in ends:
+        copy.wait()
+    grown = jnp.dot(mixed, weights[...], preferred_element_type=jnp.float32)
     out[...] = (feat[...].astype(jnp.float32) + grown).astype(jnp.bfloat16)
 
 
 SMEM = pl.BlockSpec(memory_space=pltpu.SMEM)
 HBM = pl.BlockSpec(memory_space=pltpu.HBM)
+ANY = pl.BlockSpec(memory_space=pl.ANY)
 
 
 def whole(*dims, at=None):
@@ -333,25 +316,20 @@
                 gated(cand_feat, ['q'] + OPTS['g']), user_row, gain_in, w_uq[0], vmem=VMEM_MOST,
             )
             env['g'] = gate
-        if OPTS['sw'][chunk]:
-            keys = OPTS['p0'] if chunk == 0 else OPTS['p1']
-            packed, = call(
-                functools.partial(pack_kernel, chips), "pack",
-                [SMEM] + [whole(BLK, 2 * wide)] * chips,
-                [shape(chips * BLK, 2 * wide)], [], OPTS['cp'],
-                hist_mask, gated(held[0], keys), *[held[d] for d in range(1, chips)],
-            )
-            blocks, kernel = [packed, over_cores(packed)], attend_kernel
-        else:
-            blocks, kernel = [], attend_blocks_kernel
-            for d in range(chips):
-                keys = OPTS['s0' if chunk == 0 else 's1'][d % 4]
-                blocks += [held[d], over_cores(gated(held[d], keys))]
+        blocks = []
+        for d in range(chips):
+            keys = OPTS['s0' if chunk == 0 else 's1'][d % 4]
+            blocks += [held[d], over_cores(gated(held[d], keys))]
         scored = call(
-            functools.partial(kernel, users, chips), "attend",
-            [SMEM] + [whole(cap, wide, at=(0, chunk))] * users + [whole(*block.shape) for block in blocks],
+            functools.partial(attend_kernel, users, chips, first), "attend",
+            [SMEM] + [ANY] * (users + 2 * chips),
             [shape(cap, wide)] * users,
-            [pltpu.VMEM((users * cap, wide), bf16), pltpu.VMEM((chips * BLK, 2 * wide), bf16)],
+            [
+                pltpu.VMEM((users * cap, wide), bf16),
+                pltpu.VMEM((chips * BLK, 2 * wide), bf16),
+                pltpu.SemaphoreType.DMA((users,)),
+                pltpu.SemaphoreType.DMA((2 * chips,)),
+            ],
             OPTS['ca'],
             hist_mask, *arrived, *blocks,
         )
@@ -362,14 +340,18 @@
 
     return call(
         functools.partial(finish_kernel, users), "finish",
+        [ANY] * (5 + len(returned)),
+        [shape(rows, width)],
         [
-            whole(rows, width), whole(rows, width), whole(rows, users * cap), whole(1, width),
-            whole(width, width),
-        ]
-        + [whole(*part.shape) for part in returned],
-        [shape(rows, width)],
-        [pltpu.VMEM((users * cap, width), bf16)],
-        OPTS["cf"],
+            pltpu.VMEM((users * cap, width), bf16),
+            pltpu.VMEM((rows, users * cap), bf16),
+            pltpu.VMEM((rows, width), jnp.float32),
+            pltpu.VMEM((1, width), jnp.float32),
+            pltpu.VMEM((width, width), bf16),
+            pltpu.VMEM((rows, width), bf16),
+            pltpu.SemaphoreType.DMA((5 + len(returned),)),
+        ],
+        OPTS['cf'],
         cand_feat, gate, pick, gain_attn, w_out[0], *returned,
     )[0]
 

time: 67.9 us -> 69.5 us (1.024)
  Pallas kernels: 19 us -> 21.4 us
  waiting for transfers between devices: 19.9 us -> 17.5 us
  starting transfers between devices: 27.5 us -> 28.9 us
    pallas_call x5, Pallas kernels: 14.4 us -> 16.8 us  [call(): pl.pallas_call(kernel, name=name, grid=(1,), in_specs=in_specs, out_specs...]
    ppermute x9, waiting for transfers between devices: 15.9 us -> 13.9 us  [to_user(): return lax.ppermute(value, 'users', [(u, u ^ d) for u in range(users)])]
  transfers between devices with their start and end apart: 23 -> 23, of which waited for: 6 -> 4; matrix products, arithmetic and copies ran while one was open for 0% -> 0% of each run, Pallas kernels for 23% -> 24%
where the time goes in v8:
time: 69.5 us; the launch traced here: 69.2 us
  starting transfers between devices  28.9 us (42%)
  Pallas kernels  21.4 us (31%)
  waiting for transfers between devices  17.5 us (25%)
  local copies, waits for them, and re-layouts  1.07 us (2%)
    pallas_call x5, Pallas kernels, call(): pl.pallas_call(kernel, name=name, grid=(1,), in_specs=in_specs, out_specs...  16.8 us
    ppermute x6, starting transfers between devices, over_z(): return lax.ppermute(value, 'ctx', [(c, c ^ 2 * d) for c in range(ctx)])  14.7 us
    ppermute x9, waiting for transfers between devices, to_user(): return lax.ppermute(value, 'users', [(u, u ^ d) for u in range(users)])  13.9 us
    ppermute x9, starting transfers between devices, to_user(): return lax.ppermute(value, 'users', [(u, u ^ d) for u in range(users)])  12.7 us
    pallas_call x1, Pallas kernels, on_device(): pl.pallas_call(functools.partial(query_kernel, cap, users), name='query',...  4.61 us
    ppermute x6, waiting for transfers between devices, over_z(): return lax.ppermute(value, 'ctx', [(c, c ^ 2 * d) for c in range(ctx)])  3.64 us
    ppermute x8, starting transfers between devices, over_cores(): return lax.ppermute(value, 'ctx', [(c, c ^ 1) for c in range(ctx)])  1.54 us
  transfers between devices with their start and end apart: 23, of which 4 were waited for; matrix products, arithmetic and copies ran while one was open for 0% of the time, Pallas kernels for 24%

profile of v8, /device:TPU:0, one launch (start us, length us, event | category | flops | bytes accessed | tf_op | source)
XLA Modules:
  0.0 69.2 jit_solution(8753620357093519508)
XLA Ops:
  0.0 1.0 %copy-done.1 = bf16[1,1,128,2048]{3,2,1,0:T(8,128)(2,1)S(1)} copy-done((bf16[1,1,128,2048]{3,2,1,0:T(8,128)(2,1)S(1)}, bf16[1,1,128,2048]{3,2,1,0:T(8,128)(2,1)}, u32[]{:S(2)}) %copy-start.1) | copy-done | bytes 524312
  1.0 0.7 %kv_split.1 = (bf16[128,1024]{1,0:T(8,128)(2,1)}, bf16[128,1024]{1,0:T(8,128)(2,1)S(1)}) custom-call(bf16[128,2048]{1,0:T(8,128)(2,1)S(1)} %bitcast.4), custom_call_target="tpu_custom_call" | custom-call | tf_op jit(solution)/shard_map/kv_split/pallas_call | solution.py:220
  1.8 5.0 %collective-permute-start.6 = (bf16[128,1024]{1,0:T(8,128)(2,1)}, bf16[128,1024]{1,0:T(8,128)(2,1)}, u32[]{:S(2)}, u32[]{:S(2)}) collective-permute-start(bf16[128,1024]{1,0:T(8,128)(2,1)} %get-tuple-element.39.rest_4_), channel_id=1, source_target_pairs={{0,6},{1,7},{2,4},{3,5},{4,2},{5,3},{6,0},{7,1},{8,14},{9,15},{10,... | collective-permute-start | bytes 786440 | tf_op jit(solution)/shard_map/ppermute | solution.py:247
  6.8 0.0 collective-permute-start.4
  6.8 4.6 %query.1 = (bf16[192,1024]{1,0:T(8,128)(2,1)}, bf16[192,1024]{1,0:T(8,128)(2,1)}, bf16[192,1024]{1,0:T(8,128)(2,1)}, bf16[192,1024]{1,0:T(8,128)(2,1)}) custom-call(bf16[384,1024]{1,0:T(8,128)(2,1)} %feat_in.3, s32[1,384]{1,0:T(1,128)} %bitcast.8, f32[1,1024]{1,0:T(1,128)} %gain_in.4, bf16[1024,2048]{1,0:T(8,128)(2,1)} %bitcast.6), custom_call_target="tpu_custom_call" | custom-call | tf_op jit(solution)/shard_map/query/pallas_call | solution.py:276
  11.5 1.6 %collective-permute-start = (bf16[192,1024]{1,0:T(8,128)(2,1)}, bf16[192,1024]{1,0:T(8,128)(2,1)}, u32[]{:S(2)}, u32[]{:S(2)}) collective-permute-start(bf16[192,1024]{1,0:T(8,128)(2,1)} %get-tuple-element.36), channel_id=1, source_target_pairs={{0,8},{8,0},{16,24},{24,16},{1,9},{9,1},{17,25},{25,17},{2,10},{10... | collective-permute-start | bytes 1179656 | tf_op jit(solution)/shard_map/ppermute | solution.py:253
  13.0 1.5 %collective-permute-start.1 = (bf16[192,1024]{1,0:T(8,128)(2,1)}, bf16[192,1024]{1,0:T(8,128)(2,1)}, u32[]{:S(2)}, u32[]{:S(2)}) collective-permute-start(bf16[192,1024]{1,0:T(8,128)(2,1)} %get-tuple-element.37), channel_id=1, source_target_pairs={{0,16},{8,24},{16,0},{24,8},{1,17},{9,25},{17,1},{25,9},{2,18},{10... | collective-permute-start | bytes 1179656 | tf_op jit(solution)/shard_map/ppermute | solution.py:253
  14.5 0.5 collective-permute-start.2
  15.0 3.8 %collective-permute-start.7 = (bf16[128,1024]{1,0:T(8,128)(2,1)}, bf16[128,1024]{1,0:T(8,128)(2,1)}, u32[]{:S(2)}, u32[]{:S(2)}) collective-permute-start(bf16[128,1024]{1,0:T(8,128)(2,1)} %collective-permute-done.6.rest_10_), channel_id=1, source_target_pairs={{0,2},{1,3},{2,0},{3,1},{4,6},{5,7},{6,4},{7,5},{8,10},{9,11},{10,... | collective-permute-start | bytes 786440 | tf_op jit(solution)/shard_map/ppermute | solution.py:247
  18.8 4.1 %gate.1 = (f32[384,1024]{1,0:T(8,128)}, bf16[384,768]{1,0:T(8,128)(2,1)}) custom-call(bf16[384,1024]{1,0:T(8,128)(2,1)} %feat_in.3, s32[1,384]{1,0:T(1,128)} %bitcast.9, f32[1,1024]{1,0:T(1,128)} %gain_in.4, bf16[1024,2048]{1,0:T(8,128)(2,1)} %bitcast.7), custom_call_target="tpu_custom_call" | custom-call | flops 399999991808 | bytes 4986368 | tf_op jit(solution)/shard_map/gate/pallas_call | solution.py:220
  22.9 0.0 collective-permute-done.4.rest_6_
  22.9 2.5 %collective-permute-start.16 = (bf16[128,1024]{1,0:T(8,128)(2,1)S(1)}, bf16[128,1024]{1,0:T(8,128)(2,1)S(1)}, u32[]{:S(2)}, u32[]{:S(2)}) collective-permute-start(bf16[128,1024]{1,0:T(8,128)(2,1)S(1)} %get-tuple-element.49.rest_4_), channel_id=1, source_target_pairs={{0,6},{1,7},{2,4},{3,5},{4,2},{5,3},{6,0},{7,1},{8,14},{9,15},{10,... | collective-permute-start | bytes 786440 | tf_op jit(solution)/shard_map/ppermute | solution.py:247
  25.5 0.5 collective-permute-start.3
  26.0 6.1 %collective-permute-done.1.rest_2_ = bf16[192,1024]{1,0:T(8,128)(2,1)} collective-permute-done((bf16[192,1024]{1,0:T(8,128)(2,1)}, bf16[192,1024]{1,0:T(8,128)(2,1)}, u32[]{:S(2)}, u32[]{:S(2)}) %collective-permute-start.1) | collective-permute-done | bytes 393248 | tf_op jit(solution)/shard_map/ppermute | solution.py:253
  32.1 0.5 collective-permute-start.8
  32.6 1.7 %collective-permute-start.14 = (bf16[128,1024]{1,0:T(8,128)(2,1)S(1)}, bf16[128,1024]{1,0:T(8,128)(2,1)S(1)}, u32[]{:S(2)}, u32[]{:S(2)}) collective-permute-start(bf16[128,1024]{1,0:T(8,128)(2,1)S(1)} %get-tuple-element.49.rest_4_), channel_id=1, source_target_pairs={{0,2},{1,3},{2,0},{3,1},{4,6},{5,7},{6,4},{7,5},{8,10},{9,11},{10,... | collective-permute-start | bytes 786440 | tf_op jit(solution)/shard_map/ppermute | solution.py:247
  34.3 1.6 %collective-permute-start.17 = (bf16[128,1024]{1,0:T(8,128)(2,1)S(1)}, bf16[128,1024]{1,0:T(8,128)(2,1)S(1)}, u32[]{:S(2)}, u32[]{:S(2)}) collective-permute-start(bf16[128,1024]{1,0:T(8,128)(2,1)S(1)} %collective-permute-done.16.rest_10_), channel_id=1, source_target_pairs={{0,2},{1,3},{2,0},{3,1},{4,6},{5,7},{6,4},{7,5},{8,10},{9,11},{10,... | collective-permute-start | bytes 786440 | tf_op jit(solution)/shard_map/ppermute | solution.py:247
  36.0 3.8 %attend.2 = (bf16[192,512]{1,0:T(8,128)(2,1)S(1)}, bf16[192,512]{1,0:T(8,128)(2,1)S(1)}, bf16[192,512]{1,0:T(8,128)(2,1)S(1)}, bf16[192,512]{1,0:T(8,128)(2,1)S(1)}) custom-call(s32[1,8]{1,0:T(1,128)S(1)} %copy-done.5, bf16[192,1024]{1,0:T(8,128)(2,1)S(1)} %copy-done.3, bf16[192,1024]{1,0:T(8,128)(2,1)} %collective-permute-done.rest_1_, ...), custom_call_target="tpu_custom_call" | custom-call | flops 2000000000 | bytes 3670048 | tf_op jit(solution)/shard_map/attend/pallas_call | solution.py:220
  39.8 2.5 %collective-permute-start.12 = (bf16[192,512]{1,0:T(8,128)(2,1)S(1)}, bf16[192,512]{1,0:T(8,128)(2,1)S(1)}, u32[]{:S(2)}, u32[]{:S(2)}) collective-permute-start(bf16[192,512]{1,0:T(8,128)(2,1)S(1)} %get-tuple-element.45), channel_id=1, source_target_pairs={{0,24},{8,16},{16,8},{24,0},{1,25},{9,17},{17,9},{25,1},{2,26},{10... | collective-permute-start | bytes 589832 | tf_op jit(solution)/shard_map/ppermute | solution.py:253
  42.3 0.5 collective-permute-start.19
  42.8 0.0 collective-permute-start.15
  42.8 3.6 %collective-permute-done.17.rest_8_ = bf16[128,1024]{1,0:T(8,128)(2,1)S(1)} collective-permute-done((bf16[128,1024]{1,0:T(8,128)(2,1)S(1)}, bf16[128,1024]{1,0:T(8,128)(2,1)S(1)}, u32[]{:S(2)}, u32[]{:S(2)}) %collective-permute-start.17) | collective-permute-done | bytes 262176 | tf_op jit(solution)/shard_map/ppermute | solution.py:247
  46.5 1.5 %collective-permute-start.10 = (bf16[192,512]{1,0:T(8,128)(2,1)S(1)}, bf16[192,512]{1,0:T(8,128)(2,1)S(1)}, u32[]{:S(2)}, u32[]{:S(2)}) collective-permute-start(bf16[192,512]{1,0:T(8,128)(2,1)S(1)} %get-tuple-element.43), channel_id=1, source_target_pairs={{0,8},{8,0},{16,24},{24,16},{1,9},{9,1},{17,25},{25,17},{2,10},{10... | collective-permute-start | bytes 589832 | tf_op jit(solution)/shard_map/ppermute | solution.py:253
  48.0 0.0 copy-start.7
  48.0 1.6 %collective-permute-start.11 = (bf16[192,512]{1,0:T(8,128)(2,1)S(1)}, bf16[192,512]{1,0:T(8,128)(2,1)S(1)}, u32[]{:S(2)}, u32[]{:S(2)}) collective-permute-start(bf16[192,512]{1,0:T(8,128)(2,1)S(1)} %get-tuple-element.44), channel_id=1, source_target_pairs={{0,16},{8,24},{16,0},{24,8},{1,17},{9,25},{17,1},{25,9},{2,18},{10... | collective-permute-start | bytes 589832 | tf_op jit(solution)/shard_map/ppermute | solution.py:253
  49.6 4.1 %attend.3 = (bf16[192,512]{1,0:T(8,128)(2,1)S(1)}, bf16[192,512]{1,0:T(8,128)(2,1)S(1)}, bf16[192,512]{1,0:T(8,128)(2,1)S(1)}, bf16[192,512]{1,0:T(8,128)(2,1)S(1)}) custom-call(s32[1,8]{1,0:T(1,128)S(1)} %copy-done.5, bf16[192,1024]{1,0:T(8,128)(2,1)S(1)} %copy-done.3, bf16[192,1024]{1,0:T(8,128)(2,1)} %collective-permute-done.rest_1_, ...), custom_call_target="tpu_custom_call" | custom-call | flops 2000000000 | bytes 3670048 | tf_op jit(solution)/shard_map/attend/pallas_call | solution.py:220
  53.6 0.6 collective-permute-start.20
  54.3 0.8 %collective-permute-start.21 = (bf16[192,512]{1,0:T(8,128)(2,1)S(1)}, bf16[192,512]{1,0:T(8,128)(2,1)S(1)}, u32[]{:S(2)}, u32[]{:S(2)}) collective-permute-start(bf16[192,512]{1,0:T(8,128)(2,1)S(1)} %get-tuple-element.53), channel_id=1, source_target_pairs={{0,16},{8,24},{16,0},{24,8},{1,17},{9,25},{17,1},{25,9},{2,18},{10... | collective-permute-start | bytes 589832 | tf_op jit(solution)/shard_map/ppermute | solution.py:253
  55.1 2.1 %collective-permute-start.22 = (bf16[192,512]{1,0:T(8,128)(2,1)S(1)}, bf16[192,512]{1,0:T(8,128)(2,1)S(1)}, u32[]{:S(2)}, u32[]{:S(2)}) collective-permute-start(bf16[192,512]{1,0:T(8,128)(2,1)S(1)} %get-tuple-element.54), channel_id=1, source_target_pairs={{0,24},{8,16},{16,8},{24,0},{1,25},{9,17},{17,9},{25,1},{2,26},{10... | collective-permute-start | bytes 589832 | tf_op jit(solution)/shard_map/ppermute | solution.py:253
  57.2 4.3 %collective-permute-done.20.rest_5_ = bf16[192,512]{1,0:T(8,128)(2,1)S(1)} collective-permute-done((bf16[192,512]{1,0:T(8,128)(2,1)S(1)}, bf16[192,512]{1,0:T(8,128)(2,1)S(1)}, u32[]{:S(2)}, u32[]{:S(2)}) %collective-permute-start.20) | collective-permute-done | bytes 196640 | tf_op jit(solution)/shard_map/ppermute | solution.py:253
  61.5 3.5 %collective-permute-done.22.rest_7_ = bf16[192,512]{1,0:T(8,128)(2,1)S(1)} collective-permute-done((bf16[192,512]{1,0:T(8,128)(2,1)S(1)}, bf16[192,512]{1,0:T(8,128)(2,1)S(1)}, u32[]{:S(2)}, u32[]{:S(2)}) %collective-permute-start.22) | collective-permute-done | bytes 196640 | tf_op jit(solution)/shard_map/ppermute | solution.py:253
  65.0 4.1 %finish.1 = bf16[384,1024]{1,0:T(8,128)(2,1)} custom-call(bf16[384,1024]{1,0:T(8,128)(2,1)S(1)} %copy-done, f32[384,1024]{1,0:T(8,128)S(1)} %copy-done.6, bf16[384,768]{1,0:T(8,128)(2,1)S(1)} %copy-done.7, f32[1,1024]{1,0:T(1,128)S(1)} %copy-done.4, bf16[1024,1024]{1,0:T(8,128)(2,1)S(1)} %bitcast.5, bf16[192,512]{1,0:T(8,128)(2,1)S(1)} %get-tuple-element.42.rest_0_, ...), custom_call_target="tpu_custom_call" | custom-call | flops 399999991808 | bytes 6623232 | tf_op jit(solution)/shard_map/finish/pallas_call | solution.py:220
  (36 shorter events, 0.1 us)
Async XLA Ops:
  0.0 1.0 %copy-start.1 = (bf16[1,1,128,2048]{3,2,1,0:T(8,128)(2,1)S(1)}, bf16[1,1,128,2048]{3,2,1,0:T(8,128)(2,1)}, u32[]{:S(2)}) copy-start(bf16[1,1,128,2048]{3,2,1,0:T(8,128)(2,1)} %param.10) | copy-start | bytes 1572868
  1.8 13.2 %collective-permute-start.6 = (bf16[128,1024]{1,0:T(8,128)(2,1)}, bf16[128,1024]{1,0:T(8,128)(2,1)}, u32[]{:S(2)}, u32[]{:S(2)}) collective-permute-start(bf16[128,1024]{1,0:T(8,128)(2,1)} %get-tuple-element.39.rest_4_), channel_id=1, source_target_pairs={{0,6},{1,7},{2,4},{3,5},{4,2},{5,3},{6,0},{7,1},{8,14},{9,15},{10,... | collective-permute-start | bytes 786440 | tf_op jit(solution)/shard_map/ppermute | solution.py:247
  6.8 16.1 %collective-permute-start.4 = (bf16[128,1024]{1,0:T(8,128)(2,1)}, bf16[128,1024]{1,0:T(8,128)(2,1)}, u32[]{:S(2)}, u32[]{:S(2)}) collective-permute-start(bf16[128,1024]{1,0:T(8,128)(2,1)} %get-tuple-element.39.rest_4_), channel_id=1, source_target_pairs={{0,2},{1,3},{2,0},{3,1},{4,6},{5,7},{6,4},{7,5},{8,10},{9,11},{10,... | collective-permute-start | bytes 786440 | tf_op jit(solution)/shard_map/ppermute | solution.py:247
  11.5 14.0 %collective-permute-start = (bf16[192,1024]{1,0:T(8,128)(2,1)}, bf16[192,1024]{1,0:T(8,128)(2,1)}, u32[]{:S(2)}, u32[]{:S(2)}) collective-permute-start(bf16[192,1024]{1,0:T(8,128)(2,1)} %get-tuple-element.36), channel_id=1, source_target_pairs={{0,8},{8,0},{16,24},{24,16},{1,9},{9,1},{17,25},{25,17},{2,10},{10... | collective-permute-start | bytes 1179656 | tf_op jit(solution)/shard_map/ppermute | solution.py:253
  13.0 19.0 %collective-permute-start.1 = (bf16[192,1024]{1,0:T(8,128)(2,1)}, bf16[192,1024]{1,0:T(8,128)(2,1)}, u32[]{:S(2)}, u32[]{:S(2)}) collective-permute-start(bf16[192,1024]{1,0:T(8,128)(2,1)} %get-tuple-element.37), channel_id=1, source_target_pairs={{0,16},{8,24},{16,0},{24,8},{1,17},{9,25},{17,1},{25,9},{2,18},{10... | collective-permute-start | bytes 1179656 | tf_op jit(solution)/shard_map/ppermute | solution.py:253
  14.5 17.5 %collective-permute-start.2 = (bf16[192,1024]{1,0:T(8,128)(2,1)}, bf16[192,1024]{1,0:T(8,128)(2,1)}, u32[]{:S(2)}, u32[]{:S(2)}) collective-permute-start(bf16[192,1024]{1,0:T(8,128)(2,1)} %get-tuple-element.38), channel_id=1, source_target_pairs={{0,24},{8,16},{16,8},{24,0},{1,25},{9,17},{17,9},{25,1},{2,26},{10... | collective-permute-start | bytes 1179656 | tf_op jit(solution)/shard_map/ppermute | solution.py:253
  15.0 10.4 %collective-permute-start.7 = (bf16[128,1024]{1,0:T(8,128)(2,1)}, bf16[128,1024]{1,0:T(8,128)(2,1)}, u32[]{:S(2)}, u32[]{:S(2)}) collective-permute-start(bf16[128,1024]{1,0:T(8,128)(2,1)} %collective-permute-done.6.rest_10_), channel_id=1, source_target_pairs={{0,2},{1,3},{2,0},{3,1},{4,6},{5,7},{6,4},{7,5},{8,10},{9,11},{10,... | collective-permute-start | bytes 786440 | tf_op jit(solution)/shard_map/ppermute | solution.py:247
  18.8 17.2 %copy-start.3 = (bf16[192,1024]{1,0:T(8,128)(2,1)S(1)}, bf16[192,1024]{1,0:T(8,128)(2,1)}, u32[]{:S(2)}) copy-start(bf16[192,1024]{1,0:T(8,128)(2,1)} %get-tuple-element.32.rest_0_) | copy-start | bytes 1179652
  18.8 17.2 %copy-start.5 = (s32[1,8]{1,0:T(1,128)S(1)}, s32[1,8]{1,0:T(1,128)}, u32[]{:S(2)}) copy-start(s32[1,8]{1,0:T(1,128)} %mask.3) | copy-start | bytes 100
  22.9 11.4 %collective-permute-start.16 = (bf16[128,1024]{1,0:T(8,128)(2,1)S(1)}, bf16[128,1024]{1,0:T(8,128)(2,1)S(1)}, u32[]{:S(2)}, u32[]{:S(2)}) collective-permute-start(bf16[128,1024]{1,0:T(8,128)(2,1)S(1)} %get-tuple-element.49.rest_4_), channel_id=1, source_target_pairs={{0,6},{1,7},{2,4},{3,5},{4,2},{5,3},{6,0},{7,1},{8,14},{9,15},{10,... | collective-permute-start | bytes 786440 | tf_op jit(solution)/shard_map/ppermute | solution.py:247
  25.5 7.1 %collective-permute-start.5 = (bf16[128,1024]{1,0:T(8,128)(2,1)}, bf16[128,1024]{1,0:T(8,128)(2,1)S(1)}, u32[]{:S(2)}, u32[]{:S(2)}) collective-permute-start(bf16[128,1024]{1,0:T(8,128)(2,1)} %collective-permute-done.4.rest_6_), channel_id=1, source_target_pairs={{0,1},{1,0},{2,3},{3,2},{4,5},{5,4},{6,7},{7,6},{8,9},{9,8},{10,11... | collective-permute-start | bytes 786440 | tf_op jit(solution)/shard_map/ppermute | solution.py:250
  25.5 10.5 %collective-permute-start.3 = (bf16[128,1024]{1,0:T(8,128)(2,1)}, bf16[128,1024]{1,0:T(8,128)(2,1)S(1)}, u32[]{:S(2)}, u32[]{:S(2)}) collective-permute-start(bf16[128,1024]{1,0:T(8,128)(2,1)} %get-tuple-element.39.rest_4_), channel_id=1, source_target_pairs={{0,1},{1,0},{2,3},{3,2},{4,5},{5,4},{6,7},{7,6},{8,9},{9,8},{10,11... | collective-permute-start | bytes 786440 | tf_op jit(solution)/shard_map/ppermute | solution.py:250
  32.1 3.9 %collective-permute-start.9 = (bf16[128,1024]{1,0:T(8,128)(2,1)}, bf16[128,1024]{1,0:T(8,128)(2,1)S(1)}, u32[]{:S(2)}, u32[]{:S(2)}) collective-permute-start(bf16[128,1024]{1,0:T(8,128)(2,1)} %collective-permute-done.6.rest_10_), channel_id=1, source_target_pairs={{0,1},{1,0},{2,3},{3,2},{4,5},{5,4},{6,7},{7,6},{8,9},{9,8},{10,11... | collective-permute-start | bytes 786440 | tf_op jit(solution)/shard_map/ppermute | solution.py:250
  32.1 3.9 %collective-permute-start.8 = (bf16[128,1024]{1,0:T(8,128)(2,1)}, bf16[128,1024]{1,0:T(8,128)(2,1)S(1)}, u32[]{:S(2)}, u32[]{:S(2)}) collective-permute-start(bf16[128,1024]{1,0:T(8,128)(2,1)} %collective-permute-done.7.rest_8_), channel_id=1, source_target_pairs={{0,1},{1,0},{2,3},{3,2},{4,5},{5,4},{6,7},{7,6},{8,9},{9,8},{10,11... | collective-permute-start | bytes 786440 | tf_op jit(solution)/shard_map/ppermute | solution.py:250
  32.6 10.3 %collective-permute-start.14 = (bf16[128,1024]{1,0:T(8,128)(2,1)S(1)}, bf16[128,1024]{1,0:T(8,128)(2,1)S(1)}, u32[]{:S(2)}, u32[]{:S(2)}) collective-permute-start(bf16[128,1024]{1,0:T(8,128)(2,1)S(1)} %get-tuple-element.49.rest_4_), channel_id=1, source_target_pairs={{0,2},{1,3},{2,0},{3,1},{4,6},{5,7},{6,4},{7,5},{8,10},{9,11},{10,... | collective-permute-start | bytes 786440 | tf_op jit(solution)/shard_map/ppermute | solution.py:247
  34.3 12.2 %collective-permute-start.17 = (bf16[128,1024]{1,0:T(8,128)(2,1)S(1)}, bf16[128,1024]{1,0:T(8,128)(2,1)S(1)}, u32[]{:S(2)}, u32[]{:S(2)}) collective-permute-start(bf16[128,1024]{1,0:T(8,128)(2,1)S(1)} %collective-permute-done.16.rest_10_), channel_id=1, source_target_pairs={{0,2},{1,3},{2,0},{3,1},{4,6},{5,7},{6,4},{7,5},{8,10},{9,11},{10,... | collective-permute-start | bytes 786440 | tf_op jit(solution)/shard_map/ppermute | solution.py:247
  39.8 6.7 %collective-permute-start.12 = (bf16[192,512]{1,0:T(8,128)(2,1)S(1)}, bf16[192,512]{1,0:T(8,128)(2,1)S(1)}, u32[]{:S(2)}, u32[]{:S(2)}) collective-permute-start(bf16[192,512]{1,0:T(8,128)(2,1)S(1)} %get-tuple-element.45), channel_id=1, source_target_pairs={{0,24},{8,16},{16,8},{24,0},{1,25},{9,17},{17,9},{25,1},{2,26},{10... | collective-permute-start | bytes 589832 | tf_op jit(solution)/shard_map/ppermute | solution.py:253
  42.3 5.6 %collective-permute-start.13 = (bf16[128,1024]{1,0:T(8,128)(2,1)S(1)}, bf16[128,1024]{1,0:T(8,128)(2,1)S(1)}, u32[]{:S(2)}, u32[]{:S(2)}) collective-permute-start(bf16[128,1024]{1,0:T(8,128)(2,1)S(1)} %get-tuple-element.49.rest_4_), channel_id=1, source_target_pairs={{0,1},{1,0},{2,3},{3,2},{4,5},{5,4},{6,7},{7,6},{8,9},{9,8},{10,11... | collective-permute-start | bytes 786440 | tf_op jit(solution)/shard_map/ppermute | solution.py:250
  42.3 7.2 %collective-permute-start.19 = (bf16[128,1024]{1,0:T(8,128)(2,1)S(1)}, bf16[128,1024]{1,0:T(8,128)(2,1)S(1)}, u32[]{:S(2)}, u32[]{:S(2)}) collective-permute-start(bf16[128,1024]{1,0:T(8,128)(2,1)S(1)} %collective-permute-done.16.rest_10_), channel_id=1, source_target_pairs={{0,1},{1,0},{2,3},{3,2},{4,5},{5,4},{6,7},{7,6},{8,9},{9,8},{10,11... | collective-permute-start | bytes 786440 | tf_op jit(solution)/shard_map/ppermute | solution.py:250
  42.8 6.7 %collective-permute-start.15 = (bf16[128,1024]{1,0:T(8,128)(2,1)S(1)}, bf16[128,1024]{1,0:T(8,128)(2,1)S(1)}, u32[]{:S(2)}, u32[]{:S(2)}) collective-permute-start(bf16[128,1024]{1,0:T(8,128)(2,1)S(1)} %collective-permute-done.14.rest_6_), channel_id=1, source_target_pairs={{0,1},{1,0},{2,3},{3,2},{4,5},{5,4},{6,7},{7,6},{8,9},{9,8},{10,11... | collective-permute-start | bytes 786440 | tf_op jit(solution)/shard_map/ppermute | solution.py:250
  46.5 3.1 %collective-permute-start.18 = (bf16[128,1024]{1,0:T(8,128)(2,1)S(1)}, bf16[128,1024]{1,0:T(8,128)(2,1)S(1)}, u32[]{:S(2)}, u32[]{:S(2)}) collective-permute-start(bf16[128,1024]{1,0:T(8,128)(2,1)S(1)} %collective-permute-done.17.rest_8_), channel_id=1, source_target_pairs={{0,1},{1,0},{2,3},{3,2},{4,5},{5,4},{6,7},{7,6},{8,9},{9,8},{10,11... | collective-permute-start | bytes 786440 | tf_op jit(solution)/shard_map/ppermute | solution.py:250
  46.5 10.7 %collective-permute-start.10 = (bf16[192,512]{1,0:T(8,128)(2,1)S(1)}, bf16[192,512]{1,0:T(8,128)(2,1)S(1)}, u32[]{:S(2)}, u32[]{:S(2)}) collective-permute-start(bf16[192,512]{1,0:T(8,128)(2,1)S(1)} %get-tuple-element.43), channel_id=1, source_target_pairs={{0,8},{8,0},{16,24},{24,16},{1,9},{9,1},{17,25},{25,17},{2,10},{10... | collective-permute-start | bytes 589832 | tf_op jit(solution)/shard_map/ppermute | solution.py:253
  47.9 17.0 %copy-start = (bf16[384,1024]{1,0:T(8,128)(2,1)S(1)}, bf16[384,1024]{1,0:T(8,128)(2,1)}, u32[]{:S(2)}) copy-start(bf16[384,1024]{1,0:T(8,128)(2,1)} %feat_in.3) | copy-start | bytes 2359300
  47.9 17.0 %copy-start.2 = (bf16[1,1024,1024]{2,1,0:T(8,128)(2,1)S(1)}, bf16[1,1024,1024]{2,1,0:T(8,128)(2,1)}, u32[]{:S(2)}) copy-start(bf16[1,1024,1024]{2,1,0:T(8,128)(2,1)} %param.15) | copy-start | bytes 6291460
  48.0 17.0 %copy-start.4 = (f32[1,1024]{1,0:T(1,128)S(1)}, f32[1,1024]{1,0:T(1,128)}, u32[]{:S(2)}) copy-start(f32[1,1024]{1,0:T(1,128)} %gain_in.5) | copy-start | bytes 12292
  48.0 17.0 %copy-start.6 = (f32[384,1024]{1,0:T(8,128)S(1)}, f32[384,1024]{1,0:T(8,128)}, u32[]{:S(2)}) copy-start(f32[384,1024]{1,0:T(8,128)} %get-tuple-element.34.gate_in) | copy-start | bytes 4718596
  48.0 17.0 %copy-start.7 = (bf16[384,768]{1,0:T(8,128)(2,1)S(1)}, bf16[384,768]{1,0:T(8,128)(2,1)}, u32[]{:S(2)}) copy-start(bf16[384,768]{1,0:T(8,128)(2,1)} %get-tuple-element.35.pick_in) | copy-start | bytes 1769476
  48.0 9.2 %collective-permute-start.11 = (bf16[192,512]{1,0:T(8,128)(2,1)S(1)}, bf16[192,512]{1,0:T(8,128)(2,1)S(1)}, u32[]{:S(2)}, u32[]{:S(2)}) collective-permute-start(bf16[192,512]{1,0:T(8,128)(2,1)S(1)} %get-tuple-element.44), channel_id=1, source_target_pairs={{0,16},{8,24},{16,0},{24,8},{1,17},{9,25},{17,1},{25,9},{2,18},{10... | collective-permute-start | bytes 589832 | tf_op jit(solution)/shard_map/ppermute | solution.py:253
  53.6 7.8 %collective-permute-start.20 = (bf16[192,512]{1,0:T(8,128)(2,1)S(1)}, bf16[192,512]{1,0:T(8,128)(2,1)S(1)}, u32[]{:S(2)}, u32[]{:S(2)}) collective-permute-start(bf16[192,512]{1,0:T(8,128)(2,1)S(1)} %get-tuple-element.52), channel_id=1, source_target_pairs={{0,8},{8,0},{16,24},{24,16},{1,9},{9,1},{17,25},{25,17},{2,10},{10... | collective-permute-start | bytes 589832 | tf_op jit(solution)/shard_map/ppermute | solution.py:253
  54.3 7.2 %collective-permute-start.21 = (bf16[192,512]{1,0:T(8,128)(2,1)S(1)}, bf16[192,512]{1,0:T(8,128)(2,1)S(1)}, u32[]{:S(2)}, u32[]{:S(2)}) collective-permute-start(bf16[192,512]{1,0:T(8,128)(2,1)S(1)} %get-tuple-element.53), channel_id=1, source_target_pairs={{0,16},{8,24},{16,0},{24,8},{1,17},{9,25},{17,1},{25,9},{2,18},{10... | collective-permute-start | bytes 589832 | tf_op jit(solution)/shard_map/ppermute | solution.py:253
  55.1 9.9 %collective-permute-start.22 = (bf16[192,512]{1,0:T(8,128)(2,1)S(1)}, bf16[192,512]{1,0:T(8,128)(2,1)S(1)}, u32[]{:S(2)}, u32[]{:S(2)}) collective-permute-start(bf16[192,512]{1,0:T(8,128)(2,1)S(1)} %get-tuple-element.54), channel_id=1, source_target_pairs={{0,24},{8,16},{16,8},{24,0},{1,25},{9,17},{17,9},{25,1},{2,26},{10... | collective-permute-start | bytes 589832 | tf_op jit(solution)/shard_map/ppermute | solution.py:253

commit v9 on v7

--- a/solution.py
+++ b/solution.py
@@ -9,7 +9,7 @@
 
 BLK = 128
 HEAD = 128
-OPTS = {'chunks': (4, 4), 'order': 0, 'qs': 1, 'cq': 400000000000, 'cg': 400000000000, 'ca': 2000000000, 'cf': 1000000000, 'cp': 0, 'sw': (0, 0), 'p0': [], 'p1': [], 'm1': ['m', 'g'], 'a1': ['a', 'g'], 'g': [], 's0': [['qx'], ['qx'], [], ['qx']], 's1': [[], ['s'], ['rd'], []]}
+OPTS = {'chunks': [4, 4], 'order': 0, 'qs': 1, 'cq': 0, 'cg': 400000000000, 'ca': 2000000000, 'cf': 400000000000, 'cp': 0, 'sw': [0, 0], 'p0': [], 'p1': [], 'm1': ['m', 'a'], 'a1': ['f', 'g'], 'g': [], 's0': [['qx'], [], ['g'], ['g', 'qx']], 's1': [[], ['s'], ['rd'], []]}
 CHUNKS = OPTS['chunks']
 SLICES = 2
 VMEM_LIMIT = 32 * 1024 * 1024

time: 67.9 us -> 67.5 us (level)
  waiting for transfers between devices: 19.9 us -> 18.3 us
  starting transfers between devices: 27.5 us -> 28.6 us
    ppermute x9, waiting for transfers between devices: 15.9 us -> 14.3 us  [to_user(): return lax.ppermute(value, 'users', [(u, u ^ d) for u in range(users)])]
  transfers between devices with their start and end apart: 23 -> 23, of which waited for: 6 -> 4; matrix products, arithmetic and copies ran while one was open for 0% -> 0% of each run, Pallas kernels for 23% -> 23%
where the time goes in v9:
time: 67.5 us; the launch traced here: 67.2 us
  starting transfers between devices  28.6 us (42%)
  Pallas kernels  19 us (28%)
  waiting for transfers between devices  18.3 us (27%)
  local copies, waits for them, and re-layouts  1.07 us (2%)
    ppermute x6, starting transfers between devices, over_z(): return lax.ppermute(value, 'ctx', [(c, c ^ 2 * d) for c in range(ctx)])  14.8 us
    pallas_call x5, Pallas kernels, call(): pl.pallas_call(kernel, name=name, grid=(1,), in_specs=in_specs, out_specs...  14.4 us
    ppermute x9, waiting for transfers between devices, to_user(): return lax.ppermute(value, 'users', [(u, u ^ d) for u in range(users)])  14.3 us
    ppermute x9, starting transfers between devices, to_user(): return lax.ppermute(value, 'users', [(u, u ^ d) for u in range(users)])  12.3 us
    pallas_call x1, Pallas kernels, on_device(): pl.pallas_call(functools.partial(query_kernel, cap, users), name='query',...  4.61 us
    ppermute x6, waiting for transfers between devices, over_z(): return lax.ppermute(value, 'ctx', [(c, c ^ 2 * d) for c in range(ctx)])  3.97 us
    ppermute x8, starting transfers between devices, over_cores(): return lax.ppermute(value, 'ctx', [(c, c ^ 1) for c in range(ctx)])  1.54 us
  transfers between devices with their start and end apart: 23, of which 4 were waited for; matrix products, arithmetic and copies ran while one was open for 0% of the time, Pallas kernels for 23%

profile of v9, /device:TPU:0, one launch (start us, length us, event | category | flops | bytes accessed | tf_op | source)
XLA Modules:
  0.0 67.2 jit_solution(2286925956720567241)
XLA Ops:
  0.0 1.0 %copy-done.1 = bf16[1,1,128,2048]{3,2,1,0:T(8,128)(2,1)S(1)} copy-done((bf16[1,1,128,2048]{3,2,1,0:T(8,128)(2,1)S(1)}, bf16[1,1,128,2048]{3,2,1,0:T(8,128)(2,1)}, u32[]{:S(2)}) %copy-start.1) | copy-done | bytes 524312
  1.0 0.7 %kv_split.1 = (bf16[128,1024]{1,0:T(8,128)(2,1)}, bf16[128,1024]{1,0:T(8,128)(2,1)S(1)}) custom-call(bf16[128,2048]{1,0:T(8,128)(2,1)S(1)} %bitcast.4), custom_call_target="tpu_custom_call" | custom-call | tf_op jit(solution)/shard_map/kv_split/pallas_call | solution.py:237
  1.8 5.0 %collective-permute-start.6 = (bf16[128,1024]{1,0:T(8,128)(2,1)}, bf16[128,1024]{1,0:T(8,128)(2,1)}, u32[]{:S(2)}, u32[]{:S(2)}) collective-permute-start(bf16[128,1024]{1,0:T(8,128)(2,1)} %get-tuple-element.39.rest_4_), channel_id=1, source_target_pairs={{0,6},{1,7},{2,4},{3,5},{4,2},{5,3},{6,0},{7,1},{8,14},{9,15},{10,... | collective-permute-start | bytes 786440 | tf_op jit(solution)/shard_map/ppermute | solution.py:264
  6.8 0.0 collective-permute-start.4
  6.8 4.6 %query.1 = (bf16[192,1024]{1,0:T(8,128)(2,1)}, bf16[192,1024]{1,0:T(8,128)(2,1)}, bf16[192,1024]{1,0:T(8,128)(2,1)}, bf16[192,1024]{1,0:T(8,128)(2,1)}) custom-call(bf16[384,1024]{1,0:T(8,128)(2,1)} %feat.1, s32[1,384]{1,0:T(1,128)} %bitcast.8, f32[1,1024]{1,0:T(1,128)} %gain_in.3, bf16[1024,2048]{1,0:T(8,128)(2,1)} %bitcast.6), custom_call_target="tpu_custom_call" | custom-call | tf_op jit(solution)/shard_map/query/pallas_call | solution.py:293
  11.5 1.6 %collective-permute-start = (bf16[192,1024]{1,0:T(8,128)(2,1)}, bf16[192,1024]{1,0:T(8,128)(2,1)}, u32[]{:S(2)}, u32[]{:S(2)}) collective-permute-start(bf16[192,1024]{1,0:T(8,128)(2,1)} %get-tuple-element.36), channel_id=1, source_target_pairs={{0,8},{8,0},{16,24},{24,16},{1,9},{9,1},{17,25},{25,17},{2,10},{10... | collective-permute-start | bytes 1179656 | tf_op jit(solution)/shard_map/ppermute | solution.py:270
  13.0 1.5 %collective-permute-start.1 = (bf16[192,1024]{1,0:T(8,128)(2,1)}, bf16[192,1024]{1,0:T(8,128)(2,1)}, u32[]{:S(2)}, u32[]{:S(2)}) collective-permute-start(bf16[192,1024]{1,0:T(8,128)(2,1)} %get-tuple-element.37), channel_id=1, source_target_pairs={{0,16},{8,24},{16,0},{24,8},{1,17},{9,25},{17,1},{25,9},{2,18},{10... | collective-permute-start | bytes 1179656 | tf_op jit(solution)/shard_map/ppermute | solution.py:270
  14.5 0.5 collective-permute-start.2
  15.0 0.0 collective-permute-done.6.rest_10_
  15.0 3.8 %collective-permute-start.7 = (bf16[128,1024]{1,0:T(8,128)(2,1)}, bf16[128,1024]{1,0:T(8,128)(2,1)}, u32[]{:S(2)}, u32[]{:S(2)}) collective-permute-start(bf16[128,1024]{1,0:T(8,128)(2,1)} %collective-permute-done.6.rest_10_), channel_id=1, source_target_pairs={{0,2},{1,3},{2,0},{3,1},{4,6},{5,7},{6,4},{7,5},{8,10},{9,11},{10,... | collective-permute-start | bytes 786440 | tf_op jit(solution)/shard_map/ppermute | solution.py:264
  18.8 4.1 %gate.1 = (f32[384,1024]{1,0:T(8,128)}, bf16[384,768]{1,0:T(8,128)(2,1)}) custom-call(bf16[384,1024]{1,0:T(8,128)(2,1)} %feat.1, s32[1,384]{1,0:T(1,128)} %bitcast.9, f32[1,1024]{1,0:T(1,128)} %gain_in.3, bf16[1024,2048]{1,0:T(8,128)(2,1)} %bitcast.7), custom_call_target="tpu_custom_call" | custom-call | flops 399999991808 | bytes 4986368 | tf_op jit(solution)/shard_map/gate/pallas_call | solution.py:237
  22.9 2.5 %collective-permute-start.16 = (bf16[128,1024]{1,0:T(8,128)(2,1)S(1)}, bf16[128,1024]{1,0:T(8,128)(2,1)S(1)}, u32[]{:S(2)}, u32[]{:S(2)}) collective-permute-start(bf16[128,1024]{1,0:T(8,128)(2,1)S(1)} %get-tuple-element.49.rest_4_), channel_id=1, source_target_pairs={{0,6},{1,7},{2,4},{3,5},{4,2},{5,3},{6,0},{7,1},{8,14},{9,15},{10,... | collective-permute-start | bytes 786440 | tf_op jit(solution)/shard_map/ppermute | solution.py:264
  25.5 0.5 collective-permute-start.3
  26.0 6.1 %collective-permute-done.1.rest_2_ = bf16[192,1024]{1,0:T(8,128)(2,1)} collective-permute-done((bf16[192,1024]{1,0:T(8,128)(2,1)}, bf16[192,1024]{1,0:T(8,128)(2,1)}, u32[]{:S(2)}, u32[]{:S(2)}) %collective-permute-start.1) | collective-permute-done | bytes 393248 | tf_op jit(solution)/shard_map/ppermute | solution.py:270
  32.1 0.5 collective-permute-start.8
  32.6 1.7 %collective-permute-start.14 = (bf16[128,1024]{1,0:T(8,128)(2,1)S(1)}, bf16[128,1024]{1,0:T(8,128)(2,1)S(1)}, u32[]{:S(2)}, u32[]{:S(2)}) collective-permute-start(bf16[128,1024]{1,0:T(8,128)(2,1)S(1)} %get-tuple-element.49.rest_4_), channel_id=1, source_target_pairs={{0,2},{1,3},{2,0},{3,1},{4,6},{5,7},{6,4},{7,5},{8,10},{9,11},{10,... | collective-permute-start | bytes 786440 | tf_op jit(solution)/shard_map/ppermute | solution.py:264
  34.3 1.6 %collective-permute-start.17 = (bf16[128,1024]{1,0:T(8,128)(2,1)S(1)}, bf16[128,1024]{1,0:T(8,128)(2,1)S(1)}, u32[]{:S(2)}, u32[]{:S(2)}) collective-permute-start(bf16[128,1024]{1,0:T(8,128)(2,1)S(1)} %collective-permute-done.16.rest_10_), channel_id=1, source_target_pairs={{0,2},{1,3},{2,0},{3,1},{4,6},{5,7},{6,4},{7,5},{8,10},{9,11},{10,... | collective-permute-start | bytes 786440 | tf_op jit(solution)/shard_map/ppermute | solution.py:264
  36.0 3.5 %attend.2 = (bf16[192,512]{1,0:T(8,128)(2,1)S(1)}, bf16[192,512]{1,0:T(8,128)(2,1)S(1)}, bf16[192,512]{1,0:T(8,128)(2,1)S(1)}, bf16[192,512]{1,0:T(8,128)(2,1)S(1)}) custom-call(s32[1,8]{1,0:T(1,128)S(1)} %copy-done.5, bf16[192,1024]{1,0:T(8,128)(2,1)S(1)} %copy-done.3, bf16[192,1024]{1,0:T(8,128)(2,1)} %collective-permute-done.rest_1_, ...), custom_call_target="tpu_custom_call" | custom-call | flops 2000000000 | bytes 3670048 | tf_op jit(solution)/shard_map/attend/pallas_call | solution.py:237
  39.5 2.5 %collective-permute-start.12 = (bf16[192,512]{1,0:T(8,128)(2,1)S(1)}, bf16[192,512]{1,0:T(8,128)(2,1)S(1)}, u32[]{:S(2)}, u32[]{:S(2)}) collective-permute-start(bf16[192,512]{1,0:T(8,128)(2,1)S(1)} %get-tuple-element.45), channel_id=1, source_target_pairs={{0,24},{8,16},{16,8},{24,0},{1,25},{9,17},{17,9},{25,1},{2,26},{10... | collective-permute-start | bytes 589832 | tf_op jit(solution)/shard_map/ppermute | solution.py:270
  42.0 0.5 collective-permute-start.19
  42.5 0.0 collective-permute-start.15
  42.5 4.0 %collective-permute-done.17.rest_8_ = bf16[128,1024]{1,0:T(8,128)(2,1)S(1)} collective-permute-done((bf16[128,1024]{1,0:T(8,128)(2,1)S(1)}, bf16[128,1024]{1,0:T(8,128)(2,1)S(1)}, u32[]{:S(2)}, u32[]{:S(2)}) %collective-permute-start.17) | collective-permute-done | bytes 262176 | tf_op jit(solution)/shard_map/ppermute | solution.py:264
  46.5 1.2 %collective-permute-start.10 = (bf16[192,512]{1,0:T(8,128)(2,1)S(1)}, bf16[192,512]{1,0:T(8,128)(2,1)S(1)}, u32[]{:S(2)}, u32[]{:S(2)}) collective-permute-start(bf16[192,512]{1,0:T(8,128)(2,1)S(1)} %get-tuple-element.43), channel_id=1, source_target_pairs={{0,8},{8,0},{16,24},{24,16},{1,9},{9,1},{17,25},{25,17},{2,10},{10... | collective-permute-start | bytes 589832 | tf_op jit(solution)/shard_map/ppermute | solution.py:270
  47.7 0.0 copy-start.7
  47.7 1.6 %collective-permute-start.11 = (bf16[192,512]{1,0:T(8,128)(2,1)S(1)}, bf16[192,512]{1,0:T(8,128)(2,1)S(1)}, u32[]{:S(2)}, u32[]{:S(2)}) collective-permute-start(bf16[192,512]{1,0:T(8,128)(2,1)S(1)} %get-tuple-element.44), channel_id=1, source_target_pairs={{0,16},{8,24},{16,0},{24,8},{1,17},{9,25},{17,1},{25,9},{2,18},{10... | collective-permute-start | bytes 589832 | tf_op jit(solution)/shard_map/ppermute | solution.py:270
  49.2 3.2 %attend.3 = (bf16[192,512]{1,0:T(8,128)(2,1)S(1)}, bf16[192,512]{1,0:T(8,128)(2,1)S(1)}, bf16[192,512]{1,0:T(8,128)(2,1)S(1)}, bf16[192,512]{1,0:T(8,128)(2,1)S(1)}) custom-call(s32[1,8]{1,0:T(1,128)S(1)} %copy-done.5, bf16[192,1024]{1,0:T(8,128)(2,1)S(1)} %copy-done.3, bf16[192,1024]{1,0:T(8,128)(2,1)} %collective-permute-done.rest_1_, ...), custom_call_target="tpu_custom_call" | custom-call | flops 2000000000 | bytes 3670048 | tf_op jit(solution)/shard_map/attend/pallas_call | solution.py:237
  52.5 1.0 %collective-permute-start.20 = (bf16[192,512]{1,0:T(8,128)(2,1)S(1)}, bf16[192,512]{1,0:T(8,128)(2,1)S(1)}, u32[]{:S(2)}, u32[]{:S(2)}) collective-permute-start(bf16[192,512]{1,0:T(8,128)(2,1)S(1)} %get-tuple-element.52), channel_id=1, source_target_pairs={{0,8},{8,0},{16,24},{24,16},{1,9},{9,1},{17,25},{25,17},{2,10},{10... | collective-permute-start | bytes 589832 | tf_op jit(solution)/shard_map/ppermute | solution.py:270
  53.4 0.8 %collective-permute-start.21 = (bf16[192,512]{1,0:T(8,128)(2,1)S(1)}, bf16[192,512]{1,0:T(8,128)(2,1)S(1)}, u32[]{:S(2)}, u32[]{:S(2)}) collective-permute-start(bf16[192,512]{1,0:T(8,128)(2,1)S(1)} %get-tuple-element.53), channel_id=1, source_target_pairs={{0,16},{8,24},{16,0},{24,8},{1,17},{9,25},{17,1},{25,9},{2,18},{10... | collective-permute-start | bytes 589832 | tf_op jit(solution)/shard_map/ppermute | solution.py:270
  54.3 1.8 %collective-permute-start.22 = (bf16[192,512]{1,0:T(8,128)(2,1)S(1)}, bf16[192,512]{1,0:T(8,128)(2,1)S(1)}, u32[]{:S(2)}, u32[]{:S(2)}) collective-permute-start(bf16[192,512]{1,0:T(8,128)(2,1)S(1)} %get-tuple-element.54), channel_id=1, source_target_pairs={{0,24},{8,16},{16,8},{24,0},{1,25},{9,17},{17,9},{25,1},{2,26},{10... | collective-permute-start | bytes 589832 | tf_op jit(solution)/shard_map/ppermute | solution.py:270
  56.0 4.3 %collective-permute-done.20.rest_5_ = bf16[192,512]{1,0:T(8,128)(2,1)S(1)} collective-permute-done((bf16[192,512]{1,0:T(8,128)(2,1)S(1)}, bf16[192,512]{1,0:T(8,128)(2,1)S(1)}, u32[]{:S(2)}, u32[]{:S(2)}) %collective-permute-start.20) | collective-permute-done | bytes 196640 | tf_op jit(solution)/shard_map/ppermute | solution.py:270
  60.3 4.0 %collective-permute-done.21.rest_6_ = bf16[192,512]{1,0:T(8,128)(2,1)S(1)} collective-permute-done((bf16[192,512]{1,0:T(8,128)(2,1)S(1)}, bf16[192,512]{1,0:T(8,128)(2,1)S(1)}, u32[]{:S(2)}, u32[]{:S(2)}) %collective-permute-start.21) | collective-permute-done | bytes 196640 | tf_op jit(solution)/shard_map/ppermute | solution.py:270
  64.3 2.9 %finish.1 = bf16[384,1024]{1,0:T(8,128)(2,1)} custom-call(bf16[384,1024]{1,0:T(8,128)(2,1)S(1)} %copy-done, f32[384,1024]{1,0:T(8,128)S(1)} %copy-done.6, bf16[384,768]{1,0:T(8,128)(2,1)S(1)} %copy-done.7, f32[1,1024]{1,0:T(1,128)S(1)} %copy-done.4, bf16[1024,1024]{1,0:T(8,128)(2,1)S(1)} %bitcast.5, bf16[192,512]{1,0:T(8,128)(2,1)S(1)} %get-tuple-element.42.rest_0_, ...), custom_call_target="tpu_custom_call" | custom-call | flops 399999991808 | bytes 6623232 | tf_op jit(solution)/shard_map/finish/pallas_call | solution.py:237
  (36 shorter events, 0.1 us)
Async XLA Ops:
  0.0 1.0 %copy-start.1 = (bf16[1,1,128,2048]{3,2,1,0:T(8,128)(2,1)S(1)}, bf16[1,1,128,2048]{3,2,1,0:T(8,128)(2,1)}, u32[]{:S(2)}) copy-start(bf16[1,1,128,2048]{3,2,1,0:T(8,128)(2,1)} %param.10) | copy-start | bytes 1572868
  1.8 13.2 %collective-permute-start.6 = (bf16[128,1024]{1,0:T(8,128)(2,1)}, bf16[128,1024]{1,0:T(8,128)(2,1)}, u32[]{:S(2)}, u32[]{:S(2)}) collective-permute-start(bf16[128,1024]{1,0:T(8,128)(2,1)} %get-tuple-element.39.rest_4_), channel_id=1, source_target_pairs={{0,6},{1,7},{2,4},{3,5},{4,2},{5,3},{6,0},{7,1},{8,14},{9,15},{10,... | collective-permute-start | bytes 786440 | tf_op jit(solution)/shard_map/ppermute | solution.py:264
  6.8 16.1 %collective-permute-start.4 = (bf16[128,1024]{1,0:T(8,128)(2,1)}, bf16[128,1024]{1,0:T(8,128)(2,1)}, u32[]{:S(2)}, u32[]{:S(2)}) collective-permute-start(bf16[128,1024]{1,0:T(8,128)(2,1)} %get-tuple-element.39.rest_4_), channel_id=1, source_target_pairs={{0,2},{1,3},{2,0},{3,1},{4,6},{5,7},{6,4},{7,5},{8,10},{9,11},{10,... | collective-permute-start | bytes 786440 | tf_op jit(solution)/shard_map/ppermute | solution.py:264
  11.5 14.0 %collective-permute-start = (bf16[192,1024]{1,0:T(8,128)(2,1)}, bf16[192,1024]{1,0:T(8,128)(2,1)}, u32[]{:S(2)}, u32[]{:S(2)}) collective-permute-start(bf16[192,1024]{1,0:T(8,128)(2,1)} %get-tuple-element.36), channel_id=1, source_target_pairs={{0,8},{8,0},{16,24},{24,16},{1,9},{9,1},{17,25},{25,17},{2,10},{10... | collective-permute-start | bytes 1179656 | tf_op jit(solution)/shard_map/ppermute | solution.py:270
  13.0 19.0 %collective-permute-start.1 = (bf16[192,1024]{1,0:T(8,128)(2,1)}, bf16[192,1024]{1,0:T(8,128)(2,1)}, u32[]{:S(2)}, u32[]{:S(2)}) collective-permute-start(bf16[192,1024]{1,0:T(8,128)(2,1)} %get-tuple-element.37), channel_id=1, source_target_pairs={{0,16},{8,24},{16,0},{24,8},{1,17},{9,25},{17,1},{25,9},{2,18},{10... | collective-permute-start | bytes 1179656 | tf_op jit(solution)/shard_map/ppermute | solution.py:270
  14.5 17.5 %collective-permute-start.2 = (bf16[192,1024]{1,0:T(8,128)(2,1)}, bf16[192,1024]{1,0:T(8,128)(2,1)}, u32[]{:S(2)}, u32[]{:S(2)}) collective-permute-start(bf16[192,1024]{1,0:T(8,128)(2,1)} %get-tuple-element.38), channel_id=1, source_target_pairs={{0,24},{8,16},{16,8},{24,0},{1,25},{9,17},{17,9},{25,1},{2,26},{10... | collective-permute-start | bytes 1179656 | tf_op jit(solution)/shard_map/ppermute | solution.py:270
  15.0 10.4 %collective-permute-start.7 = (bf16[128,1024]{1,0:T(8,128)(2,1)}, bf16[128,1024]{1,0:T(8,128)(2,1)}, u32[]{:S(2)}, u32[]{:S(2)}) collective-permute-start(bf16[128,1024]{1,0:T(8,128)(2,1)} %collective-permute-done.6.rest_10_), channel_id=1, source_target_pairs={{0,2},{1,3},{2,0},{3,1},{4,6},{5,7},{6,4},{7,5},{8,10},{9,11},{10,... | collective-permute-start | bytes 786440 | tf_op jit(solution)/shard_map/ppermute | solution.py:264
  18.8 17.2 %copy-start.3 = (bf16[192,1024]{1,0:T(8,128)(2,1)S(1)}, bf16[192,1024]{1,0:T(8,128)(2,1)}, u32[]{:S(2)}) copy-start(bf16[192,1024]{1,0:T(8,128)(2,1)} %get-tuple-element.32.rest_0_) | copy-start | bytes 1179652
  18.8 17.2 %copy-start.5 = (s32[1,8]{1,0:T(1,128)S(1)}, s32[1,8]{1,0:T(1,128)}, u32[]{:S(2)}) copy-start(s32[1,8]{1,0:T(1,128)} %mask.3) | copy-start | bytes 100
  22.9 11.4 %collective-permute-start.16 = (bf16[128,1024]{1,0:T(8,128)(2,1)S(1)}, bf16[128,1024]{1,0:T(8,128)(2,1)S(1)}, u32[]{:S(2)}, u32[]{:S(2)}) collective-permute-start(bf16[128,1024]{1,0:T(8,128)(2,1)S(1)} %get-tuple-element.49.rest_4_), channel_id=1, source_target_pairs={{0,6},{1,7},{2,4},{3,5},{4,2},{5,3},{6,0},{7,1},{8,14},{9,15},{10,... | collective-permute-start | bytes 786440 | tf_op jit(solution)/shard_map/ppermute | solution.py:264
  25.4 7.1 %collective-permute-start.5 = (bf16[128,1024]{1,0:T(8,128)(2,1)}, bf16[128,1024]{1,0:T(8,128)(2,1)S(1)}, u32[]{:S(2)}, u32[]{:S(2)}) collective-permute-start(bf16[128,1024]{1,0:T(8,128)(2,1)} %collective-permute-done.4.rest_6_), channel_id=1, source_target_pairs={{0,1},{1,0},{2,3},{3,2},{4,5},{5,4},{6,7},{7,6},{8,9},{9,8},{10,11... | collective-permute-start | bytes 786440 | tf_op jit(solution)/shard_map/ppermute | solution.py:267
  25.5 10.5 %collective-permute-start.3 = (bf16[128,1024]{1,0:T(8,128)(2,1)}, bf16[128,1024]{1,0:T(8,128)(2,1)S(1)}, u32[]{:S(2)}, u32[]{:S(2)}) collective-permute-start(bf16[128,1024]{1,0:T(8,128)(2,1)} %get-tuple-element.39.rest_4_), channel_id=1, source_target_pairs={{0,1},{1,0},{2,3},{3,2},{4,5},{5,4},{6,7},{7,6},{8,9},{9,8},{10,11... | collective-permute-start | bytes 786440 | tf_op jit(solution)/shard_map/ppermute | solution.py:267
  32.0 3.9 %collective-permute-start.9 = (bf16[128,1024]{1,0:T(8,128)(2,1)}, bf16[128,1024]{1,0:T(8,128)(2,1)S(1)}, u32[]{:S(2)}, u32[]{:S(2)}) collective-permute-start(bf16[128,1024]{1,0:T(8,128)(2,1)} %collective-permute-done.6.rest_10_), channel_id=1, source_target_pairs={{0,1},{1,0},{2,3},{3,2},{4,5},{5,4},{6,7},{7,6},{8,9},{9,8},{10,11... | collective-permute-start | bytes 786440 | tf_op jit(solution)/shard_map/ppermute | solution.py:267
  32.1 3.9 %collective-permute-start.8 = (bf16[128,1024]{1,0:T(8,128)(2,1)}, bf16[128,1024]{1,0:T(8,128)(2,1)S(1)}, u32[]{:S(2)}, u32[]{:S(2)}) collective-permute-start(bf16[128,1024]{1,0:T(8,128)(2,1)} %collective-permute-done.7.rest_8_), channel_id=1, source_target_pairs={{0,1},{1,0},{2,3},{3,2},{4,5},{5,4},{6,7},{7,6},{8,9},{9,8},{10,11... | collective-permute-start | bytes 786440 | tf_op jit(solution)/shard_map/ppermute | solution.py:267
  32.6 9.9 %collective-permute-start.14 = (bf16[128,1024]{1,0:T(8,128)(2,1)S(1)}, bf16[128,1024]{1,0:T(8,128)(2,1)S(1)}, u32[]{:S(2)}, u32[]{:S(2)}) collective-permute-start(bf16[128,1024]{1,0:T(8,128)(2,1)S(1)} %get-tuple-element.49.rest_4_), channel_id=1, source_target_pairs={{0,2},{1,3},{2,0},{3,1},{4,6},{5,7},{6,4},{7,5},{8,10},{9,11},{10,... | collective-permute-start | bytes 786440 | tf_op jit(solution)/shard_map/ppermute | solution.py:264
  34.3 12.2 %collective-permute-start.17 = (bf16[128,1024]{1,0:T(8,128)(2,1)S(1)}, bf16[128,1024]{1,0:T(8,128)(2,1)S(1)}, u32[]{:S(2)}, u32[]{:S(2)}) collective-permute-start(bf16[128,1024]{1,0:T(8,128)(2,1)S(1)} %collective-permute-done.16.rest_10_), channel_id=1, source_target_pairs={{0,2},{1,3},{2,0},{3,1},{4,6},{5,7},{6,4},{7,5},{8,10},{9,11},{10,... | collective-permute-start | bytes 786440 | tf_op jit(solution)/shard_map/ppermute | solution.py:264
  39.5 7.0 %collective-permute-start.12 = (bf16[192,512]{1,0:T(8,128)(2,1)S(1)}, bf16[192,512]{1,0:T(8,128)(2,1)S(1)}, u32[]{:S(2)}, u32[]{:S(2)}) collective-permute-start(bf16[192,512]{1,0:T(8,128)(2,1)S(1)} %get-tuple-element.45), channel_id=1, source_target_pairs={{0,24},{8,16},{16,8},{24,0},{1,25},{9,17},{17,9},{25,1},{2,26},{10... | collective-permute-start | bytes 589832 | tf_op jit(solution)/shard_map/ppermute | solution.py:270
  42.0 5.6 %collective-permute-start.13 = (bf16[128,1024]{1,0:T(8,128)(2,1)S(1)}, bf16[128,1024]{1,0:T(8,128)(2,1)S(1)}, u32[]{:S(2)}, u32[]{:S(2)}) collective-permute-start(bf16[128,1024]{1,0:T(8,128)(2,1)S(1)} %get-tuple-element.49.rest_4_), channel_id=1, source_target_pairs={{0,1},{1,0},{2,3},{3,2},{4,5},{5,4},{6,7},{7,6},{8,9},{9,8},{10,11... | collective-permute-start | bytes 786440 | tf_op jit(solution)/shard_map/ppermute | solution.py:267
  42.0 7.2 %collective-permute-start.19 = (bf16[128,1024]{1,0:T(8,128)(2,1)S(1)}, bf16[128,1024]{1,0:T(8,128)(2,1)S(1)}, u32[]{:S(2)}, u32[]{:S(2)}) collective-permute-start(bf16[128,1024]{1,0:T(8,128)(2,1)S(1)} %collective-permute-done.16.rest_10_), channel_id=1, source_target_pairs={{0,1},{1,0},{2,3},{3,2},{4,5},{5,4},{6,7},{7,6},{8,9},{9,8},{10,11... | collective-permute-start | bytes 786440 | tf_op jit(solution)/shard_map/ppermute | solution.py:267
  42.5 6.7 %collective-permute-start.15 = (bf16[128,1024]{1,0:T(8,128)(2,1)S(1)}, bf16[128,1024]{1,0:T(8,128)(2,1)S(1)}, u32[]{:S(2)}, u32[]{:S(2)}) collective-permute-start(bf16[128,1024]{1,0:T(8,128)(2,1)S(1)} %collective-permute-done.14.rest_6_), channel_id=1, source_target_pairs={{0,1},{1,0},{2,3},{3,2},{4,5},{5,4},{6,7},{7,6},{8,9},{9,8},{10,11... | collective-permute-start | bytes 786440 | tf_op jit(solution)/shard_map/ppermute | solution.py:267
  46.5 2.8 %collective-permute-start.18 = (bf16[128,1024]{1,0:T(8,128)(2,1)S(1)}, bf16[128,1024]{1,0:T(8,128)(2,1)S(1)}, u32[]{:S(2)}, u32[]{:S(2)}) collective-permute-start(bf16[128,1024]{1,0:T(8,128)(2,1)S(1)} %collective-permute-done.17.rest_8_), channel_id=1, source_target_pairs={{0,1},{1,0},{2,3},{3,2},{4,5},{5,4},{6,7},{7,6},{8,9},{9,8},{10,11... | collective-permute-start | bytes 786440 | tf_op jit(solution)/shard_map/ppermute | solution.py:267
  46.5 9.5 %collective-permute-start.10 = (bf16[192,512]{1,0:T(8,128)(2,1)S(1)}, bf16[192,512]{1,0:T(8,128)(2,1)S(1)}, u32[]{:S(2)}, u32[]{:S(2)}) collective-permute-start(bf16[192,512]{1,0:T(8,128)(2,1)S(1)} %get-tuple-element.43), channel_id=1, source_target_pairs={{0,8},{8,0},{16,24},{24,16},{1,9},{9,1},{17,25},{25,17},{2,10},{10... | collective-permute-start | bytes 589832 | tf_op jit(solution)/shard_map/ppermute | solution.py:270
  47.6 16.6 %copy-start = (bf16[384,1024]{1,0:T(8,128)(2,1)S(1)}, bf16[384,1024]{1,0:T(8,128)(2,1)}, u32[]{:S(2)}) copy-start(bf16[384,1024]{1,0:T(8,128)(2,1)} %feat.1) | copy-start | bytes 2359300
  47.6 16.6 %copy-start.2 = (bf16[1,1024,1024]{2,1,0:T(8,128)(2,1)S(1)}, bf16[1,1024,1024]{2,1,0:T(8,128)(2,1)}, u32[]{:S(2)}) copy-start(bf16[1,1024,1024]{2,1,0:T(8,128)(2,1)} %param.15) | copy-start | bytes 6291460
  47.6 16.6 %copy-start.4 = (f32[1,1024]{1,0:T(1,128)S(1)}, f32[1,1024]{1,0:T(1,128)}, u32[]{:S(2)}) copy-start(f32[1,1024]{1,0:T(1,128)} %gain.1) | copy-start | bytes 12292
  47.7 16.6 %copy-start.6 = (f32[384,1024]{1,0:T(8,128)S(1)}, f32[384,1024]{1,0:T(8,128)}, u32[]{:S(2)}) copy-start(f32[384,1024]{1,0:T(8,128)} %get-tuple-element.34.gate) | copy-start | bytes 4718596
  47.7 16.6 %copy-start.7 = (bf16[384,768]{1,0:T(8,128)(2,1)S(1)}, bf16[384,768]{1,0:T(8,128)(2,1)}, u32[]{:S(2)}) copy-start(bf16[384,768]{1,0:T(8,128)(2,1)} %get-tuple-element.35.pick) | copy-start | bytes 1769476
  47.7 8.3 %collective-permute-start.11 = (bf16[192,512]{1,0:T(8,128)(2,1)S(1)}, bf16[192,512]{1,0:T(8,128)(2,1)S(1)}, u32[]{:S(2)}, u32[]{:S(2)}) collective-permute-start(bf16[192,512]{1,0:T(8,128)(2,1)S(1)} %get-tuple-element.44), channel_id=1, source_target_pairs={{0,16},{8,24},{16,0},{24,8},{1,17},{9,25},{17,1},{25,9},{2,18},{10... | collective-permute-start | bytes 589832 | tf_op jit(solution)/shard_map/ppermute | solution.py:270
  52.5 7.8 %collective-permute-start.20 = (bf16[192,512]{1,0:T(8,128)(2,1)S(1)}, bf16[192,512]{1,0:T(8,128)(2,1)S(1)}, u32[]{:S(2)}, u32[]{:S(2)}) collective-permute-start(bf16[192,512]{1,0:T(8,128)(2,1)S(1)} %get-tuple-element.52), channel_id=1, source_target_pairs={{0,8},{8,0},{16,24},{24,16},{1,9},{9,1},{17,25},{25,17},{2,10},{10... | collective-permute-start | bytes 589832 | tf_op jit(solution)/shard_map/ppermute | solution.py:270
  53.4 10.9 %collective-permute-start.21 = (bf16[192,512]{1,0:T(8,128)(2,1)S(1)}, bf16[192,512]{1,0:T(8,128)(2,1)S(1)}, u32[]{:S(2)}, u32[]{:S(2)}) collective-permute-start(bf16[192,512]{1,0:T(8,128)(2,1)S(1)} %get-tuple-element.53), channel_id=1, source_target_pairs={{0,16},{8,24},{16,0},{24,8},{1,17},{9,25},{17,1},{25,9},{2,18},{10... | collective-permute-start | bytes 589832 | tf_op jit(solution)/shard_map/ppermute | solution.py:270
  54.3 10.0 %collective-permute-start.22 = (bf16[192,512]{1,0:T(8,128)(2,1)S(1)}, bf16[192,512]{1,0:T(8,128)(2,1)S(1)}, u32[]{:S(2)}, u32[]{:S(2)}) collective-permute-start(bf16[192,512]{1,0:T(8,128)(2,1)S(1)} %get-tuple-element.54), channel_id=1, source_target_pairs={{0,24},{8,16},{16,8},{24,0},{1,25},{9,17},{17,9},{25,1},{2,26},{10... | collective-permute-start | bytes 589832 | tf_op jit(solution)/shard_map/ppermute | solution.py:270

commit v10 on v9

--- a/solution.py
+++ b/solution.py
@@ -9,7 +9,7 @@
 
 BLK = 128
 HEAD = 128
-OPTS = {'chunks': [4, 4], 'order': 0, 'qs': 1, 'cq': 0, 'cg': 400000000000, 'ca': 2000000000, 'cf': 400000000000, 'cp': 0, 'sw': [0, 0], 'p0': [], 'p1': [], 'm1': ['m', 'a'], 'a1': ['f', 'g'], 'g': [], 's0': [['qx'], [], ['g'], ['g', 'qx']], 's1': [[], ['s'], ['rd'], []]}
+OPTS = {'chunks': [4, 4], 'order': 0, 'qs': 1, 'cq': 0, 'cg': 400000000000, 'ca': 2000000000, 'cf': 400000000000, 'cp': 0, 'sw': [0, 0], 'p0': [], 'p1': [], 'm1': [], 'a1': [], 'g': ['a0'], 's0': [['qx'], [], ['g'], ['g', 'qx']], 's1': [[], ['s'], ['rd'], []], 'cl': 400000000000}
 CHUNKS = OPTS['chunks']
 SLICES = 2
 VMEM_LIMIT = 32 * 1024 * 1024
@@ -112,15 +112,18 @@
         write.wait()
 
 
-def gate_kernel(cap, users, feat_in, user_in, gain_in, w_in, gate, pick, feat, user, gain, weights, sems):
-    rows, _ = feat.shape
+def gate_kernel(feat_in, user_in, gain_in, w_in, gate, feat, user, gain, weights, sems):
     copies = load_operands(0, feat_in, user_in, gain_in, w_in, feat, user, gain, weights, sems)
     copies[0].wait()
+    gate[...] = project(copies, feat, gain, weights)
+
+
+def pick_kernel(cap, users, user, pick):
+    rows = user.shape[1]
     slot = slots_of(user[...], lax.axis_index("users"), cap, users)
     slot = jnp.transpose(jnp.broadcast_to(slot, (128, rows)))[:, 0:1]
     places = lax.broadcasted_iota(jnp.int32, (rows, users * cap), 1).astype(jnp.float32)
     pick[...] = (places == slot).astype(jnp.bfloat16)
-    gate[...] = project(copies, feat, gain, weights)
 
 
 def pack_kernel(chips, mask, *rest):
@@ -324,15 +327,12 @@
             held[d] = over_z(held[3], 1) if d == 2 else over_z(near if d == 1 else far, d)
         env.update({'a' + str(chunk): held[1], 'm' + str(chunk): held[3], 'f' + str(chunk): held[2]})
         if chunk == 0:
-            gate, pick = call(
-                functools.partial(gate_kernel, cap, users), "gate",
-                [HBM] * 4,
-                [shape(rows, width, dtype=jnp.float32), shape(rows, users * cap)],
-                operands + [pltpu.SemaphoreType.DMA((3 + SLICES,))],
-                OPTS['cg'],
-                gated(cand_feat, ['q'] + OPTS['g']), user_row, gain_in, w_uq[0], vmem=VMEM_MOST,
+            pick, = call(
+                functools.partial(pick_kernel, cap, users), "pick", [whole(1, rows)],
+                [shape(rows, users * cap)], [], OPTS['cg'],
+                gated(user_row, ['q'] + OPTS['g']), vmem=VMEM_MOST,
             )
-            env['g'] = gate
+            env['g'] = pick
         if OPTS['sw'][chunk]:
             keys = OPTS['p0'] if chunk == 0 else OPTS['p1']
             packed, = call(
@@ -360,6 +360,12 @@
         returned += back
         first += wide
 
+    gate, = call(
+        gate_kernel, "gate", [HBM] * 4, [shape(rows, width, dtype=jnp.float32)],
+        operands + [pltpu.SemaphoreType.DMA((3 + SLICES,))],
+        OPTS['cl'],
+        after(cand_feat, scored[0]), user_row, gain_in, w_uq[0], vmem=VMEM_MOST,
+    )
     return call(
         functools.partial(finish_kernel, users), "finish",
         [

time: 67.5 us -> 72 us (1.067)
  Pallas kernels: 19 us -> 23.8 us
  local copies, waits for them, and re-layouts: 1.07 us -> 3.17 us
  waiting for transfers between devices: 18.3 us -> 16.9 us
  starting transfers between devices: 28.6 us -> 27.6 us
    ppermute x9, waiting for transfers between devices: 14.3 us -> 5.18 us  [to_user(): return lax.ppermute(value, 'users', [(u, u ^ d) for u in range(users)])]
    ppermute x6, waiting for transfers between devices: 3.97 us -> 11.7 us  [over_z(): return lax.ppermute(value, 'ctx', [(c, c ^ 2 * d) for c in range(ctx)])]
    pallas_call x5 -> x6, Pallas kernels: 14.4 us -> 19.2 us  [call(): pl.pallas_call(kernel, name=name, grid=(1,), in_specs=in_specs, out_specs...]
    unnamed x16 -> x28, local copies, waits for them, and re-layouts: 1.07 us -> 3.17 us
    ppermute x9, starting transfers between devices: 12.3 us -> 11.2 us  [to_user(): return lax.ppermute(value, 'users', [(u, u ^ d) for u in range(users)])]
  transfers between devices with their start and end apart: 23 -> 23, of which waited for: 4 -> 6; matrix products, arithmetic and copies ran while one was open for 0% -> 0% of each run, Pallas kernels for 23% -> 26%
where the time goes in v10:
time: 72 us; the launch traced here: 71.7 us
  starting transfers between devices  27.6 us (38%)
  Pallas kernels  23.8 us (33%)
  waiting for transfers between devices  16.9 us (23%)
  local copies, waits for them, and re-layouts  3.17 us (4%)
    pallas_call x6, Pallas kernels, call(): pl.pallas_call(kernel, name=name, grid=(1,), in_specs=in_specs, out_specs...  19.2 us
    ppermute x6, starting transfers between devices, over_z(): return lax.ppermute(value, 'ctx', [(c, c ^ 2 * d) for c in range(ctx)])  15.4 us
    ppermute x6, waiting for transfers between devices, over_z(): return lax.ppermute(value, 'ctx', [(c, c ^ 2 * d) for c in range(ctx)])  11.7 us
    ppermute x9, starting transfers between devices, to_user(): return lax.ppermute(value, 'users', [(u, u ^ d) for u in range(users)])  11.2 us
    ppermute x9, waiting for transfers between devices, to_user(): return lax.ppermute(value, 'users', [(u, u ^ d) for u in range(users)])  5.18 us
    pallas_call x1, Pallas kernels, on_device(): pl.pallas_call(functools.partial(query_kernel, cap, users), name='query',...  4.6 us
    unnamed x28, local copies, waits for them, and re-layouts  3.17 us
  transfers between devices with their start and end apart: 23, of which 6 were waited for; matrix products, arithmetic and copies ran while one was open for 0% of the time, Pallas kernels for 26%

profile of v10, /device:TPU:0, one launch (start us, length us, event | category | flops | bytes accessed | tf_op | source)
XLA Modules:
  0.0 71.7 jit_solution(11542047392822092703)
XLA Ops:
  0.0 1.0 %copy-done.1 = bf16[1,1,128,2048]{3,2,1,0:T(8,128)(2,1)S(1)} copy-done((bf16[1,1,128,2048]{3,2,1,0:T(8,128)(2,1)S(1)}, bf16[1,1,128,2048]{3,2,1,0:T(8,128)(2,1)}, u32[]{:S(2)}) %copy-start.1) | copy-done | bytes 524312
  1.0 0.7 %kv_split.1 = (bf16[128,1024]{1,0:T(8,128)(2,1)S(1)}, bf16[128,1024]{1,0:T(8,128)(2,1)}) custom-call(bf16[128,2048]{1,0:T(8,128)(2,1)S(1)} %bitcast.4), custom_call_target="tpu_custom_call" | custom-call | tf_op jit(solution)/shard_map/kv_split/pallas_call | solution.py:240
  1.8 3.0 %collective-permute-start.6 = (bf16[128,1024]{1,0:T(8,128)(2,1)S(1)}, bf16[128,1024]{1,0:T(8,128)(2,1)S(1)}, u32[]{:S(2)}, u32[]{:S(2)}) collective-permute-start(bf16[128,1024]{1,0:T(8,128)(2,1)S(1)} %get-tuple-element.34.rest_4_), channel_id=1, source_target_pairs={{0,2},{1,3},{2,0},{3,1},{4,6},{5,7},{6,4},{7,5},{8,10},{9,11},{10,... | collective-permute-start | bytes 786440 | tf_op jit(solution)/shard_map/ppermute | solution.py:267
  4.8 2.5 %collective-permute-start.8 = (bf16[128,1024]{1,0:T(8,128)(2,1)S(1)}, bf16[128,1024]{1,0:T(8,128)(2,1)}, u32[]{:S(2)}, u32[]{:S(2)}) collective-permute-start(bf16[128,1024]{1,0:T(8,128)(2,1)S(1)} %get-tuple-element.34.rest_4_), channel_id=1, source_target_pairs={{0,6},{1,7},{2,4},{3,5},{4,2},{5,3},{6,0},{7,1},{8,14},{9,15},{10,... | collective-permute-start | bytes 786440 | tf_op jit(solution)/shard_map/ppermute | solution.py:267
  7.3 4.6 %query.1 = (bf16[192,1024]{1,0:T(8,128)(2,1)}, bf16[192,1024]{1,0:T(8,128)(2,1)}, bf16[192,1024]{1,0:T(8,128)(2,1)}, bf16[192,1024]{1,0:T(8,128)(2,1)}) custom-call(bf16[384,1024]{1,0:T(8,128)(2,1)} %feat.1, s32[1,384]{1,0:T(1,128)} %bitcast.8, f32[1,1024]{1,0:T(1,128)} %gain_in.3, bf16[1024,2048]{1,0:T(8,128)(2,1)} %bitcast.6), custom_call_target="tpu_custom_call" | custom-call | tf_op jit(solution)/shard_map/query/pallas_call | solution.py:296
  11.9 1.6 %collective-permute-start = (bf16[192,1024]{1,0:T(8,128)(2,1)}, bf16[192,1024]{1,0:T(8,128)(2,1)}, u32[]{:S(2)}, u32[]{:S(2)}) collective-permute-start(bf16[192,1024]{1,0:T(8,128)(2,1)} %get-tuple-element.30), channel_id=1, source_target_pairs={{0,8},{8,0},{16,24},{24,16},{1,9},{9,1},{17,25},{25,17},{2,10},{10... | collective-permute-start | bytes 1179656 | tf_op jit(solution)/shard_map/ppermute | solution.py:273
  13.5 1.5 %collective-permute-start.1 = (bf16[192,1024]{1,0:T(8,128)(2,1)}, bf16[192,1024]{1,0:T(8,128)(2,1)}, u32[]{:S(2)}, u32[]{:S(2)}) collective-permute-start(bf16[192,1024]{1,0:T(8,128)(2,1)} %get-tuple-element.31), channel_id=1, source_target_pairs={{0,16},{8,24},{16,0},{24,8},{1,17},{9,25},{17,1},{25,9},{2,18},{10... | collective-permute-start | bytes 1179656 | tf_op jit(solution)/shard_map/ppermute | solution.py:273
  15.0 0.5 collective-permute-start.2
  15.5 7.9 %collective-permute-start.13 = (bf16[128,1024]{1,0:T(8,128)(2,1)}, bf16[128,1024]{1,0:T(8,128)(2,1)}, u32[]{:S(2)}, u32[]{:S(2)}) collective-permute-start(bf16[128,1024]{1,0:T(8,128)(2,1)} %get-tuple-element.33.rest_4_), channel_id=1, source_target_pairs={{0,6},{1,7},{2,4},{3,5},{4,2},{5,3},{6,0},{7,1},{8,14},{9,15},{10,... | collective-permute-start | bytes 786440 | tf_op jit(solution)/shard_map/ppermute | solution.py:267
  23.4 2.0 %pick.1 = bf16[384,768]{1,0:T(8,128)(2,1)} custom-call(s32[1,384]{1,0:T(1,128)} %bitcast.9), custom_call_target="tpu_custom_call" | custom-call | flops 399999991808 | bytes 1536 | tf_op jit(solution)/shard_map/pick/pallas_call | solution.py:240
  25.4 5.5 %collective-permute-done.9.rest_8_ = bf16[128,1024]{1,0:T(8,128)(2,1)} collective-permute-done((bf16[128,1024]{1,0:T(8,128)(2,1)}, bf16[128,1024]{1,0:T(8,128)(2,1)}, u32[]{:S(2)}, u32[]{:S(2)}) %collective-permute-start.9) | collective-permute-done | bytes 262176 | tf_op jit(solution)/shard_map/ppermute | solution.py:267
  30.9 0.5 collective-permute-start.5
  31.4 0.8 %collective-permute-done.1.rest_2_ = bf16[192,1024]{1,0:T(8,128)(2,1)} collective-permute-done((bf16[192,1024]{1,0:T(8,128)(2,1)}, bf16[192,1024]{1,0:T(8,128)(2,1)}, u32[]{:S(2)}, u32[]{:S(2)}) %collective-permute-start.1) | collective-permute-done | bytes 393248 | tf_op jit(solution)/shard_map/ppermute | solution.py:273
  32.2 1.2 %collective-permute-start.4 = (bf16[128,1024]{1,0:T(8,128)(2,1)}, bf16[128,1024]{1,0:T(8,128)(2,1)S(1)}, u32[]{:S(2)}, u32[]{:S(2)}) collective-permute-start(bf16[128,1024]{1,0:T(8,128)(2,1)} %get-tuple-element.33.rest_4_), channel_id=1, source_target_pairs={{0,2},{1,3},{2,0},{3,1},{4,6},{5,7},{6,4},{7,5},{8,10},{9,11},{10,... | collective-permute-start | bytes 786440 | tf_op jit(solution)/shard_map/ppermute | solution.py:267
  33.5 0.8 %collective-permute-start.14 = (bf16[128,1024]{1,0:T(8,128)(2,1)}, bf16[128,1024]{1,0:T(8,128)(2,1)S(1)}, u32[]{:S(2)}, u32[]{:S(2)}) collective-permute-start(bf16[128,1024]{1,0:T(8,128)(2,1)} %collective-permute-done.13.rest_10_), channel_id=1, source_target_pairs={{0,2},{1,3},{2,0},{3,1},{4,6},{5,7},{6,4},{7,5},{8,10},{9,11},{10,... | collective-permute-start | bytes 786440 | tf_op jit(solution)/shard_map/ppermute | solution.py:267
  34.3 4.0 %attend.2 = (bf16[192,512]{1,0:T(8,128)(2,1)S(1)}, bf16[192,512]{1,0:T(8,128)(2,1)}, bf16[192,512]{1,0:T(8,128)(2,1)}, bf16[192,512]{1,0:T(8,128)(2,1)S(1)}) custom-call(s32[1,8]{1,0:T(1,128)S(1)} %copy-done.11, bf16[192,1024]{1,0:T(8,128)(2,1)S(1)} %copy-done.3, bf16[192,1024]{1,0:T(8,128)(2,1)} %collective-permute-done.rest_1_, ...), custom_call_target="tpu_custom_call" | custom-call | flops 2000000000 | bytes 3670048 | tf_op jit(solution)/shard_map/attend/pallas_call | solution.py:240
  38.3 1.7 %collective-permute-start.15 = (bf16[192,512]{1,0:T(8,128)(2,1)S(1)}, bf16[192,512]{1,0:T(8,128)(2,1)S(1)}, u32[]{:S(2)}, u32[]{:S(2)}) collective-permute-start(bf16[192,512]{1,0:T(8,128)(2,1)S(1)} %get-tuple-element.40), channel_id=1, source_target_pairs={{0,24},{8,16},{16,8},{24,0},{1,25},{9,17},{17,9},{25,1},{2,26},{10... | collective-permute-start | bytes 589832 | tf_op jit(solution)/shard_map/ppermute | solution.py:273
  40.1 0.5 collective-permute-start.17
  40.6 1.0 %collective-permute-done.4.rest_6_ = bf16[128,1024]{1,0:T(8,128)(2,1)S(1)} collective-permute-done((bf16[128,1024]{1,0:T(8,128)(2,1)}, bf16[128,1024]{1,0:T(8,128)(2,1)S(1)}, u32[]{:S(2)}, u32[]{:S(2)}) %collective-permute-start.4) | collective-permute-done | bytes 262176 | tf_op jit(solution)/shard_map/ppermute | solution.py:267
  41.5 5.2 %collective-permute-done.14.rest_8_ = bf16[128,1024]{1,0:T(8,128)(2,1)S(1)} collective-permute-done((bf16[128,1024]{1,0:T(8,128)(2,1)}, bf16[128,1024]{1,0:T(8,128)(2,1)S(1)}, u32[]{:S(2)}, u32[]{:S(2)}) %collective-permute-start.14) | collective-permute-done | bytes 262176 | tf_op jit(solution)/shard_map/ppermute | solution.py:267
  46.8 0.7 copy-done.8
  47.5 0.9 %collective-permute-start.18 = (bf16[192,512]{1,0:T(8,128)(2,1)}, bf16[192,512]{1,0:T(8,128)(2,1)}, u32[]{:S(2)}, u32[]{:S(2)}) collective-permute-start(bf16[192,512]{1,0:T(8,128)(2,1)} %get-tuple-element.44), channel_id=1, source_target_pairs={{0,8},{8,0},{16,24},{24,16},{1,9},{9,1},{17,25},{25,17},{2,10},{10... | collective-permute-start | bytes 589832 | tf_op jit(solution)/shard_map/ppermute | solution.py:273
  48.4 1.5 %collective-permute-start.19 = (bf16[192,512]{1,0:T(8,128)(2,1)}, bf16[192,512]{1,0:T(8,128)(2,1)}, u32[]{:S(2)}, u32[]{:S(2)}) collective-permute-start(bf16[192,512]{1,0:T(8,128)(2,1)} %get-tuple-element.45), channel_id=1, source_target_pairs={{0,16},{8,24},{16,0},{24,8},{1,17},{9,25},{17,1},{25,9},{2,18},{10... | collective-permute-start | bytes 589832 | tf_op jit(solution)/shard_map/ppermute | solution.py:273
  49.9 4.1 %attend.3 = (bf16[192,512]{1,0:T(8,128)(2,1)S(1)}, bf16[192,512]{1,0:T(8,128)(2,1)}, bf16[192,512]{1,0:T(8,128)(2,1)}, bf16[192,512]{1,0:T(8,128)(2,1)}) custom-call(s32[1,8]{1,0:T(1,128)S(1)} %copy-done.11, bf16[192,1024]{1,0:T(8,128)(2,1)S(1)} %copy-done.3, bf16[192,1024]{1,0:T(8,128)(2,1)} %collective-permute-done.rest_1_, ...), custom_call_target="tpu_custom_call" | custom-call | flops 2000000000 | bytes 3670048 | tf_op jit(solution)/shard_map/attend/pallas_call | solution.py:240
  54.0 1.1 %collective-permute-start.20 = (bf16[192,512]{1,0:T(8,128)(2,1)}, bf16[192,512]{1,0:T(8,128)(2,1)}, u32[]{:S(2)}, u32[]{:S(2)}) collective-permute-start(bf16[192,512]{1,0:T(8,128)(2,1)} %get-tuple-element.46), channel_id=1, source_target_pairs={{0,8},{8,0},{16,24},{24,16},{1,9},{9,1},{17,25},{25,17},{2,10},{10... | collective-permute-start | bytes 589832 | tf_op jit(solution)/shard_map/ppermute | solution.py:273
  55.1 0.5 collective-permute-start.21
  55.6 1.9 %collective-permute-start.22 = (bf16[192,512]{1,0:T(8,128)(2,1)}, bf16[192,512]{1,0:T(8,128)(2,1)}, u32[]{:S(2)}, u32[]{:S(2)}) collective-permute-start(bf16[192,512]{1,0:T(8,128)(2,1)} %get-tuple-element.48), channel_id=1, source_target_pairs={{0,24},{8,16},{16,8},{24,0},{1,25},{9,17},{17,9},{25,1},{2,26},{10... | collective-permute-start | bytes 589832 | tf_op jit(solution)/shard_map/ppermute | solution.py:273
  57.5 4.2 %gate.1 = f32[384,1024]{1,0:T(8,128)} custom-call(bf16[384,1024]{1,0:T(8,128)(2,1)} %feat.1, s32[1,384]{1,0:T(1,128)} %bitcast.10, f32[1,1024]{1,0:T(1,128)} %gain_in.3, bf16[1024,2048]{1,0:T(8,128)(2,1)} %bitcast.7), custom_call_target="tpu_custom_call" | custom-call | flops 399999991808 | bytes 4986368 | tf_op jit(solution)/shard_map/gate/pallas_call | solution.py:240
  61.8 0.3 collective-permute-done.20.rest_5_
  62.1 4.0 %collective-permute-done.21.rest_6_ = bf16[192,512]{1,0:T(8,128)(2,1)} collective-permute-done((bf16[192,512]{1,0:T(8,128)(2,1)}, bf16[192,512]{1,0:T(8,128)(2,1)}, u32[]{:S(2)}, u32[]{:S(2)}) %collective-permute-start.21) | collective-permute-done | bytes 196640 | tf_op jit(solution)/shard_map/ppermute | solution.py:273
  66.2 1.4 %copy-done.12 = f32[384,1024]{1,0:T(8,128)S(1)} copy-done((f32[384,1024]{1,0:T(8,128)S(1)}, f32[384,1024]{1,0:T(8,128)}, u32[]{:S(2)}) %copy-start.12) | copy-done | bytes 1572888
  67.6 4.1 %finish.1 = bf16[384,1024]{1,0:T(8,128)(2,1)} custom-call(bf16[384,1024]{1,0:T(8,128)(2,1)S(1)} %copy-done, f32[384,1024]{1,0:T(8,128)S(1)} %copy-done.12, bf16[384,768]{1,0:T(8,128)(2,1)S(1)} %copy-done.13, f32[1,1024]{1,0:T(1,128)S(1)} %copy-done.10, bf16[1024,1024]{1,0:T(8,128)(2,1)S(1)} %bitcast.5, bf16[192,512]{1,0:T(8,128)(2,1)S(1)} %get-tuple-element.38.rest_0_, ...), custom_call_target="tpu_custom_call" | custom-call | flops 399999991808 | bytes 6623232 | tf_op jit(solution)/shard_map/finish/pallas_call | solution.py:240
  (49 shorter events, 0.1 us)
Async XLA Ops:
  1.8 10.1 %copy-start.4 = (bf16[128,1024]{1,0:T(8,128)(2,1)}, bf16[128,1024]{1,0:T(8,128)(2,1)S(1)}, u32[]{:S(2)}) copy-start(bf16[128,1024]{1,0:T(8,128)(2,1)S(1)} %get-tuple-element.34.rest_4_) | copy-start | bytes 786436
  1.8 13.7 %collective-permute-start.6 = (bf16[128,1024]{1,0:T(8,128)(2,1)S(1)}, bf16[128,1024]{1,0:T(8,128)(2,1)S(1)}, u32[]{:S(2)}, u32[]{:S(2)}) collective-permute-start(bf16[128,1024]{1,0:T(8,128)(2,1)S(1)} %get-tuple-element.34.rest_4_), channel_id=1, source_target_pairs={{0,2},{1,3},{2,0},{3,1},{4,6},{5,7},{6,4},{7,5},{8,10},{9,11},{10,... | collective-permute-start | bytes 786440 | tf_op jit(solution)/shard_map/ppermute | solution.py:267
  4.8 18.5 %collective-permute-start.8 = (bf16[128,1024]{1,0:T(8,128)(2,1)S(1)}, bf16[128,1024]{1,0:T(8,128)(2,1)}, u32[]{:S(2)}, u32[]{:S(2)}) collective-permute-start(bf16[128,1024]{1,0:T(8,128)(2,1)S(1)} %get-tuple-element.34.rest_4_), channel_id=1, source_target_pairs={{0,6},{1,7},{2,4},{3,5},{4,2},{5,3},{6,0},{7,1},{8,14},{9,15},{10,... | collective-permute-start | bytes 786440 | tf_op jit(solution)/shard_map/ppermute | solution.py:267
  11.9 13.5 %collective-permute-start = (bf16[192,1024]{1,0:T(8,128)(2,1)}, bf16[192,1024]{1,0:T(8,128)(2,1)}, u32[]{:S(2)}, u32[]{:S(2)}) collective-permute-start(bf16[192,1024]{1,0:T(8,128)(2,1)} %get-tuple-element.30), channel_id=1, source_target_pairs={{0,8},{8,0},{16,24},{24,16},{1,9},{9,1},{17,25},{25,17},{2,10},{10... | collective-permute-start | bytes 1179656 | tf_op jit(solution)/shard_map/ppermute | solution.py:273
  13.5 18.8 %collective-permute-start.1 = (bf16[192,1024]{1,0:T(8,128)(2,1)}, bf16[192,1024]{1,0:T(8,128)(2,1)}, u32[]{:S(2)}, u32[]{:S(2)}) collective-permute-start(bf16[192,1024]{1,0:T(8,128)(2,1)} %get-tuple-element.31), channel_id=1, source_target_pairs={{0,16},{8,24},{16,0},{24,8},{1,17},{9,25},{17,1},{25,9},{2,18},{10... | collective-permute-start | bytes 1179656 | tf_op jit(solution)/shard_map/ppermute | solution.py:273
  15.0 17.2 %collective-permute-start.2 = (bf16[192,1024]{1,0:T(8,128)(2,1)}, bf16[192,1024]{1,0:T(8,128)(2,1)}, u32[]{:S(2)}, u32[]{:S(2)}) collective-permute-start(bf16[192,1024]{1,0:T(8,128)(2,1)} %get-tuple-element.32), channel_id=1, source_target_pairs={{0,24},{8,16},{16,8},{24,0},{1,25},{9,17},{17,9},{25,1},{2,26},{10... | collective-permute-start | bytes 1179656 | tf_op jit(solution)/shard_map/ppermute | solution.py:273
  15.5 7.9 %copy-start.6 = (bf16[128,1024]{1,0:T(8,128)(2,1)}, bf16[128,1024]{1,0:T(8,128)(2,1)S(1)}, u32[]{:S(2)}) copy-start(bf16[128,1024]{1,0:T(8,128)(2,1)S(1)} %collective-permute-done.6.rest_6_) | copy-start | bytes 786436
  15.5 15.4 %collective-permute-start.13 = (bf16[128,1024]{1,0:T(8,128)(2,1)}, bf16[128,1024]{1,0:T(8,128)(2,1)}, u32[]{:S(2)}, u32[]{:S(2)}) collective-permute-start(bf16[128,1024]{1,0:T(8,128)(2,1)} %get-tuple-element.33.rest_4_), channel_id=1, source_target_pairs={{0,6},{1,7},{2,4},{3,5},{4,2},{5,3},{6,0},{7,1},{8,14},{9,15},{10,... | collective-permute-start | bytes 786440 | tf_op jit(solution)/shard_map/ppermute | solution.py:267
  23.3 7.6 %collective-permute-start.9 = (bf16[128,1024]{1,0:T(8,128)(2,1)}, bf16[128,1024]{1,0:T(8,128)(2,1)}, u32[]{:S(2)}, u32[]{:S(2)}) collective-permute-start(bf16[128,1024]{1,0:T(8,128)(2,1)} %collective-permute-done.8.rest_10_), channel_id=1, source_target_pairs={{0,2},{1,3},{2,0},{3,1},{4,6},{5,7},{6,4},{7,5},{8,10},{9,11},{10,... | collective-permute-start | bytes 786440 | tf_op jit(solution)/shard_map/ppermute | solution.py:267
  23.4 10.9 %copy-start.3 = (bf16[192,1024]{1,0:T(8,128)(2,1)S(1)}, bf16[192,1024]{1,0:T(8,128)(2,1)}, u32[]{:S(2)}) copy-start(bf16[192,1024]{1,0:T(8,128)(2,1)} %get-tuple-element.29.rest_0_) | copy-start | bytes 1179652
  23.4 10.9 %copy-start.11 = (s32[1,8]{1,0:T(1,128)S(1)}, s32[1,8]{1,0:T(1,128)}, u32[]{:S(2)}) copy-start(s32[1,8]{1,0:T(1,128)} %mask.3) | copy-start | bytes 100
  25.4 8.1 %collective-permute-start.7 = (bf16[128,1024]{1,0:T(8,128)(2,1)S(1)}, bf16[128,1024]{1,0:T(8,128)(2,1)S(1)}, u32[]{:S(2)}, u32[]{:S(2)}) collective-permute-start(bf16[128,1024]{1,0:T(8,128)(2,1)S(1)} %copy-done.7), channel_id=1, source_target_pairs={{0,1},{1,0},{2,3},{3,2},{4,5},{5,4},{6,7},{7,6},{8,9},{9,8},{10,11... | collective-permute-start | bytes 786440 | tf_op jit(solution)/shard_map/ppermute | solution.py:270
  30.9 3.4 %collective-permute-start.11 = (bf16[128,1024]{1,0:T(8,128)(2,1)}, bf16[128,1024]{1,0:T(8,128)(2,1)S(1)}, u32[]{:S(2)}, u32[]{:S(2)}) collective-permute-start(bf16[128,1024]{1,0:T(8,128)(2,1)} %collective-permute-done.8.rest_10_), channel_id=1, source_target_pairs={{0,1},{1,0},{2,3},{3,2},{4,5},{5,4},{6,7},{7,6},{8,9},{9,8},{10,11... | collective-permute-start | bytes 786440 | tf_op jit(solution)/shard_map/ppermute | solution.py:270
  30.9 3.4 %collective-permute-start.5 = (bf16[128,1024]{1,0:T(8,128)(2,1)S(1)}, bf16[128,1024]{1,0:T(8,128)(2,1)S(1)}, u32[]{:S(2)}, u32[]{:S(2)}) collective-permute-start(bf16[128,1024]{1,0:T(8,128)(2,1)S(1)} %copy-done.5), channel_id=1, source_target_pairs={{0,1},{1,0},{2,3},{3,2},{4,5},{5,4},{6,7},{7,6},{8,9},{9,8},{10,11... | collective-permute-start | bytes 786440 | tf_op jit(solution)/shard_map/ppermute | solution.py:270
  32.2 2.0 %collective-permute-start.10 = (bf16[128,1024]{1,0:T(8,128)(2,1)}, bf16[128,1024]{1,0:T(8,128)(2,1)S(1)}, u32[]{:S(2)}, u32[]{:S(2)}) collective-permute-start(bf16[128,1024]{1,0:T(8,128)(2,1)} %collective-permute-done.9.rest_8_), channel_id=1, source_target_pairs={{0,1},{1,0},{2,3},{3,2},{4,5},{5,4},{6,7},{7,6},{8,9},{9,8},{10,11... | collective-permute-start | bytes 786440 | tf_op jit(solution)/shard_map/ppermute | solution.py:270
  32.2 9.3 %collective-permute-start.4 = (bf16[128,1024]{1,0:T(8,128)(2,1)}, bf16[128,1024]{1,0:T(8,128)(2,1)S(1)}, u32[]{:S(2)}, u32[]{:S(2)}) collective-permute-start(bf16[128,1024]{1,0:T(8,128)(2,1)} %get-tuple-element.33.rest_4_), channel_id=1, source_target_pairs={{0,2},{1,3},{2,0},{3,1},{4,6},{5,7},{6,4},{7,5},{8,10},{9,11},{10,... | collective-permute-start | bytes 786440 | tf_op jit(solution)/shard_map/ppermute | solution.py:267
  33.5 13.3 %collective-permute-start.14 = (bf16[128,1024]{1,0:T(8,128)(2,1)}, bf16[128,1024]{1,0:T(8,128)(2,1)S(1)}, u32[]{:S(2)}, u32[]{:S(2)}) collective-permute-start(bf16[128,1024]{1,0:T(8,128)(2,1)} %collective-permute-done.13.rest_10_), channel_id=1, source_target_pairs={{0,2},{1,3},{2,0},{3,1},{4,6},{5,7},{6,4},{7,5},{8,10},{9,11},{10,... | collective-permute-start | bytes 786440 | tf_op jit(solution)/shard_map/ppermute | solution.py:267
  38.3 8.5 %collective-permute-start.15 = (bf16[192,512]{1,0:T(8,128)(2,1)S(1)}, bf16[192,512]{1,0:T(8,128)(2,1)S(1)}, u32[]{:S(2)}, u32[]{:S(2)}) collective-permute-start(bf16[192,512]{1,0:T(8,128)(2,1)S(1)} %get-tuple-element.40), channel_id=1, source_target_pairs={{0,24},{8,16},{16,8},{24,0},{1,25},{9,17},{17,9},{25,1},{2,26},{10... | collective-permute-start | bytes 589832 | tf_op jit(solution)/shard_map/ppermute | solution.py:273
  40.0 8.3 %collective-permute-start.3 = (bf16[128,1024]{1,0:T(8,128)(2,1)}, bf16[128,1024]{1,0:T(8,128)(2,1)S(1)}, u32[]{:S(2)}, u32[]{:S(2)}) collective-permute-start(bf16[128,1024]{1,0:T(8,128)(2,1)} %get-tuple-element.33.rest_4_), channel_id=1, source_target_pairs={{0,1},{1,0},{2,3},{3,2},{4,5},{5,4},{6,7},{7,6},{8,9},{9,8},{10,11... | collective-permute-start | bytes 786440 | tf_op jit(solution)/shard_map/ppermute | solution.py:270
  40.1 9.9 %collective-permute-start.17 = (bf16[128,1024]{1,0:T(8,128)(2,1)}, bf16[128,1024]{1,0:T(8,128)(2,1)S(1)}, u32[]{:S(2)}, u32[]{:S(2)}) collective-permute-start(bf16[128,1024]{1,0:T(8,128)(2,1)} %collective-permute-done.13.rest_10_), channel_id=1, source_target_pairs={{0,1},{1,0},{2,3},{3,2},{4,5},{5,4},{6,7},{7,6},{8,9},{9,8},{10,11... | collective-permute-start | bytes 786440 | tf_op jit(solution)/shard_map/ppermute | solution.py:270
  41.5 8.4 %collective-permute-start.12 = (bf16[128,1024]{1,0:T(8,128)(2,1)S(1)}, bf16[128,1024]{1,0:T(8,128)(2,1)S(1)}, u32[]{:S(2)}, u32[]{:S(2)}) collective-permute-start(bf16[128,1024]{1,0:T(8,128)(2,1)S(1)} %collective-permute-done.4.rest_6_), channel_id=1, source_target_pairs={{0,1},{1,0},{2,3},{3,2},{4,5},{5,4},{6,7},{7,6},{8,9},{9,8},{10,11... | collective-permute-start | bytes 786440 | tf_op jit(solution)/shard_map/ppermute | solution.py:270
  47.5 2.5 %collective-permute-start.16 = (bf16[128,1024]{1,0:T(8,128)(2,1)S(1)}, bf16[128,1024]{1,0:T(8,128)(2,1)S(1)}, u32[]{:S(2)}, u32[]{:S(2)}) collective-permute-start(bf16[128,1024]{1,0:T(8,128)(2,1)S(1)} %collective-permute-done.14.rest_8_), channel_id=1, source_target_pairs={{0,1},{1,0},{2,3},{3,2},{4,5},{5,4},{6,7},{7,6},{8,9},{9,8},{10,11... | collective-permute-start | bytes 786440 | tf_op jit(solution)/shard_map/ppermute | solution.py:270
  47.5 14.3 %collective-permute-start.18 = (bf16[192,512]{1,0:T(8,128)(2,1)}, bf16[192,512]{1,0:T(8,128)(2,1)}, u32[]{:S(2)}, u32[]{:S(2)}) collective-permute-start(bf16[192,512]{1,0:T(8,128)(2,1)} %get-tuple-element.44), channel_id=1, source_target_pairs={{0,8},{8,0},{16,24},{24,16},{1,9},{9,1},{17,25},{25,17},{2,10},{10... | collective-permute-start | bytes 589832 | tf_op jit(solution)/shard_map/ppermute | solution.py:273
  48.4 13.4 %collective-permute-start.19 = (bf16[192,512]{1,0:T(8,128)(2,1)}, bf16[192,512]{1,0:T(8,128)(2,1)}, u32[]{:S(2)}, u32[]{:S(2)}) collective-permute-start(bf16[192,512]{1,0:T(8,128)(2,1)} %get-tuple-element.45), channel_id=1, source_target_pairs={{0,16},{8,24},{16,0},{24,8},{1,17},{9,25},{17,1},{25,9},{2,18},{10... | collective-permute-start | bytes 589832 | tf_op jit(solution)/shard_map/ppermute | solution.py:273
  54.0 8.1 %collective-permute-start.20 = (bf16[192,512]{1,0:T(8,128)(2,1)}, bf16[192,512]{1,0:T(8,128)(2,1)}, u32[]{:S(2)}, u32[]{:S(2)}) collective-permute-start(bf16[192,512]{1,0:T(8,128)(2,1)} %get-tuple-element.46), channel_id=1, source_target_pairs={{0,8},{8,0},{16,24},{24,16},{1,9},{9,1},{17,25},{25,17},{2,10},{10... | collective-permute-start | bytes 589832 | tf_op jit(solution)/shard_map/ppermute | solution.py:273
  55.1 11.0 %collective-permute-start.21 = (bf16[192,512]{1,0:T(8,128)(2,1)}, bf16[192,512]{1,0:T(8,128)(2,1)}, u32[]{:S(2)}, u32[]{:S(2)}) collective-permute-start(bf16[192,512]{1,0:T(8,128)(2,1)} %get-tuple-element.47), channel_id=1, source_target_pairs={{0,16},{8,24},{16,0},{24,8},{1,17},{9,25},{17,1},{25,9},{2,18},{10... | collective-permute-start | bytes 589832 | tf_op jit(solution)/shard_map/ppermute | solution.py:273
  55.6 10.5 %collective-permute-start.22 = (bf16[192,512]{1,0:T(8,128)(2,1)}, bf16[192,512]{1,0:T(8,128)(2,1)}, u32[]{:S(2)}, u32[]{:S(2)}) collective-permute-start(bf16[192,512]{1,0:T(8,128)(2,1)} %get-tuple-element.48), channel_id=1, source_target_pairs={{0,24},{8,16},{16,8},{24,0},{1,25},{9,17},{17,9},{25,1},{2,26},{10... | collective-permute-start | bytes 589832 | tf_op jit(solution)/shard_map/ppermute | solution.py:273
  57.5 8.6 %copy-start = (bf16[384,1024]{1,0:T(8,128)(2,1)S(1)}, bf16[384,1024]{1,0:T(8,128)(2,1)}, u32[]{:S(2)}) copy-start(bf16[384,1024]{1,0:T(8,128)(2,1)} %feat.1) | copy-start | bytes 2359300
  57.5 8.6 %copy-start.2 = (bf16[1,1024,1024]{2,1,0:T(8,128)(2,1)S(1)}, bf16[1,1024,1024]{2,1,0:T(8,128)(2,1)}, u32[]{:S(2)}) copy-start(bf16[1,1024,1024]{2,1,0:T(8,128)(2,1)} %param.15) | copy-start | bytes 6291460
  57.5 8.6 %copy-start.9 = (bf16[192,512]{1,0:T(8,128)(2,1)S(1)}, bf16[192,512]{1,0:T(8,128)(2,1)}, u32[]{:S(2)}) copy-start(bf16[192,512]{1,0:T(8,128)(2,1)} %copy-done.8) | copy-start | bytes 589828
  57.5 8.6 %copy-start.10 = (f32[1,1024]{1,0:T(1,128)S(1)}, f32[1,1024]{1,0:T(1,128)}, u32[]{:S(2)}) copy-start(f32[1,1024]{1,0:T(1,128)} %gain.1) | copy-start | bytes 12292
  57.5 8.6 %copy-start.13 = (bf16[384,768]{1,0:T(8,128)(2,1)S(1)}, bf16[384,768]{1,0:T(8,128)(2,1)}, u32[]{:S(2)}) copy-start(bf16[384,768]{1,0:T(8,128)(2,1)} %pick.1) | copy-start | bytes 1769476
  (5 other events, 12.7 us)

commit v11 on v9

--- a/solution.py
+++ b/solution.py
@@ -9,8 +9,7 @@
 
 BLK = 128
 HEAD = 128
-OPTS = {'chunks': [4, 4], 'order': 0, 'qs': 1, 'cq': 0, 'cg': 400000000000, 'ca': 2000000000, 'cf': 400000000000, 'cp': 0, 'sw': [0, 0], 'p0': [], 'p1': [], 'm1': ['m', 'a'], 'a1': ['f', 'g'], 'g': [], 's0': [['qx'], [], ['g'], ['g', 'qx']], 's1': [[], ['s'], ['rd'], []]}
-CHUNKS = OPTS['chunks']
+CHUNKS = (4, 4)
 SLICES = 2
 VMEM_LIMIT = 32 * 1024 * 1024
 VMEM_MOST = 60 * 1024 * 1024
@@ -123,59 +122,7 @@
     gate[...] = project(copies, feat, gain, weights)
 
 
-def pack_kernel(chips, mask, *rest):
-    blocks, out = rest[:-1], rest[-1]
-    place = lax.axis_index("ctx")
-    core, z = place % 2, place // 2
-    taken = jnp.int32(0)
-    for d, block in enumerate(blocks):
-        live = mask[0, 2 * (z ^ d) + core] > 0
-
-        def take(block=block, taken=taken):
-            at = pl.multiple_of(taken * BLK, BLK)
-            out[pl.ds(at, BLK), :] = block[...]
-
-        pl.when(live)(take)
-        taken = taken + live.astype(jnp.int32)
-
-
 def attend_kernel(users, chips, mask, *rest):
-    queries, (mine, other) = rest[:users], rest[users:users + 2]
-    outs, (all_q, live_kv) = rest[users + 2:2 * users + 2], rest[2 * users + 2:]
-    cap, wide = outs[0].shape
-    core = lax.axis_index("ctx") % 2
-    count = jnp.int32(0)
-    for z in range(chips):
-        count = count + (mask[0, 2 * z + core] > 0).astype(jnp.int32)
-    for slot in range(chips):
-        at = slice(slot * BLK, (slot + 1) * BLK)
-
-        def from_mine(at=at):
-            live_kv[at, :] = mine[at, :]
-
-        def from_other(at=at, slot=slot):
-            source = pl.multiple_of(jnp.maximum(slot - count, 0) * BLK, BLK)
-            live_kv[at, :] = other[pl.ds(source, BLK), :]
-
-        pl.when(slot < count)(from_mine)
-        pl.when(slot >= count)(from_other)
-    for i, q in enumerate(queries):
-        all_q[i * cap:(i + 1) * cap, :] = q[...]
-    scale = 0.5 * HEAD ** (-0.5)
-    for head in range(wide // HEAD):
-        cols = slice(head * HEAD, (head + 1) * HEAD)
-        keys = live_kv[:, cols]
-        values = live_kv[:, wide + head * HEAD:wide + (head + 1) * HEAD]
-        scores = lax.dot_general(
-            all_q[:, cols], keys, (((1,), (1,)), ((), ())), preferred_element_type=jnp.float32
-        )
-        weight = silu_halved(scores * scale).astype(jnp.bfloat16)
-        got = jnp.dot(weight, values, preferred_element_type=jnp.float32).astype(jnp.bfloat16)
-        for i, out in enumerate(outs):
-            out[:, cols] = got[i * cap:(i + 1) * cap, :]
-
-
-def attend_blocks_kernel(users, chips, mask, *rest):
     queries = rest[:users]
     blocks = rest[users:users + 2 * chips]
     outs, (all_q, live_kv) = rest[-2 - users:-2], rest[-2:]
@@ -273,10 +220,8 @@
         return lax.optimization_barrier((value, *others))[0]
 
     def over_users(values):
-        if OPTS['order'] == 0:
-            got = [to_user(values[d], d) for d in range(users - 1, 0, -1)]
-            return [values[0]] + got[::-1]
-        return [values[0]] + [to_user(values[d], d) for d in range(1, users)]
+        got = [to_user(values[d], d) for d in range(users - 1, 0, -1)]
+        return [values[0]] + got[::-1]
 
     kv = hist_kv[0, 0]
     split = call(
@@ -301,64 +246,48 @@
             pltpu.SemaphoreType.DMA((3 + SLICES,)),
             pltpu.SemaphoreType.DMA((users,)),
         ],
-        cost_estimate=pl.CostEstimate(flops=OPTS['cq'], bytes_accessed=0, transcendentals=0),
+        cost_estimate=pl.CostEstimate(flops=0, bytes_accessed=0, transcendentals=0),
         compiler_params=pltpu.CompilerParams(vmem_limit_bytes=VMEM_MOST),
-    )(*([after(cand_feat, split[0])] if OPTS['qs'] else [cand_feat]), user_row, gain_in, w_uq[0])
+    )(after(cand_feat, split[0]), user_row, gain_in, w_uq[0])
     arrived = over_users(queries)
 
-    returned, first, env = [], 0, {}
-    env.update({'qx': arrived[1], 'qy': arrived[2], 'qd': arrived[3], 'q': queries[0]})
-
-    def gated(value, keys):
-        ready = [env[k] for k in keys]
-        return after(value, *ready) if ready else value
-
+    returned, first = [], None
     for chunk, wide in enumerate(wides):
         held = {0: split[chunk]}
         far = near = split[chunk]
         if chunk:
-            c = str(chunk - 1)
-            far = gated(far, [k + c if k in 'maf' else k for k in OPTS['m1']])
-            near = gated(near, [k + c if k in 'maf' else k for k in OPTS['a1']])
+            far = after(far, first[3], first[1])
+            near = after(near, first[2], gate)
         for d in [3, 1, 2] + list(range(4, chips)):
             held[d] = over_z(held[3], 1) if d == 2 else over_z(near if d == 1 else far, d)
-        env.update({'a' + str(chunk): held[1], 'm' + str(chunk): held[3], 'f' + str(chunk): held[2]})
         if chunk == 0:
+            first = held
             gate, pick = call(
                 functools.partial(gate_kernel, cap, users), "gate",
                 [HBM] * 4,
                 [shape(rows, width, dtype=jnp.float32), shape(rows, users * cap)],
                 operands + [pltpu.SemaphoreType.DMA((3 + SLICES,))],
-                OPTS['cg'],
-                gated(cand_feat, ['q'] + OPTS['g']), user_row, gain_in, w_uq[0], vmem=VMEM_MOST,
+                HEAVY,
+                after(cand_feat, queries[0]), user_row, gain_in, w_uq[0], vmem=VMEM_MOST,
             )
-            env['g'] = gate
-        if OPTS['sw'][chunk]:
-            keys = OPTS['p0'] if chunk == 0 else OPTS['p1']
-            packed, = call(
-                functools.partial(pack_kernel, chips), "pack",
-                [SMEM] + [whole(BLK, 2 * wide)] * chips,
-                [shape(chips * BLK, 2 * wide)], [], OPTS['cp'],
-                hist_mask, gated(held[0], keys), *[held[d] for d in range(1, chips)],
-            )
-            blocks, kernel = [packed, over_cores(packed)], attend_kernel
+            waits = {0: [arrived[1]], 2: [gate], 3: [gate, arrived[1]]}
         else:
-            blocks, kernel = [], attend_blocks_kernel
-            for d in range(chips):
-                keys = OPTS['s0' if chunk == 0 else 's1'][d % 4]
-                blocks += [held[d], over_cores(gated(held[d], keys))]
+            waits = {1: [scored[0]], 2: [returned[3]]}
+        blocks = []
+        for d in range(chips):
+            own = after(held[d], *waits[d]) if d in waits else held[d]
+            blocks += [held[d], over_cores(own)]
         scored = call(
-            functools.partial(kernel, users, chips), "attend",
-            [SMEM] + [whole(cap, wide, at=(0, chunk))] * users + [whole(*block.shape) for block in blocks],
+            functools.partial(attend_kernel, users, chips), "attend",
+            [SMEM]
+            + [whole(cap, wide, at=(0, chunk))] * users
+            + [whole(*block.shape) for block in blocks],
             [shape(cap, wide)] * users,
             [pltpu.VMEM((users * cap, wide), bf16), pltpu.VMEM((chips * BLK, 2 * wide), bf16)],
-            OPTS['ca'],
+            2 * 10**9,
             hist_mask, *arrived, *blocks,
         )
-        back = over_users(scored)
-        env.update({'s': scored[0], 'rx': back[1], 'ry': back[2], 'rd': back[3]})
-        returned += back
-        first += wide
+        returned += over_users(scored)
 
     return call(
         functools.partial(finish_kernel, users), "finish",
@@ -369,7 +298,7 @@
         + [whole(*part.shape) for part in returned],
         [shape(rows, width)],
         [pltpu.VMEM((users * cap, width), bf16)],
-        OPTS["cf"],
+        HEAVY,
         cand_feat, gate, pick, gain_attn, w_out[0], *returned,
     )[0]
 

time: 67.5 us -> 67.5 us (level)
  no operation moved by 1% of the time
where the time goes in v11:
time: 67.5 us; the launch traced here: 67.2 us
  starting transfers between devices  28.6 us (42%)
  Pallas kernels  19 us (28%)
  waiting for transfers between devices  18.3 us (27%)
  local copies, waits for them, and re-layouts  1.07 us (2%)
    ppermute x6, starting transfers between devices, over_z(): return lax.ppermute(value, 'ctx', [(c, c ^ 2 * d) for c in range(ctx)])  14.7 us
    pallas_call x5, Pallas kernels, call(): pl.pallas_call(kernel, name=name, grid=(1,), in_specs=in_specs, out_specs...  14.4 us
    ppermute x9, waiting for transfers between devices, to_user(): return lax.ppermute(value, 'users', [(u, u ^ d) for u in range(users)])  14.3 us
    ppermute x9, starting transfers between devices, to_user(): return lax.ppermute(value, 'users', [(u, u ^ d) for u in range(users)])  12.3 us
    pallas_call x1, Pallas kernels, on_device(): pl.pallas_call(functools.partial(query_kernel, cap, users), name='query',...  4.61 us
    ppermute x6, waiting for transfers between devices, over_z(): return lax.ppermute(value, 'ctx', [(c, c ^ 2 * d) for c in range(ctx)])  3.97 us
    ppermute x8, starting transfers between devices, over_cores(): return lax.ppermute(value, 'ctx', [(c, c ^ 1) for c in range(ctx)])  1.54 us
  transfers between devices with their start and end apart: 23, of which 4 were waited for; matrix products, arithmetic and copies ran while one was open for 0% of the time, Pallas kernels for 23%

profile of v11, /device:TPU:0, one launch (start us, length us, event | category | flops | bytes accessed | tf_op | source)
XLA Modules:
  0.0 67.2 jit_solution(2286925956720567241)
XLA Ops:
  0.0 1.0 %copy-done.1 = bf16[1,1,128,2048]{3,2,1,0:T(8,128)(2,1)S(1)} copy-done((bf16[1,1,128,2048]{3,2,1,0:T(8,128)(2,1)S(1)}, bf16[1,1,128,2048]{3,2,1,0:T(8,128)(2,1)}, u32[]{:S(2)}) %copy-start.1) | copy-done | bytes 524312
  1.0 0.7 %kv_split.1 = (bf16[128,1024]{1,0:T(8,128)(2,1)}, bf16[128,1024]{1,0:T(8,128)(2,1)S(1)}) custom-call(bf16[128,2048]{1,0:T(8,128)(2,1)S(1)} %bitcast.4), custom_call_target="tpu_custom_call" | custom-call | tf_op jit(solution)/shard_map/kv_split/pallas_call | solution.py:184
  1.8 5.0 %collective-permute-start.6 = (bf16[128,1024]{1,0:T(8,128)(2,1)}, bf16[128,1024]{1,0:T(8,128)(2,1)}, u32[]{:S(2)}, u32[]{:S(2)}) collective-permute-start(bf16[128,1024]{1,0:T(8,128)(2,1)} %get-tuple-element.39.rest_4_), channel_id=1, source_target_pairs={{0,6},{1,7},{2,4},{3,5},{4,2},{5,3},{6,0},{7,1},{8,14},{9,15},{10,... | collective-permute-start | bytes 786440 | tf_op jit(solution)/shard_map/ppermute | solution.py:211
  6.8 0.0 collective-permute-start.4
  6.8 4.6 %query.1 = (bf16[192,1024]{1,0:T(8,128)(2,1)}, bf16[192,1024]{1,0:T(8,128)(2,1)}, bf16[192,1024]{1,0:T(8,128)(2,1)}, bf16[192,1024]{1,0:T(8,128)(2,1)}) custom-call(bf16[384,1024]{1,0:T(8,128)(2,1)} %feat.1, s32[1,384]{1,0:T(1,128)} %bitcast.8, f32[1,1024]{1,0:T(1,128)} %gain_in.3, bf16[1024,2048]{1,0:T(8,128)(2,1)} %bitcast.6), custom_call_target="tpu_custom_call" | custom-call | tf_op jit(solution)/shard_map/query/pallas_call | solution.py:238
  11.5 1.6 %collective-permute-start = (bf16[192,1024]{1,0:T(8,128)(2,1)}, bf16[192,1024]{1,0:T(8,128)(2,1)}, u32[]{:S(2)}, u32[]{:S(2)}) collective-permute-start(bf16[192,1024]{1,0:T(8,128)(2,1)} %get-tuple-element.36), channel_id=1, source_target_pairs={{0,8},{8,0},{16,24},{24,16},{1,9},{9,1},{17,25},{25,17},{2,10},{10... | collective-permute-start | bytes 1179656 | tf_op jit(solution)/shard_map/ppermute | solution.py:217
  13.0 1.5 %collective-permute-start.1 = (bf16[192,1024]{1,0:T(8,128)(2,1)}, bf16[192,1024]{1,0:T(8,128)(2,1)}, u32[]{:S(2)}, u32[]{:S(2)}) collective-permute-start(bf16[192,1024]{1,0:T(8,128)(2,1)} %get-tuple-element.37), channel_id=1, source_target_pairs={{0,16},{8,24},{16,0},{24,8},{1,17},{9,25},{17,1},{25,9},{2,18},{10... | collective-permute-start | bytes 1179656 | tf_op jit(solution)/shard_map/ppermute | solution.py:217
  14.5 0.5 collective-permute-start.2
  15.0 3.8 %collective-permute-start.7 = (bf16[128,1024]{1,0:T(8,128)(2,1)}, bf16[128,1024]{1,0:T(8,128)(2,1)}, u32[]{:S(2)}, u32[]{:S(2)}) collective-permute-start(bf16[128,1024]{1,0:T(8,128)(2,1)} %collective-permute-done.6.rest_10_), channel_id=1, source_target_pairs={{0,2},{1,3},{2,0},{3,1},{4,6},{5,7},{6,4},{7,5},{8,10},{9,11},{10,... | collective-permute-start | bytes 786440 | tf_op jit(solution)/shard_map/ppermute | solution.py:211
  18.8 4.1 %gate.1 = (f32[384,1024]{1,0:T(8,128)}, bf16[384,768]{1,0:T(8,128)(2,1)}) custom-call(bf16[384,1024]{1,0:T(8,128)(2,1)} %feat.1, s32[1,384]{1,0:T(1,128)} %bitcast.9, f32[1,1024]{1,0:T(1,128)} %gain_in.3, bf16[1024,2048]{1,0:T(8,128)(2,1)} %bitcast.7), custom_call_target="tpu_custom_call" | custom-call | flops 399999991808 | bytes 4986368 | tf_op jit(solution)/shard_map/gate/pallas_call | solution.py:184
  22.9 2.5 %collective-permute-start.16 = (bf16[128,1024]{1,0:T(8,128)(2,1)S(1)}, bf16[128,1024]{1,0:T(8,128)(2,1)S(1)}, u32[]{:S(2)}, u32[]{:S(2)}) collective-permute-start(bf16[128,1024]{1,0:T(8,128)(2,1)S(1)} %get-tuple-element.49.rest_4_), channel_id=1, source_target_pairs={{0,6},{1,7},{2,4},{3,5},{4,2},{5,3},{6,0},{7,1},{8,14},{9,15},{10,... | collective-permute-start | bytes 786440 | tf_op jit(solution)/shard_map/ppermute | solution.py:211
  25.4 0.0 collective-permute-start.5
  25.5 0.5 collective-permute-start.3
  26.0 6.1 %collective-permute-done.1.rest_2_ = bf16[192,1024]{1,0:T(8,128)(2,1)} collective-permute-done((bf16[192,1024]{1,0:T(8,128)(2,1)}, bf16[192,1024]{1,0:T(8,128)(2,1)}, u32[]{:S(2)}, u32[]{:S(2)}) %collective-permute-start.1) | collective-permute-done | bytes 393248 | tf_op jit(solution)/shard_map/ppermute | solution.py:217
  32.1 0.5 collective-permute-start.8
  32.6 1.7 %collective-permute-start.14 = (bf16[128,1024]{1,0:T(8,128)(2,1)S(1)}, bf16[128,1024]{1,0:T(8,128)(2,1)S(1)}, u32[]{:S(2)}, u32[]{:S(2)}) collective-permute-start(bf16[128,1024]{1,0:T(8,128)(2,1)S(1)} %get-tuple-element.49.rest_4_), channel_id=1, source_target_pairs={{0,2},{1,3},{2,0},{3,1},{4,6},{5,7},{6,4},{7,5},{8,10},{9,11},{10,... | collective-permute-start | bytes 786440 | tf_op jit(solution)/shard_map/ppermute | solution.py:211
  34.3 1.6 %collective-permute-start.17 = (bf16[128,1024]{1,0:T(8,128)(2,1)S(1)}, bf16[128,1024]{1,0:T(8,128)(2,1)S(1)}, u32[]{:S(2)}, u32[]{:S(2)}) collective-permute-start(bf16[128,1024]{1,0:T(8,128)(2,1)S(1)} %collective-permute-done.16.rest_10_), channel_id=1, source_target_pairs={{0,2},{1,3},{2,0},{3,1},{4,6},{5,7},{6,4},{7,5},{8,10},{9,11},{10,... | collective-permute-start | bytes 786440 | tf_op jit(solution)/shard_map/ppermute | solution.py:211
  36.0 3.5 %attend.2 = (bf16[192,512]{1,0:T(8,128)(2,1)S(1)}, bf16[192,512]{1,0:T(8,128)(2,1)S(1)}, bf16[192,512]{1,0:T(8,128)(2,1)S(1)}, bf16[192,512]{1,0:T(8,128)(2,1)S(1)}) custom-call(s32[1,8]{1,0:T(1,128)S(1)} %copy-done.5, bf16[192,1024]{1,0:T(8,128)(2,1)S(1)} %copy-done.3, bf16[192,1024]{1,0:T(8,128)(2,1)} %collective-permute-done.rest_1_, ...), custom_call_target="tpu_custom_call" | custom-call | flops 2000000000 | bytes 3670048 | tf_op jit(solution)/shard_map/attend/pallas_call | solution.py:184
  39.5 2.5 %collective-permute-start.12 = (bf16[192,512]{1,0:T(8,128)(2,1)S(1)}, bf16[192,512]{1,0:T(8,128)(2,1)S(1)}, u32[]{:S(2)}, u32[]{:S(2)}) collective-permute-start(bf16[192,512]{1,0:T(8,128)(2,1)S(1)} %get-tuple-element.45), channel_id=1, source_target_pairs={{0,24},{8,16},{16,8},{24,0},{1,25},{9,17},{17,9},{25,1},{2,26},{10... | collective-permute-start | bytes 589832 | tf_op jit(solution)/shard_map/ppermute | solution.py:217
  42.0 0.5 collective-permute-start.19
  42.5 0.0 collective-permute-start.15
  42.5 4.0 %collective-permute-done.17.rest_8_ = bf16[128,1024]{1,0:T(8,128)(2,1)S(1)} collective-permute-done((bf16[128,1024]{1,0:T(8,128)(2,1)S(1)}, bf16[128,1024]{1,0:T(8,128)(2,1)S(1)}, u32[]{:S(2)}, u32[]{:S(2)}) %collective-permute-start.17) | collective-permute-done | bytes 262176 | tf_op jit(solution)/shard_map/ppermute | solution.py:211
  46.5 1.2 %collective-permute-start.10 = (bf16[192,512]{1,0:T(8,128)(2,1)S(1)}, bf16[192,512]{1,0:T(8,128)(2,1)S(1)}, u32[]{:S(2)}, u32[]{:S(2)}) collective-permute-start(bf16[192,512]{1,0:T(8,128)(2,1)S(1)} %get-tuple-element.43), channel_id=1, source_target_pairs={{0,8},{8,0},{16,24},{24,16},{1,9},{9,1},{17,25},{25,17},{2,10},{10... | collective-permute-start | bytes 589832 | tf_op jit(solution)/shard_map/ppermute | solution.py:217
  47.7 0.0 copy-start.7
  47.7 1.6 %collective-permute-start.11 = (bf16[192,512]{1,0:T(8,128)(2,1)S(1)}, bf16[192,512]{1,0:T(8,128)(2,1)S(1)}, u32[]{:S(2)}, u32[]{:S(2)}) collective-permute-start(bf16[192,512]{1,0:T(8,128)(2,1)S(1)} %get-tuple-element.44), channel_id=1, source_target_pairs={{0,16},{8,24},{16,0},{24,8},{1,17},{9,25},{17,1},{25,9},{2,18},{10... | collective-permute-start | bytes 589832 | tf_op jit(solution)/shard_map/ppermute | solution.py:217
  49.2 3.2 %attend.3 = (bf16[192,512]{1,0:T(8,128)(2,1)S(1)}, bf16[192,512]{1,0:T(8,128)(2,1)S(1)}, bf16[192,512]{1,0:T(8,128)(2,1)S(1)}, bf16[192,512]{1,0:T(8,128)(2,1)S(1)}) custom-call(s32[1,8]{1,0:T(1,128)S(1)} %copy-done.5, bf16[192,1024]{1,0:T(8,128)(2,1)S(1)} %copy-done.3, bf16[192,1024]{1,0:T(8,128)(2,1)} %collective-permute-done.rest_1_, ...), custom_call_target="tpu_custom_call" | custom-call | flops 2000000000 | bytes 3670048 | tf_op jit(solution)/shard_map/attend/pallas_call | solution.py:184
  52.5 1.0 %collective-permute-start.20 = (bf16[192,512]{1,0:T(8,128)(2,1)S(1)}, bf16[192,512]{1,0:T(8,128)(2,1)S(1)}, u32[]{:S(2)}, u32[]{:S(2)}) collective-permute-start(bf16[192,512]{1,0:T(8,128)(2,1)S(1)} %get-tuple-element.52), channel_id=1, source_target_pairs={{0,8},{8,0},{16,24},{24,16},{1,9},{9,1},{17,25},{25,17},{2,10},{10... | collective-permute-start | bytes 589832 | tf_op jit(solution)/shard_map/ppermute | solution.py:217
  53.4 0.8 %collective-permute-start.21 = (bf16[192,512]{1,0:T(8,128)(2,1)S(1)}, bf16[192,512]{1,0:T(8,128)(2,1)S(1)}, u32[]{:S(2)}, u32[]{:S(2)}) collective-permute-start(bf16[192,512]{1,0:T(8,128)(2,1)S(1)} %get-tuple-element.53), channel_id=1, source_target_pairs={{0,16},{8,24},{16,0},{24,8},{1,17},{9,25},{17,1},{25,9},{2,18},{10... | collective-permute-start | bytes 589832 | tf_op jit(solution)/shard_map/ppermute | solution.py:217
  54.2 1.8 %collective-permute-start.22 = (bf16[192,512]{1,0:T(8,128)(2,1)S(1)}, bf16[192,512]{1,0:T(8,128)(2,1)S(1)}, u32[]{:S(2)}, u32[]{:S(2)}) collective-permute-start(bf16[192,512]{1,0:T(8,128)(2,1)S(1)} %get-tuple-element.54), channel_id=1, source_target_pairs={{0,24},{8,16},{16,8},{24,0},{1,25},{9,17},{17,9},{25,1},{2,26},{10... | collective-permute-start | bytes 589832 | tf_op jit(solution)/shard_map/ppermute | solution.py:217
  56.0 4.3 %collective-permute-done.20.rest_5_ = bf16[192,512]{1,0:T(8,128)(2,1)S(1)} collective-permute-done((bf16[192,512]{1,0:T(8,128)(2,1)S(1)}, bf16[192,512]{1,0:T(8,128)(2,1)S(1)}, u32[]{:S(2)}, u32[]{:S(2)}) %collective-permute-start.20) | collective-permute-done | bytes 196640 | tf_op jit(solution)/shard_map/ppermute | solution.py:217
  60.3 4.0 %collective-permute-done.21.rest_6_ = bf16[192,512]{1,0:T(8,128)(2,1)S(1)} collective-permute-done((bf16[192,512]{1,0:T(8,128)(2,1)S(1)}, bf16[192,512]{1,0:T(8,128)(2,1)S(1)}, u32[]{:S(2)}, u32[]{:S(2)}) %collective-permute-start.21) | collective-permute-done | bytes 196640 | tf_op jit(solution)/shard_map/ppermute | solution.py:217
  64.3 2.9 %finish.1 = bf16[384,1024]{1,0:T(8,128)(2,1)} custom-call(bf16[384,1024]{1,0:T(8,128)(2,1)S(1)} %copy-done, f32[384,1024]{1,0:T(8,128)S(1)} %copy-done.6, bf16[384,768]{1,0:T(8,128)(2,1)S(1)} %copy-done.7, f32[1,1024]{1,0:T(1,128)S(1)} %copy-done.4, bf16[1024,1024]{1,0:T(8,128)(2,1)S(1)} %bitcast.5, bf16[192,512]{1,0:T(8,128)(2,1)S(1)} %get-tuple-element.42.rest_0_, ...), custom_call_target="tpu_custom_call" | custom-call | flops 399999991808 | bytes 6623232 | tf_op jit(solution)/shard_map/finish/pallas_call | solution.py:184
  (36 shorter events, 0.1 us)
Async XLA Ops:
  0.0 1.0 %copy-start.1 = (bf16[1,1,128,2048]{3,2,1,0:T(8,128)(2,1)S(1)}, bf16[1,1,128,2048]{3,2,1,0:T(8,128)(2,1)}, u32[]{:S(2)}) copy-start(bf16[1,1,128,2048]{3,2,1,0:T(8,128)(2,1)} %param.10) | copy-start | bytes 1572868
  1.8 13.2 %collective-permute-start.6 = (bf16[128,1024]{1,0:T(8,128)(2,1)}, bf16[128,1024]{1,0:T(8,128)(2,1)}, u32[]{:S(2)}, u32[]{:S(2)}) collective-permute-start(bf16[128,1024]{1,0:T(8,128)(2,1)} %get-tuple-element.39.rest_4_), channel_id=1, source_target_pairs={{0,6},{1,7},{2,4},{3,5},{4,2},{5,3},{6,0},{7,1},{8,14},{9,15},{10,... | collective-permute-start | bytes 786440 | tf_op jit(solution)/shard_map/ppermute | solution.py:211
  6.8 16.1 %collective-permute-start.4 = (bf16[128,1024]{1,0:T(8,128)(2,1)}, bf16[128,1024]{1,0:T(8,128)(2,1)}, u32[]{:S(2)}, u32[]{:S(2)}) collective-permute-start(bf16[128,1024]{1,0:T(8,128)(2,1)} %get-tuple-element.39.rest_4_), channel_id=1, source_target_pairs={{0,2},{1,3},{2,0},{3,1},{4,6},{5,7},{6,4},{7,5},{8,10},{9,11},{10,... | collective-permute-start | bytes 786440 | tf_op jit(solution)/shard_map/ppermute | solution.py:211
  11.5 14.0 %collective-permute-start = (bf16[192,1024]{1,0:T(8,128)(2,1)}, bf16[192,1024]{1,0:T(8,128)(2,1)}, u32[]{:S(2)}, u32[]{:S(2)}) collective-permute-start(bf16[192,1024]{1,0:T(8,128)(2,1)} %get-tuple-element.36), channel_id=1, source_target_pairs={{0,8},{8,0},{16,24},{24,16},{1,9},{9,1},{17,25},{25,17},{2,10},{10... | collective-permute-start | bytes 1179656 | tf_op jit(solution)/shard_map/ppermute | solution.py:217
  13.0 19.0 %collective-permute-start.1 = (bf16[192,1024]{1,0:T(8,128)(2,1)}, bf16[192,1024]{1,0:T(8,128)(2,1)}, u32[]{:S(2)}, u32[]{:S(2)}) collective-permute-start(bf16[192,1024]{1,0:T(8,128)(2,1)} %get-tuple-element.37), channel_id=1, source_target_pairs={{0,16},{8,24},{16,0},{24,8},{1,17},{9,25},{17,1},{25,9},{2,18},{10... | collective-permute-start | bytes 1179656 | tf_op jit(solution)/shard_map/ppermute | solution.py:217
  14.5 17.5 %collective-permute-start.2 = (bf16[192,1024]{1,0:T(8,128)(2,1)}, bf16[192,1024]{1,0:T(8,128)(2,1)}, u32[]{:S(2)}, u32[]{:S(2)}) collective-permute-start(bf16[192,1024]{1,0:T(8,128)(2,1)} %get-tuple-element.38), channel_id=1, source_target_pairs={{0,24},{8,16},{16,8},{24,0},{1,25},{9,17},{17,9},{25,1},{2,26},{10... | collective-permute-start | bytes 1179656 | tf_op jit(solution)/shard_map/ppermute | solution.py:217
  15.0 10.4 %collective-permute-start.7 = (bf16[128,1024]{1,0:T(8,128)(2,1)}, bf16[128,1024]{1,0:T(8,128)(2,1)}, u32[]{:S(2)}, u32[]{:S(2)}) collective-permute-start(bf16[128,1024]{1,0:T(8,128)(2,1)} %collective-permute-done.6.rest_10_), channel_id=1, source_target_pairs={{0,2},{1,3},{2,0},{3,1},{4,6},{5,7},{6,4},{7,5},{8,10},{9,11},{10,... | collective-permute-start | bytes 786440 | tf_op jit(solution)/shard_map/ppermute | solution.py:211
  18.8 17.2 %copy-start.3 = (bf16[192,1024]{1,0:T(8,128)(2,1)S(1)}, bf16[192,1024]{1,0:T(8,128)(2,1)}, u32[]{:S(2)}) copy-start(bf16[192,1024]{1,0:T(8,128)(2,1)} %get-tuple-element.32.rest_0_) | copy-start | bytes 1179652
  18.8 17.2 %copy-start.5 = (s32[1,8]{1,0:T(1,128)S(1)}, s32[1,8]{1,0:T(1,128)}, u32[]{:S(2)}) copy-start(s32[1,8]{1,0:T(1,128)} %mask.3) | copy-start | bytes 100
  22.9 11.4 %collective-permute-start.16 = (bf16[128,1024]{1,0:T(8,128)(2,1)S(1)}, bf16[128,1024]{1,0:T(8,128)(2,1)S(1)}, u32[]{:S(2)}, u32[]{:S(2)}) collective-permute-start(bf16[128,1024]{1,0:T(8,128)(2,1)S(1)} %get-tuple-element.49.rest_4_), channel_id=1, source_target_pairs={{0,6},{1,7},{2,4},{3,5},{4,2},{5,3},{6,0},{7,1},{8,14},{9,15},{10,... | collective-permute-start | bytes 786440 | tf_op jit(solution)/shard_map/ppermute | solution.py:211
  25.4 7.1 %collective-permute-start.5 = (bf16[128,1024]{1,0:T(8,128)(2,1)}, bf16[128,1024]{1,0:T(8,128)(2,1)S(1)}, u32[]{:S(2)}, u32[]{:S(2)}) collective-permute-start(bf16[128,1024]{1,0:T(8,128)(2,1)} %collective-permute-done.4.rest_6_), channel_id=1, source_target_pairs={{0,1},{1,0},{2,3},{3,2},{4,5},{5,4},{6,7},{7,6},{8,9},{9,8},{10,11... | collective-permute-start | bytes 786440 | tf_op jit(solution)/shard_map/ppermute | solution.py:214
  25.5 10.5 %collective-permute-start.3 = (bf16[128,1024]{1,0:T(8,128)(2,1)}, bf16[128,1024]{1,0:T(8,128)(2,1)S(1)}, u32[]{:S(2)}, u32[]{:S(2)}) collective-permute-start(bf16[128,1024]{1,0:T(8,128)(2,1)} %get-tuple-element.39.rest_4_), channel_id=1, source_target_pairs={{0,1},{1,0},{2,3},{3,2},{4,5},{5,4},{6,7},{7,6},{8,9},{9,8},{10,11... | collective-permute-start | bytes 786440 | tf_op jit(solution)/shard_map/ppermute | solution.py:214
  32.0 3.9 %collective-permute-start.9 = (bf16[128,1024]{1,0:T(8,128)(2,1)}, bf16[128,1024]{1,0:T(8,128)(2,1)S(1)}, u32[]{:S(2)}, u32[]{:S(2)}) collective-permute-start(bf16[128,1024]{1,0:T(8,128)(2,1)} %collective-permute-done.6.rest_10_), channel_id=1, source_target_pairs={{0,1},{1,0},{2,3},{3,2},{4,5},{5,4},{6,7},{7,6},{8,9},{9,8},{10,11... | collective-permute-start | bytes 786440 | tf_op jit(solution)/shard_map/ppermute | solution.py:214
  32.1 3.9 %collective-permute-start.8 = (bf16[128,1024]{1,0:T(8,128)(2,1)}, bf16[128,1024]{1,0:T(8,128)(2,1)S(1)}, u32[]{:S(2)}, u32[]{:S(2)}) collective-permute-start(bf16[128,1024]{1,0:T(8,128)(2,1)} %collective-permute-done.7.rest_8_), channel_id=1, source_target_pairs={{0,1},{1,0},{2,3},{3,2},{4,5},{5,4},{6,7},{7,6},{8,9},{9,8},{10,11... | collective-permute-start | bytes 786440 | tf_op jit(solution)/shard_map/ppermute | solution.py:214
  32.6 9.9 %collective-permute-start.14 = (bf16[128,1024]{1,0:T(8,128)(2,1)S(1)}, bf16[128,1024]{1,0:T(8,128)(2,1)S(1)}, u32[]{:S(2)}, u32[]{:S(2)}) collective-permute-start(bf16[128,1024]{1,0:T(8,128)(2,1)S(1)} %get-tuple-element.49.rest_4_), channel_id=1, source_target_pairs={{0,2},{1,3},{2,0},{3,1},{4,6},{5,7},{6,4},{7,5},{8,10},{9,11},{10,... | collective-permute-start | bytes 786440 | tf_op jit(solution)/shard_map/ppermute | solution.py:211
  34.3 12.2 %collective-permute-start.17 = (bf16[128,1024]{1,0:T(8,128)(2,1)S(1)}, bf16[128,1024]{1,0:T(8,128)(2,1)S(1)}, u32[]{:S(2)}, u32[]{:S(2)}) collective-permute-start(bf16[128,1024]{1,0:T(8,128)(2,1)S(1)} %collective-permute-done.16.rest_10_), channel_id=1, source_target_pairs={{0,2},{1,3},{2,0},{3,1},{4,6},{5,7},{6,4},{7,5},{8,10},{9,11},{10,... | collective-permute-start | bytes 786440 | tf_op jit(solution)/shard_map/ppermute | solution.py:211
  39.5 7.0 %collective-permute-start.12 = (bf16[192,512]{1,0:T(8,128)(2,1)S(1)}, bf16[192,512]{1,0:T(8,128)(2,1)S(1)}, u32[]{:S(2)}, u32[]{:S(2)}) collective-permute-start(bf16[192,512]{1,0:T(8,128)(2,1)S(1)} %get-tuple-element.45), channel_id=1, source_target_pairs={{0,24},{8,16},{16,8},{24,0},{1,25},{9,17},{17,9},{25,1},{2,26},{10... | collective-permute-start | bytes 589832 | tf_op jit(solution)/shard_map/ppermute | solution.py:217
  42.0 5.6 %collective-permute-start.13 = (bf16[128,1024]{1,0:T(8,128)(2,1)S(1)}, bf16[128,1024]{1,0:T(8,128)(2,1)S(1)}, u32[]{:S(2)}, u32[]{:S(2)}) collective-permute-start(bf16[128,1024]{1,0:T(8,128)(2,1)S(1)} %get-tuple-element.49.rest_4_), channel_id=1, source_target_pairs={{0,1},{1,0},{2,3},{3,2},{4,5},{5,4},{6,7},{7,6},{8,9},{9,8},{10,11... | collective-permute-start | bytes 786440 | tf_op jit(solution)/shard_map/ppermute | solution.py:214
  42.0 7.2 %collective-permute-start.19 = (bf16[128,1024]{1,0:T(8,128)(2,1)S(1)}, bf16[128,1024]{1,0:T(8,128)(2,1)S(1)}, u32[]{:S(2)}, u32[]{:S(2)}) collective-permute-start(bf16[128,1024]{1,0:T(8,128)(2,1)S(1)} %collective-permute-done.16.rest_10_), channel_id=1, source_target_pairs={{0,1},{1,0},{2,3},{3,2},{4,5},{5,4},{6,7},{7,6},{8,9},{9,8},{10,11... | collective-permute-start | bytes 786440 | tf_op jit(solution)/shard_map/ppermute | solution.py:214
  42.5 6.7 %collective-permute-start.15 = (bf16[128,1024]{1,0:T(8,128)(2,1)S(1)}, bf16[128,1024]{1,0:T(8,128)(2,1)S(1)}, u32[]{:S(2)}, u32[]{:S(2)}) collective-permute-start(bf16[128,1024]{1,0:T(8,128)(2,1)S(1)} %collective-permute-done.14.rest_6_), channel_id=1, source_target_pairs={{0,1},{1,0},{2,3},{3,2},{4,5},{5,4},{6,7},{7,6},{8,9},{9,8},{10,11... | collective-permute-start | bytes 786440 | tf_op jit(solution)/shard_map/ppermute | solution.py:214
  46.5 2.8 %collective-permute-start.18 = (bf16[128,1024]{1,0:T(8,128)(2,1)S(1)}, bf16[128,1024]{1,0:T(8,128)(2,1)S(1)}, u32[]{:S(2)}, u32[]{:S(2)}) collective-permute-start(bf16[128,1024]{1,0:T(8,128)(2,1)S(1)} %collective-permute-done.17.rest_8_), channel_id=1, source_target_pairs={{0,1},{1,0},{2,3},{3,2},{4,5},{5,4},{6,7},{7,6},{8,9},{9,8},{10,11... | collective-permute-start | bytes 786440 | tf_op jit(solution)/shard_map/ppermute | solution.py:214
  46.5 9.5 %collective-permute-start.10 = (bf16[192,512]{1,0:T(8,128)(2,1)S(1)}, bf16[192,512]{1,0:T(8,128)(2,1)S(1)}, u32[]{:S(2)}, u32[]{:S(2)}) collective-permute-start(bf16[192,512]{1,0:T(8,128)(2,1)S(1)} %get-tuple-element.43), channel_id=1, source_target_pairs={{0,8},{8,0},{16,24},{24,16},{1,9},{9,1},{17,25},{25,17},{2,10},{10... | collective-permute-start | bytes 589832 | tf_op jit(solution)/shard_map/ppermute | solution.py:217
  47.6 16.6 %copy-start = (bf16[384,1024]{1,0:T(8,128)(2,1)S(1)}, bf16[384,1024]{1,0:T(8,128)(2,1)}, u32[]{:S(2)}) copy-start(bf16[384,1024]{1,0:T(8,128)(2,1)} %feat.1) | copy-start | bytes 2359300
  47.6 16.6 %copy-start.2 = (bf16[1,1024,1024]{2,1,0:T(8,128)(2,1)S(1)}, bf16[1,1024,1024]{2,1,0:T(8,128)(2,1)}, u32[]{:S(2)}) copy-start(bf16[1,1024,1024]{2,1,0:T(8,128)(2,1)} %param.15) | copy-start | bytes 6291460
  47.6 16.6 %copy-start.4 = (f32[1,1024]{1,0:T(1,128)S(1)}, f32[1,1024]{1,0:T(1,128)}, u32[]{:S(2)}) copy-start(f32[1,1024]{1,0:T(1,128)} %gain.1) | copy-start | bytes 12292
  47.7 16.6 %copy-start.6 = (f32[384,1024]{1,0:T(8,128)S(1)}, f32[384,1024]{1,0:T(8,128)}, u32[]{:S(2)}) copy-start(f32[384,1024]{1,0:T(8,128)} %get-tuple-element.34.gate) | copy-start | bytes 4718596
  47.7 16.6 %copy-start.7 = (bf16[384,768]{1,0:T(8,128)(2,1)S(1)}, bf16[384,768]{1,0:T(8,128)(2,1)}, u32[]{:S(2)}) copy-start(bf16[384,768]{1,0:T(8,128)(2,1)} %get-tuple-element.35.pick) | copy-start | bytes 1769476
  47.7 8.3 %collective-permute-start.11 = (bf16[192,512]{1,0:T(8,128)(2,1)S(1)}, bf16[192,512]{1,0:T(8,128)(2,1)S(1)}, u32[]{:S(2)}, u32[]{:S(2)}) collective-permute-start(bf16[192,512]{1,0:T(8,128)(2,1)S(1)} %get-tuple-element.44), channel_id=1, source_target_pairs={{0,16},{8,24},{16,0},{24,8},{1,17},{9,25},{17,1},{25,9},{2,18},{10... | collective-permute-start | bytes 589832 | tf_op jit(solution)/shard_map/ppermute | solution.py:217
  52.5 7.8 %collective-permute-start.20 = (bf16[192,512]{1,0:T(8,128)(2,1)S(1)}, bf16[192,512]{1,0:T(8,128)(2,1)S(1)}, u32[]{:S(2)}, u32[]{:S(2)}) collective-permute-start(bf16[192,512]{1,0:T(8,128)(2,1)S(1)} %get-tuple-element.52), channel_id=1, source_target_pairs={{0,8},{8,0},{16,24},{24,16},{1,9},{9,1},{17,25},{25,17},{2,10},{10... | collective-permute-start | bytes 589832 | tf_op jit(solution)/shard_map/ppermute | solution.py:217
  53.4 10.9 %collective-permute-start.21 = (bf16[192,512]{1,0:T(8,128)(2,1)S(1)}, bf16[192,512]{1,0:T(8,128)(2,1)S(1)}, u32[]{:S(2)}, u32[]{:S(2)}) collective-permute-start(bf16[192,512]{1,0:T(8,128)(2,1)S(1)} %get-tuple-element.53), channel_id=1, source_target_pairs={{0,16},{8,24},{16,0},{24,8},{1,17},{9,25},{17,1},{25,9},{2,18},{10... | collective-permute-start | bytes 589832 | tf_op jit(solution)/shard_map/ppermute | solution.py:217
  54.2 10.0 %collective-permute-start.22 = (bf16[192,512]{1,0:T(8,128)(2,1)S(1)}, bf16[192,512]{1,0:T(8,128)(2,1)S(1)}, u32[]{:S(2)}, u32[]{:S(2)}) collective-permute-start(bf16[192,512]{1,0:T(8,128)(2,1)S(1)} %get-tuple-element.54), channel_id=1, source_target_pairs={{0,24},{8,16},{16,8},{24,0},{1,25},{9,17},{17,9},{25,1},{2,26},{10... | collective-permute-start | bytes 589832 | tf_op jit(solution)/shard_map/ppermute | solution.py:217
